TPU v7x, 32 devices: a whole 2x2x4 slice. The times are simulated.
32 devices in a mesh: group: 4 (over y, x), member: 2 (over core), space: 4 (over z).
Axes of the slice: x: 2, y: 2, z: 4, core: 2. Of those that a mesh axis runs over, the one named last changes fastest.
Arguments:
- height_velocity_tensor: float32 [256, 3, 128, 128], P(('group', 'member'), None, 'space'), may hold values from -6 to 6
- obs_values: float32 [32, 768], P(('group', 'member', 'space')), may hold values from -6 to 6
- obs_precision: float32 [32, 768], P(('group', 'member', 'space')), may hold values from 0.3 to 3
- obs_index: int32 [32, 768], P(('group', 'member', 'space')), may hold values from 0 to 1535, as said below
Outputs:
- analysis: float32 [256, 3, 128, 128], P(('group', 'member'), None, 'space')
Inputs may be any that keep to these rules, and one draw needn't show every extreme that they name: `obs_index`: each row holds 768 distinct positions among the 1536 values of its block.
All inputs are finite; a program needn't handle non-finite values.
Results may differ from a plain program's by a relative error of at most 0.00013.
Values sent between devices are 32-bit elements; how exact they have to be, the bound alone decides.
No kernel may reach another device: no remote copies, remote signals or barrier semaphores. Data moves between devices by JAX's collectives and lax.ppermute only.
A program may use at most 64 MiB of HBM per device.

v0:
```python
import math

import jax
import jax.numpy as jnp
from jax import lax
from jax.sharding import PartitionSpec as P

STEPS = 2


grav_coef = 0.4
depth_coef = 0.4


def padded(cells, sides, width):
    for axis, dim in sides:
        count = lax.axis_size(axis)
        ends = count - 1
        head = lax.slice_in_dim(cells, 0, width, axis=dim)
        tail = lax.slice_in_dim(cells, cells.shape[dim] - width, cells.shape[dim], axis=dim)
        cells = jnp.concatenate(
            [
                lax.ppermute(tail, axis, [(i, (i + 1) % count) for i in range(ends)]),
                cells,
                lax.ppermute(head, axis, [((i + 1) % count, i) for i in range(ends)]),
            ],
            axis=dim,
        )
    return cells


def across_y(field):
    return jnp.roll(field, -1, axis=-1) - jnp.roll(field, 1, axis=-1)


def make_transform(gram, pull):
    identity = jnp.eye(gram.shape[0], dtype=jnp.float32)
    factor = jnp.linalg.cholesky(identity + gram)
    inverse = jax.scipy.linalg.solve_triangular(factor, identity, lower=True)
    inner = jnp.dot(inverse, pull, precision=lax.Precision.HIGHEST)
    weights_mean = jnp.dot(inverse.T, inner, precision=lax.Precision.HIGHEST)
    return inverse + weights_mean[None, :]


def predicted_margins(height_velocity_tensor):
    height, flow_x, flow_y = (
        height_velocity_tensor[:, 0],
        height_velocity_tensor[:, 1],
        height_velocity_tensor[:, 2],
    )
    for stepped in range(STEPS):
        height_ext = padded(height, (("space", 1),), 1)
        new_x = flow_x - grav_coef * (height_ext[:, 2:] - height_ext[:, :-2])
        new_y = flow_y - grav_coef * across_y(height)
        flow_ext = padded(new_x, (("space", 1),), 1)
        height = height - depth_coef * (flow_ext[:, 2:] - flow_ext[:, :-2] + across_y(new_y))
        flow_x, flow_y = (new_x, new_y)
    return jnp.stack([height, flow_x, flow_y], axis=1)


def total_terms(first_term, second_term):
    whole_first, whole_second = lax.psum((first_term, second_term), ("group", "member", "space"))
    return (whole_first, whole_second)


def on_device(height_velocity_tensor, obs_values, obs_precision, obs_index):
    predicted_model_vector = predicted_margins(height_velocity_tensor)
    trajectory_slices, layered_quantities, horizontal_slices, vertical_slices = (
        predicted_model_vector.shape
    )
    trajectory_clusters = lax.axis_size("group") * lax.axis_size("member")
    block_cell_values = horizontal_slices * vertical_slices // trajectory_clusters
    tile_portions = predicted_model_vector.reshape(
        trajectory_slices, layered_quantities, trajectory_clusters, block_cell_values
    )
    arrived = lax.all_to_all(
        tile_portions, ("group", "member"), split_axis=2, concat_axis=0, tiled=True
    )
    members = arrived.shape[0]
    values = arrived.reshape(members, layered_quantities * block_cell_values)
    ens_mean = jnp.mean(values, axis=0)
    anomaly = values - ens_mean
    positions = obs_index[0]
    precision = obs_precision[0]
    scale = 1.0 / math.sqrt(members - 1)
    seen = jnp.take(anomaly, positions, axis=1)
    seen_mean = jnp.take(ens_mean, positions, axis=0)
    scaled = seen * precision[None, :] * scale
    innovation = precision * (obs_values[0] - seen_mean) * scale
    gram_part = jnp.dot(scaled, scaled.T, precision=lax.Precision.HIGHEST)
    pull_part = jnp.dot(scaled, innovation, precision=lax.Precision.HIGHEST)
    gram, pull = total_terms(gram_part, pull_part)
    transform = make_transform(gram, pull)
    update = jnp.dot(transform, anomaly, precision=lax.Precision.HIGHEST)
    updated = (ens_mean[None, :] + update).reshape(
        members, layered_quantities, 1, block_cell_values
    )
    returned = lax.all_to_all(updated, ("group", "member"), split_axis=0, concat_axis=2, tiled=True)
    return returned.reshape(
        trajectory_slices, layered_quantities, horizontal_slices, vertical_slices
    )


def solution(mesh):
    return jax.shard_map(
        on_device,
        mesh=mesh,
        in_specs=(
            P(("group", "member"), None, "space", None),
            P(("group", "member", "space"), None),
            P(("group", "member", "space"), None),
            P(("group", "member", "space"), None),
        ),
        out_specs=P(("group", "member"), None, "space", None),
        check_vma=False,
    )
```

profile of v0, /device:TPU:1, one launch (start us, length us, event | category | flops | bytes accessed | tf_op | source)
XLA Modules:
  0.0 427.1 jit_solution(14490233739322702113)
XLA Ops:
  8.9 2.9 copy.241
  11.7 2.7 fusion.66
  17.1 4.0 collective-permute-start.1
  21.1 2.7 copy.209
  25.3 3.8 fusion.64
  29.1 2.8 copy.243
  31.9 3.6 fusion.15
  38.0 2.8 copy.242
  40.9 2.9 copy.212
  43.7 2.9 copy.210
  46.6 4.5 %fusion.13 = f32[32,32,128]{1,0,2:T(8,128)S(1)} fusion(f32[32,32,128]{1,0,2:T(8,128)S(1)} %bitcast.93, f32[32,1,128]{1,0,2:T(8,128)} %copy.212, f32[32,1,128]{1,0,2:T(8,128)} %copy.210, f32[32,1,32,128]{2,0,3,1:T(8,128)} %copy.242), kind=kLoop, calls=%fused_computation.25 | loop fusion | flops 655360 | bytes 1605632 | tf_op jit(solution)/shard_map/sub | solution.py:53
  55.9 4.0 collective-permute-start.3
  63.5 2.9 copy.216
  66.4 2.8 copy.214
  69.2 7.1 %fusion.10 = f32[32,32,128]{1,0,2:T(8,128)S(1)} fusion(f32[32,32,128]{1,0,2:T(8,128)} %copy-done.1, f32[32,1,128]{1,0,2:T(8,128)} %copy.216, f32[32,1,128]{1,0,2:T(8,128)} %copy.214, f32[32,32,1]{1,0,2:T(8,128)S(1)} %get-tuple-element.42, f32[32,32,127]{1,0,2:T(8,128)} %get-tuple-element.44, f32[32,32,127]{1,0,2:T(8,128)} %get-tuple-element.43, ...), kind=kLoop, calls=%fused_computation.20 | loop fusion | flops 1179648 | bytes 2654208 | tf_op jit(solution)/shard_map/sub | solution.py:56
  76.3 3.8 fusion.58
  80.2 2.7 fusion.60
  82.9 2.7 copy.220
  85.5 4.0 collective-permute-start.5
  89.5 2.7 copy.218
  94.0 3.8 fusion.17
  100.0 4.2 fusion.20
  106.7 2.9 copy.221
  109.6 2.9 copy.219
  112.4 4.5 %fusion.6 = f32[32,32,128]{1,0,2:T(8,128)S(1)} fusion(f32[32,32,128]{1,0,2:T(8,128)} %copy-done.1, f32[32,32,128]{1,0,2:T(8,128)S(1)} %fusion.10, f32[32,1,128]{1,0,2:T(8,128)} %copy.221, f32[32,1,128]{1,0,2:T(8,128)} %copy.219), kind=kLoop, calls=%fused_computation.14 | loop fusion | flops 655360 | bytes 1605632 | tf_op jit(solution)/shard_map/sub | solution.py:53
  117.0 2.7 fusion.59
  119.7 2.7 copy.224
  122.4 4.0 collective-permute-start.7
  126.4 2.7 copy.222
  131.2 2.7 copy.228
  134.0 2.7 copy.227
  137.5 2.9 copy.225
  140.4 2.9 copy.223
  143.3 7.8 %fusion.3 = f32[32,32,128]{1,0,2:T(8,128)} fusion(f32[32,32,128]{1,0,2:T(8,128)S(1)} %fusion.10, f32[32,32,128]{1,0,2:T(8,128)} %copy-done.2, f32[32,1,128]{1,0,2:T(8,128)} %copy.225, f32[32,1,128]{1,0,2:T(8,128)} %copy.223, f32[32,32,1]{1,0,2:T(8,128)S(1)} %get-tuple-element.26, f32[32,32,127]{1,0,2:T(8,128)} %get-tuple-element.28, ...), kind=kLoop, calls=%fused_computation.9 | loop fusion | flops 1179648 | bytes 2654208 | tf_op jit(solution)/shard_map/sub | solution.py:56
  151.1 2.7 copy.226
  156.1 6.5 %all-to-all-start = ((f32[32,3,8,512]{3,0,1,2:T(8,128)}), f32[32,3,8,512]{3,0,1,2:T(8,128)S(1)}, u32[]{:S(2)}, u32[]{:S(2)}) async-start(f32[32,3,8,512]{3,0,1,2:T(8,128)} %copy.229), calls=%async_computation | async-start | bytes 3145728 | tf_op jit(solution)/shard_map/all_to_all | solution.py:76
  162.8 17.4 %all-to-all-done = f32[32,3,8,512]{3,0,1,2:T(8,128)S(1)} async-done(((f32[32,3,8,512]{3,0,1,2:T(8,128)}), f32[32,3,8,512]{3,0,1,2:T(8,128)S(1)}, u32[]{:S(2)}, u32[]{:S(2)}) %all-to-all-start) | async-done | bytes 1572896 | tf_op jit(solution)/shard_map/all_to_all | solution.py:76
  185.3 4.5 %gather_fusion.1 = f32[768]{0:T(1024)S(1)} fusion(f32[1536]{0:T(1024)S(1)} %div.18, s32[1024]{0:T(1024)S(1)} %pad_clamp_fusion), kind=kCustom, calls=%fused_computation.1 | custom fusion | bytes 9216 | tf_op jit(solution)/shard_map/jit(_take)/gather | solution.py:87
  189.8 2.9 gather_fusion
  192.7 4.0 fusion.24
  198.5 43.1 %psum.15 = f32[256]{0:T(256)S(1)} all-reduce(f32[256]{0:T(256)S(1)} %bitcast.102), channel_id=1, replica_groups=mesh['group'=4,'member'=2,'space'=4] {'group','member','space'}, use_global_device_ids=true, to_apply=%region_6.7 | all-reduce | flops 256 | bytes 2048 | tf_op jit(solution)/shard_map/psum | solution.py:62
  241.5 82.8 %all-reduce.3.cloned.1.call-done = f32[256,256]{0,1:T(8,128)} async-done(((f32[256,256]{0,1:T(8,128)}), f32[256,256]{0,1:T(8,128)}) %all-reduce.3.cloned.1.call-update) | async-done | bytes 262160 | tf_op jit(solution)/shard_map/psum | solution.py:62
  326.5 11.7 %cholesky.50 = f32[128,128]{1,0:T(8,128)S(1)} custom-call(f32[128,128]{1,0:T(8,128)S(1)} %cholesky.118), custom_call_target="Cholesky" | custom-call | tf_op jit(solution)/shard_map/jit(cholesky)/cholesky | solution.py:38
  338.3 9.8 %custom-call.15 = f32[1,128,128]{1,2,0:T(8,128)S(1)} custom-call(f32[1,128,128]{2,1,0:T(8,128)S(1)} %get-tuple-element.63), custom_call_target="InvertDiagBlocksLowerTriangular" | custom-call | tf_op jit(solution)/shard_map/jit(cholesky)/cholesky | solution.py:38
  348.6 11.7 %cholesky.105 = f32[128,128]{1,0:T(8,128)S(1)} custom-call(f32[128,128]{1,0:T(8,128)S(1)} %convolution_subtract_fusion.1), custom_call_target="Cholesky" | custom-call | tf_op jit(solution)/shard_map/jit(cholesky)/cholesky | solution.py:38
  362.4 5.2 %while.1 = (s32[]{:T(128)}, f32[256,256]{1,0:T(8,128)S(1)}, s32[2,2]{1,0:T(2,128)S(1)}, f32[2,128,128]{2,1,0:T(8,128)}, s32[]{:T(128)}) while((s32[]{:T(128)}, f32[256,256]{1,0:T(8,128)S(1)}, s32[2,2]{1,0:T(2,128)S(1)}, f32[2,128,128]{2,1,0:T(8,128)}, s32[]{:T(128)}) %tuple.46), condition=%wide.while_cond, body=%wide.while_body.sunk | while | flops 2 | bytes 132205 | solution.py:39
  367.6 20.7 %custom-call.16 = f32[2,128,128]{1,2,0:T(8,128)S(1)} custom-call(f32[2,128,128]{2,1,0:T(8,128)} %get-tuple-element.12), custom_call_target="InvertDiagBlocksLowerTriangular" | custom-call | tf_op jit(solution)/shard_map/jit(_solve_triangular)/triangular_solve | solution.py:39
  393.0 24.5 %all_to_all.30 = f32[256,3,1,512]{3,2,1,0:T(1,128)S(1)} all-to-all(f32[256,3,1,512]{3,2,1,0:T(1,128)S(1)} %copy.236), channel_id=1, replica_groups=mesh['group'=4,'member'=2,'space'=4] {'group','member'}, dimensions={0} | all-to-all | bytes 3145728 | tf_op jit(solution)/shard_map/all_to_all | solution.py:98
  (104 shorter events, 51.8 us)
Async XLA Ops:
  11.7 34.9 %copy-start = (f32[32,1,32,128]{2,0,3,1:T(8,128)}, f32[32,1,32,128]{2,0,3,1:T(8,128)S(1)}, u32[]{:S(2)}) copy-start(f32[32,1,32,128]{2,0,3,1:T(8,128)S(1)} %copy.241) | copy-start | bytes 1572868
  17.1 23.8 %collective-permute-start.1 = (f32[32,1,128]{2,0,1:T(8,128)S(1)}, f32[32,1,128]{2,0,1:T(8,128)S(1)}, u32[]{:S(2)}, u32[]{:S(2)}) collective-permute-start(f32[32,1,128]{2,0,1:T(8,128)S(1)} %copy.211), channel_id=1, source_target_pairs={{0,1},{1,2},{2,3},{4,5},{5,6},{6,7},{8,9},{9,10},{10,11},{12,13},{... | collective-permute-start | bytes 49160 | tf_op jit(solution)/shard_map/ppermute | solution.py:23
  23.8 20.0 %collective-permute-start = (f32[32,1,128]{2,0,1:T(8,128)S(1)}, f32[32,1,128]{2,0,1:T(8,128)S(1)}, u32[]{:S(2)}, u32[]{:S(2)}) collective-permute-start(f32[32,1,128]{2,0,1:T(8,128)S(1)} %copy.209), channel_id=1, source_target_pairs={{1,0},{2,1},{3,2},{5,4},{6,5},{7,6},{9,8},{10,9},{11,10},{13,12},{... | collective-permute-start | bytes 49160 | tf_op jit(solution)/shard_map/ppermute | solution.py:25
  35.5 2.5 copy-start.3
  51.2 2.1 copy-start.1
  55.9 7.6 %collective-permute-start.3 = (f32[32,1,128]{2,0,1:T(8,128)S(1)}, f32[32,1,128]{2,0,1:T(8,128)S(1)}, u32[]{:S(2)}, u32[]{:S(2)}) collective-permute-start(f32[32,1,128]{2,0,1:T(8,128)S(1)} %copy.215), channel_id=1, source_target_pairs={{0,1},{1,2},{2,3},{4,5},{5,6},{6,7},{8,9},{9,10},{10,11},{12,13},{... | collective-permute-start | bytes 49160 | tf_op jit(solution)/shard_map/ppermute | solution.py:23
  61.2 5.2 %collective-permute-start.2 = (f32[32,1,128]{2,0,1:T(8,128)S(1)}, f32[32,1,128]{2,0,1:T(8,128)S(1)}, u32[]{:S(2)}, u32[]{:S(2)}) collective-permute-start(f32[32,1,128]{2,0,1:T(8,128)S(1)} %copy.213), channel_id=1, source_target_pairs={{1,0},{2,1},{3,2},{5,4},{6,5},{7,6},{9,8},{10,9},{11,10},{13,12},{... | collective-permute-start | bytes 49160 | tf_op jit(solution)/shard_map/ppermute | solution.py:25
  85.5 21.2 %collective-permute-start.5 = (f32[32,1,128]{2,0,1:T(8,128)S(1)}, f32[32,1,128]{2,0,1:T(8,128)S(1)}, u32[]{:S(2)}, u32[]{:S(2)}) collective-permute-start(f32[32,1,128]{2,0,1:T(8,128)S(1)} %copy.220), channel_id=1, source_target_pairs={{0,1},{1,2},{2,3},{4,5},{5,6},{6,7},{8,9},{9,10},{10,11},{12,13},{... | collective-permute-start | bytes 49160 | tf_op jit(solution)/shard_map/ppermute | solution.py:23
  92.2 17.4 %collective-permute-start.4 = (f32[32,1,128]{2,0,1:T(8,128)S(1)}, f32[32,1,128]{2,0,1:T(8,128)S(1)}, u32[]{:S(2)}, u32[]{:S(2)}) collective-permute-start(f32[32,1,128]{2,0,1:T(8,128)S(1)} %copy.218), channel_id=1, source_target_pairs={{1,0},{2,1},{3,2},{5,4},{6,5},{7,6},{9,8},{10,9},{11,10},{13,12},{... | collective-permute-start | bytes 49160 | tf_op jit(solution)/shard_map/ppermute | solution.py:25
  93.9 3.9 copy-start.4
  93.9 4.1 copy-start.6
  94.0 4.7 %copy-start.7 = (f32[32,1,32,127]{2,0,3,1:T(8,128)S(1)}, f32[32,1,32,127]{2,0,3,1:T(8,128)}, u32[]{:S(2)}) copy-start(f32[32,1,32,127]{2,0,3,1:T(8,128)} %get-tuple-element.51) | copy-start | bytes 1560580
  94.0 6.0 %copy-start.8 = (f32[32,1,32,127]{2,0,3,1:T(8,128)S(1)}, f32[32,1,32,127]{2,0,3,1:T(8,128)}, u32[]{:S(2)}) copy-start(f32[32,1,32,127]{2,0,3,1:T(8,128)} %get-tuple-element.34) | copy-start | bytes 1560580
  97.8 6.5 %copy-start.5 = (f32[32,32,128]{1,0,2:T(8,128)}, f32[32,32,128]{1,0,2:T(8,128)S(1)}, u32[]{:S(2)}) copy-start(f32[32,32,128]{1,0,2:T(8,128)S(1)} %fusion.17) | copy-start | bytes 1572868
  117.0 2.7 copy-start.2
  122.4 15.1 %collective-permute-start.7 = (f32[32,1,128]{2,0,1:T(8,128)S(1)}, f32[32,1,128]{2,0,1:T(8,128)S(1)}, u32[]{:S(2)}, u32[]{:S(2)}) collective-permute-start(f32[32,1,128]{2,0,1:T(8,128)S(1)} %copy.224), channel_id=1, source_target_pairs={{0,1},{1,2},{2,3},{4,5},{5,6},{6,7},{8,9},{9,10},{10,11},{12,13},{... | collective-permute-start | bytes 49160 | tf_op jit(solution)/shard_map/ppermute | solution.py:23
  129.0 11.3 %collective-permute-start.6 = (f32[32,1,128]{2,0,1:T(8,128)S(1)}, f32[32,1,128]{2,0,1:T(8,128)S(1)}, u32[]{:S(2)}, u32[]{:S(2)}) collective-permute-start(f32[32,1,128]{2,0,1:T(8,128)S(1)} %copy.222), channel_id=1, source_target_pairs={{1,0},{2,1},{3,2},{5,4},{6,5},{7,6},{9,8},{10,9},{11,10},{13,12},{... | collective-permute-start | bytes 49160 | tf_op jit(solution)/shard_map/ppermute | solution.py:25
  151.1 2.8 copy-start.9
  156.1 6.5 %copy-start.11 = (f32[1,768]{1,0:T(1,128)S(1)}, f32[1,768]{1,0:T(1,128)}, u32[]{:S(2)}) copy-start(f32[1,768]{1,0:T(1,128)} %param.6) | copy-start | bytes 9220
  156.1 6.5 %copy-start.12 = (f32[1,768]{1,0:T(1,128)S(1)}, f32[1,768]{1,0:T(1,128)}, u32[]{:S(2)}) copy-start(f32[1,768]{1,0:T(1,128)} %param.5) | copy-start | bytes 9220
  156.1 6.6 %copy-start.10 = (s32[1,768]{1,0:T(1,128)S(1)}, s32[1,768]{1,0:T(1,128)}, u32[]{:S(2)}) copy-start(s32[1,768]{1,0:T(1,128)} %param.7) | copy-start | bytes 9220
  156.1 24.1 %all-to-all-start = ((f32[32,3,8,512]{3,0,1,2:T(8,128)}), f32[32,3,8,512]{3,0,1,2:T(8,128)S(1)}, u32[]{:S(2)}, u32[]{:S(2)}) async-start(f32[32,3,8,512]{3,0,1,2:T(8,128)} %copy.229), calls=%async_computation | async-start | bytes 3145728 | tf_op jit(solution)/shard_map/all_to_all | solution.py:76
  162.6 161.8 %all-reduce.3.cloned.1.call-start = ((), (), s32[]{:S(2)}) async-start(), calls=%async_computation.2 | async-start | bytes 524288 | tf_op jit(solution)/shard_map/psum | solution.py:62
Sparse Core Ops, SparseCore 0:
  196.8 127.5 all-reduce.2
where the time goes:
time: 433 us; the launch traced here: 427 us
  local copies, waits for them, and re-layouts  112 us (26%)
  waiting for transfers between devices  100 us (23%)
  other arithmetic  94.1 us (22%)
  blocking collectives  67.6 us (16%)
  starting transfers between devices  28.7 us (7%)
  between operations  15.6 us (4%)
  matrix products  9.21 us (2%)
    psum x1, waiting for transfers between devices, total_terms(): lax.psum((first_term, second_term), ('group', 'member', 'space'))  82.8 us
    psum x1, blocking collectives, total_terms(): lax.psum((first_term, second_term), ('group', 'member', 'space'))  43.1 us
    another operation x6, other arithmetic, make_transform(): factor = jnp.linalg.cholesky(identity + gram)  34 us
    all_to_all x1, blocking collectives, on_device(): lax.all_to_all(updated, ('group', 'member'), split_axis=0, concat_axis=2,...  24.5 us
    another operation x3, other arithmetic, make_transform(): inverse = jax.scipy.linalg.solve_triangular(factor, identity, lower=True)  20.7 us
    slice x8, local copies, waits for them, and re-layouts, padded(): head = lax.slice_in_dim(cells, 0, width, axis=dim)  19.5 us
    all_to_all x1, waiting for transfers between devices, on_device(): lax.all_to_all(tile_portions, ('group', 'member'), split_axis=2, concat_a...  17.4 us
    ppermute x4, starting transfers between devices, padded(): lax.ppermute(tail, axis, [(i, (i + 1) % count) for i in range(ends)])  15.9 us
  transfers between devices with their start and end apart: 10, of which 2 were waited for; matrix products, arithmetic and copies ran while one was open for 13% of the time, Pallas kernels for 0%

commit v1 on v0

v1 whole, which is shorter than its diff:
```python
import functools
import math

import jax
import jax.numpy as jnp
from jax import lax
from jax.experimental import pallas as pl
from jax.experimental.pallas import tpu as pltpu
from jax.sharding import PartitionSpec as P

STEPS = 2
GRAV = 0.4
DEPTH = 0.4
HALO = (4, 3, 2)
HALO_ROWS = sum(HALO)
LANES = 128
VMEM_LIMIT = 40 * 1024 * 1024


def whole(shape, memory_space=pltpu.VMEM):
    return pl.BlockSpec(memory_space=memory_space)


def call(kernel, out_shape, n_in, scratch=(), **kw):
    single = not isinstance(out_shape, (list, tuple))
    n_out = 1 if single else len(out_shape)
    spec = pl.BlockSpec(memory_space=pltpu.VMEM)
    return pl.pallas_call(
        kernel,
        out_shape=out_shape,
        in_specs=[spec] * n_in,
        out_specs=spec if single else [spec] * n_out,
        scratch_shapes=list(scratch),
        compiler_params=pltpu.CompilerParams(vmem_limit_bytes=VMEM_LIMIT),
        **kw,
    )


def f32(*shape):
    return jax.ShapeDtypeStruct(shape, jnp.float32)


def pack_kernel(top_ref, bottom_ref, to_prev_ref, to_next_ref):
    fields, edge = top_ref.shape[1], top_ref.shape[2]
    at = 0
    for field, rows in enumerate(HALO):
        for row in range(rows):
            to_prev_ref[at] = top_ref[:, field, row, :]
            to_next_ref[at] = bottom_ref[:, field, edge - rows + row, :]
            at += 1


def pack_edges(state):
    members, fields, rows, cols = state.shape
    edge = 8
    last = rows // edge - 1
    block = (members, fields, edge, cols)
    out = f32(HALO_ROWS, members, cols)
    out_spec = pl.BlockSpec((HALO_ROWS, members, cols), lambda i: (0, 0, 0))
    return pl.pallas_call(
        pack_kernel,
        grid=(1,),
        out_shape=[out, out],
        in_specs=[
            pl.BlockSpec(block, lambda i: (0, 0, 0, 0)),
            pl.BlockSpec(block, lambda i: (0, 0, last, 0)),
        ],
        out_specs=[out_spec, out_spec],
        compiler_params=pltpu.CompilerParams(vmem_limit_bytes=VMEM_LIMIT),
    )(state, state)


def forecast_kernel(dims, state_ref, before_ref, after_ref, out_ref):
    members, fields, rows, cols, block_rows = dims
    here = lax.axis_index("space")
    has_before = (here > 0).astype(jnp.float32)
    has_after = (here < lax.axis_size("space") - 1).astype(jnp.float32)

    def across_y(value):
        return pltpu.roll(value, cols - 1, 1) - pltpu.roll(value, 1, 1)

    def inside(value, row):
        if row < 0:
            return value * has_before
        if row >= rows:
            return value * has_after
        return value

    for first in range(0, members, 8):

        def load(field, row):
            offset = sum(HALO[:field])
            if row < 0:
                return before_ref[offset + HALO[field] + row, first : first + 8, :]
            if row >= rows:
                return after_ref[offset + row - rows, first : first + 8, :]
            start = (first * fields + field) * rows + row
            return state_ref[pl.ds(start, 8, stride=fields * rows), :]

        height, flow_x, flow_y = {}, {}, {}
        height_1, flow_x1, flow_y1 = {}, {}, {}
        flow_x2, flow_y2 = {}, {}

        def store(field, row, value):
            out_ref[row // block_rows, field * block_rows + row % block_rows, first : first + 8, :] = value

        height[-4] = load(0, -4)
        height[-3] = load(0, -3)
        for lead in range(-3, rows + 7):
            row = lead
            if row < rows + 3:
                height[row + 1] = load(0, row + 1)
                flow_x1[row] = inside(
                    load(1, row) - GRAV * (height[row + 1] - height[row - 1]), row
                )
                if -2 <= row < rows + 2:
                    flow_y1[row] = load(2, row) - GRAV * across_y(height[row])
            row = lead - 1
            if -2 <= row < rows + 2:
                height_1[row] = inside(
                    height[row]
                    - DEPTH * (flow_x1[row + 1] - flow_x1[row - 1] + across_y(flow_y1[row])),
                    row,
                )
            row = lead - 2
            if -1 <= row < rows + 1:
                flow_x2[row] = inside(
                    flow_x1[row] - GRAV * (height_1[row + 1] - height_1[row - 1]), row
                )
                if 0 <= row < rows:
                    flow_y2[row] = flow_y1[row] - GRAV * across_y(height_1[row])
                    store(1, row, flow_x2[row])
                    store(2, row, flow_y2[row])
            row = lead - 3
            if 0 <= row < rows:
                store(
                    0,
                    row,
                    height_1[row]
                    - DEPTH * (flow_x2[row + 1] - flow_x2[row - 1] + across_y(flow_y2[row])),
                )


def forecast(state, clusters):
    members, fields, rows, cols = state.shape
    block_rows = rows // clusters
    to_prev, to_next = pack_edges(state)
    count = lax.axis_size("space")
    before = lax.ppermute(to_next, "space", [(i, i + 1) for i in range(count - 1)])
    after = lax.ppermute(to_prev, "space", [(i + 1, i) for i in range(count - 1)])
    dims = (members, fields, rows, cols, block_rows)
    return call(
        functools.partial(forecast_kernel, dims),
        f32(clusters, fields * block_rows, members, cols),
        3,
    )(state.reshape(members * fields * rows, cols), before, after)


def split(value):
    high = value.astype(jnp.bfloat16)
    rest = value - high.astype(jnp.float32)
    middle = rest.astype(jnp.bfloat16)
    low = (rest - middle.astype(jnp.float32)).astype(jnp.bfloat16)
    return high, middle, low


def observed_kernel(values_ref, precision_ref, index_ref, out_ref):
    count = index_ref.shape[1]
    width = out_ref.shape[1]
    parts = list(split(precision_ref[...])) + list(split(values_ref[...]))
    pad = jnp.zeros((16 - len(parts), count), jnp.bfloat16)
    rows = jnp.concatenate(parts + [pad], axis=0)
    position = lax.broadcasted_iota(jnp.int32, (width, count), 0)
    hit = (position == index_ref[...]).astype(jnp.float32).astype(jnp.bfloat16)
    placed = lax.dot_general(
        rows, hit, (((1,), (1,)), ((), ())), preferred_element_type=jnp.float32
    )
    out_ref[0:1, :] = placed[0:1] + placed[1:2] + placed[2:3]
    out_ref[1:2, :] = placed[3:4] + placed[4:5] + placed[5:6]
    out_ref[2:8, :] = jnp.zeros((6, width), jnp.float32)


def gram_kernel(dims, forecast_ref, observed_ref, out_ref, scaled_ref):
    clusters, terms, members, cols = dims
    total = clusters * members
    scale = 1.0 / math.sqrt(total - 1)
    half = LANES
    for term in range(terms):
        at = slice(term * cols, (term + 1) * cols)
        values = forecast_ref[:, term].reshape(total, cols)
        mean = jnp.sum(values, axis=0, keepdims=True) * (1.0 / total)
        weight = observed_ref[0:1, at] * scale
        scaled_ref[0:total, at] = (values - mean) * weight
        innovation = (observed_ref[1:2, at] - mean) * weight
        scaled_ref[total : total + 8, at] = jnp.concatenate(
            [innovation, jnp.zeros((7, cols), jnp.float32)], axis=0
        )
    product = lax.dot_general(
        scaled_ref[...],
        scaled_ref[0:total, :],
        (((1,), (1,)), ((), ())),
        precision=lax.Precision.HIGHEST,
        preferred_element_type=jnp.float32,
    )
    at = 0
    for first in range(0, total, half):
        out_ref[at : at + total - first, :] = product[first:total, first : first + half]
        at += total - first
    for k, first in enumerate(range(0, total, half)):
        out_ref[at + 8 * k : at + 8 * k + 8, :] = product[total : total + 8, first : first + half]
    at += 8 * (total // half)
    if at < out_ref.shape[0]:
        out_ref[at:, :] = jnp.zeros((out_ref.shape[0] - at, half), jnp.float32)


def flip(value, axis, bits):
    return lax.ppermute(value, axis, [(i, i ^ bits) for i in range(lax.axis_size(axis))])


def total_over_devices(value):
    sizes = tuple(lax.axis_size(axis) for axis in ("group", "member", "space"))
    if sizes != (4, 2, 4):
        return lax.psum(value, ("group", "member", "space"))
    rows, cols = value.shape
    core = lax.axis_index("member")
    chip = lax.axis_index("group")
    half = rows // 2
    part = half // 4
    kept = lax.dynamic_slice_in_dim(value, core * half, half, 0)
    given = lax.dynamic_slice_in_dim(value, (1 - core) * half, half, 0)
    summed = (kept + flip(given, "member", 1)).reshape(4, part, cols)
    pieces = [lax.dynamic_index_in_dim(summed, chip ^ s, 0, False) for s in range(4)]
    piece = pieces[0] + (
        flip(pieces[1], "group", 1) + flip(pieces[2], "group", 2) + flip(pieces[3], "group", 3)
    )
    piece = piece + (flip(piece, "space", 1) + flip(piece, "space", 2) + flip(piece, "space", 3))
    got = jnp.stack([piece] + [flip(piece, "group", s) for s in (1, 2, 3)], axis=0)
    mine = jnp.concatenate(
        [lax.dynamic_index_in_dim(got, chip ^ i, 0, False) for i in range(4)], axis=0
    )
    other = flip(mine, "member", 1)
    return jnp.concatenate(
        [jnp.where(core == 0, mine, other), jnp.where(core == 0, other, mine)], axis=0
    )


def make_transform(packed, total):
    half = LANES
    columns = []
    at = 0
    for first in range(0, total, half):
        column = packed[at : at + total - first]
        columns.append(jnp.pad(column, ((first, 0), (0, 0))))
        at += total - first
    gram = jnp.concatenate(columns, axis=1)
    pull = jnp.concatenate([packed[at + 8 * k] for k in range(total // half)])
    identity = jnp.eye(total, dtype=jnp.float32)
    factor = lax.linalg.cholesky(identity + gram, symmetrize_input=False)
    inverse = jax.scipy.linalg.solve_triangular(factor, identity, lower=True)
    inner = jnp.dot(inverse, pull, precision=lax.Precision.HIGHEST)
    weights_mean = jnp.dot(inverse.T, inner, precision=lax.Precision.HIGHEST)
    return inverse + weights_mean[None, :]


def update_kernel(dims, forecast_ref, transform_ref, out_ref):
    clusters, terms, members, cols = dims
    total = clusters * members
    transform = transform_ref[...]
    step = 2
    for first in range(0, terms, step):
        some = range(first, min(first + step, terms))
        values = [forecast_ref[:, term].reshape(total, cols) for term in some]
        means = [jnp.sum(v, axis=0, keepdims=True) * (1.0 / total) for v in values]
        anomaly = jnp.concatenate([v - m for v, m in zip(values, means)], axis=1)
        updated = lax.dot_general(
            transform,
            anomaly,
            (((1,), (0,)), ((), ())),
            precision=lax.Precision.HIGHEST,
            preferred_element_type=jnp.float32,
        ) + jnp.concatenate(means, axis=1)
        for k, term in enumerate(some):
            out_ref[:, term] = updated[:, k * cols : (k + 1) * cols].reshape(clusters, members, cols)


def place_kernel(dims, in_ref, out_ref):
    clusters, fields, block_rows, members, cols = dims
    rows = clusters * block_rows
    for cluster in range(clusters):
        for field in range(fields):
            for row in range(block_rows):
                at = field * rows + cluster * block_rows + row
                out_ref[pl.ds(at, members, stride=fields * rows), :] = in_ref[
                    cluster, field * block_rows + row
                ]


def on_device(state, obs_values, obs_precision, obs_index):
    members, fields, rows, cols = state.shape
    clusters = lax.axis_size("group") * lax.axis_size("member")
    block_rows = rows // clusters
    terms = fields * block_rows
    total = clusters * members
    dims = (clusters, terms, members, cols)
    predicted = forecast(state, clusters)
    arrived = lax.all_to_all(predicted, ("group", "member"), split_axis=0, concat_axis=0, tiled=True)
    observed = call(observed_kernel, f32(8, terms * cols), 3)(obs_values, obs_precision, obs_index)
    packed = call(
        functools.partial(gram_kernel, dims),
        f32(448, LANES),
        2,
        [pltpu.VMEM((total + 8, terms * cols), jnp.float32)],
    )(arrived, observed)
    packed = total_over_devices(packed)
    transform = make_transform(packed, total)
    updated = call(
        functools.partial(update_kernel, dims), f32(clusters, terms, members, cols), 2
    )(arrived, transform)
    returned = lax.all_to_all(updated, ("group", "member"), split_axis=0, concat_axis=0, tiled=True)
    placed = call(
        functools.partial(place_kernel, (clusters, fields, block_rows, members, cols)),
        f32(members * fields * rows, cols),
        1,
    )(returned)
    return placed.reshape(members, fields, rows, cols)


def solution(mesh):
    blocks = P(("group", "member", "space"), None)
    state = P(("group", "member"), None, "space", None)
    return jax.shard_map(
        on_device,
        mesh=mesh,
        in_specs=(state, blocks, blocks, blocks),
        out_specs=state,
        check_vma=False,
    )
```

time: 433 us -> 162 us (0.37); the launches traced: 427 us -> 161 us
  local copies, waits for them, and re-layouts: 112 us -> 5.64 us
  waiting for transfers between devices: 100 us -> 31.9 us
  blocking collectives: 67.6 us -> 22.4 us
  other arithmetic: 94.1 us -> 54.2 us
  between operations: 15.6 us -> 1.58 us
  Pallas kernels: 0 us -> 14 us
  matrix products: 9.21 us -> 1.85 us
    psum x1 -> x0, waiting for transfers between devices: 82.8 us -> none  [total_terms(): lax.psum((first_term, second_term), ('group', 'member', 'space'))]
    slice x21 -> x1, local copies, waits for them, and re-layouts: 46.6 us -> 0.01 us  [make_transform(): column = packed[at:at + total - first]]
    psum x1 -> x0, blocking collectives: 43.1 us -> none  [total_terms(): lax.psum((first_term, second_term), ('group', 'member', 'space'))]
    sub x8 -> x0, other arithmetic: 37 us -> none  [the longest x2 14.9 us: predicted_margins(): height - depth_coef * (flow_ext[:, 2:] - flow_ext[:, :-2] + across_y(new_y))]
    ppermute x8 -> x0, local copies, waits for them, and re-layouts: 23 us -> none  [the longest x4 11.5 us: padded(): lax.ppermute(head, axis, [((i + 1) % count, i) for i in range(ends)])]
    ppermute x8 -> x13, waiting for transfers between devices: 0.02 us -> 15.1 us  [the longest x11 10.1 us: flip(): lax.ppermute(value, axis, [(i, i ^ bits) for i in range(lax.axis_size(axi...]
    pallas_call x0 -> x6, Pallas kernels: none -> 14 us  [the longest x1 7.28 us: forecast(): call(functools.partial(forecast_kernel, dims), f32(clusters, fields * blo...]
    unnamed x30 -> x8, local copies, waits for them, and re-layouts: 11.4 us -> 1.42 us
  transfers between devices with their start and end apart: 10 -> 14, of which waited for: 2 -> 13; matrix products, arithmetic and copies ran while one was open for 13% -> 0% of each run, Pallas kernels for 0% -> 0%
where the time goes in v1:
time: 162 us; the launch traced here: 161 us
  other arithmetic  54.2 us (33%)
  waiting for transfers between devices  31.9 us (20%)
  starting transfers between devices  28.9 us (18%)
  blocking collectives  22.4 us (14%)
  Pallas kernels  14 us (9%)
  local copies, waits for them, and re-layouts  5.64 us (3%)
  matrix products  1.85 us (1%)
    another operation x6, other arithmetic, make_transform(): factor = lax.linalg.cholesky(identity + gram, symmetrize_input=False)  34.2 us
    all_to_all x1, blocking collectives, on_device(): lax.all_to_all(updated, ('group', 'member'), split_axis=0, concat_axis=0,...  22.4 us
    another operation x3, other arithmetic, make_transform(): inverse = jax.scipy.linalg.solve_triangular(factor, identity, lower=True)  19.7 us
    ppermute x11, starting transfers between devices, flip(): lax.ppermute(value, axis, [(i, i ^ bits) for i in range(lax.axis_size(axi...  17.8 us
    all_to_all x1, waiting for transfers between devices, on_device(): lax.all_to_all(predicted, ('group', 'member'), split_axis=0, concat_axis=...  16.8 us
    ppermute x11, waiting for transfers between devices, flip(): lax.ppermute(value, axis, [(i, i ^ bits) for i in range(lax.axis_size(axi...  10.1 us
    pallas_call x1, Pallas kernels, forecast(): call(functools.partial(forecast_kernel, dims), f32(clusters, fields * blo...  7.28 us
    all_to_all x1, starting transfers between devices, on_device(): lax.all_to_all(predicted, ('group', 'member'), split_axis=0, concat_axis=...  5.72 us
  transfers between devices with their start and end apart: 14, of which 13 were waited for; matrix products, arithmetic and copies ran while one was open for 0% of the time, Pallas kernels for 0%

profile of v1, /device:TPU:1, one launch (start us, length us, event | category | flops | bytes accessed | tf_op | source)
XLA Modules:
  0.0 160.5 jit_solution(5780369672132296598)
XLA Ops:
  0.0 1.4 copy-done
  1.6 4.0 %collective-permute-start = (f32[9,32,128]{2,1,0:T(8,128)S(1)}, f32[9,32,128]{2,1,0:T(8,128)S(1)}, u32[]{:S(2)}, u32[]{:S(2)}) collective-permute-start(f32[9,32,128]{2,1,0:T(8,128)S(1)} %get-tuple-element.7), channel_id=1, source_target_pairs={{0,1},{1,2},{2,3},{4,5},{5,6},{6,7},{8,9},{9,10},{10,11},{12,13},{... | collective-permute-start | bytes 442376 | tf_op jit(solution)/shard_map/ppermute | solution.py:149
  5.7 1.3 collective-permute-start.1
  7.0 1.2 collective-permute-done.before_ref
  8.2 3.8 %collective-permute-done.1.after_ref = f32[9,32,128]{2,1,0:T(8,128)S(1)} collective-permute-done((f32[9,32,128]{2,1,0:T(8,128)S(1)}, f32[9,32,128]{2,1,0:T(8,128)S(1)}, u32[]{:S(2)}, u32[]{:S(2)}) %collective-permute-start.1) | collective-permute-done | bytes 147488 | tf_op jit(solution)/shard_map/ppermute | solution.py:150
  12.0 7.3 %shard_map.47 = f32[8,12,32,128]{3,2,1,0:T(8,128)} custom-call(f32[3072,128]{1,0:T(8,128)S(1)} %bitcast.64, f32[9,32,128]{2,1,0:T(8,128)S(1)} %collective-permute-done.before_ref, f32[9,32,128]{2,1,0:T(8,128)S(1)} %collective-permute-done.1.after_ref), custom_call_target="tpu_custom_call" | custom-call | tf_op jit(solution)/shard_map/pallas_call | solution.py:152
  19.3 5.7 %all-to-all-start = ((f32[8,12,32,128]{3,2,1,0:T(8,128)}), f32[8,12,32,128]{3,2,1,0:T(8,128)S(1)}, u32[]{:S(2)}, u32[]{:S(2)}) async-start(f32[8,12,32,128]{3,2,1,0:T(8,128)} %shard_map.47), calls=%async_computation | async-start | bytes 3145728 | tf_op jit(solution)/shard_map/all_to_all | solution.py:306
  25.0 0.7 shard_map.48.observed_ref
  25.7 16.8 %all-to-all-done.forecast_ref = f32[8,12,32,128]{3,2,1,0:T(8,128)S(1)} async-done(((f32[8,12,32,128]{3,2,1,0:T(8,128)}), f32[8,12,32,128]{3,2,1,0:T(8,128)S(1)}, u32[]{:S(2)}, u32[]{:S(2)}) %all-to-all-start) | async-done | bytes 1572896 | tf_op jit(solution)/shard_map/all_to_all | solution.py:306
  42.5 1.6 %shard_map.49 = f32[448,128]{1,0:T(8,128)S(1)} custom-call(f32[8,12,32,128]{3,2,1,0:T(8,128)S(1)} %all-to-all-done.forecast_ref, f32[8,1536]{1,0:T(8,128)S(1)} %shard_map.48.observed_ref), custom_call_target="tpu_custom_call" | custom-call | tf_op jit(solution)/shard_map/pallas_call | solution.py:308
  44.2 3.5 %collective-permute-start.2 = (f32[224,128]{1,0:T(8,128)S(1)}, f32[224,128]{1,0:T(8,128)S(1)}, u32[]{:S(2)}, u32[]{:S(2)}) collective-permute-start(f32[224,128]{1,0:T(8,128)S(1)} %constant_dynamic-slice_fusion.1), channel_id=1, source_target_pairs={{0,4},{4,0},{1,5},{5,1},{2,6},{6,2},{3,7},{7,3},{8,12},{12,8},{9,1... | collective-permute-start | bytes 344072 | tf_op jit(solution)/shard_map/ppermute | solution.py:217
  47.8 1.0 collective-permute-done.2
  48.8 0.3 collective-permute-start.3
  49.1 0.4 collective-permute-start.4
  49.4 2.0 %collective-permute-start.5 = (f32[56,128]{1,0:T(8,128)S(1)}, f32[56,128]{1,0:T(8,128)S(1)}, u32[]{:S(2)}, u32[]{:S(2)}) collective-permute-start(f32[56,128]{1,0:T(8,128)S(1)} %get-tuple-element.36), channel_id=1, source_target_pairs={{0,24},{8,16},{16,8},{24,0},{1,25},{9,17},{17,9},{25,1},{2,26},{10... | collective-permute-start | bytes 86024 | tf_op jit(solution)/shard_map/ppermute | solution.py:217
  51.6 0.2 collective-permute-done.4
  51.8 1.4 collective-permute-done.5
  53.2 1.4 collective-permute-start.6
  54.5 1.1 collective-permute-start.7
  55.6 1.2 collective-permute-start.8
  56.8 1.7 %collective-permute-done.7 = f32[56,128]{1,0:T(8,128)S(1)} collective-permute-done((f32[56,128]{1,0:T(8,128)S(1)}, f32[56,128]{1,0:T(8,128)S(1)}, u32[]{:S(2)}, u32[]{:S(2)}) %collective-permute-start.7) | collective-permute-done | bytes 28704 | tf_op jit(solution)/shard_map/ppermute | solution.py:217
  58.5 1.7 %collective-permute-done.8 = f32[56,128]{1,0:T(8,128)S(1)} collective-permute-done((f32[56,128]{1,0:T(8,128)S(1)}, f32[56,128]{1,0:T(8,128)S(1)}, u32[]{:S(2)}, u32[]{:S(2)}) %collective-permute-start.8) | collective-permute-done | bytes 28704 | tf_op jit(solution)/shard_map/ppermute | solution.py:217
  60.2 1.2 collective-permute-start.9
  61.4 1.0 collective-permute-start.10
  62.4 0.5 collective-permute-start.11
  63.1 1.0 collective-permute-done.10
  64.1 1.9 %collective-permute-done.11 = f32[56,128]{1,0:T(8,128)S(1)} collective-permute-done((f32[56,128]{1,0:T(8,128)S(1)}, f32[56,128]{1,0:T(8,128)S(1)}, u32[]{:S(2)}, u32[]{:S(2)}) %collective-permute-start.11) | collective-permute-done | bytes 28704 | tf_op jit(solution)/shard_map/ppermute | solution.py:217
  66.1 5.3 %collective-permute-start.12 = (f32[224,128]{1,0:T(8,128)S(1)}, f32[224,128]{1,0:T(8,128)S(1)}, u32[]{:S(2)}, u32[]{:S(2)}) collective-permute-start(f32[224,128]{1,0:T(8,128)S(1)} %pad_maximum_fusion.5), channel_id=1, source_target_pairs={{0,4},{4,0},{1,5},{5,1},{2,6},{6,2},{3,7},{7,3},{8,12},{12,8},{9,1... | collective-permute-start | bytes 344072 | tf_op jit(solution)/shard_map/ppermute | solution.py:217
  71.4 0.9 collective-permute-done.12
  72.5 11.7 %cholesky.50 = f32[128,128]{1,0:T(8,128)S(1)} custom-call(f32[128,128]{1,0:T(8,128)S(1)} %cholesky.118), custom_call_target="Cholesky" | custom-call | tf_op jit(solution)/shard_map/cholesky | solution.py:258
  84.2 9.8 %custom-call.12 = f32[1,128,128]{1,2,0:T(8,128)S(1)} custom-call(f32[1,128,128]{2,1,0:T(8,128)S(1)} %get-tuple-element.41), custom_call_target="InvertDiagBlocksLowerTriangular" | custom-call | tf_op jit(solution)/shard_map/cholesky | solution.py:258
  94.3 0.3 convolution_subtract_fusion.1
  94.5 11.9 %cholesky.105 = f32[128,128]{1,0:T(8,128)S(1)} custom-call(f32[128,128]{1,0:T(8,128)S(1)} %convolution_subtract_fusion.1), custom_call_target="Cholesky" | custom-call | tf_op jit(solution)/shard_map/cholesky | solution.py:258
  106.5 0.7 compare_reduce_fusion
  108.7 4.1 %while.1 = (s32[]{:T(128)}, f32[256,256]{1,0:T(8,128)S(1)}, s32[2,2]{1,0:T(2,128)S(1)}, f32[2,128,128]{2,1,0:T(8,128)S(1)}, s32[]{:T(128)}) while((s32[]{:T(128)}, f32[256,256]{1,0:T(8,128)S(1)}, s32[2,2]{1,0:T(2,128)S(1)}, f32[2,128,128]{2,1,0:T(8,128)S(1)}, s32[]{:T(128)}) %tuple.30), condition=%wide.while_cond, body=%wide.while_body.sunk | while | flops 2 | bytes 131181 | solution.py:259
  108.7 0.6 fusion.22
  109.3 1.4 bitcast_dynamic-update-slice_fusion.2
  110.7 0.6 fusion.22
  111.3 1.4 bitcast_dynamic-update-slice_fusion.2
  112.8 19.7 %custom-call.13 = f32[2,128,128]{1,2,0:T(8,128)S(1)} custom-call(f32[2,128,128]{2,1,0:T(8,128)S(1)} %get-tuple-element.16), custom_call_target="InvertDiagBlocksLowerTriangular" | custom-call | tf_op jit(solution)/shard_map/jit(_solve_triangular)/triangular_solve | solution.py:259
  132.4 0.3 fusion.4
  132.7 0.3 convolution_subtract_fusion
  133.0 0.3 fusion.8
  133.3 0.3 convolution_bitcast_fusion
  133.6 0.3 fusion.1
  133.9 1.6 shard_map.50
  135.5 22.4 %all_to_all.10.in_ref = f32[8,12,32,128]{3,2,1,0:T(8,128)S(1)} all-to-all(f32[8,12,32,128]{3,2,1,0:T(8,128)S(1)} %shard_map.50), channel_id=1, replica_groups=mesh['group'=4,'member'=2,'space'=4] {'group','member'}, dimensions={0} | all-to-all | bytes 3145728 | tf_op jit(solution)/shard_map/all_to_all | solution.py:319
  157.9 2.6 %shard_map.51 = f32[3072,128]{1,0:T(8,128)} custom-call(f32[8,12,32,128]{3,2,1,0:T(8,128)S(1)} %all_to_all.10.in_ref), custom_call_target="tpu_custom_call" | custom-call | tf_op jit(solution)/shard_map/pallas_call | solution.py:320
  (38 shorter events, 1.2 us)
Async XLA Ops:
  0.0 1.4 copy-start
  1.6 6.5 %collective-permute-start = (f32[9,32,128]{2,1,0:T(8,128)S(1)}, f32[9,32,128]{2,1,0:T(8,128)S(1)}, u32[]{:S(2)}, u32[]{:S(2)}) collective-permute-start(f32[9,32,128]{2,1,0:T(8,128)S(1)} %get-tuple-element.7), channel_id=1, source_target_pairs={{0,1},{1,2},{2,3},{4,5},{5,6},{6,7},{8,9},{9,10},{10,11},{12,13},{... | collective-permute-start | bytes 442376 | tf_op jit(solution)/shard_map/ppermute | solution.py:149
  5.7 6.3 %collective-permute-start.1 = (f32[9,32,128]{2,1,0:T(8,128)S(1)}, f32[9,32,128]{2,1,0:T(8,128)S(1)}, u32[]{:S(2)}, u32[]{:S(2)}) collective-permute-start(f32[9,32,128]{2,1,0:T(8,128)S(1)} %get-tuple-element.8), channel_id=1, source_target_pairs={{1,0},{2,1},{3,2},{5,4},{6,5},{7,6},{9,8},{10,9},{11,10},{13,12},{... | collective-permute-start | bytes 442376 | tf_op jit(solution)/shard_map/ppermute | solution.py:150
  19.3 5.7 %copy-start.1 = (f32[1,768]{1,0:T(1,128)S(1)}, f32[1,768]{1,0:T(1,128)}, u32[]{:S(2)}) copy-start(f32[1,768]{1,0:T(1,128)} %values_ref.1) | copy-start | bytes 9220
  19.3 5.7 %copy-start.2 = (f32[1,768]{1,0:T(1,128)S(1)}, f32[1,768]{1,0:T(1,128)}, u32[]{:S(2)}) copy-start(f32[1,768]{1,0:T(1,128)} %precision_ref.1) | copy-start | bytes 9220
  19.3 5.7 %copy-start.3 = (s32[1,768]{1,0:T(1,128)S(1)}, s32[1,768]{1,0:T(1,128)}, u32[]{:S(2)}) copy-start(s32[1,768]{1,0:T(1,128)} %index_ref.1) | copy-start | bytes 9220
  19.3 23.3 %all-to-all-start = ((f32[8,12,32,128]{3,2,1,0:T(8,128)}), f32[8,12,32,128]{3,2,1,0:T(8,128)S(1)}, u32[]{:S(2)}, u32[]{:S(2)}) async-start(f32[8,12,32,128]{3,2,1,0:T(8,128)} %shard_map.47), calls=%async_computation | async-start | bytes 3145728 | tf_op jit(solution)/shard_map/all_to_all | solution.py:306
  44.2 4.5 %collective-permute-start.2 = (f32[224,128]{1,0:T(8,128)S(1)}, f32[224,128]{1,0:T(8,128)S(1)}, u32[]{:S(2)}, u32[]{:S(2)}) collective-permute-start(f32[224,128]{1,0:T(8,128)S(1)} %constant_dynamic-slice_fusion.1), channel_id=1, source_target_pairs={{0,4},{4,0},{1,5},{5,1},{2,6},{6,2},{3,7},{7,3},{8,12},{12,8},{9,1... | collective-permute-start | bytes 344072 | tf_op jit(solution)/shard_map/ppermute | solution.py:217
  48.8 2.8 %collective-permute-start.3 = (f32[56,128]{1,0:T(8,128)S(1)}, f32[56,128]{1,0:T(8,128)S(1)}, u32[]{:S(2)}, u32[]{:S(2)}) collective-permute-start(f32[56,128]{1,0:T(8,128)S(1)} %get-tuple-element.37), channel_id=1, source_target_pairs={{0,8},{8,0},{16,24},{24,16},{1,9},{9,1},{17,25},{25,17},{2,10},{10... | collective-permute-start | bytes 86024 | tf_op jit(solution)/shard_map/ppermute | solution.py:217
  49.1 2.7 %collective-permute-start.4 = (f32[56,128]{1,0:T(8,128)S(1)}, f32[56,128]{1,0:T(8,128)S(1)}, u32[]{:S(2)}, u32[]{:S(2)}) collective-permute-start(f32[56,128]{1,0:T(8,128)S(1)} %get-tuple-element.35), channel_id=1, source_target_pairs={{0,16},{8,24},{16,0},{24,8},{1,17},{9,25},{17,1},{25,9},{2,18},{10... | collective-permute-start | bytes 86024 | tf_op jit(solution)/shard_map/ppermute | solution.py:217
  49.4 3.7 %collective-permute-start.5 = (f32[56,128]{1,0:T(8,128)S(1)}, f32[56,128]{1,0:T(8,128)S(1)}, u32[]{:S(2)}, u32[]{:S(2)}) collective-permute-start(f32[56,128]{1,0:T(8,128)S(1)} %get-tuple-element.36), channel_id=1, source_target_pairs={{0,24},{8,16},{16,8},{24,0},{1,25},{9,17},{17,9},{25,1},{2,26},{10... | collective-permute-start | bytes 86024 | tf_op jit(solution)/shard_map/ppermute | solution.py:217
  53.2 3.6 %collective-permute-start.6 = (f32[56,128]{1,0:T(8,128)S(1)}, f32[56,128]{1,0:T(8,128)S(1)}, u32[]{:S(2)}, u32[]{:S(2)}) collective-permute-start(f32[56,128]{1,0:T(8,128)S(1)} %bitcast_add_fusion), channel_id=1, source_target_pairs={{0,1},{1,0},{2,3},{3,2},{4,5},{5,4},{6,7},{7,6},{8,9},{9,8},{10,11... | collective-permute-start | bytes 86024 | tf_op jit(solution)/shard_map/ppermute | solution.py:217
  54.5 3.9 %collective-permute-start.7 = (f32[56,128]{1,0:T(8,128)S(1)}, f32[56,128]{1,0:T(8,128)S(1)}, u32[]{:S(2)}, u32[]{:S(2)}) collective-permute-start(f32[56,128]{1,0:T(8,128)S(1)} %bitcast_add_fusion), channel_id=1, source_target_pairs={{0,2},{1,3},{2,0},{3,1},{4,6},{5,7},{6,4},{7,5},{8,10},{9,11},{10,... | collective-permute-start | bytes 86024 | tf_op jit(solution)/shard_map/ppermute | solution.py:217
  55.6 4.6 %collective-permute-start.8 = (f32[56,128]{1,0:T(8,128)S(1)}, f32[56,128]{1,0:T(8,128)S(1)}, u32[]{:S(2)}, u32[]{:S(2)}) collective-permute-start(f32[56,128]{1,0:T(8,128)S(1)} %bitcast_add_fusion), channel_id=1, source_target_pairs={{0,3},{1,2},{2,1},{3,0},{4,7},{5,6},{6,5},{7,4},{8,11},{9,10},{10,... | collective-permute-start | bytes 86024 | tf_op jit(solution)/shard_map/ppermute | solution.py:217
  60.2 2.9 %collective-permute-start.9 = (f32[56,128]{1,0:T(8,128)S(1)}, f32[56,128]{1,0:T(8,128)S(1)}, u32[]{:S(2)}, u32[]{:S(2)}) collective-permute-start(f32[56,128]{1,0:T(8,128)S(1)} %add_add_fusion), channel_id=1, source_target_pairs={{0,8},{8,0},{16,24},{24,16},{1,9},{9,1},{17,25},{25,17},{2,10},{10... | collective-permute-start | bytes 86024 | tf_op jit(solution)/shard_map/ppermute | solution.py:217
  61.4 2.7 %collective-permute-start.10 = (f32[56,128]{1,0:T(8,128)S(1)}, f32[56,128]{1,0:T(8,128)S(1)}, u32[]{:S(2)}, u32[]{:S(2)}) collective-permute-start(f32[56,128]{1,0:T(8,128)S(1)} %add_add_fusion), channel_id=1, source_target_pairs={{0,16},{8,24},{16,0},{24,8},{1,17},{9,25},{17,1},{25,9},{2,18},{10... | collective-permute-start | bytes 86024 | tf_op jit(solution)/shard_map/ppermute | solution.py:217
  62.4 3.6 %collective-permute-start.11 = (f32[56,128]{1,0:T(8,128)S(1)}, f32[56,128]{1,0:T(8,128)S(1)}, u32[]{:S(2)}, u32[]{:S(2)}) collective-permute-start(f32[56,128]{1,0:T(8,128)S(1)} %add_add_fusion), channel_id=1, source_target_pairs={{0,24},{8,16},{16,8},{24,0},{1,25},{9,17},{17,9},{25,1},{2,26},{10... | collective-permute-start | bytes 86024 | tf_op jit(solution)/shard_map/ppermute | solution.py:217
  66.1 6.2 %collective-permute-start.12 = (f32[224,128]{1,0:T(8,128)S(1)}, f32[224,128]{1,0:T(8,128)S(1)}, u32[]{:S(2)}, u32[]{:S(2)}) collective-permute-start(f32[224,128]{1,0:T(8,128)S(1)} %pad_maximum_fusion.5), channel_id=1, source_target_pairs={{0,4},{4,0},{1,5},{5,1},{2,6},{6,2},{3,7},{7,3},{8,12},{12,8},{9,1... | collective-permute-start | bytes 344072 | tf_op jit(solution)/shard_map/ppermute | solution.py:217

commit v2 on v1

--- a/solution.py
+++ b/solution.py
@@ -244,27 +244,131 @@
     )
 
 
-def make_transform(packed, total):
+def product(left, right, contract):
+    return lax.dot_general(
+        left,
+        right,
+        (contract, ((), ())),
+        precision=lax.Precision.HIGHEST,
+        preferred_element_type=jnp.float32,
+    )
+
+
+def inverse_factor(block):
+    size = block.shape[0]
+    tile = 8
+    count = size // tile
+    rows = [block[at : at + tile, :] for at in range(0, size, tile)]
+    lane = lax.broadcasted_iota(jnp.int32, (tile, size), 1)
+    sublane = lax.broadcasted_iota(jnp.int32, (tile, size), 0)
+
+    def row(value, at):
+        return jnp.broadcast_to(value[at : at + 1, :], (tile, size))
+
+    def column(value, at):
+        return jnp.broadcast_to(value[:, at : at + 1], (tile, size))
+
+    for own in range(count):
+        start = own * tile
+        columns = [[column(value, start + k) for k in range(tile)] for value in rows[own:]]
+        pivots = (lane >= start) & (lane < start + tile)
+        cleared = [jnp.where(pivots, 0.0, value) for value in rows[own:]]
+        local = columns[0]
+        right = jnp.where(lane - start == sublane, 1.0, cleared[0])
+        done = right
+        solved = []
+        for p in range(0, tile, 2):
+            s00, s10, s11 = row(local[p], p), row(local[p], p + 1), row(local[p + 1], p + 1)
+            inv0 = 1.0 / s00
+            inv1 = s00 * (1.0 / (s00 * s11 - s10 * s10))
+            low = s10 * inv0
+            upper = []
+            for k in range(p + 2, tile):
+                u0 = row(local[k], p)
+                upper.append((u0 * inv0, (row(local[k], p + 1) - low * u0) * inv1))
+            r0 = row(right, p)
+            r1 = row(right, p + 1) - low * r0
+            solved += [r0 * inv0, r1 * inv1]
+            done = jnp.where(sublane == p, r0 * lax.rsqrt(s00), done)
+            done = jnp.where(sublane == p + 1, r1 * (inv1 * lax.rsqrt(inv1)), done)
+            for value in columns:
+                value[p + 1] = value[p + 1] - low * value[p]
+                for k, (u0, u1) in zip(range(p + 2, tile), upper):
+                    value[k] = value[k] - (value[p] * u0 + value[p + 1] * u1)
+            if p + 2 < tile:
+                right = right - (local[p] * solved[p] + local[p + 1] * solved[p + 1])
+        rows[own] = jnp.where(lane - start <= sublane, done, 0.0)
+        for k in range(own + 1, count):
+            terms = [left * value for left, value in zip(columns[k - own], solved)]
+            while len(terms) > 1:
+                terms = [x + y for x, y in zip(terms[::2], terms[1::2])]
+            rows[k] = cleared[k - own] - terms[0]
+    return jnp.concatenate(rows, axis=0)
+
+
+def transform_of(packed_ref, total):
     half = LANES
-    columns = []
-    at = 0
-    for first in range(0, total, half):
-        column = packed[at : at + total - first]
-        columns.append(jnp.pad(column, ((first, 0), (0, 0))))
-        at += total - first
-    gram = jnp.concatenate(columns, axis=1)
-    pull = jnp.concatenate([packed[at + 8 * k] for k in range(total // half)])
-    identity = jnp.eye(total, dtype=jnp.float32)
-    factor = lax.linalg.cholesky(identity + gram, symmetrize_input=False)
-    inverse = jax.scipy.linalg.solve_triangular(factor, identity, lower=True)
-    inner = jnp.dot(inverse, pull, precision=lax.Precision.HIGHEST)
-    weights_mean = jnp.dot(inverse.T, inner, precision=lax.Precision.HIGHEST)
-    return inverse + weights_mean[None, :]
-
-
-def update_kernel(dims, forecast_ref, transform_ref, out_ref):
+    count = total // half
+    ROWS, LAST = ((1,), (0,)), ((1,), (1,))
+    gram, at = {}, 0
+    for column in range(count):
+        for row in range(column, count):
+            gram[row, column] = packed_ref[at : at + half, :]
+            at += half
+    pull = [packed_ref[at + 8 * k : at + 8 * k + 1, :] for k in range(count)]
+    diagonal = lax.broadcasted_iota(jnp.int32, (half, half), 0) == lax.broadcasted_iota(
+        jnp.int32, (half, half), 1
+    )
+    identity = jnp.where(diagonal, 1.0, 0.0)
+    factor, inverse = {}, {}
+    for column in range(count):
+        for row in range(column, count):
+            left = gram[row, column]
+            if row == column:
+                left = left + identity
+            for k in range(column):
+                left = left - product(factor[row, k], factor[column, k], LAST)
+            if row == column:
+                inverse[row, row] = inverse_factor(left)
+            else:
+                factor[row, column] = product(left, inverse[column, column], LAST)
+    for row in range(count):
+        for column in range(row):
+            total_term = product(factor[row, column], inverse[column, column], ROWS)
+            for k in range(column + 1, row):
+                total_term = total_term + product(factor[row, k], inverse[k, column], ROWS)
+            inverse[row, column] = -product(inverse[row, row], total_term, ROWS)
+    inner = [
+        sum(
+            jnp.sum(inverse[row, column] * pull[column], axis=1, keepdims=True)
+            for column in range(row + 1)
+        )
+        for row in range(count)
+    ]
+    weights = [
+        sum(
+            jnp.sum(inverse[row, column] * inner[row], axis=0, keepdims=True)
+            for row in range(column, count)
+        )
+        for column in range(count)
+    ]
+    zero = jnp.zeros((half, half), jnp.float32)
+    return jnp.concatenate(
+        [
+            jnp.concatenate(
+                [inverse.get((row, column), zero) + weights[column] for column in range(count)],
+                axis=1,
+            )
+            for row in range(count)
+        ],
+        axis=0,
+    )
+
+
+def update_kernel(dims, forecast_ref, packed_ref, out_ref, transform_ref):
     clusters, terms, members, cols = dims
     total = clusters * members
+    transform_ref[...] = transform_of(packed_ref, total)
     transform = transform_ref[...]
     step = 2
     for first in range(0, terms, step):
@@ -272,13 +376,7 @@
         values = [forecast_ref[:, term].reshape(total, cols) for term in some]
         means = [jnp.sum(v, axis=0, keepdims=True) * (1.0 / total) for v in values]
         anomaly = jnp.concatenate([v - m for v, m in zip(values, means)], axis=1)
-        updated = lax.dot_general(
-            transform,
-            anomaly,
-            (((1,), (0,)), ((), ())),
-            precision=lax.Precision.HIGHEST,
-            preferred_element_type=jnp.float32,
-        ) + jnp.concatenate(means, axis=1)
+        updated = product(transform, anomaly, ((1,), (0,))) + jnp.concatenate(means, axis=1)
         for k, term in enumerate(some):
             out_ref[:, term] = updated[:, k * cols : (k + 1) * cols].reshape(clusters, members, cols)
 
@@ -312,10 +410,12 @@
         [pltpu.VMEM((total + 8, terms * cols), jnp.float32)],
     )(arrived, observed)
     packed = total_over_devices(packed)
-    transform = make_transform(packed, total)
     updated = call(
-        functools.partial(update_kernel, dims), f32(clusters, terms, members, cols), 2
-    )(arrived, transform)
+        functools.partial(update_kernel, dims),
+        f32(clusters, terms, members, cols),
+        2,
+        [pltpu.VMEM((total, total), jnp.float32)],
+    )(arrived, packed)
     returned = lax.all_to_all(updated, ("group", "member"), split_axis=0, concat_axis=0, tiled=True)
     placed = call(
         functools.partial(place_kernel, (clusters, fields, block_rows, members, cols)),

time: 162 us -> 108 us (0.67)
  other arithmetic: 54.2 us -> 0.1 us
  Pallas kernels: 14 us -> 23.4 us
  local copies, waits for them, and re-layouts: 5.64 us -> 1.48 us
  waiting for transfers between devices: 31.9 us -> 29.7 us
  matrix products: 1.85 us -> 0 us
    another operation x9 -> x0, other arithmetic: 53.9 us -> none  [the longest x6 34.2 us: make_transform(): factor = lax.linalg.cholesky(identity + gram, symmetrize_input=False)]
    pallas_call x1, Pallas kernels: 1.58 us -> 10.9 us  [on_device(): call(functools.partial(update_kernel, dims), f32(clusters, terms, members...]
    another operation x9 -> x0, local copies, waits for them, and re-layouts: 4.15 us -> none
    ppermute x11, waiting for transfers between devices: 10.1 us -> 7.87 us  [flip(): lax.ppermute(value, axis, [(i, i ^ bits) for i in range(lax.axis_size(axi...]
  transfers between devices with their start and end apart: 14 -> 14, of which waited for: 13 -> 14; matrix products, arithmetic and copies ran while one was open for 0% -> 0% of each run, Pallas kernels for 0% -> 1%
where the time goes in v2:
time: 108 us; the launch traced here: 106 us
  waiting for transfers between devices  29.7 us (28%)
  starting transfers between devices  28.8 us (27%)
  Pallas kernels  23.4 us (22%)
  blocking collectives  22.4 us (21%)
  local copies, waits for them, and re-layouts  1.48 us (1%)
    all_to_all x1, blocking collectives, on_device(): lax.all_to_all(updated, ('group', 'member'), split_axis=0, concat_axis=0,...  22.4 us
    ppermute x11, starting transfers between devices, flip(): lax.ppermute(value, axis, [(i, i ^ bits) for i in range(lax.axis_size(axi...  17.8 us
    all_to_all x1, waiting for transfers between devices, on_device(): lax.all_to_all(predicted, ('group', 'member'), split_axis=0, concat_axis=...  16.8 us
    pallas_call x1, Pallas kernels, on_device(): call(functools.partial(update_kernel, dims), f32(clusters, terms, members...  10.9 us
    ppermute x11, waiting for transfers between devices, flip(): lax.ppermute(value, axis, [(i, i ^ bits) for i in range(lax.axis_size(axi...  7.87 us
    pallas_call x1, Pallas kernels, forecast(): call(functools.partial(forecast_kernel, dims), f32(clusters, fields * blo...  7.28 us
    all_to_all x1, starting transfers between devices, on_device(): lax.all_to_all(predicted, ('group', 'member'), split_axis=0, concat_axis=...  5.72 us
    ppermute x1, starting transfers between devices, forecast(): lax.ppermute(to_next, 'space', [(i, i + 1) for i in range(count - 1)])  4.04 us
  transfers between devices with their start and end apart: 14, of which 14 were waited for; matrix products, arithmetic and copies ran while one was open for 0% of the time, Pallas kernels for 1%

profile of v2, /device:TPU:1, one launch (start us, length us, event | category | flops | bytes accessed | tf_op | source)
XLA Modules:
  0.0 106.0 jit_solution(10576573910093739921)
XLA Ops:
  0.0 0.0 copy-start
  0.0 1.4 %copy-done = f32[32,3,32,128]{3,2,1,0:T(8,128)S(1)} copy-done((f32[32,3,32,128]{3,2,1,0:T(8,128)S(1)}, f32[32,3,32,128]{3,2,1,0:T(8,128)}, u32[]{:S(2)}) %copy-start) | copy-done | bytes 1572888
  1.4 0.2 shard_map.46
  1.6 4.0 %collective-permute-start = (f32[9,32,128]{2,1,0:T(8,128)S(1)}, f32[9,32,128]{2,1,0:T(8,128)S(1)}, u32[]{:S(2)}, u32[]{:S(2)}) collective-permute-start(f32[9,32,128]{2,1,0:T(8,128)S(1)} %get-tuple-element.7), channel_id=1, source_target_pairs={{0,1},{1,2},{2,3},{4,5},{5,6},{6,7},{8,9},{9,10},{10,11},{12,13},{... | collective-permute-start | bytes 442376 | tf_op jit(solution)/shard_map/ppermute | solution.py:149
  5.7 1.3 %collective-permute-start.1 = (f32[9,32,128]{2,1,0:T(8,128)S(1)}, f32[9,32,128]{2,1,0:T(8,128)S(1)}, u32[]{:S(2)}, u32[]{:S(2)}) collective-permute-start(f32[9,32,128]{2,1,0:T(8,128)S(1)} %get-tuple-element.8), channel_id=1, source_target_pairs={{1,0},{2,1},{3,2},{5,4},{6,5},{7,6},{9,8},{10,9},{11,10},{13,12},{... | collective-permute-start | bytes 442376 | tf_op jit(solution)/shard_map/ppermute | solution.py:150
  7.0 1.2 %collective-permute-done.before_ref = f32[9,32,128]{2,1,0:T(8,128)S(1)} collective-permute-done((f32[9,32,128]{2,1,0:T(8,128)S(1)}, f32[9,32,128]{2,1,0:T(8,128)S(1)}, u32[]{:S(2)}, u32[]{:S(2)}) %collective-permute-start) | collective-permute-done | bytes 147488 | tf_op jit(solution)/shard_map/ppermute | solution.py:149
  8.2 3.8 %collective-permute-done.1.after_ref = f32[9,32,128]{2,1,0:T(8,128)S(1)} collective-permute-done((f32[9,32,128]{2,1,0:T(8,128)S(1)}, f32[9,32,128]{2,1,0:T(8,128)S(1)}, u32[]{:S(2)}, u32[]{:S(2)}) %collective-permute-start.1) | collective-permute-done | bytes 147488 | tf_op jit(solution)/shard_map/ppermute | solution.py:150
  12.0 7.3 %shard_map.47 = f32[8,12,32,128]{3,2,1,0:T(8,128)} custom-call(f32[3072,128]{1,0:T(8,128)S(1)} %bitcast.23, f32[9,32,128]{2,1,0:T(8,128)S(1)} %collective-permute-done.before_ref, f32[9,32,128]{2,1,0:T(8,128)S(1)} %collective-permute-done.1.after_ref), custom_call_target="tpu_custom_call" | custom-call | tf_op jit(solution)/shard_map/pallas_call | solution.py:152
  19.3 0.0 copy-start.1
  19.3 0.0 copy-start.2
  19.3 0.0 copy-start.3
  19.3 5.7 %all-to-all-start = ((f32[8,12,32,128]{3,2,1,0:T(8,128)}), f32[8,12,32,128]{3,2,1,0:T(8,128)S(1)}, u32[]{:S(2)}, u32[]{:S(2)}) async-start(f32[8,12,32,128]{3,2,1,0:T(8,128)} %shard_map.47), calls=%async_computation | async-start | bytes 3145728 | tf_op jit(solution)/shard_map/all_to_all | solution.py:404
  25.0 0.0 copy-done.1
  25.0 0.0 copy-done.2
  25.0 0.0 copy-done.3
  25.0 0.7 shard_map.48.observed_ref
  25.7 16.8 %all-to-all-done.forecast_ref = f32[8,12,32,128]{3,2,1,0:T(8,128)S(1)} async-done(((f32[8,12,32,128]{3,2,1,0:T(8,128)}), f32[8,12,32,128]{3,2,1,0:T(8,128)S(1)}, u32[]{:S(2)}, u32[]{:S(2)}) %all-to-all-start) | async-done | bytes 1572896 | tf_op jit(solution)/shard_map/all_to_all | solution.py:404
  42.5 1.6 %shard_map.49 = f32[448,128]{1,0:T(8,128)S(1)} custom-call(f32[8,12,32,128]{3,2,1,0:T(8,128)S(1)} %all-to-all-done.forecast_ref, f32[8,1536]{1,0:T(8,128)S(1)} %shard_map.48.observed_ref), custom_call_target="tpu_custom_call" | custom-call | tf_op jit(solution)/shard_map/pallas_call | solution.py:406
  44.2 3.5 %collective-permute-start.2 = (f32[224,128]{1,0:T(8,128)S(1)}, f32[224,128]{1,0:T(8,128)S(1)}, u32[]{:S(2)}, u32[]{:S(2)}) collective-permute-start(f32[224,128]{1,0:T(8,128)S(1)} %constant_dynamic-slice_fusion), channel_id=1, source_target_pairs={{0,4},{4,0},{1,5},{5,1},{2,6},{6,2},{3,7},{7,3},{8,12},{12,8},{9,1... | collective-permute-start | bytes 344072 | tf_op jit(solution)/shard_map/ppermute | solution.py:217
  47.8 1.0 collective-permute-done.2
  48.8 0.3 collective-permute-start.4
  49.1 1.1 %collective-permute-start.5 = (f32[56,128]{1,0:T(8,128)S(1)}, f32[56,128]{1,0:T(8,128)S(1)}, u32[]{:S(2)}, u32[]{:S(2)}) collective-permute-start(f32[56,128]{1,0:T(8,128)S(1)} %get-tuple-element.16), channel_id=1, source_target_pairs={{0,24},{8,16},{16,8},{24,0},{1,25},{9,17},{17,9},{25,1},{2,26},{10... | collective-permute-start | bytes 86024 | tf_op jit(solution)/shard_map/ppermute | solution.py:217
  50.2 1.2 %collective-permute-start.3 = (f32[56,128]{1,0:T(8,128)S(1)}, f32[56,128]{1,0:T(8,128)S(1)}, u32[]{:S(2)}, u32[]{:S(2)}) collective-permute-start(f32[56,128]{1,0:T(8,128)S(1)} %get-tuple-element.17), channel_id=1, source_target_pairs={{0,8},{8,0},{16,24},{24,16},{1,9},{9,1},{17,25},{25,17},{2,10},{10... | collective-permute-start | bytes 86024 | tf_op jit(solution)/shard_map/ppermute | solution.py:217
  51.5 0.1 collective-permute-done.4
  51.6 1.2 %collective-permute-done.5 = f32[56,128]{1,0:T(8,128)S(1)} collective-permute-done((f32[56,128]{1,0:T(8,128)S(1)}, f32[56,128]{1,0:T(8,128)S(1)}, u32[]{:S(2)}, u32[]{:S(2)}) %collective-permute-start.5) | collective-permute-done | bytes 28704 | tf_op jit(solution)/shard_map/ppermute | solution.py:217
  52.7 0.3 collective-permute-done.3
  53.1 1.4 %collective-permute-start.8 = (f32[56,128]{1,0:T(8,128)S(1)}, f32[56,128]{1,0:T(8,128)S(1)}, u32[]{:S(2)}, u32[]{:S(2)}) collective-permute-start(f32[56,128]{1,0:T(8,128)S(1)} %bitcast_add_fusion), channel_id=1, source_target_pairs={{0,3},{1,2},{2,1},{3,0},{4,7},{5,6},{6,5},{7,4},{8,11},{9,10},{10,... | collective-permute-start | bytes 86024 | tf_op jit(solution)/shard_map/ppermute | solution.py:217
  54.4 1.2 %collective-permute-start.7 = (f32[56,128]{1,0:T(8,128)S(1)}, f32[56,128]{1,0:T(8,128)S(1)}, u32[]{:S(2)}, u32[]{:S(2)}) collective-permute-start(f32[56,128]{1,0:T(8,128)S(1)} %bitcast_add_fusion), channel_id=1, source_target_pairs={{0,2},{1,3},{2,0},{3,1},{4,6},{5,7},{6,4},{7,5},{8,10},{9,11},{10,... | collective-permute-start | bytes 86024 | tf_op jit(solution)/shard_map/ppermute | solution.py:217
  55.6 1.1 %collective-permute-start.6 = (f32[56,128]{1,0:T(8,128)S(1)}, f32[56,128]{1,0:T(8,128)S(1)}, u32[]{:S(2)}, u32[]{:S(2)}) collective-permute-start(f32[56,128]{1,0:T(8,128)S(1)} %bitcast_add_fusion), channel_id=1, source_target_pairs={{0,1},{1,0},{2,3},{3,2},{4,5},{5,4},{6,7},{7,6},{8,9},{9,8},{10,11... | collective-permute-start | bytes 86024 | tf_op jit(solution)/shard_map/ppermute | solution.py:217
  56.7 1.0 collective-permute-done.8
  57.6 0.4 collective-permute-done.7
  58.0 0.3 collective-permute-done.6
  58.3 1.5 %collective-permute-start.11 = (f32[56,128]{1,0:T(8,128)S(1)}, f32[56,128]{1,0:T(8,128)S(1)}, u32[]{:S(2)}, u32[]{:S(2)}) collective-permute-start(f32[56,128]{1,0:T(8,128)S(1)} %add_add_fusion), channel_id=1, source_target_pairs={{0,24},{8,16},{16,8},{24,0},{1,25},{9,17},{17,9},{25,1},{2,26},{10... | collective-permute-start | bytes 86024 | tf_op jit(solution)/shard_map/ppermute | solution.py:217
  59.8 1.4 %collective-permute-start.10 = (f32[56,128]{1,0:T(8,128)S(1)}, f32[56,128]{1,0:T(8,128)S(1)}, u32[]{:S(2)}, u32[]{:S(2)}) collective-permute-start(f32[56,128]{1,0:T(8,128)S(1)} %add_add_fusion), channel_id=1, source_target_pairs={{0,16},{8,24},{16,0},{24,8},{1,17},{9,25},{17,1},{25,9},{2,18},{10... | collective-permute-start | bytes 86024 | tf_op jit(solution)/shard_map/ppermute | solution.py:217
  61.2 0.0 collective-permute-start.9
  61.2 0.8 collective-permute-done.11
  62.0 0.5 collective-permute-done.10
  62.6 1.4 %collective-permute-done.9 = f32[56,128]{1,0:T(8,128)S(1)} collective-permute-done((f32[56,128]{1,0:T(8,128)S(1)}, f32[56,128]{1,0:T(8,128)S(1)}, u32[]{:S(2)}, u32[]{:S(2)}) %collective-permute-start.9) | collective-permute-done | bytes 28704 | tf_op jit(solution)/shard_map/ppermute | solution.py:217
  64.0 5.1 %collective-permute-start.12 = (f32[224,128]{1,0:T(8,128)S(1)}, f32[224,128]{1,0:T(8,128)S(1)}, u32[]{:S(2)}, u32[]{:S(2)}) collective-permute-start(f32[224,128]{1,0:T(8,128)S(1)} %pad_maximum_fusion.2), channel_id=1, source_target_pairs={{0,4},{4,0},{1,5},{5,1},{2,6},{6,2},{3,7},{7,3},{8,12},{12,8},{9,1... | collective-permute-start | bytes 344072 | tf_op jit(solution)/shard_map/ppermute | solution.py:217
  69.1 1.0 collective-permute-done.12
  70.1 10.9 %shard_map.50 = f32[8,12,32,128]{3,2,1,0:T(8,128)S(1)} custom-call(f32[8,12,32,128]{3,2,1,0:T(8,128)S(1)} %all-to-all-done.forecast_ref, f32[448,128]{1,0:T(8,128)S(1)} %pad_maximum_fusion.packed_ref), custom_call_target="tpu_custom_call" | custom-call | tf_op jit(solution)/shard_map/pallas_call | solution.py:413
  81.0 22.4 %all_to_all.10.in_ref = f32[8,12,32,128]{3,2,1,0:T(8,128)S(1)} all-to-all(f32[8,12,32,128]{3,2,1,0:T(8,128)S(1)} %shard_map.50), channel_id=1, replica_groups=mesh['group'=4,'member'=2,'space'=4] {'group','member'}, dimensions={0} | all-to-all | bytes 3145728 | tf_op jit(solution)/shard_map/all_to_all | solution.py:419
  103.4 2.6 %shard_map.51 = f32[3072,128]{1,0:T(8,128)} custom-call(f32[8,12,32,128]{3,2,1,0:T(8,128)S(1)} %all_to_all.10.in_ref), custom_call_target="tpu_custom_call" | custom-call | tf_op jit(solution)/shard_map/pallas_call | solution.py:420
  (10 shorter events, 0.2 us)
Async XLA Ops:
  0.0 1.4 %copy-start = (f32[32,3,32,128]{3,2,1,0:T(8,128)S(1)}, f32[32,3,32,128]{3,2,1,0:T(8,128)}, u32[]{:S(2)}) copy-start(f32[32,3,32,128]{3,2,1,0:T(8,128)} %bottom_ref.1) | copy-start | bytes 4718596
  1.6 6.5 %collective-permute-start = (f32[9,32,128]{2,1,0:T(8,128)S(1)}, f32[9,32,128]{2,1,0:T(8,128)S(1)}, u32[]{:S(2)}, u32[]{:S(2)}) collective-permute-start(f32[9,32,128]{2,1,0:T(8,128)S(1)} %get-tuple-element.7), channel_id=1, source_target_pairs={{0,1},{1,2},{2,3},{4,5},{5,6},{6,7},{8,9},{9,10},{10,11},{12,13},{... | collective-permute-start | bytes 442376 | tf_op jit(solution)/shard_map/ppermute | solution.py:149
  5.7 6.3 %collective-permute-start.1 = (f32[9,32,128]{2,1,0:T(8,128)S(1)}, f32[9,32,128]{2,1,0:T(8,128)S(1)}, u32[]{:S(2)}, u32[]{:S(2)}) collective-permute-start(f32[9,32,128]{2,1,0:T(8,128)S(1)} %get-tuple-element.8), channel_id=1, source_target_pairs={{1,0},{2,1},{3,2},{5,4},{6,5},{7,6},{9,8},{10,9},{11,10},{13,12},{... | collective-permute-start | bytes 442376 | tf_op jit(solution)/shard_map/ppermute | solution.py:150
  19.3 5.7 %copy-start.1 = (f32[1,768]{1,0:T(1,128)S(1)}, f32[1,768]{1,0:T(1,128)}, u32[]{:S(2)}) copy-start(f32[1,768]{1,0:T(1,128)} %values_ref.1) | copy-start | bytes 9220
  19.3 5.7 %copy-start.2 = (f32[1,768]{1,0:T(1,128)S(1)}, f32[1,768]{1,0:T(1,128)}, u32[]{:S(2)}) copy-start(f32[1,768]{1,0:T(1,128)} %precision_ref.1) | copy-start | bytes 9220
  19.3 5.7 %copy-start.3 = (s32[1,768]{1,0:T(1,128)S(1)}, s32[1,768]{1,0:T(1,128)}, u32[]{:S(2)}) copy-start(s32[1,768]{1,0:T(1,128)} %index_ref.1) | copy-start | bytes 9220
  19.3 23.3 %all-to-all-start = ((f32[8,12,32,128]{3,2,1,0:T(8,128)}), f32[8,12,32,128]{3,2,1,0:T(8,128)S(1)}, u32[]{:S(2)}, u32[]{:S(2)}) async-start(f32[8,12,32,128]{3,2,1,0:T(8,128)} %shard_map.47), calls=%async_computation | async-start | bytes 3145728 | tf_op jit(solution)/shard_map/all_to_all | solution.py:404
  44.2 4.5 %collective-permute-start.2 = (f32[224,128]{1,0:T(8,128)S(1)}, f32[224,128]{1,0:T(8,128)S(1)}, u32[]{:S(2)}, u32[]{:S(2)}) collective-permute-start(f32[224,128]{1,0:T(8,128)S(1)} %constant_dynamic-slice_fusion), channel_id=1, source_target_pairs={{0,4},{4,0},{1,5},{5,1},{2,6},{6,2},{3,7},{7,3},{8,12},{12,8},{9,1... | collective-permute-start | bytes 344072 | tf_op jit(solution)/shard_map/ppermute | solution.py:217
  48.8 2.8 %collective-permute-start.4 = (f32[56,128]{1,0:T(8,128)S(1)}, f32[56,128]{1,0:T(8,128)S(1)}, u32[]{:S(2)}, u32[]{:S(2)}) collective-permute-start(f32[56,128]{1,0:T(8,128)S(1)} %get-tuple-element.15), channel_id=1, source_target_pairs={{0,16},{8,24},{16,0},{24,8},{1,17},{9,25},{17,1},{25,9},{2,18},{10... | collective-permute-start | bytes 86024 | tf_op jit(solution)/shard_map/ppermute | solution.py:217
  49.1 3.6 %collective-permute-start.5 = (f32[56,128]{1,0:T(8,128)S(1)}, f32[56,128]{1,0:T(8,128)S(1)}, u32[]{:S(2)}, u32[]{:S(2)}) collective-permute-start(f32[56,128]{1,0:T(8,128)S(1)} %get-tuple-element.16), channel_id=1, source_target_pairs={{0,24},{8,16},{16,8},{24,0},{1,25},{9,17},{17,9},{25,1},{2,26},{10... | collective-permute-start | bytes 86024 | tf_op jit(solution)/shard_map/ppermute | solution.py:217
  50.2 2.8 %collective-permute-start.3 = (f32[56,128]{1,0:T(8,128)S(1)}, f32[56,128]{1,0:T(8,128)S(1)}, u32[]{:S(2)}, u32[]{:S(2)}) collective-permute-start(f32[56,128]{1,0:T(8,128)S(1)} %get-tuple-element.17), channel_id=1, source_target_pairs={{0,8},{8,0},{16,24},{24,16},{1,9},{9,1},{17,25},{25,17},{2,10},{10... | collective-permute-start | bytes 86024 | tf_op jit(solution)/shard_map/ppermute | solution.py:217
  53.1 4.6 %collective-permute-start.8 = (f32[56,128]{1,0:T(8,128)S(1)}, f32[56,128]{1,0:T(8,128)S(1)}, u32[]{:S(2)}, u32[]{:S(2)}) collective-permute-start(f32[56,128]{1,0:T(8,128)S(1)} %bitcast_add_fusion), channel_id=1, source_target_pairs={{0,3},{1,2},{2,1},{3,0},{4,7},{5,6},{6,5},{7,4},{8,11},{9,10},{10,... | collective-permute-start | bytes 86024 | tf_op jit(solution)/shard_map/ppermute | solution.py:217
  54.4 3.6 %collective-permute-start.7 = (f32[56,128]{1,0:T(8,128)S(1)}, f32[56,128]{1,0:T(8,128)S(1)}, u32[]{:S(2)}, u32[]{:S(2)}) collective-permute-start(f32[56,128]{1,0:T(8,128)S(1)} %bitcast_add_fusion), channel_id=1, source_target_pairs={{0,2},{1,3},{2,0},{3,1},{4,6},{5,7},{6,4},{7,5},{8,10},{9,11},{10,... | collective-permute-start | bytes 86024 | tf_op jit(solution)/shard_map/ppermute | solution.py:217
  55.6 2.7 %collective-permute-start.6 = (f32[56,128]{1,0:T(8,128)S(1)}, f32[56,128]{1,0:T(8,128)S(1)}, u32[]{:S(2)}, u32[]{:S(2)}) collective-permute-start(f32[56,128]{1,0:T(8,128)S(1)} %bitcast_add_fusion), channel_id=1, source_target_pairs={{0,1},{1,0},{2,3},{3,2},{4,5},{5,4},{6,7},{7,6},{8,9},{9,8},{10,11... | collective-permute-start | bytes 86024 | tf_op jit(solution)/shard_map/ppermute | solution.py:217
  58.3 3.7 %collective-permute-start.11 = (f32[56,128]{1,0:T(8,128)S(1)}, f32[56,128]{1,0:T(8,128)S(1)}, u32[]{:S(2)}, u32[]{:S(2)}) collective-permute-start(f32[56,128]{1,0:T(8,128)S(1)} %add_add_fusion), channel_id=1, source_target_pairs={{0,24},{8,16},{16,8},{24,0},{1,25},{9,17},{17,9},{25,1},{2,26},{10... | collective-permute-start | bytes 86024 | tf_op jit(solution)/shard_map/ppermute | solution.py:217
  59.8 2.7 %collective-permute-start.10 = (f32[56,128]{1,0:T(8,128)S(1)}, f32[56,128]{1,0:T(8,128)S(1)}, u32[]{:S(2)}, u32[]{:S(2)}) collective-permute-start(f32[56,128]{1,0:T(8,128)S(1)} %add_add_fusion), channel_id=1, source_target_pairs={{0,16},{8,24},{16,0},{24,8},{1,17},{9,25},{17,1},{25,9},{2,18},{10... | collective-permute-start | bytes 86024 | tf_op jit(solution)/shard_map/ppermute | solution.py:217
  61.2 2.7 %collective-permute-start.9 = (f32[56,128]{1,0:T(8,128)S(1)}, f32[56,128]{1,0:T(8,128)S(1)}, u32[]{:S(2)}, u32[]{:S(2)}) collective-permute-start(f32[56,128]{1,0:T(8,128)S(1)} %add_add_fusion), channel_id=1, source_target_pairs={{0,8},{8,0},{16,24},{24,16},{1,9},{9,1},{17,25},{25,17},{2,10},{10... | collective-permute-start | bytes 86024 | tf_op jit(solution)/shard_map/ppermute | solution.py:217
  64.0 6.0 %collective-permute-start.12 = (f32[224,128]{1,0:T(8,128)S(1)}, f32[224,128]{1,0:T(8,128)S(1)}, u32[]{:S(2)}, u32[]{:S(2)}) collective-permute-start(f32[224,128]{1,0:T(8,128)S(1)} %pad_maximum_fusion.2), channel_id=1, source_target_pairs={{0,4},{4,0},{1,5},{5,1},{2,6},{6,2},{3,7},{7,3},{8,12},{12,8},{9,1... | collective-permute-start | bytes 344072 | tf_op jit(solution)/shard_map/ppermute | solution.py:217

commit v3 on v2

--- a/solution.py
+++ b/solution.py
@@ -14,6 +14,7 @@
 HALO = (4, 3, 2)
 HALO_ROWS = sum(HALO)
 LANES = 128
+DIRECT = 8
 VMEM_LIMIT = 40 * 1024 * 1024
 
 
@@ -70,14 +71,78 @@
     )(state, state)
 
 
-def forecast_kernel(dims, state_ref, before_ref, after_ref, out_ref):
-    members, fields, rows, cols, block_rows = dims
+def sweep(first, last, rows, cols, load, store, inside):
+    def across_y(value):
+        return pltpu.roll(value, cols - 1, 1) - pltpu.roll(value, 1, 1)
+
+    height, height_1 = {}, {}
+    flow_x1, flow_y1, flow_x2, flow_y2 = {}, {}, {}, {}
+    height[first - 4] = load(0, first - 4)
+    height[first - 3] = load(0, first - 3)
+    for lead in range(first - 3, last + 7):
+        row = lead
+        if row < last + 3:
+            height[row + 1] = load(0, row + 1)
+            flow_x1[row] = inside(
+                load(1, row) - GRAV * (height[row + 1] - height[row - 1]), row
+            )
+            if first - 2 <= row < last + 2:
+                flow_y1[row] = load(2, row) - GRAV * across_y(height[row])
+        row = lead - 1
+        if first - 2 <= row < last + 2:
+            height_1[row] = inside(
+                height[row]
+                - DEPTH * (flow_x1[row + 1] - flow_x1[row - 1] + across_y(flow_y1[row])),
+                row,
+            )
+        row = lead - 2
+        if first - 1 <= row < last + 1:
+            flow_x2[row] = inside(
+                flow_x1[row] - GRAV * (height_1[row + 1] - height_1[row - 1]), row
+            )
+            if first <= row < last:
+                flow_y2[row] = flow_y1[row] - GRAV * across_y(height_1[row])
+                store(1, row, flow_x2[row])
+                store(2, row, flow_y2[row])
+        row = lead - 3
+        if first <= row < last:
+            store(
+                0,
+                row,
+                height_1[row]
+                - DEPTH * (flow_x2[row + 1] - flow_x2[row - 1] + across_y(flow_y2[row])),
+            )
+
+
+def interior_kernel(dims, state_ref, out_ref):
+    members, fields, rows, cols, block_rows, edge = dims
+    for at in range(0, members, 8):
+
+        def load(field, row):
+            start = (at * fields + field) * rows + row
+            return state_ref[pl.ds(start, 8, stride=fields * rows), :]
+
+        def store(field, row, value):
+            block, within = divmod(row, block_rows)
+            out_ref[block, field * block_rows + within, at : at + 8, :] = value
+
+        sweep(edge, rows - edge, rows, cols, load, store, lambda value, row: value)
+
+
+def own_cluster(clusters):
+    if clusters > DIRECT:
+        return 0
+    return lax.axis_index("group") * lax.axis_size("member") + lax.axis_index("member")
+
+
+def edge_kernel(dims, state_ref, before_ref, after_ref, interior_ref, *refs):
+    members, fields, rows, cols, block_rows, edge = dims
+    clusters = rows // block_rows
+    slots, edges_ref = refs[:clusters], refs[clusters]
     here = lax.axis_index("space")
     has_before = (here > 0).astype(jnp.float32)
     has_after = (here < lax.axis_size("space") - 1).astype(jnp.float32)
-
-    def across_y(value):
-        return pltpu.roll(value, cols - 1, 1) - pltpu.roll(value, 1, 1)
+    own = own_cluster(clusters)
 
     def inside(value, row):
         if row < 0:
@@ -86,74 +151,76 @@
             return value * has_after
         return value
 
-    for first in range(0, members, 8):
+    for at in range(0, members, 8):
 
         def load(field, row):
             offset = sum(HALO[:field])
             if row < 0:
-                return before_ref[offset + HALO[field] + row, first : first + 8, :]
+                return before_ref[offset + HALO[field] + row, at : at + 8, :]
             if row >= rows:
-                return after_ref[offset + row - rows, first : first + 8, :]
-            start = (first * fields + field) * rows + row
+                return after_ref[offset + row - rows, at : at + 8, :]
+            start = (at * fields + field) * rows + row
             return state_ref[pl.ds(start, 8, stride=fields * rows), :]
 
-        height, flow_x, flow_y = {}, {}, {}
-        height_1, flow_x1, flow_y1 = {}, {}, {}
-        flow_x2, flow_y2 = {}, {}
-
         def store(field, row, value):
-            out_ref[row // block_rows, field * block_rows + row % block_rows, first : first + 8, :] = value
-
-        height[-4] = load(0, -4)
-        height[-3] = load(0, -3)
-        for lead in range(-3, rows + 7):
-            row = lead
-            if row < rows + 3:
-                height[row + 1] = load(0, row + 1)
-                flow_x1[row] = inside(
-                    load(1, row) - GRAV * (height[row + 1] - height[row - 1]), row
-                )
-                if -2 <= row < rows + 2:
-                    flow_y1[row] = load(2, row) - GRAV * across_y(height[row])
-            row = lead - 1
-            if -2 <= row < rows + 2:
-                height_1[row] = inside(
-                    height[row]
-                    - DEPTH * (flow_x1[row + 1] - flow_x1[row - 1] + across_y(flow_y1[row])),
-                    row,
-                )
-            row = lead - 2
-            if -1 <= row < rows + 1:
-                flow_x2[row] = inside(
-                    flow_x1[row] - GRAV * (height_1[row + 1] - height_1[row - 1]), row
-                )
-                if 0 <= row < rows:
-                    flow_y2[row] = flow_y1[row] - GRAV * across_y(height_1[row])
-                    store(1, row, flow_x2[row])
-                    store(2, row, flow_y2[row])
-            row = lead - 3
-            if 0 <= row < rows:
-                store(
-                    0,
-                    row,
-                    height_1[row]
-                    - DEPTH * (flow_x2[row + 1] - flow_x2[row - 1] + across_y(flow_y2[row])),
-                )
+            block, within = divmod(row, block_rows)
+            edges_ref[block, field * block_rows + within, at : at + 8, :] = value
+
+        sweep(0, edge, rows, cols, load, store, inside)
+        sweep(rows - edge, rows, rows, cols, load, store, inside)
+    edges_ref[edge // block_rows : clusters - edge // block_rows] = interior_ref[
+        edge // block_rows : clusters - edge // block_rows
+    ]
+    for slot, ref in zip(slot_order(clusters), slots):
+        ref[...] = edges_ref[own ^ slot]
 
 
 def forecast(state, clusters):
     members, fields, rows, cols = state.shape
     block_rows = rows // clusters
+    terms = fields * block_rows
+    edge = -(-4 // block_rows) * block_rows
     to_prev, to_next = pack_edges(state)
     count = lax.axis_size("space")
     before = lax.ppermute(to_next, "space", [(i, i + 1) for i in range(count - 1)])
     after = lax.ppermute(to_prev, "space", [(i + 1, i) for i in range(count - 1)])
-    dims = (members, fields, rows, cols, block_rows)
+    dims = (members, fields, rows, cols, block_rows, edge)
+    flat = state.reshape(members * fields * rows, cols)
+    size = members * fields * rows * cols
+    interior = call(
+        functools.partial(interior_kernel, dims),
+        f32(clusters, terms, members, cols),
+        1,
+        cost_estimate=pl.CostEstimate(
+            flops=200 * size, bytes_accessed=16 * size, transcendentals=0
+        ),
+    )(flat)
     return call(
-        functools.partial(forecast_kernel, dims),
-        f32(clusters, fields * block_rows, members, cols),
-        3,
-    )(state.reshape(members * fields * rows, cols), before, after)
+        functools.partial(edge_kernel, dims),
+        [f32(terms, members, cols)] * clusters,
+        4,
+        [pltpu.VMEM((clusters, terms, members, cols), jnp.float32)],
+    )(flat, before, after, interior)
+
+
+def slot_order(clusters):
+    if clusters > DIRECT:
+        return list(range(clusters))
+    cores = lax.axis_size("member")
+    return [0] + sorted(range(1, clusters), key=lambda s: (s < cores, s % cores, s))
+
+
+def exchange(slots):
+    clusters = len(slots)
+    if clusters > DIRECT:
+        stacked = jnp.stack(slots, axis=0)
+        got = lax.all_to_all(stacked, ("group", "member"), split_axis=0, concat_axis=0, tiled=True)
+        return [got[k] for k in range(clusters)]
+    got = [slots[0]]
+    for slot, value in list(zip(slot_order(clusters), slots))[1:]:
+        pairs = [(i, i ^ slot) for i in range(clusters)]
+        got.append(lax.ppermute(value, ("group", "member"), pairs))
+    return got
 
 
 def split(value):
@@ -180,34 +247,38 @@
     out_ref[2:8, :] = jnp.zeros((6, width), jnp.float32)
 
 
-def gram_kernel(dims, forecast_ref, observed_ref, out_ref, scaled_ref):
+def gram_kernel(dims, observed_ref, *refs):
     clusters, terms, members, cols = dims
+    arrived, (out_ref, anomaly_ref, mean_ref, scaled_ref) = refs[:clusters], refs[clusters:]
     total = clusters * members
     scale = 1.0 / math.sqrt(total - 1)
     half = LANES
+    own = own_cluster(clusters)
+    places = [pl.multiple_of((own ^ slot) * members, members) for slot in slot_order(clusters)]
     for term in range(terms):
         at = slice(term * cols, (term + 1) * cols)
-        values = forecast_ref[:, term].reshape(total, cols)
-        mean = jnp.sum(values, axis=0, keepdims=True) * (1.0 / total)
+        values = [ref[term] for ref in arrived]
+        summed = values[0]
+        for value in values[1:]:
+            summed = summed + value
+        mean = jnp.sum(summed, axis=0, keepdims=True) * (1.0 / total)
+        mean_ref[:, at] = jnp.broadcast_to(mean, (8, cols))
         weight = observed_ref[0:1, at] * scale
-        scaled_ref[0:total, at] = (values - mean) * weight
+        for place, value in zip(places, values):
+            anomaly = value - mean
+            anomaly_ref[pl.ds(place, members), at] = anomaly
+            scaled_ref[pl.ds(place, members), at] = anomaly * weight
         innovation = (observed_ref[1:2, at] - mean) * weight
         scaled_ref[total : total + 8, at] = jnp.concatenate(
             [innovation, jnp.zeros((7, cols), jnp.float32)], axis=0
         )
-    product = lax.dot_general(
-        scaled_ref[...],
-        scaled_ref[0:total, :],
-        (((1,), (1,)), ((), ())),
-        precision=lax.Precision.HIGHEST,
-        preferred_element_type=jnp.float32,
-    )
+    result = product(scaled_ref[...], scaled_ref[0:total, :], ((1,), (1,)))
     at = 0
     for first in range(0, total, half):
-        out_ref[at : at + total - first, :] = product[first:total, first : first + half]
+        out_ref[at : at + total - first, :] = result[first:total, first : first + half]
         at += total - first
     for k, first in enumerate(range(0, total, half)):
-        out_ref[at + 8 * k : at + 8 * k + 8, :] = product[total : total + 8, first : first + half]
+        out_ref[at + 8 * k : at + 8 * k + 8, :] = result[total : total + 8, first : first + half]
     at += 8 * (total // half)
     if at < out_ref.shape[0]:
         out_ref[at:, :] = jnp.zeros((out_ref.shape[0] - at, half), jnp.float32)
@@ -365,64 +436,81 @@
     )
 
 
-def update_kernel(dims, forecast_ref, packed_ref, out_ref, transform_ref):
+def update_kernel(dims, anomaly_ref, mean_ref, packed_ref, *refs):
     clusters, terms, members, cols = dims
+    slots, transform_ref = refs[:clusters], refs[clusters]
     total = clusters * members
+    own = own_cluster(clusters)
     transform_ref[...] = transform_of(packed_ref, total)
-    transform = transform_ref[...]
-    step = 2
-    for first in range(0, terms, step):
-        some = range(first, min(first + step, terms))
-        values = [forecast_ref[:, term].reshape(total, cols) for term in some]
-        means = [jnp.sum(v, axis=0, keepdims=True) * (1.0 / total) for v in values]
-        anomaly = jnp.concatenate([v - m for v, m in zip(values, means)], axis=1)
-        updated = product(transform, anomaly, ((1,), (0,))) + jnp.concatenate(means, axis=1)
-        for k, term in enumerate(some):
-            out_ref[:, term] = updated[:, k * cols : (k + 1) * cols].reshape(clusters, members, cols)
-
-
-def place_kernel(dims, in_ref, out_ref):
-    clusters, fields, block_rows, members, cols = dims
+    transform = jnp.concatenate(
+        [
+            transform_ref[pl.ds(pl.multiple_of((own ^ slot) * members, members), members), :]
+            for slot in slot_order(clusters)
+        ],
+        axis=0,
+    )
+    step = 2 * cols
+    width = terms * cols
+    for first in range(0, width, step):
+        at = slice(first, min(first + step, width))
+        updated = product(transform, anomaly_ref[:, at], ((1,), (0,))) + mean_ref[0:1, at]
+        for k in range((at.stop - first) // cols):
+            for at_slot, ref in enumerate(slots):
+                ref[first // cols + k] = updated[
+                    at_slot * members : (at_slot + 1) * members, k * cols : (k + 1) * cols
+                ]
+
+
+def place_kernel(dims, *refs):
+    clusters, fields, block_rows, cols = dims
+    slots, out_ref = refs[:clusters], refs[clusters]
     rows = clusters * block_rows
-    for cluster in range(clusters):
+    own = own_cluster(clusters)
+    for slot, ref in zip(slot_order(clusters), slots):
+        first = (own ^ slot) * block_rows
         for field in range(fields):
             for row in range(block_rows):
-                at = field * rows + cluster * block_rows + row
-                out_ref[pl.ds(at, members, stride=fields * rows), :] = in_ref[
-                    cluster, field * block_rows + row
-                ]
+                at = field * rows + row + first
+                out_ref[pl.ds(at, 8, stride=fields * rows), :] = ref[field * block_rows + row]
+
+
+def place(slots, fields):
+    clusters = len(slots)
+    terms, members, cols = slots[0].shape
+    rows = clusters * terms
+    return pl.pallas_call(
+        functools.partial(place_kernel, (clusters, fields, terms // fields, cols)),
+        grid=(members // 8,),
+        out_shape=f32(members * rows, cols),
+        in_specs=[pl.BlockSpec((terms, 8, cols), lambda i: (0, i, 0))] * clusters,
+        out_specs=pl.BlockSpec((8 * rows, cols), lambda i: (i, 0)),
+        compiler_params=pltpu.CompilerParams(vmem_limit_bytes=VMEM_LIMIT),
+    )(*slots)
 
 
 def on_device(state, obs_values, obs_precision, obs_index):
     members, fields, rows, cols = state.shape
     clusters = lax.axis_size("group") * lax.axis_size("member")
-    block_rows = rows // clusters
-    terms = fields * block_rows
+    terms = fields * (rows // clusters)
     total = clusters * members
+    width = terms * cols
     dims = (clusters, terms, members, cols)
-    predicted = forecast(state, clusters)
-    arrived = lax.all_to_all(predicted, ("group", "member"), split_axis=0, concat_axis=0, tiled=True)
-    observed = call(observed_kernel, f32(8, terms * cols), 3)(obs_values, obs_precision, obs_index)
-    packed = call(
+    arrived = exchange(forecast(state, clusters))
+    observed = call(observed_kernel, f32(8, width), 3)(obs_values, obs_precision, obs_index)
+    packed, anomaly, mean = call(
         functools.partial(gram_kernel, dims),
-        f32(448, LANES),
-        2,
-        [pltpu.VMEM((total + 8, terms * cols), jnp.float32)],
-    )(arrived, observed)
+        [f32(448, LANES), f32(total, width), f32(8, width)],
+        1 + clusters,
+        [pltpu.VMEM((total + 8, width), jnp.float32)],
+    )(observed, *arrived)
     packed = total_over_devices(packed)
     updated = call(
         functools.partial(update_kernel, dims),
-        f32(clusters, terms, members, cols),
-        2,
+        [f32(terms, members, cols)] * clusters,
+        3,
         [pltpu.VMEM((total, total), jnp.float32)],
-    )(arrived, packed)
-    returned = lax.all_to_all(updated, ("group", "member"), split_axis=0, concat_axis=0, tiled=True)
-    placed = call(
-        functools.partial(place_kernel, (clusters, fields, block_rows, members, cols)),
-        f32(members * fields * rows, cols),
-        1,
-    )(returned)
-    return placed.reshape(members, fields, rows, cols)
+    )(anomaly, mean, packed)
+    return place(exchange(updated), fields).reshape(members, fields, rows, cols)
 
 
 def solution(mesh):

time: 108 us -> 96.8 us (0.90); the launches traced: 106 us -> 96.6 us
  blocking collectives: 22.4 us -> 0 us
  starting transfers between devices: 28.8 us -> 45.8 us
  waiting for transfers between devices: 29.7 us -> 26.6 us
    ppermute x0 -> x14, starting transfers between devices: none -> 25.9 us  [exchange(): got.append(lax.ppermute(value, ('group', 'member'), pairs))]
    all_to_all x1 -> x0, blocking collectives: 22.4 us -> none  [on_device(): lax.all_to_all(updated, ('group', 'member'), split_axis=0, concat_axis=0,...]
    all_to_all x1 -> x0, waiting for transfers between devices: 16.8 us -> none  [on_device(): lax.all_to_all(predicted, ('group', 'member'), split_axis=0, concat_axis=...]
    ppermute x0 -> x14, waiting for transfers between devices: none -> 14.5 us  [exchange(): got.append(lax.ppermute(value, ('group', 'member'), pairs))]
    all_to_all x1 -> x0, starting transfers between devices: 5.72 us -> none  [on_device(): lax.all_to_all(predicted, ('group', 'member'), split_axis=0, concat_axis=...]
    ppermute x11, waiting for transfers between devices: 7.87 us -> 11.5 us  [flip(): lax.ppermute(value, axis, [(i, i ^ bits) for i in range(lax.axis_size(axi...]
    ppermute x1, waiting for transfers between devices: 3.8 us -> 0.62 us  [forecast(): lax.ppermute(to_prev, 'space', [(i + 1, i) for i in range(count - 1)])]
    ppermute x11, starting transfers between devices: 17.8 us -> 14.6 us  [flip(): lax.ppermute(value, axis, [(i, i ^ bits) for i in range(lax.axis_size(axi...]
  transfers between devices with their start and end apart: 14 -> 27, of which waited for: 14 -> 17; matrix products, arithmetic and copies ran while one was open for 0% -> 0% of each run, Pallas kernels for 1% -> 5%
where the time goes in v3:
time: 96.8 us; the launch traced here: 96.6 us
  starting transfers between devices  45.8 us (47%)
  waiting for transfers between devices  26.6 us (27%)
  Pallas kernels  22.4 us (23%)
  local copies, waits for them, and re-layouts  1.49 us (2%)
    ppermute x14, starting transfers between devices, exchange(): got.append(lax.ppermute(value, ('group', 'member'), pairs))  25.9 us
    ppermute x11, starting transfers between devices, flip(): lax.ppermute(value, axis, [(i, i ^ bits) for i in range(lax.axis_size(axi...  14.6 us
    ppermute x14, waiting for transfers between devices, exchange(): got.append(lax.ppermute(value, ('group', 'member'), pairs))  14.5 us
    ppermute x11, waiting for transfers between devices, flip(): lax.ppermute(value, axis, [(i, i ^ bits) for i in range(lax.axis_size(axi...  11.5 us
    pallas_call x1, Pallas kernels, on_device(): call(functools.partial(update_kernel, dims), [f32(terms, members, cols)]...  11 us
    pallas_call x1, Pallas kernels, forecast(): call(functools.partial(interior_kernel, dims), f32(clusters, terms, membe...  4.32 us
    ppermute x1, starting transfers between devices, forecast(): lax.ppermute(to_next, 'space', [(i, i + 1) for i in range(count - 1)])  4.04 us
    pallas_call x1, Pallas kernels, place(): pl.pallas_call(functools.partial(place_kernel, (clusters, fields, terms /...  2.46 us
  transfers between devices with their start and end apart: 27, of which 17 were waited for; matrix products, arithmetic and copies ran while one was open for 0% of the time, Pallas kernels for 5%

profile of v3, /device:TPU:1, one launch (start us, length us, event | category | flops | bytes accessed | tf_op | source)
XLA Modules:
  0.0 96.6 jit_solution(2755830582016769648)
XLA Ops:
  0.0 1.4 %copy-done = f32[32,3,32,128]{3,2,1,0:T(8,128)S(1)} copy-done((f32[32,3,32,128]{3,2,1,0:T(8,128)S(1)}, f32[32,3,32,128]{3,2,1,0:T(8,128)}, u32[]{:S(2)}) %copy-start) | copy-done | bytes 1572888
  1.4 0.2 shard_map.47
  1.6 4.0 %collective-permute-start = (f32[9,32,128]{2,1,0:T(8,128)S(1)}, f32[9,32,128]{2,1,0:T(8,128)S(1)}, u32[]{:S(2)}, u32[]{:S(2)}) collective-permute-start(f32[9,32,128]{2,1,0:T(8,128)S(1)} %get-tuple-element.26), channel_id=1, source_target_pairs={{0,1},{1,2},{2,3},{4,5},{5,6},{6,7},{8,9},{9,10},{10,11},{12,13},{... | collective-permute-start | bytes 442376 | tf_op jit(solution)/shard_map/ppermute | solution.py:185
  5.7 1.3 %collective-permute-start.1 = (f32[9,32,128]{2,1,0:T(8,128)S(1)}, f32[9,32,128]{2,1,0:T(8,128)S(1)}, u32[]{:S(2)}, u32[]{:S(2)}) collective-permute-start(f32[9,32,128]{2,1,0:T(8,128)S(1)} %get-tuple-element.27), channel_id=1, source_target_pairs={{1,0},{2,1},{3,2},{5,4},{6,5},{7,6},{9,8},{10,9},{11,10},{13,12},{... | collective-permute-start | bytes 442376 | tf_op jit(solution)/shard_map/ppermute | solution.py:186
  7.0 4.3 %shard_map.48.interior_ref = f32[8,12,32,128]{3,2,1,0:T(8,128)S(1)} custom-call(f32[3072,128]{1,0:T(8,128)S(1)} %bitcast.23), custom_call_target="tpu_custom_call" | custom-call | flops 78643200 | bytes 6291456 | tf_op jit(solution)/shard_map/pallas_call | solution.py:190
  11.4 0.6 collective-permute-done.1.after_ref
  12.0 1.6 %shard_map.49 = (f32[12,32,128]{2,1,0:T(8,128)S(1)}, f32[12,32,128]{2,1,0:T(8,128)S(1)}, f32[12,32,128]{2,1,0:T(8,128)S(1)}, f32[12,32,128]{2,1,0:T(8,128)S(1)},...) custom-call(f32[3072,128]{1,0:T(8,128)S(1)} %bitcast.24, ...), custom_call_target="tpu_custom_call" | custom-call | tf_op jit(solution)/shard_map/pallas_call | solution.py:198
  13.6 1.3 %collective-permute-start.2 = (f32[12,32,128]{2,1,0:T(8,128)S(1)}, f32[12,32,128]{2,1,0:T(8,128)S(1)}, u32[]{:S(2)}, u32[]{:S(2)}) collective-permute-start(f32[12,32,128]{2,1,0:T(8,128)S(1)} %get-tuple-element.29), channel_id=1, source_target_pairs={{0,8},{4,12},{8,0},{12,4},{16,24},{20,28},{24,16},{28,20},{1,9},{5... | collective-permute-start | bytes 589832 | tf_op jit(solution)/shard_map/ppermute | solution.py:222
  14.8 1.2 %collective-permute-start.3 = (f32[12,32,128]{2,1,0:T(8,128)S(1)}, f32[12,32,128]{2,1,0:T(8,128)S(1)}, u32[]{:S(2)}, u32[]{:S(2)}) collective-permute-start(f32[12,32,128]{2,1,0:T(8,128)S(1)} %get-tuple-element.30), channel_id=1, source_target_pairs={{0,16},{4,20},{8,24},{12,28},{16,0},{20,4},{24,8},{28,12},{1,17},{... | collective-permute-start | bytes 589832 | tf_op jit(solution)/shard_map/ppermute | solution.py:222
  16.1 0.2 collective-permute-start.4
  16.3 3.8 %collective-permute-start.5 = (f32[12,32,128]{2,1,0:T(8,128)S(1)}, f32[12,32,128]{2,1,0:T(8,128)S(1)}, u32[]{:S(2)}, u32[]{:S(2)}) collective-permute-start(f32[12,32,128]{2,1,0:T(8,128)S(1)} %get-tuple-element.32), channel_id=1, source_target_pairs={{0,12},{4,8},{8,4},{12,0},{16,28},{20,24},{24,20},{28,16},{1,13},{... | collective-permute-start | bytes 589832 | tf_op jit(solution)/shard_map/ppermute | solution.py:222
  20.1 5.3 %collective-permute-start.7 = (f32[12,32,128]{2,1,0:T(8,128)S(1)}, f32[12,32,128]{2,1,0:T(8,128)S(1)}, u32[]{:S(2)}, u32[]{:S(2)}) collective-permute-start(f32[12,32,128]{2,1,0:T(8,128)S(1)} %get-tuple-element.34), channel_id=1, source_target_pairs={{0,28},{4,24},{8,20},{12,16},{16,12},{20,8},{24,4},{28,0},{1,29},{... | collective-permute-start | bytes 589832 | tf_op jit(solution)/shard_map/ppermute | solution.py:222
  25.4 1.6 %collective-permute-start.8 = (f32[12,32,128]{2,1,0:T(8,128)S(1)}, f32[12,32,128]{2,1,0:T(8,128)S(1)}, u32[]{:S(2)}, u32[]{:S(2)}) collective-permute-start(f32[12,32,128]{2,1,0:T(8,128)S(1)} %get-tuple-element.35), channel_id=1, source_target_pairs={{0,4},{4,0},{8,12},{12,8},{16,20},{20,16},{24,28},{28,24},{1,5},{5... | collective-permute-start | bytes 589832 | tf_op jit(solution)/shard_map/ppermute | solution.py:222
  26.9 0.7 shard_map.46.observed_ref
  27.7 3.5 %collective-permute-done.5.refs_4_ = f32[12,32,128]{2,1,0:T(8,128)S(1)} collective-permute-done((f32[12,32,128]{2,1,0:T(8,128)S(1)}, f32[12,32,128]{2,1,0:T(8,128)S(1)}, u32[]{:S(2)}, u32[]{:S(2)}) %collective-permute-start.5) | collective-permute-done | bytes 196640 | tf_op jit(solution)/shard_map/ppermute | solution.py:222
  31.2 3.1 %collective-permute-done.6.refs_5_ = f32[12,32,128]{2,1,0:T(8,128)S(1)} collective-permute-done((f32[12,32,128]{2,1,0:T(8,128)S(1)}, f32[12,32,128]{2,1,0:T(8,128)S(1)}, u32[]{:S(2)}, u32[]{:S(2)}) %collective-permute-start.6) | collective-permute-done | bytes 196640 | tf_op jit(solution)/shard_map/ppermute | solution.py:222
  34.4 2.1 %shard_map.50 = (f32[448,128]{1,0:T(8,128)S(1)}, f32[256,1536]{1,0:T(8,128)S(1)}, f32[8,1536]{1,0:T(8,128)S(1)}) custom-call(f32[8,1536]{1,0:T(8,128)S(1)} %shard_map.46.observed_ref, f32[12,32,128]{2,1,0:T(8,128)S(1)} %get-tuple-element.28.refs_0_, f32[12,32,128]{2,1,0:T(8,128)S(1)} %collective-permute-done.2.refs_1_, ...), custom_call_target="tpu_custom_call" | custom-call | tf_op jit(solution)/shard_map/pallas_call | solution.py:500
  36.6 1.3 %collective-permute-done.9 = f32[224,128]{1,0:T(8,128)S(1)} collective-permute-done((f32[224,128]{1,0:T(8,128)S(1)}, f32[224,128]{1,0:T(8,128)S(1)}, u32[]{:S(2)}, u32[]{:S(2)}) %collective-permute-start.9) | collective-permute-done | bytes 114720 | tf_op jit(solution)/shard_map/ppermute | solution.py:288
  37.9 0.8 collective-permute-start.10
  38.7 0.5 collective-permute-start.11
  39.2 1.4 %collective-permute-start.12 = (f32[56,128]{1,0:T(8,128)S(1)}, f32[56,128]{1,0:T(8,128)S(1)}, u32[]{:S(2)}, u32[]{:S(2)}) collective-permute-start(f32[56,128]{1,0:T(8,128)S(1)} %get-tuple-element.54), channel_id=1, source_target_pairs={{0,24},{8,16},{16,8},{24,0},{1,25},{9,17},{17,9},{25,1},{2,26},{10... | collective-permute-start | bytes 86024 | tf_op jit(solution)/shard_map/ppermute | solution.py:288
  40.7 0.9 collective-permute-done.11
  41.6 1.2 %collective-permute-done.12 = f32[56,128]{1,0:T(8,128)S(1)} collective-permute-done((f32[56,128]{1,0:T(8,128)S(1)}, f32[56,128]{1,0:T(8,128)S(1)}, u32[]{:S(2)}, u32[]{:S(2)}) %collective-permute-start.12) | collective-permute-done | bytes 28704 | tf_op jit(solution)/shard_map/ppermute | solution.py:288
  42.8 1.5 %collective-permute-start.13 = (f32[56,128]{1,0:T(8,128)S(1)}, f32[56,128]{1,0:T(8,128)S(1)}, u32[]{:S(2)}, u32[]{:S(2)}) collective-permute-start(f32[56,128]{1,0:T(8,128)S(1)} %bitcast_add_fusion), channel_id=1, source_target_pairs={{0,1},{1,0},{2,3},{3,2},{4,5},{5,4},{6,7},{7,6},{8,9},{9,8},{10,11... | collective-permute-start | bytes 86024 | tf_op jit(solution)/shard_map/ppermute | solution.py:288
  44.4 2.3 %collective-permute-start.14 = (f32[56,128]{1,0:T(8,128)S(1)}, f32[56,128]{1,0:T(8,128)S(1)}, u32[]{:S(2)}, u32[]{:S(2)}) collective-permute-start(f32[56,128]{1,0:T(8,128)S(1)} %bitcast_add_fusion), channel_id=1, source_target_pairs={{0,2},{1,3},{2,0},{3,1},{4,6},{5,7},{6,4},{7,5},{8,10},{9,11},{10,... | collective-permute-start | bytes 86024 | tf_op jit(solution)/shard_map/ppermute | solution.py:288
  46.7 1.6 %collective-permute-done.14 = f32[56,128]{1,0:T(8,128)S(1)} collective-permute-done((f32[56,128]{1,0:T(8,128)S(1)}, f32[56,128]{1,0:T(8,128)S(1)}, u32[]{:S(2)}, u32[]{:S(2)}) %collective-permute-start.14) | collective-permute-done | bytes 28704 | tf_op jit(solution)/shard_map/ppermute | solution.py:288
  48.3 2.9 %collective-permute-done.15 = f32[56,128]{1,0:T(8,128)S(1)} collective-permute-done((f32[56,128]{1,0:T(8,128)S(1)}, f32[56,128]{1,0:T(8,128)S(1)}, u32[]{:S(2)}, u32[]{:S(2)}) %collective-permute-start.15) | collective-permute-done | bytes 28704 | tf_op jit(solution)/shard_map/ppermute | solution.py:288
  51.2 1.3 %collective-permute-start.16 = (f32[56,128]{1,0:T(8,128)S(1)}, f32[56,128]{1,0:T(8,128)S(1)}, u32[]{:S(2)}, u32[]{:S(2)}) collective-permute-start(f32[56,128]{1,0:T(8,128)S(1)} %add_add_fusion), channel_id=1, source_target_pairs={{0,8},{8,0},{16,24},{24,16},{1,9},{9,1},{17,25},{25,17},{2,10},{10... | collective-permute-start | bytes 86024 | tf_op jit(solution)/shard_map/ppermute | solution.py:288
  52.5 0.3 collective-permute-start.17
  52.8 1.1 %collective-permute-start.18 = (f32[56,128]{1,0:T(8,128)S(1)}, f32[56,128]{1,0:T(8,128)S(1)}, u32[]{:S(2)}, u32[]{:S(2)}) collective-permute-start(f32[56,128]{1,0:T(8,128)S(1)} %add_add_fusion), channel_id=1, source_target_pairs={{0,24},{8,16},{16,8},{24,0},{1,25},{9,17},{17,9},{25,1},{2,26},{10... | collective-permute-start | bytes 86024 | tf_op jit(solution)/shard_map/ppermute | solution.py:288
  53.9 0.4 collective-permute-done.16
  54.3 0.9 collective-permute-done.17
  55.2 1.2 %collective-permute-done.18 = f32[56,128]{1,0:T(8,128)S(1)} collective-permute-done((f32[56,128]{1,0:T(8,128)S(1)}, f32[56,128]{1,0:T(8,128)S(1)}, u32[]{:S(2)}, u32[]{:S(2)}) %collective-permute-start.18) | collective-permute-done | bytes 28704 | tf_op jit(solution)/shard_map/ppermute | solution.py:288
  56.5 5.3 %collective-permute-start.19 = (f32[224,128]{1,0:T(8,128)S(1)}, f32[224,128]{1,0:T(8,128)S(1)}, u32[]{:S(2)}, u32[]{:S(2)}) collective-permute-start(f32[224,128]{1,0:T(8,128)S(1)} %pad_maximum_fusion.2), channel_id=1, source_target_pairs={{0,4},{4,0},{1,5},{5,1},{2,6},{6,2},{3,7},{7,3},{8,12},{12,8},{9,1... | collective-permute-start | bytes 344072 | tf_op jit(solution)/shard_map/ppermute | solution.py:288
  61.8 1.0 collective-permute-done.19
  62.8 11.0 %shard_map.51 = (f32[12,32,128]{2,1,0:T(8,128)S(1)}, f32[12,32,128]{2,1,0:T(8,128)S(1)}, f32[12,32,128]{2,1,0:T(8,128)S(1)}, f32[12,32,128]{2,1,0:T(8,128)S(1)},...) custom-call(f32[256,1536]{1,0:T(8,128)S(1)} %get-tuple-element.36.an, ...), custom_call_target="tpu_custom_call" | custom-call | tf_op jit(solution)/shard_map/pallas_call | solution.py:507
  73.8 1.0 %collective-permute-start.20 = (f32[12,32,128]{2,1,0:T(8,128)S(1)}, f32[12,32,128]{2,1,0:T(8,128)S(1)}, u32[]{:S(2)}, u32[]{:S(2)}) collective-permute-start(f32[12,32,128]{2,1,0:T(8,128)S(1)} %get-tuple-element.40), channel_id=1, source_target_pairs={{0,8},{4,12},{8,0},{12,4},{16,24},{20,28},{24,16},{28,20},{1,9},{5... | collective-permute-start | bytes 589832 | tf_op jit(solution)/shard_map/ppermute | solution.py:222
  74.8 0.5 collective-permute-start.21
  75.4 1.2 %collective-permute-start.22 = (f32[12,32,128]{2,1,0:T(8,128)S(1)}, f32[12,32,128]{2,1,0:T(8,128)S(1)}, u32[]{:S(2)}, u32[]{:S(2)}) collective-permute-start(f32[12,32,128]{2,1,0:T(8,128)S(1)} %get-tuple-element.42), channel_id=1, source_target_pairs={{0,24},{4,28},{8,16},{12,20},{16,8},{20,12},{24,0},{28,4},{1,25},{... | collective-permute-start | bytes 589832 | tf_op jit(solution)/shard_map/ppermute | solution.py:222
  76.5 2.0 %collective-permute-start.23 = (f32[12,32,128]{2,1,0:T(8,128)S(1)}, f32[12,32,128]{2,1,0:T(8,128)S(1)}, u32[]{:S(2)}, u32[]{:S(2)}) collective-permute-start(f32[12,32,128]{2,1,0:T(8,128)S(1)} %get-tuple-element.43), channel_id=1, source_target_pairs={{0,12},{4,8},{8,4},{12,0},{16,28},{20,24},{24,20},{28,16},{1,13},{... | collective-permute-start | bytes 589832 | tf_op jit(solution)/shard_map/ppermute | solution.py:222
  78.6 0.3 collective-permute-start.24
  78.8 1.1 %collective-permute-done.20.refs_1_ = f32[12,32,128]{2,1,0:T(8,128)S(1)} collective-permute-done((f32[12,32,128]{2,1,0:T(8,128)S(1)}, f32[12,32,128]{2,1,0:T(8,128)S(1)}, u32[]{:S(2)}, u32[]{:S(2)}) %collective-permute-start.20) | collective-permute-done | bytes 196640 | tf_op jit(solution)/shard_map/ppermute | solution.py:222
  80.0 3.1 %collective-permute-start.25 = (f32[12,32,128]{2,1,0:T(8,128)S(1)}, f32[12,32,128]{2,1,0:T(8,128)S(1)}, u32[]{:S(2)}, u32[]{:S(2)}) collective-permute-start(f32[12,32,128]{2,1,0:T(8,128)S(1)} %get-tuple-element.45), channel_id=1, source_target_pairs={{0,28},{4,24},{8,20},{12,16},{16,12},{20,8},{24,4},{28,0},{1,29},{... | collective-permute-start | bytes 589832 | tf_op jit(solution)/shard_map/ppermute | solution.py:222
  83.1 4.4 %collective-permute-start.26 = (f32[12,32,128]{2,1,0:T(8,128)S(1)}, f32[12,32,128]{2,1,0:T(8,128)S(1)}, u32[]{:S(2)}, u32[]{:S(2)}) collective-permute-start(f32[12,32,128]{2,1,0:T(8,128)S(1)} %get-tuple-element.46), channel_id=1, source_target_pairs={{0,4},{4,0},{8,12},{12,8},{16,20},{20,16},{24,28},{28,24},{1,5},{5... | collective-permute-start | bytes 589832 | tf_op jit(solution)/shard_map/ppermute | solution.py:222
  87.5 2.6 %collective-permute-done.23.refs_4_ = f32[12,32,128]{2,1,0:T(8,128)S(1)} collective-permute-done((f32[12,32,128]{2,1,0:T(8,128)S(1)}, f32[12,32,128]{2,1,0:T(8,128)S(1)}, u32[]{:S(2)}, u32[]{:S(2)}) %collective-permute-start.23) | collective-permute-done | bytes 196640 | tf_op jit(solution)/shard_map/ppermute | solution.py:222
  90.0 0.8 collective-permute-done.24.refs_5_
  90.9 3.2 %collective-permute-done.25.refs_6_ = f32[12,32,128]{2,1,0:T(8,128)S(1)} collective-permute-done((f32[12,32,128]{2,1,0:T(8,128)S(1)}, f32[12,32,128]{2,1,0:T(8,128)S(1)}, u32[]{:S(2)}, u32[]{:S(2)}) %collective-permute-start.25) | collective-permute-done | bytes 196640 | tf_op jit(solution)/shard_map/ppermute | solution.py:222
  94.1 2.5 %shard_map.52 = f32[3072,128]{1,0:T(8,128)} custom-call(f32[12,32,128]{2,1,0:T(8,128)S(1)} %get-tuple-element.39.refs_0_, f32[12,32,128]{2,1,0:T(8,128)S(1)} %collective-permute-done.20.refs_1_, f32[12,32,128]{2,1,0:T(8,128)S(1)} %collective-permute-done.21.refs_2_, f32[12,32,128]{2,1,0:T(8,128)S(1)} %collective-permute-done.22.refs_3_, ...), custom_call_target="tpu_custom_call" | custom-call | tf_op jit(solution)/shard_map/pallas_call | solution.py:481
  (31 shorter events, 0.4 us)
Async XLA Ops:
  0.0 1.4 %copy-start = (f32[32,3,32,128]{3,2,1,0:T(8,128)S(1)}, f32[32,3,32,128]{3,2,1,0:T(8,128)}, u32[]{:S(2)}) copy-start(f32[32,3,32,128]{3,2,1,0:T(8,128)} %bottom_ref.1) | copy-start | bytes 4718596
  1.6 9.7 %collective-permute-start = (f32[9,32,128]{2,1,0:T(8,128)S(1)}, f32[9,32,128]{2,1,0:T(8,128)S(1)}, u32[]{:S(2)}, u32[]{:S(2)}) collective-permute-start(f32[9,32,128]{2,1,0:T(8,128)S(1)} %get-tuple-element.26), channel_id=1, source_target_pairs={{0,1},{1,2},{2,3},{4,5},{5,6},{6,7},{8,9},{9,10},{10,11},{12,13},{... | collective-permute-start | bytes 442376 | tf_op jit(solution)/shard_map/ppermute | solution.py:185
  5.7 6.3 %collective-permute-start.1 = (f32[9,32,128]{2,1,0:T(8,128)S(1)}, f32[9,32,128]{2,1,0:T(8,128)S(1)}, u32[]{:S(2)}, u32[]{:S(2)}) collective-permute-start(f32[9,32,128]{2,1,0:T(8,128)S(1)} %get-tuple-element.27), channel_id=1, source_target_pairs={{1,0},{2,1},{3,2},{5,4},{6,5},{7,6},{9,8},{10,9},{11,10},{13,12},{... | collective-permute-start | bytes 442376 | tf_op jit(solution)/shard_map/ppermute | solution.py:186
  11.3 15.6 %copy-start.1 = (f32[1,768]{1,0:T(1,128)S(1)}, f32[1,768]{1,0:T(1,128)}, u32[]{:S(2)}) copy-start(f32[1,768]{1,0:T(1,128)} %values_ref.1) | copy-start | bytes 9220
  11.3 15.6 %copy-start.2 = (f32[1,768]{1,0:T(1,128)S(1)}, f32[1,768]{1,0:T(1,128)}, u32[]{:S(2)}) copy-start(f32[1,768]{1,0:T(1,128)} %precision_ref.1) | copy-start | bytes 9220
  11.3 15.6 %copy-start.3 = (s32[1,768]{1,0:T(1,128)S(1)}, s32[1,768]{1,0:T(1,128)}, u32[]{:S(2)}) copy-start(s32[1,768]{1,0:T(1,128)} %index_ref.1) | copy-start | bytes 9220
  13.6 6.6 %collective-permute-start.2 = (f32[12,32,128]{2,1,0:T(8,128)S(1)}, f32[12,32,128]{2,1,0:T(8,128)S(1)}, u32[]{:S(2)}, u32[]{:S(2)}) collective-permute-start(f32[12,32,128]{2,1,0:T(8,128)S(1)} %get-tuple-element.29), channel_id=1, source_target_pairs={{0,8},{4,12},{8,0},{12,4},{16,24},{20,28},{24,16},{28,20},{1,9},{5... | collective-permute-start | bytes 589832 | tf_op jit(solution)/shard_map/ppermute | solution.py:222
  14.8 10.5 %collective-permute-start.3 = (f32[12,32,128]{2,1,0:T(8,128)S(1)}, f32[12,32,128]{2,1,0:T(8,128)S(1)}, u32[]{:S(2)}, u32[]{:S(2)}) collective-permute-start(f32[12,32,128]{2,1,0:T(8,128)S(1)} %get-tuple-element.30), channel_id=1, source_target_pairs={{0,16},{4,20},{8,24},{12,28},{16,0},{20,4},{24,8},{28,12},{1,17},{... | collective-permute-start | bytes 589832 | tf_op jit(solution)/shard_map/ppermute | solution.py:222
  16.1 11.6 %collective-permute-start.4 = (f32[12,32,128]{2,1,0:T(8,128)S(1)}, f32[12,32,128]{2,1,0:T(8,128)S(1)}, u32[]{:S(2)}, u32[]{:S(2)}) collective-permute-start(f32[12,32,128]{2,1,0:T(8,128)S(1)} %get-tuple-element.31), channel_id=1, source_target_pairs={{0,24},{4,28},{8,16},{12,20},{16,8},{20,12},{24,0},{28,4},{1,25},{... | collective-permute-start | bytes 589832 | tf_op jit(solution)/shard_map/ppermute | solution.py:222
  16.3 15.0 %collective-permute-start.5 = (f32[12,32,128]{2,1,0:T(8,128)S(1)}, f32[12,32,128]{2,1,0:T(8,128)S(1)}, u32[]{:S(2)}, u32[]{:S(2)}) collective-permute-start(f32[12,32,128]{2,1,0:T(8,128)S(1)} %get-tuple-element.32), channel_id=1, source_target_pairs={{0,12},{4,8},{8,4},{12,0},{16,28},{20,24},{24,20},{28,16},{1,13},{... | collective-permute-start | bytes 589832 | tf_op jit(solution)/shard_map/ppermute | solution.py:222
  20.1 14.3 %collective-permute-start.6 = (f32[12,32,128]{2,1,0:T(8,128)S(1)}, f32[12,32,128]{2,1,0:T(8,128)S(1)}, u32[]{:S(2)}, u32[]{:S(2)}) collective-permute-start(f32[12,32,128]{2,1,0:T(8,128)S(1)} %get-tuple-element.33), channel_id=1, source_target_pairs={{0,20},{4,16},{8,28},{12,24},{16,4},{20,0},{24,12},{28,8},{1,21},{... | collective-permute-start | bytes 589832 | tf_op jit(solution)/shard_map/ppermute | solution.py:222
  20.1 14.3 %collective-permute-start.7 = (f32[12,32,128]{2,1,0:T(8,128)S(1)}, f32[12,32,128]{2,1,0:T(8,128)S(1)}, u32[]{:S(2)}, u32[]{:S(2)}) collective-permute-start(f32[12,32,128]{2,1,0:T(8,128)S(1)} %get-tuple-element.34), channel_id=1, source_target_pairs={{0,28},{4,24},{8,20},{12,16},{16,12},{20,8},{24,4},{28,0},{1,29},{... | collective-permute-start | bytes 589832 | tf_op jit(solution)/shard_map/ppermute | solution.py:222
  25.4 9.0 %collective-permute-start.8 = (f32[12,32,128]{2,1,0:T(8,128)S(1)}, f32[12,32,128]{2,1,0:T(8,128)S(1)}, u32[]{:S(2)}, u32[]{:S(2)}) collective-permute-start(f32[12,32,128]{2,1,0:T(8,128)S(1)} %get-tuple-element.35), channel_id=1, source_target_pairs={{0,4},{4,0},{8,12},{12,8},{16,20},{20,16},{24,28},{28,24},{1,5},{5... | collective-permute-start | bytes 589832 | tf_op jit(solution)/shard_map/ppermute | solution.py:222
  36.5 1.4 %collective-permute-start.9 = (f32[224,128]{1,0:T(8,128)S(1)}, f32[224,128]{1,0:T(8,128)S(1)}, u32[]{:S(2)}, u32[]{:S(2)}) collective-permute-start(f32[224,128]{1,0:T(8,128)S(1)} %constant_dynamic-slice_fusion), channel_id=1, source_target_pairs={{0,4},{4,0},{1,5},{5,1},{2,6},{6,2},{3,7},{7,3},{8,12},{12,8},{9,1... | collective-permute-start | bytes 344072 | tf_op jit(solution)/shard_map/ppermute | solution.py:288
  37.9 2.8 %collective-permute-start.10 = (f32[56,128]{1,0:T(8,128)S(1)}, f32[56,128]{1,0:T(8,128)S(1)}, u32[]{:S(2)}, u32[]{:S(2)}) collective-permute-start(f32[56,128]{1,0:T(8,128)S(1)} %get-tuple-element.55), channel_id=1, source_target_pairs={{0,8},{8,0},{16,24},{24,16},{1,9},{9,1},{17,25},{25,17},{2,10},{10... | collective-permute-start | bytes 86024 | tf_op jit(solution)/shard_map/ppermute | solution.py:288
  38.7 3.0 %collective-permute-start.11 = (f32[56,128]{1,0:T(8,128)S(1)}, f32[56,128]{1,0:T(8,128)S(1)}, u32[]{:S(2)}, u32[]{:S(2)}) collective-permute-start(f32[56,128]{1,0:T(8,128)S(1)} %get-tuple-element.53), channel_id=1, source_target_pairs={{0,16},{8,24},{16,0},{24,8},{1,17},{9,25},{17,1},{25,9},{2,18},{10... | collective-permute-start | bytes 86024 | tf_op jit(solution)/shard_map/ppermute | solution.py:288
  39.2 3.6 %collective-permute-start.12 = (f32[56,128]{1,0:T(8,128)S(1)}, f32[56,128]{1,0:T(8,128)S(1)}, u32[]{:S(2)}, u32[]{:S(2)}) collective-permute-start(f32[56,128]{1,0:T(8,128)S(1)} %get-tuple-element.54), channel_id=1, source_target_pairs={{0,24},{8,16},{16,8},{24,0},{1,25},{9,17},{17,9},{25,1},{2,26},{10... | collective-permute-start | bytes 86024 | tf_op jit(solution)/shard_map/ppermute | solution.py:288
  42.8 3.9 %collective-permute-start.13 = (f32[56,128]{1,0:T(8,128)S(1)}, f32[56,128]{1,0:T(8,128)S(1)}, u32[]{:S(2)}, u32[]{:S(2)}) collective-permute-start(f32[56,128]{1,0:T(8,128)S(1)} %bitcast_add_fusion), channel_id=1, source_target_pairs={{0,1},{1,0},{2,3},{3,2},{4,5},{5,4},{6,7},{7,6},{8,9},{9,8},{10,11... | collective-permute-start | bytes 86024 | tf_op jit(solution)/shard_map/ppermute | solution.py:288
  44.4 3.9 %collective-permute-start.14 = (f32[56,128]{1,0:T(8,128)S(1)}, f32[56,128]{1,0:T(8,128)S(1)}, u32[]{:S(2)}, u32[]{:S(2)}) collective-permute-start(f32[56,128]{1,0:T(8,128)S(1)} %bitcast_add_fusion), channel_id=1, source_target_pairs={{0,2},{1,3},{2,0},{3,1},{4,6},{5,7},{6,4},{7,5},{8,10},{9,11},{10,... | collective-permute-start | bytes 86024 | tf_op jit(solution)/shard_map/ppermute | solution.py:288
  46.7 4.5 %collective-permute-start.15 = (f32[56,128]{1,0:T(8,128)S(1)}, f32[56,128]{1,0:T(8,128)S(1)}, u32[]{:S(2)}, u32[]{:S(2)}) collective-permute-start(f32[56,128]{1,0:T(8,128)S(1)} %bitcast_add_fusion), channel_id=1, source_target_pairs={{0,3},{1,2},{2,1},{3,0},{4,7},{5,6},{6,5},{7,4},{8,11},{9,10},{10,... | collective-permute-start | bytes 86024 | tf_op jit(solution)/shard_map/ppermute | solution.py:288
  51.2 3.1 %collective-permute-start.16 = (f32[56,128]{1,0:T(8,128)S(1)}, f32[56,128]{1,0:T(8,128)S(1)}, u32[]{:S(2)}, u32[]{:S(2)}) collective-permute-start(f32[56,128]{1,0:T(8,128)S(1)} %add_add_fusion), channel_id=1, source_target_pairs={{0,8},{8,0},{16,24},{24,16},{1,9},{9,1},{17,25},{25,17},{2,10},{10... | collective-permute-start | bytes 86024 | tf_op jit(solution)/shard_map/ppermute | solution.py:288
  52.5 2.7 %collective-permute-start.17 = (f32[56,128]{1,0:T(8,128)S(1)}, f32[56,128]{1,0:T(8,128)S(1)}, u32[]{:S(2)}, u32[]{:S(2)}) collective-permute-start(f32[56,128]{1,0:T(8,128)S(1)} %add_add_fusion), channel_id=1, source_target_pairs={{0,16},{8,24},{16,0},{24,8},{1,17},{9,25},{17,1},{25,9},{2,18},{10... | collective-permute-start | bytes 86024 | tf_op jit(solution)/shard_map/ppermute | solution.py:288
  52.8 3.6 %collective-permute-start.18 = (f32[56,128]{1,0:T(8,128)S(1)}, f32[56,128]{1,0:T(8,128)S(1)}, u32[]{:S(2)}, u32[]{:S(2)}) collective-permute-start(f32[56,128]{1,0:T(8,128)S(1)} %add_add_fusion), channel_id=1, source_target_pairs={{0,24},{8,16},{16,8},{24,0},{1,25},{9,17},{17,9},{25,1},{2,26},{10... | collective-permute-start | bytes 86024 | tf_op jit(solution)/shard_map/ppermute | solution.py:288
  56.5 6.2 %collective-permute-start.19 = (f32[224,128]{1,0:T(8,128)S(1)}, f32[224,128]{1,0:T(8,128)S(1)}, u32[]{:S(2)}, u32[]{:S(2)}) collective-permute-start(f32[224,128]{1,0:T(8,128)S(1)} %pad_maximum_fusion.2), channel_id=1, source_target_pairs={{0,4},{4,0},{1,5},{5,1},{2,6},{6,2},{3,7},{7,3},{8,12},{12,8},{9,1... | collective-permute-start | bytes 344072 | tf_op jit(solution)/shard_map/ppermute | solution.py:288
  73.8 6.2 %collective-permute-start.20 = (f32[12,32,128]{2,1,0:T(8,128)S(1)}, f32[12,32,128]{2,1,0:T(8,128)S(1)}, u32[]{:S(2)}, u32[]{:S(2)}) collective-permute-start(f32[12,32,128]{2,1,0:T(8,128)S(1)} %get-tuple-element.40), channel_id=1, source_target_pairs={{0,8},{4,12},{8,0},{12,4},{16,24},{20,28},{24,16},{28,20},{1,9},{5... | collective-permute-start | bytes 589832 | tf_op jit(solution)/shard_map/ppermute | solution.py:222
  74.8 8.3 %collective-permute-start.21 = (f32[12,32,128]{2,1,0:T(8,128)S(1)}, f32[12,32,128]{2,1,0:T(8,128)S(1)}, u32[]{:S(2)}, u32[]{:S(2)}) collective-permute-start(f32[12,32,128]{2,1,0:T(8,128)S(1)} %get-tuple-element.41), channel_id=1, source_target_pairs={{0,16},{4,20},{8,24},{12,28},{16,0},{20,4},{24,8},{28,12},{1,17},{... | collective-permute-start | bytes 589832 | tf_op jit(solution)/shard_map/ppermute | solution.py:222
  75.4 12.1 %collective-permute-start.22 = (f32[12,32,128]{2,1,0:T(8,128)S(1)}, f32[12,32,128]{2,1,0:T(8,128)S(1)}, u32[]{:S(2)}, u32[]{:S(2)}) collective-permute-start(f32[12,32,128]{2,1,0:T(8,128)S(1)} %get-tuple-element.42), channel_id=1, source_target_pairs={{0,24},{4,28},{8,16},{12,20},{16,8},{20,12},{24,0},{28,4},{1,25},{... | collective-permute-start | bytes 589832 | tf_op jit(solution)/shard_map/ppermute | solution.py:222
  76.5 13.5 %collective-permute-start.23 = (f32[12,32,128]{2,1,0:T(8,128)S(1)}, f32[12,32,128]{2,1,0:T(8,128)S(1)}, u32[]{:S(2)}, u32[]{:S(2)}) collective-permute-start(f32[12,32,128]{2,1,0:T(8,128)S(1)} %get-tuple-element.43), channel_id=1, source_target_pairs={{0,12},{4,8},{8,4},{12,0},{16,28},{20,24},{24,20},{28,16},{1,13},{... | collective-permute-start | bytes 589832 | tf_op jit(solution)/shard_map/ppermute | solution.py:222
  78.6 12.3 %collective-permute-start.24 = (f32[12,32,128]{2,1,0:T(8,128)S(1)}, f32[12,32,128]{2,1,0:T(8,128)S(1)}, u32[]{:S(2)}, u32[]{:S(2)}) collective-permute-start(f32[12,32,128]{2,1,0:T(8,128)S(1)} %get-tuple-element.44), channel_id=1, source_target_pairs={{0,20},{4,16},{8,28},{12,24},{16,4},{20,0},{24,12},{28,8},{1,21},{... | collective-permute-start | bytes 589832 | tf_op jit(solution)/shard_map/ppermute | solution.py:222
  80.0 14.1 %collective-permute-start.25 = (f32[12,32,128]{2,1,0:T(8,128)S(1)}, f32[12,32,128]{2,1,0:T(8,128)S(1)}, u32[]{:S(2)}, u32[]{:S(2)}) collective-permute-start(f32[12,32,128]{2,1,0:T(8,128)S(1)} %get-tuple-element.45), channel_id=1, source_target_pairs={{0,28},{4,24},{8,20},{12,16},{16,12},{20,8},{24,4},{28,0},{1,29},{... | collective-permute-start | bytes 589832 | tf_op jit(solution)/shard_map/ppermute | solution.py:222
  83.1 11.1 %collective-permute-start.26 = (f32[12,32,128]{2,1,0:T(8,128)S(1)}, f32[12,32,128]{2,1,0:T(8,128)S(1)}, u32[]{:S(2)}, u32[]{:S(2)}) collective-permute-start(f32[12,32,128]{2,1,0:T(8,128)S(1)} %get-tuple-element.46), channel_id=1, source_target_pairs={{0,4},{4,0},{8,12},{12,8},{16,20},{20,16},{24,28},{28,24},{1,5},{5... | collective-permute-start | bytes 589832 | tf_op jit(solution)/shard_map/ppermute | solution.py:222

commit v4 on v3

--- a/solution.py
+++ b/solution.py
@@ -304,7 +304,7 @@
     piece = pieces[0] + (
         flip(pieces[1], "group", 1) + flip(pieces[2], "group", 2) + flip(pieces[3], "group", 3)
     )
-    piece = piece + (flip(piece, "space", 1) + flip(piece, "space", 2) + flip(piece, "space", 3))
+    piece = piece + (flip(piece, "space", 3) + flip(piece, "space", 2) + flip(piece, "space", 1))
     got = jnp.stack([piece] + [flip(piece, "group", s) for s in (1, 2, 3)], axis=0)
     mine = jnp.concatenate(
         [lax.dynamic_index_in_dim(got, chip ^ i, 0, False) for i in range(4)], axis=0
@@ -325,23 +325,29 @@
     )
 
 
-def inverse_factor(block):
-    size = block.shape[0]
+def eliminate(panel, first):
     tile = 8
+    size, width = panel.shape
     count = size // tile
-    rows = [block[at : at + tile, :] for at in range(0, size, tile)]
-    lane = lax.broadcasted_iota(jnp.int32, (tile, size), 1)
-    sublane = lax.broadcasted_iota(jnp.int32, (tile, size), 0)
+    rows = [panel[at : at + tile, :] for at in range(0, size, tile)]
+    lane = lax.broadcasted_iota(jnp.int32, (tile, width), 1)
+    sublane = lax.broadcasted_iota(jnp.int32, (tile, width), 0)
 
     def row(value, at):
-        return jnp.broadcast_to(value[at : at + 1, :], (tile, size))
+        return jnp.broadcast_to(value[at : at + 1, :], (tile, width))
 
     def column(value, at):
-        return jnp.broadcast_to(value[:, at : at + 1], (tile, size))
-
+        return jnp.broadcast_to(value[:, at : at + 1], (tile, width))
+
+    ahead = None
     for own in range(count):
-        start = own * tile
+        start = first + own * tile
         columns = [[column(value, start + k) for k in range(tile)] for value in rows[own:]]
+        if ahead is not None:
+            columns[0] = ahead
+        if own + 1 < count:
+            for value, spread in zip(rows[own : own + 2], columns):
+                spread += [column(value, start + k) for k in range(tile, 2 * tile)]
         pivots = (lane >= start) & (lane < start + tile)
         cleared = [jnp.where(pivots, 0.0, value) for value in rows[own:]]
         local = columns[0]
@@ -354,7 +360,7 @@
             inv1 = s00 * (1.0 / (s00 * s11 - s10 * s10))
             low = s10 * inv0
             upper = []
-            for k in range(p + 2, tile):
+            for k in range(p + 2, len(local)):
                 u0 = row(local[k], p)
                 upper.append((u0 * inv0, (row(local[k], p + 1) - low * u0) * inv1))
             r0 = row(right, p)
@@ -364,17 +370,36 @@
             done = jnp.where(sublane == p + 1, r1 * (inv1 * lax.rsqrt(inv1)), done)
             for value in columns:
                 value[p + 1] = value[p + 1] - low * value[p]
-                for k, (u0, u1) in zip(range(p + 2, tile), upper):
+                for k, (u0, u1) in zip(range(p + 2, len(value)), upper):
                     value[k] = value[k] - (value[p] * u0 + value[p + 1] * u1)
             if p + 2 < tile:
                 right = right - (local[p] * solved[p] + local[p + 1] * solved[p + 1])
-        rows[own] = jnp.where(lane - start <= sublane, done, 0.0)
+        rows[own] = jnp.where((lane - start > sublane) & (lane < first + size), 0.0, done)
+        if own + 1 < count:
+            ahead = columns[1][tile:]
         for k in range(own + 1, count):
             terms = [left * value for left, value in zip(columns[k - own], solved)]
             while len(terms) > 1:
                 terms = [x + y for x, y in zip(terms[::2], terms[1::2])]
             rows[k] = cleared[k - own] - terms[0]
     return jnp.concatenate(rows, axis=0)
+
+
+def inverse_factor(block, panel=64):
+    size = block.shape[0]
+    done = []
+    rest = block
+    for first in range(0, size, panel):
+        rows = eliminate(rest[:panel], first)
+        lane = lax.broadcasted_iota(jnp.int32, rows.shape, 1)
+        done.append(jnp.where(lane < first + panel, rows, 0.0))
+        if first + panel < size:
+            rest = rest[panel:]
+            lane = lax.broadcasted_iota(jnp.int32, rest.shape, 1)
+            pivots = (lane >= first) & (lane < first + panel)
+            change = product(rows, rows, ((0,), (0,)))
+            rest = jnp.where(pivots, 0.0, rest) - change[first + panel :]
+    return jnp.concatenate(done, axis=0)
 
 
 def transform_of(packed_ref, total):

time: 96.8 us -> 93.2 us (0.963)
  Pallas kernels: 22.4 us -> 20.2 us
  waiting for transfers between devices: 26.6 us -> 25.6 us
    pallas_call x1, Pallas kernels: 11 us -> 8.88 us  [on_device(): call(functools.partial(update_kernel, dims), [f32(terms, members, cols)]...]
    ppermute x11, waiting for transfers between devices: 11.5 us -> 10.4 us  [flip(): lax.ppermute(value, axis, [(i, i ^ bits) for i in range(lax.axis_size(axi...]
where the time goes in v4:
time: 93.2 us; the launch traced here: 93 us
  starting transfers between devices  45.4 us (49%)
  waiting for transfers between devices  25.6 us (27%)
  Pallas kernels  20.2 us (22%)
  local copies, waits for them, and re-layouts  1.49 us (2%)
    ppermute x14, starting transfers between devices, exchange(): got.append(lax.ppermute(value, ('group', 'member'), pairs))  25.9 us
    ppermute x14, waiting for transfers between devices, exchange(): got.append(lax.ppermute(value, ('group', 'member'), pairs))  14.5 us
    ppermute x11, starting transfers between devices, flip(): lax.ppermute(value, axis, [(i, i ^ bits) for i in range(lax.axis_size(axi...  14.2 us
    ppermute x11, waiting for transfers between devices, flip(): lax.ppermute(value, axis, [(i, i ^ bits) for i in range(lax.axis_size(axi...  10.4 us
    pallas_call x1, Pallas kernels, on_device(): call(functools.partial(update_kernel, dims), [f32(terms, members, cols)]...  8.88 us
    pallas_call x1, Pallas kernels, forecast(): call(functools.partial(interior_kernel, dims), f32(clusters, terms, membe...  4.32 us
    ppermute x1, starting transfers between devices, forecast(): lax.ppermute(to_next, 'space', [(i, i + 1) for i in range(count - 1)])  4.04 us
    pallas_call x1, Pallas kernels, place(): pl.pallas_call(functools.partial(place_kernel, (clusters, fields, terms /...  2.46 us
  transfers between devices with their start and end apart: 27, of which 17 were waited for; matrix products, arithmetic and copies ran while one was open for 0% of the time, Pallas kernels for 5%

profile of v4, /device:TPU:1, one launch (start us, length us, event | category | flops | bytes accessed | tf_op | source)
XLA Modules:
  0.0 93.0 jit_solution(5347988515776704057)
XLA Ops:
  0.0 1.4 %copy-done = f32[32,3,32,128]{3,2,1,0:T(8,128)S(1)} copy-done((f32[32,3,32,128]{3,2,1,0:T(8,128)S(1)}, f32[32,3,32,128]{3,2,1,0:T(8,128)}, u32[]{:S(2)}) %copy-start) | copy-done | bytes 1572888
  1.4 0.2 shard_map.47
  1.6 4.0 %collective-permute-start = (f32[9,32,128]{2,1,0:T(8,128)S(1)}, f32[9,32,128]{2,1,0:T(8,128)S(1)}, u32[]{:S(2)}, u32[]{:S(2)}) collective-permute-start(f32[9,32,128]{2,1,0:T(8,128)S(1)} %get-tuple-element.26), channel_id=1, source_target_pairs={{0,1},{1,2},{2,3},{4,5},{5,6},{6,7},{8,9},{9,10},{10,11},{12,13},{... | collective-permute-start | bytes 442376 | tf_op jit(solution)/shard_map/ppermute | solution.py:185
  5.7 1.3 %collective-permute-start.1 = (f32[9,32,128]{2,1,0:T(8,128)S(1)}, f32[9,32,128]{2,1,0:T(8,128)S(1)}, u32[]{:S(2)}, u32[]{:S(2)}) collective-permute-start(f32[9,32,128]{2,1,0:T(8,128)S(1)} %get-tuple-element.27), channel_id=1, source_target_pairs={{1,0},{2,1},{3,2},{5,4},{6,5},{7,6},{9,8},{10,9},{11,10},{13,12},{... | collective-permute-start | bytes 442376 | tf_op jit(solution)/shard_map/ppermute | solution.py:186
  7.0 4.3 %shard_map.48.interior_ref = f32[8,12,32,128]{3,2,1,0:T(8,128)S(1)} custom-call(f32[3072,128]{1,0:T(8,128)S(1)} %bitcast.23), custom_call_target="tpu_custom_call" | custom-call | flops 78643200 | bytes 6291456 | tf_op jit(solution)/shard_map/pallas_call | solution.py:190
  11.4 0.6 collective-permute-done.1.after_ref
  12.0 1.6 %shard_map.49 = (f32[12,32,128]{2,1,0:T(8,128)S(1)}, f32[12,32,128]{2,1,0:T(8,128)S(1)}, f32[12,32,128]{2,1,0:T(8,128)S(1)}, f32[12,32,128]{2,1,0:T(8,128)S(1)},...) custom-call(f32[3072,128]{1,0:T(8,128)S(1)} %bitcast.24, ...), custom_call_target="tpu_custom_call" | custom-call | tf_op jit(solution)/shard_map/pallas_call | solution.py:198
  13.6 1.3 %collective-permute-start.2 = (f32[12,32,128]{2,1,0:T(8,128)S(1)}, f32[12,32,128]{2,1,0:T(8,128)S(1)}, u32[]{:S(2)}, u32[]{:S(2)}) collective-permute-start(f32[12,32,128]{2,1,0:T(8,128)S(1)} %get-tuple-element.29), channel_id=1, source_target_pairs={{0,8},{4,12},{8,0},{12,4},{16,24},{20,28},{24,16},{28,20},{1,9},{5... | collective-permute-start | bytes 589832 | tf_op jit(solution)/shard_map/ppermute | solution.py:222
  14.8 1.2 %collective-permute-start.3 = (f32[12,32,128]{2,1,0:T(8,128)S(1)}, f32[12,32,128]{2,1,0:T(8,128)S(1)}, u32[]{:S(2)}, u32[]{:S(2)}) collective-permute-start(f32[12,32,128]{2,1,0:T(8,128)S(1)} %get-tuple-element.30), channel_id=1, source_target_pairs={{0,16},{4,20},{8,24},{12,28},{16,0},{20,4},{24,8},{28,12},{1,17},{... | collective-permute-start | bytes 589832 | tf_op jit(solution)/shard_map/ppermute | solution.py:222
  16.1 0.2 collective-permute-start.4
  16.3 3.8 %collective-permute-start.5 = (f32[12,32,128]{2,1,0:T(8,128)S(1)}, f32[12,32,128]{2,1,0:T(8,128)S(1)}, u32[]{:S(2)}, u32[]{:S(2)}) collective-permute-start(f32[12,32,128]{2,1,0:T(8,128)S(1)} %get-tuple-element.32), channel_id=1, source_target_pairs={{0,12},{4,8},{8,4},{12,0},{16,28},{20,24},{24,20},{28,16},{1,13},{... | collective-permute-start | bytes 589832 | tf_op jit(solution)/shard_map/ppermute | solution.py:222
  20.1 5.3 %collective-permute-start.7 = (f32[12,32,128]{2,1,0:T(8,128)S(1)}, f32[12,32,128]{2,1,0:T(8,128)S(1)}, u32[]{:S(2)}, u32[]{:S(2)}) collective-permute-start(f32[12,32,128]{2,1,0:T(8,128)S(1)} %get-tuple-element.34), channel_id=1, source_target_pairs={{0,28},{4,24},{8,20},{12,16},{16,12},{20,8},{24,4},{28,0},{1,29},{... | collective-permute-start | bytes 589832 | tf_op jit(solution)/shard_map/ppermute | solution.py:222
  25.4 1.6 %collective-permute-start.8 = (f32[12,32,128]{2,1,0:T(8,128)S(1)}, f32[12,32,128]{2,1,0:T(8,128)S(1)}, u32[]{:S(2)}, u32[]{:S(2)}) collective-permute-start(f32[12,32,128]{2,1,0:T(8,128)S(1)} %get-tuple-element.35), channel_id=1, source_target_pairs={{0,4},{4,0},{8,12},{12,8},{16,20},{20,16},{24,28},{28,24},{1,5},{5... | collective-permute-start | bytes 589832 | tf_op jit(solution)/shard_map/ppermute | solution.py:222
  26.9 0.7 shard_map.46.observed_ref
  27.7 3.5 %collective-permute-done.5.refs_4_ = f32[12,32,128]{2,1,0:T(8,128)S(1)} collective-permute-done((f32[12,32,128]{2,1,0:T(8,128)S(1)}, f32[12,32,128]{2,1,0:T(8,128)S(1)}, u32[]{:S(2)}, u32[]{:S(2)}) %collective-permute-start.5) | collective-permute-done | bytes 196640 | tf_op jit(solution)/shard_map/ppermute | solution.py:222
  31.2 3.1 %collective-permute-done.6.refs_5_ = f32[12,32,128]{2,1,0:T(8,128)S(1)} collective-permute-done((f32[12,32,128]{2,1,0:T(8,128)S(1)}, f32[12,32,128]{2,1,0:T(8,128)S(1)}, u32[]{:S(2)}, u32[]{:S(2)}) %collective-permute-start.6) | collective-permute-done | bytes 196640 | tf_op jit(solution)/shard_map/ppermute | solution.py:222
  34.4 2.1 %shard_map.50 = (f32[448,128]{1,0:T(8,128)S(1)}, f32[256,1536]{1,0:T(8,128)S(1)}, f32[8,1536]{1,0:T(8,128)S(1)}) custom-call(f32[8,1536]{1,0:T(8,128)S(1)} %shard_map.46.observed_ref, f32[12,32,128]{2,1,0:T(8,128)S(1)} %get-tuple-element.28.refs_0_, f32[12,32,128]{2,1,0:T(8,128)S(1)} %collective-permute-done.2.refs_1_, ...), custom_call_target="tpu_custom_call" | custom-call | tf_op jit(solution)/shard_map/pallas_call | solution.py:525
  36.6 1.3 %collective-permute-done.9 = f32[224,128]{1,0:T(8,128)S(1)} collective-permute-done((f32[224,128]{1,0:T(8,128)S(1)}, f32[224,128]{1,0:T(8,128)S(1)}, u32[]{:S(2)}, u32[]{:S(2)}) %collective-permute-start.9) | collective-permute-done | bytes 114720 | tf_op jit(solution)/shard_map/ppermute | solution.py:288
  37.9 0.8 collective-permute-start.10
  38.7 0.5 collective-permute-start.11
  39.2 1.4 %collective-permute-start.12 = (f32[56,128]{1,0:T(8,128)S(1)}, f32[56,128]{1,0:T(8,128)S(1)}, u32[]{:S(2)}, u32[]{:S(2)}) collective-permute-start(f32[56,128]{1,0:T(8,128)S(1)} %get-tuple-element.54), channel_id=1, source_target_pairs={{0,24},{8,16},{16,8},{24,0},{1,25},{9,17},{17,9},{25,1},{2,26},{10... | collective-permute-start | bytes 86024 | tf_op jit(solution)/shard_map/ppermute | solution.py:288
  40.7 0.9 collective-permute-done.11
  41.6 1.2 %collective-permute-done.12 = f32[56,128]{1,0:T(8,128)S(1)} collective-permute-done((f32[56,128]{1,0:T(8,128)S(1)}, f32[56,128]{1,0:T(8,128)S(1)}, u32[]{:S(2)}, u32[]{:S(2)}) %collective-permute-start.12) | collective-permute-done | bytes 28704 | tf_op jit(solution)/shard_map/ppermute | solution.py:288
  42.8 3.6 %collective-permute-start.13 = (f32[56,128]{1,0:T(8,128)S(1)}, f32[56,128]{1,0:T(8,128)S(1)}, u32[]{:S(2)}, u32[]{:S(2)}) collective-permute-start(f32[56,128]{1,0:T(8,128)S(1)} %bitcast_add_fusion), channel_id=1, source_target_pairs={{0,3},{1,2},{2,1},{3,0},{4,7},{5,6},{6,5},{7,4},{8,11},{9,10},{10,... | collective-permute-start | bytes 86024 | tf_op jit(solution)/shard_map/ppermute | solution.py:288
  46.4 0.4 collective-permute-start.15
  46.8 0.9 collective-permute-done.13
  47.7 2.4 %collective-permute-done.14 = f32[56,128]{1,0:T(8,128)S(1)} collective-permute-done((f32[56,128]{1,0:T(8,128)S(1)}, f32[56,128]{1,0:T(8,128)S(1)}, u32[]{:S(2)}, u32[]{:S(2)}) %collective-permute-start.14) | collective-permute-done | bytes 28704 | tf_op jit(solution)/shard_map/ppermute | solution.py:288
  50.1 1.3 %collective-permute-start.16 = (f32[56,128]{1,0:T(8,128)S(1)}, f32[56,128]{1,0:T(8,128)S(1)}, u32[]{:S(2)}, u32[]{:S(2)}) collective-permute-start(f32[56,128]{1,0:T(8,128)S(1)} %add_add_fusion), channel_id=1, source_target_pairs={{0,8},{8,0},{16,24},{24,16},{1,9},{9,1},{17,25},{25,17},{2,10},{10... | collective-permute-start | bytes 86024 | tf_op jit(solution)/shard_map/ppermute | solution.py:288
  51.4 0.5 collective-permute-start.17
  51.9 0.9 %collective-permute-start.18 = (f32[56,128]{1,0:T(8,128)S(1)}, f32[56,128]{1,0:T(8,128)S(1)}, u32[]{:S(2)}, u32[]{:S(2)}) collective-permute-start(f32[56,128]{1,0:T(8,128)S(1)} %add_add_fusion), channel_id=1, source_target_pairs={{0,24},{8,16},{16,8},{24,0},{1,25},{9,17},{17,9},{25,1},{2,26},{10... | collective-permute-start | bytes 86024 | tf_op jit(solution)/shard_map/ppermute | solution.py:288
  52.8 0.1 collective-permute-done.16
  52.9 1.1 %collective-permute-done.17 = f32[56,128]{1,0:T(8,128)S(1)} collective-permute-done((f32[56,128]{1,0:T(8,128)S(1)}, f32[56,128]{1,0:T(8,128)S(1)}, u32[]{:S(2)}, u32[]{:S(2)}) %collective-permute-start.17) | collective-permute-done | bytes 28704 | tf_op jit(solution)/shard_map/ppermute | solution.py:288
  54.1 1.4 %collective-permute-done.18 = f32[56,128]{1,0:T(8,128)S(1)} collective-permute-done((f32[56,128]{1,0:T(8,128)S(1)}, f32[56,128]{1,0:T(8,128)S(1)}, u32[]{:S(2)}, u32[]{:S(2)}) %collective-permute-start.18) | collective-permute-done | bytes 28704 | tf_op jit(solution)/shard_map/ppermute | solution.py:288
  55.5 4.8 %collective-permute-start.19 = (f32[224,128]{1,0:T(8,128)S(1)}, f32[224,128]{1,0:T(8,128)S(1)}, u32[]{:S(2)}, u32[]{:S(2)}) collective-permute-start(f32[224,128]{1,0:T(8,128)S(1)} %pad_maximum_fusion.2), channel_id=1, source_target_pairs={{0,4},{4,0},{1,5},{5,1},{2,6},{6,2},{3,7},{7,3},{8,12},{12,8},{9,1... | collective-permute-start | bytes 344072 | tf_op jit(solution)/shard_map/ppermute | solution.py:288
  60.3 1.0 %collective-permute-done.19 = f32[224,128]{1,0:T(8,128)S(1)} collective-permute-done((f32[224,128]{1,0:T(8,128)S(1)}, f32[224,128]{1,0:T(8,128)S(1)}, u32[]{:S(2)}, u32[]{:S(2)}) %collective-permute-start.19) | collective-permute-done | bytes 114720 | tf_op jit(solution)/shard_map/ppermute | solution.py:288
  61.3 8.9 %shard_map.51 = (f32[12,32,128]{2,1,0:T(8,128)S(1)}, f32[12,32,128]{2,1,0:T(8,128)S(1)}, f32[12,32,128]{2,1,0:T(8,128)S(1)}, f32[12,32,128]{2,1,0:T(8,128)S(1)},...) custom-call(f32[256,1536]{1,0:T(8,128)S(1)} %get-tuple-element.36.an, ...), custom_call_target="tpu_custom_call" | custom-call | tf_op jit(solution)/shard_map/pallas_call | solution.py:532
  70.2 1.0 %collective-permute-start.20 = (f32[12,32,128]{2,1,0:T(8,128)S(1)}, f32[12,32,128]{2,1,0:T(8,128)S(1)}, u32[]{:S(2)}, u32[]{:S(2)}) collective-permute-start(f32[12,32,128]{2,1,0:T(8,128)S(1)} %get-tuple-element.40), channel_id=1, source_target_pairs={{0,8},{4,12},{8,0},{12,4},{16,24},{20,28},{24,16},{28,20},{1,9},{5... | collective-permute-start | bytes 589832 | tf_op jit(solution)/shard_map/ppermute | solution.py:222
  71.2 0.5 collective-permute-start.21
  71.8 1.2 %collective-permute-start.22 = (f32[12,32,128]{2,1,0:T(8,128)S(1)}, f32[12,32,128]{2,1,0:T(8,128)S(1)}, u32[]{:S(2)}, u32[]{:S(2)}) collective-permute-start(f32[12,32,128]{2,1,0:T(8,128)S(1)} %get-tuple-element.42), channel_id=1, source_target_pairs={{0,24},{4,28},{8,16},{12,20},{16,8},{20,12},{24,0},{28,4},{1,25},{... | collective-permute-start | bytes 589832 | tf_op jit(solution)/shard_map/ppermute | solution.py:222
  72.9 2.0 %collective-permute-start.23 = (f32[12,32,128]{2,1,0:T(8,128)S(1)}, f32[12,32,128]{2,1,0:T(8,128)S(1)}, u32[]{:S(2)}, u32[]{:S(2)}) collective-permute-start(f32[12,32,128]{2,1,0:T(8,128)S(1)} %get-tuple-element.43), channel_id=1, source_target_pairs={{0,12},{4,8},{8,4},{12,0},{16,28},{20,24},{24,20},{28,16},{1,13},{... | collective-permute-start | bytes 589832 | tf_op jit(solution)/shard_map/ppermute | solution.py:222
  75.0 0.3 collective-permute-start.24
  75.2 1.1 %collective-permute-done.20.refs_1_ = f32[12,32,128]{2,1,0:T(8,128)S(1)} collective-permute-done((f32[12,32,128]{2,1,0:T(8,128)S(1)}, f32[12,32,128]{2,1,0:T(8,128)S(1)}, u32[]{:S(2)}, u32[]{:S(2)}) %collective-permute-start.20) | collective-permute-done | bytes 196640 | tf_op jit(solution)/shard_map/ppermute | solution.py:222
  76.4 3.1 %collective-permute-start.25 = (f32[12,32,128]{2,1,0:T(8,128)S(1)}, f32[12,32,128]{2,1,0:T(8,128)S(1)}, u32[]{:S(2)}, u32[]{:S(2)}) collective-permute-start(f32[12,32,128]{2,1,0:T(8,128)S(1)} %get-tuple-element.45), channel_id=1, source_target_pairs={{0,28},{4,24},{8,20},{12,16},{16,12},{20,8},{24,4},{28,0},{1,29},{... | collective-permute-start | bytes 589832 | tf_op jit(solution)/shard_map/ppermute | solution.py:222
  79.5 4.4 %collective-permute-start.26 = (f32[12,32,128]{2,1,0:T(8,128)S(1)}, f32[12,32,128]{2,1,0:T(8,128)S(1)}, u32[]{:S(2)}, u32[]{:S(2)}) collective-permute-start(f32[12,32,128]{2,1,0:T(8,128)S(1)} %get-tuple-element.46), channel_id=1, source_target_pairs={{0,4},{4,0},{8,12},{12,8},{16,20},{20,16},{24,28},{28,24},{1,5},{5... | collective-permute-start | bytes 589832 | tf_op jit(solution)/shard_map/ppermute | solution.py:222
  83.9 2.6 %collective-permute-done.23.refs_4_ = f32[12,32,128]{2,1,0:T(8,128)S(1)} collective-permute-done((f32[12,32,128]{2,1,0:T(8,128)S(1)}, f32[12,32,128]{2,1,0:T(8,128)S(1)}, u32[]{:S(2)}, u32[]{:S(2)}) %collective-permute-start.23) | collective-permute-done | bytes 196640 | tf_op jit(solution)/shard_map/ppermute | solution.py:222
  86.5 0.9 collective-permute-done.24.refs_5_
  87.3 3.2 %collective-permute-done.25.refs_6_ = f32[12,32,128]{2,1,0:T(8,128)S(1)} collective-permute-done((f32[12,32,128]{2,1,0:T(8,128)S(1)}, f32[12,32,128]{2,1,0:T(8,128)S(1)}, u32[]{:S(2)}, u32[]{:S(2)}) %collective-permute-start.25) | collective-permute-done | bytes 196640 | tf_op jit(solution)/shard_map/ppermute | solution.py:222
  90.5 2.5 %shard_map.52 = f32[3072,128]{1,0:T(8,128)} custom-call(f32[12,32,128]{2,1,0:T(8,128)S(1)} %get-tuple-element.39.refs_0_, f32[12,32,128]{2,1,0:T(8,128)S(1)} %collective-permute-done.20.refs_1_, f32[12,32,128]{2,1,0:T(8,128)S(1)} %collective-permute-done.21.refs_2_, f32[12,32,128]{2,1,0:T(8,128)S(1)} %collective-permute-done.22.refs_3_, ...), custom_call_target="tpu_custom_call" | custom-call | tf_op jit(solution)/shard_map/pallas_call | solution.py:506
  (31 shorter events, 0.4 us)
Async XLA Ops:
  0.0 1.4 %copy-start = (f32[32,3,32,128]{3,2,1,0:T(8,128)S(1)}, f32[32,3,32,128]{3,2,1,0:T(8,128)}, u32[]{:S(2)}) copy-start(f32[32,3,32,128]{3,2,1,0:T(8,128)} %bottom_ref.1) | copy-start | bytes 4718596
  1.6 9.7 %collective-permute-start = (f32[9,32,128]{2,1,0:T(8,128)S(1)}, f32[9,32,128]{2,1,0:T(8,128)S(1)}, u32[]{:S(2)}, u32[]{:S(2)}) collective-permute-start(f32[9,32,128]{2,1,0:T(8,128)S(1)} %get-tuple-element.26), channel_id=1, source_target_pairs={{0,1},{1,2},{2,3},{4,5},{5,6},{6,7},{8,9},{9,10},{10,11},{12,13},{... | collective-permute-start | bytes 442376 | tf_op jit(solution)/shard_map/ppermute | solution.py:185
  5.7 6.3 %collective-permute-start.1 = (f32[9,32,128]{2,1,0:T(8,128)S(1)}, f32[9,32,128]{2,1,0:T(8,128)S(1)}, u32[]{:S(2)}, u32[]{:S(2)}) collective-permute-start(f32[9,32,128]{2,1,0:T(8,128)S(1)} %get-tuple-element.27), channel_id=1, source_target_pairs={{1,0},{2,1},{3,2},{5,4},{6,5},{7,6},{9,8},{10,9},{11,10},{13,12},{... | collective-permute-start | bytes 442376 | tf_op jit(solution)/shard_map/ppermute | solution.py:186
  11.3 15.6 %copy-start.1 = (f32[1,768]{1,0:T(1,128)S(1)}, f32[1,768]{1,0:T(1,128)}, u32[]{:S(2)}) copy-start(f32[1,768]{1,0:T(1,128)} %values_ref.1) | copy-start | bytes 9220
  11.3 15.6 %copy-start.2 = (f32[1,768]{1,0:T(1,128)S(1)}, f32[1,768]{1,0:T(1,128)}, u32[]{:S(2)}) copy-start(f32[1,768]{1,0:T(1,128)} %precision_ref.1) | copy-start | bytes 9220
  11.3 15.6 %copy-start.3 = (s32[1,768]{1,0:T(1,128)S(1)}, s32[1,768]{1,0:T(1,128)}, u32[]{:S(2)}) copy-start(s32[1,768]{1,0:T(1,128)} %index_ref.1) | copy-start | bytes 9220
  13.6 6.6 %collective-permute-start.2 = (f32[12,32,128]{2,1,0:T(8,128)S(1)}, f32[12,32,128]{2,1,0:T(8,128)S(1)}, u32[]{:S(2)}, u32[]{:S(2)}) collective-permute-start(f32[12,32,128]{2,1,0:T(8,128)S(1)} %get-tuple-element.29), channel_id=1, source_target_pairs={{0,8},{4,12},{8,0},{12,4},{16,24},{20,28},{24,16},{28,20},{1,9},{5... | collective-permute-start | bytes 589832 | tf_op jit(solution)/shard_map/ppermute | solution.py:222
  14.8 10.5 %collective-permute-start.3 = (f32[12,32,128]{2,1,0:T(8,128)S(1)}, f32[12,32,128]{2,1,0:T(8,128)S(1)}, u32[]{:S(2)}, u32[]{:S(2)}) collective-permute-start(f32[12,32,128]{2,1,0:T(8,128)S(1)} %get-tuple-element.30), channel_id=1, source_target_pairs={{0,16},{4,20},{8,24},{12,28},{16,0},{20,4},{24,8},{28,12},{1,17},{... | collective-permute-start | bytes 589832 | tf_op jit(solution)/shard_map/ppermute | solution.py:222
  16.1 11.6 %collective-permute-start.4 = (f32[12,32,128]{2,1,0:T(8,128)S(1)}, f32[12,32,128]{2,1,0:T(8,128)S(1)}, u32[]{:S(2)}, u32[]{:S(2)}) collective-permute-start(f32[12,32,128]{2,1,0:T(8,128)S(1)} %get-tuple-element.31), channel_id=1, source_target_pairs={{0,24},{4,28},{8,16},{12,20},{16,8},{20,12},{24,0},{28,4},{1,25},{... | collective-permute-start | bytes 589832 | tf_op jit(solution)/shard_map/ppermute | solution.py:222
  16.3 15.0 %collective-permute-start.5 = (f32[12,32,128]{2,1,0:T(8,128)S(1)}, f32[12,32,128]{2,1,0:T(8,128)S(1)}, u32[]{:S(2)}, u32[]{:S(2)}) collective-permute-start(f32[12,32,128]{2,1,0:T(8,128)S(1)} %get-tuple-element.32), channel_id=1, source_target_pairs={{0,12},{4,8},{8,4},{12,0},{16,28},{20,24},{24,20},{28,16},{1,13},{... | collective-permute-start | bytes 589832 | tf_op jit(solution)/shard_map/ppermute | solution.py:222
  20.1 14.3 %collective-permute-start.6 = (f32[12,32,128]{2,1,0:T(8,128)S(1)}, f32[12,32,128]{2,1,0:T(8,128)S(1)}, u32[]{:S(2)}, u32[]{:S(2)}) collective-permute-start(f32[12,32,128]{2,1,0:T(8,128)S(1)} %get-tuple-element.33), channel_id=1, source_target_pairs={{0,20},{4,16},{8,28},{12,24},{16,4},{20,0},{24,12},{28,8},{1,21},{... | collective-permute-start | bytes 589832 | tf_op jit(solution)/shard_map/ppermute | solution.py:222
  20.1 14.3 %collective-permute-start.7 = (f32[12,32,128]{2,1,0:T(8,128)S(1)}, f32[12,32,128]{2,1,0:T(8,128)S(1)}, u32[]{:S(2)}, u32[]{:S(2)}) collective-permute-start(f32[12,32,128]{2,1,0:T(8,128)S(1)} %get-tuple-element.34), channel_id=1, source_target_pairs={{0,28},{4,24},{8,20},{12,16},{16,12},{20,8},{24,4},{28,0},{1,29},{... | collective-permute-start | bytes 589832 | tf_op jit(solution)/shard_map/ppermute | solution.py:222
  25.4 9.0 %collective-permute-start.8 = (f32[12,32,128]{2,1,0:T(8,128)S(1)}, f32[12,32,128]{2,1,0:T(8,128)S(1)}, u32[]{:S(2)}, u32[]{:S(2)}) collective-permute-start(f32[12,32,128]{2,1,0:T(8,128)S(1)} %get-tuple-element.35), channel_id=1, source_target_pairs={{0,4},{4,0},{8,12},{12,8},{16,20},{20,16},{24,28},{28,24},{1,5},{5... | collective-permute-start | bytes 589832 | tf_op jit(solution)/shard_map/ppermute | solution.py:222
  36.5 1.4 %collective-permute-start.9 = (f32[224,128]{1,0:T(8,128)S(1)}, f32[224,128]{1,0:T(8,128)S(1)}, u32[]{:S(2)}, u32[]{:S(2)}) collective-permute-start(f32[224,128]{1,0:T(8,128)S(1)} %constant_dynamic-slice_fusion), channel_id=1, source_target_pairs={{0,4},{4,0},{1,5},{5,1},{2,6},{6,2},{3,7},{7,3},{8,12},{12,8},{9,1... | collective-permute-start | bytes 344072 | tf_op jit(solution)/shard_map/ppermute | solution.py:288
  37.9 2.8 %collective-permute-start.10 = (f32[56,128]{1,0:T(8,128)S(1)}, f32[56,128]{1,0:T(8,128)S(1)}, u32[]{:S(2)}, u32[]{:S(2)}) collective-permute-start(f32[56,128]{1,0:T(8,128)S(1)} %get-tuple-element.55), channel_id=1, source_target_pairs={{0,8},{8,0},{16,24},{24,16},{1,9},{9,1},{17,25},{25,17},{2,10},{10... | collective-permute-start | bytes 86024 | tf_op jit(solution)/shard_map/ppermute | solution.py:288
  38.7 3.0 %collective-permute-start.11 = (f32[56,128]{1,0:T(8,128)S(1)}, f32[56,128]{1,0:T(8,128)S(1)}, u32[]{:S(2)}, u32[]{:S(2)}) collective-permute-start(f32[56,128]{1,0:T(8,128)S(1)} %get-tuple-element.53), channel_id=1, source_target_pairs={{0,16},{8,24},{16,0},{24,8},{1,17},{9,25},{17,1},{25,9},{2,18},{10... | collective-permute-start | bytes 86024 | tf_op jit(solution)/shard_map/ppermute | solution.py:288
  39.2 3.6 %collective-permute-start.12 = (f32[56,128]{1,0:T(8,128)S(1)}, f32[56,128]{1,0:T(8,128)S(1)}, u32[]{:S(2)}, u32[]{:S(2)}) collective-permute-start(f32[56,128]{1,0:T(8,128)S(1)} %get-tuple-element.54), channel_id=1, source_target_pairs={{0,24},{8,16},{16,8},{24,0},{1,25},{9,17},{17,9},{25,1},{2,26},{10... | collective-permute-start | bytes 86024 | tf_op jit(solution)/shard_map/ppermute | solution.py:288
  42.8 4.8 %collective-permute-start.13 = (f32[56,128]{1,0:T(8,128)S(1)}, f32[56,128]{1,0:T(8,128)S(1)}, u32[]{:S(2)}, u32[]{:S(2)}) collective-permute-start(f32[56,128]{1,0:T(8,128)S(1)} %bitcast_add_fusion), channel_id=1, source_target_pairs={{0,3},{1,2},{2,1},{3,0},{4,7},{5,6},{6,5},{7,4},{8,11},{9,10},{10,... | collective-permute-start | bytes 86024 | tf_op jit(solution)/shard_map/ppermute | solution.py:288
  46.4 3.7 %collective-permute-start.14 = (f32[56,128]{1,0:T(8,128)S(1)}, f32[56,128]{1,0:T(8,128)S(1)}, u32[]{:S(2)}, u32[]{:S(2)}) collective-permute-start(f32[56,128]{1,0:T(8,128)S(1)} %bitcast_add_fusion), channel_id=1, source_target_pairs={{0,2},{1,3},{2,0},{3,1},{4,6},{5,7},{6,4},{7,5},{8,10},{9,11},{10,... | collective-permute-start | bytes 86024 | tf_op jit(solution)/shard_map/ppermute | solution.py:288
  46.4 3.7 %collective-permute-start.15 = (f32[56,128]{1,0:T(8,128)S(1)}, f32[56,128]{1,0:T(8,128)S(1)}, u32[]{:S(2)}, u32[]{:S(2)}) collective-permute-start(f32[56,128]{1,0:T(8,128)S(1)} %bitcast_add_fusion), channel_id=1, source_target_pairs={{0,1},{1,0},{2,3},{3,2},{4,5},{5,4},{6,7},{7,6},{8,9},{9,8},{10,11... | collective-permute-start | bytes 86024 | tf_op jit(solution)/shard_map/ppermute | solution.py:288
  50.1 2.9 %collective-permute-start.16 = (f32[56,128]{1,0:T(8,128)S(1)}, f32[56,128]{1,0:T(8,128)S(1)}, u32[]{:S(2)}, u32[]{:S(2)}) collective-permute-start(f32[56,128]{1,0:T(8,128)S(1)} %add_add_fusion), channel_id=1, source_target_pairs={{0,8},{8,0},{16,24},{24,16},{1,9},{9,1},{17,25},{25,17},{2,10},{10... | collective-permute-start | bytes 86024 | tf_op jit(solution)/shard_map/ppermute | solution.py:288
  51.4 2.7 %collective-permute-start.17 = (f32[56,128]{1,0:T(8,128)S(1)}, f32[56,128]{1,0:T(8,128)S(1)}, u32[]{:S(2)}, u32[]{:S(2)}) collective-permute-start(f32[56,128]{1,0:T(8,128)S(1)} %add_add_fusion), channel_id=1, source_target_pairs={{0,16},{8,24},{16,0},{24,8},{1,17},{9,25},{17,1},{25,9},{2,18},{10... | collective-permute-start | bytes 86024 | tf_op jit(solution)/shard_map/ppermute | solution.py:288
  51.9 3.6 %collective-permute-start.18 = (f32[56,128]{1,0:T(8,128)S(1)}, f32[56,128]{1,0:T(8,128)S(1)}, u32[]{:S(2)}, u32[]{:S(2)}) collective-permute-start(f32[56,128]{1,0:T(8,128)S(1)} %add_add_fusion), channel_id=1, source_target_pairs={{0,24},{8,16},{16,8},{24,0},{1,25},{9,17},{17,9},{25,1},{2,26},{10... | collective-permute-start | bytes 86024 | tf_op jit(solution)/shard_map/ppermute | solution.py:288
  55.5 5.7 %collective-permute-start.19 = (f32[224,128]{1,0:T(8,128)S(1)}, f32[224,128]{1,0:T(8,128)S(1)}, u32[]{:S(2)}, u32[]{:S(2)}) collective-permute-start(f32[224,128]{1,0:T(8,128)S(1)} %pad_maximum_fusion.2), channel_id=1, source_target_pairs={{0,4},{4,0},{1,5},{5,1},{2,6},{6,2},{3,7},{7,3},{8,12},{12,8},{9,1... | collective-permute-start | bytes 344072 | tf_op jit(solution)/shard_map/ppermute | solution.py:288
  70.2 6.2 %collective-permute-start.20 = (f32[12,32,128]{2,1,0:T(8,128)S(1)}, f32[12,32,128]{2,1,0:T(8,128)S(1)}, u32[]{:S(2)}, u32[]{:S(2)}) collective-permute-start(f32[12,32,128]{2,1,0:T(8,128)S(1)} %get-tuple-element.40), channel_id=1, source_target_pairs={{0,8},{4,12},{8,0},{12,4},{16,24},{20,28},{24,16},{28,20},{1,9},{5... | collective-permute-start | bytes 589832 | tf_op jit(solution)/shard_map/ppermute | solution.py:222
  71.2 8.2 %collective-permute-start.21 = (f32[12,32,128]{2,1,0:T(8,128)S(1)}, f32[12,32,128]{2,1,0:T(8,128)S(1)}, u32[]{:S(2)}, u32[]{:S(2)}) collective-permute-start(f32[12,32,128]{2,1,0:T(8,128)S(1)} %get-tuple-element.41), channel_id=1, source_target_pairs={{0,16},{4,20},{8,24},{12,28},{16,0},{20,4},{24,8},{28,12},{1,17},{... | collective-permute-start | bytes 589832 | tf_op jit(solution)/shard_map/ppermute | solution.py:222
  71.8 12.1 %collective-permute-start.22 = (f32[12,32,128]{2,1,0:T(8,128)S(1)}, f32[12,32,128]{2,1,0:T(8,128)S(1)}, u32[]{:S(2)}, u32[]{:S(2)}) collective-permute-start(f32[12,32,128]{2,1,0:T(8,128)S(1)} %get-tuple-element.42), channel_id=1, source_target_pairs={{0,24},{4,28},{8,16},{12,20},{16,8},{20,12},{24,0},{28,4},{1,25},{... | collective-permute-start | bytes 589832 | tf_op jit(solution)/shard_map/ppermute | solution.py:222
  72.9 13.5 %collective-permute-start.23 = (f32[12,32,128]{2,1,0:T(8,128)S(1)}, f32[12,32,128]{2,1,0:T(8,128)S(1)}, u32[]{:S(2)}, u32[]{:S(2)}) collective-permute-start(f32[12,32,128]{2,1,0:T(8,128)S(1)} %get-tuple-element.43), channel_id=1, source_target_pairs={{0,12},{4,8},{8,4},{12,0},{16,28},{20,24},{24,20},{28,16},{1,13},{... | collective-permute-start | bytes 589832 | tf_op jit(solution)/shard_map/ppermute | solution.py:222
  75.0 12.4 %collective-permute-start.24 = (f32[12,32,128]{2,1,0:T(8,128)S(1)}, f32[12,32,128]{2,1,0:T(8,128)S(1)}, u32[]{:S(2)}, u32[]{:S(2)}) collective-permute-start(f32[12,32,128]{2,1,0:T(8,128)S(1)} %get-tuple-element.44), channel_id=1, source_target_pairs={{0,20},{4,16},{8,28},{12,24},{16,4},{20,0},{24,12},{28,8},{1,21},{... | collective-permute-start | bytes 589832 | tf_op jit(solution)/shard_map/ppermute | solution.py:222
  76.4 14.1 %collective-permute-start.25 = (f32[12,32,128]{2,1,0:T(8,128)S(1)}, f32[12,32,128]{2,1,0:T(8,128)S(1)}, u32[]{:S(2)}, u32[]{:S(2)}) collective-permute-start(f32[12,32,128]{2,1,0:T(8,128)S(1)} %get-tuple-element.45), channel_id=1, source_target_pairs={{0,28},{4,24},{8,20},{12,16},{16,12},{20,8},{24,4},{28,0},{1,29},{... | collective-permute-start | bytes 589832 | tf_op jit(solution)/shard_map/ppermute | solution.py:222
  79.5 11.1 %collective-permute-start.26 = (f32[12,32,128]{2,1,0:T(8,128)S(1)}, f32[12,32,128]{2,1,0:T(8,128)S(1)}, u32[]{:S(2)}, u32[]{:S(2)}) collective-permute-start(f32[12,32,128]{2,1,0:T(8,128)S(1)} %get-tuple-element.46), channel_id=1, source_target_pairs={{0,4},{4,0},{8,12},{12,8},{16,20},{20,16},{24,28},{28,24},{1,5},{5... | collective-permute-start | bytes 589832 | tf_op jit(solution)/shard_map/ppermute | solution.py:222

commit v5 on v4

--- a/solution.py
+++ b/solution.py
@@ -210,17 +210,44 @@
     return [0] + sorted(range(1, clusters), key=lambda s: (s < cores, s % cores, s))
 
 
-def exchange(slots):
-    clusters = len(slots)
+def exchange(values, slots):
+    clusters = lax.axis_size("group") * lax.axis_size("member")
     if clusters > DIRECT:
-        stacked = jnp.stack(slots, axis=0)
+        stacked = jnp.stack(values, axis=0)
         got = lax.all_to_all(stacked, ("group", "member"), split_axis=0, concat_axis=0, tiled=True)
         return [got[k] for k in range(clusters)]
-    got = [slots[0]]
-    for slot, value in list(zip(slot_order(clusters), slots))[1:]:
-        pairs = [(i, i ^ slot) for i in range(clusters)]
-        got.append(lax.ppermute(value, ("group", "member"), pairs))
-    return got
+    return [
+        lax.ppermute(value, ("group", "member"), [(i, i ^ slot) for i in range(clusters)])
+        if slot
+        else value
+        for slot, value in zip(slots, values)
+    ]
+
+
+def shares():
+    return (lax.axis_size("group"), lax.axis_size("member")) == (4, 2)
+
+
+def term_parts(terms):
+    cuts = [0, terms // 3, terms // 2, terms // 2 + terms // 3, terms] if shares() else [0, terms]
+    return [range(first, last) for first, last in zip(cuts, cuts[1:])]
+
+
+def pieces(slot):
+    if not shares():
+        return [(0, 0)]
+    first, second = 2, 4
+    along_first = [(0, 2), (0, 3), (second, 2), (second, 3)]
+    along_second = [(0, 0), (0, 1), (first, 0), (first, 1)]
+    if slot < first:
+        return along_second + along_first
+    if slot & first and slot & second:
+        return []
+    return along_first if slot & first else along_second
+
+
+def return_slots(clusters):
+    return [slot for slot in slot_order(clusters) if pieces(slot)]
 
 
 def split(value):
@@ -247,9 +274,19 @@
     out_ref[2:8, :] = jnp.zeros((6, width), jnp.float32)
 
 
+def product(left, right, contract):
+    return lax.dot_general(
+        left,
+        right,
+        (contract, ((), ())),
+        precision=lax.Precision.HIGHEST,
+        preferred_element_type=jnp.float32,
+    )
+
+
 def gram_kernel(dims, observed_ref, *refs):
     clusters, terms, members, cols = dims
-    arrived, (out_ref, anomaly_ref, mean_ref, scaled_ref) = refs[:clusters], refs[clusters:]
+    arrived, (out_ref, *parts, scaled_ref) = refs[:clusters], refs[clusters:]
     total = clusters * members
     scale = 1.0 / math.sqrt(total - 1)
     half = LANES
@@ -262,17 +299,20 @@
         for value in values[1:]:
             summed = summed + value
         mean = jnp.sum(summed, axis=0, keepdims=True) * (1.0 / total)
-        mean_ref[:, at] = jnp.broadcast_to(mean, (8, cols))
+        part = [term in held for held in term_parts(terms)].index(True)
+        there = term - term_parts(terms)[part].start
+        there = slice(there * cols, (there + 1) * cols)
+        parts[part][total : total + 8, there] = jnp.broadcast_to(mean, (8, cols))
         weight = observed_ref[0:1, at] * scale
         for place, value in zip(places, values):
             anomaly = value - mean
-            anomaly_ref[pl.ds(place, members), at] = anomaly
+            parts[part][pl.ds(place, members), there] = anomaly
             scaled_ref[pl.ds(place, members), at] = anomaly * weight
         innovation = (observed_ref[1:2, at] - mean) * weight
         scaled_ref[total : total + 8, at] = jnp.concatenate(
             [innovation, jnp.zeros((7, cols), jnp.float32)], axis=0
         )
-    result = product(scaled_ref[...], scaled_ref[0:total, :], ((1,), (1,)))
+    result = short_product(scaled_ref[...], scaled_ref[0:total, :], ((1,), (1,)))
     at = 0
     for first in range(0, total, half):
         out_ref[at : at + total - first, :] = result[first:total, first : first + half]
@@ -288,10 +328,14 @@
     return lax.ppermute(value, axis, [(i, i ^ bits) for i in range(lax.axis_size(axis))])
 
 
-def total_over_devices(value):
-    sizes = tuple(lax.axis_size(axis) for axis in ("group", "member", "space"))
-    if sizes != (4, 2, 4):
-        return lax.psum(value, ("group", "member", "space"))
+def total_over_devices(value, parts):
+    held = {(0, k): part for k, part in enumerate(parts)}
+    if not shares() or lax.axis_size("space") != 4:
+        if shares():
+            for k, part in enumerate(parts):
+                bit = 1 + k // 2
+                held[2 * bit, k] = flip(part, "group", bit)
+        return lax.psum(value, ("group", "member", "space")), held
     rows, cols = value.shape
     core = lax.axis_index("member")
     chip = lax.axis_index("group")
@@ -304,25 +348,32 @@
     piece = pieces[0] + (
         flip(pieces[1], "group", 1) + flip(pieces[2], "group", 2) + flip(pieces[3], "group", 3)
     )
+    piece, early0, early2 = lax.optimization_barrier((piece, parts[0], parts[2]))
+    early0, early2 = flip(early0, "group", 1), flip(early2, "group", 2)
     piece = piece + (flip(piece, "space", 3) + flip(piece, "space", 2) + flip(piece, "space", 1))
+    piece, held[2, 0], held[4, 2] = lax.optimization_barrier((piece, early0, early2))
     got = jnp.stack([piece] + [flip(piece, "group", s) for s in (1, 2, 3)], axis=0)
     mine = jnp.concatenate(
         [lax.dynamic_index_in_dim(got, chip ^ i, 0, False) for i in range(4)], axis=0
     )
+    mine, late1, late3 = lax.optimization_barrier((mine, parts[1], parts[3]))
+    held[2, 1], held[4, 3] = flip(late1, "group", 1), flip(late3, "group", 2)
     other = flip(mine, "member", 1)
-    return jnp.concatenate(
+    whole_sum = jnp.concatenate(
         [jnp.where(core == 0, mine, other), jnp.where(core == 0, other, mine)], axis=0
     )
-
-
-def product(left, right, contract):
-    return lax.dot_general(
-        left,
-        right,
-        (contract, ((), ())),
-        precision=lax.Precision.HIGHEST,
-        preferred_element_type=jnp.float32,
-    )
+    return whole_sum, held
+
+
+def short_product(left, right, contract):
+    left_high, right_high = left.astype(jnp.bfloat16), right.astype(jnp.bfloat16)
+    left_low = (left - left_high.astype(jnp.float32)).astype(jnp.bfloat16)
+    right_low = (right - right_high.astype(jnp.float32)).astype(jnp.bfloat16)
+
+    def dot(x, y):
+        return lax.dot_general(x, y, (contract, ((), ())), preferred_element_type=jnp.float32)
+
+    return dot(left_high, right_high) + (dot(left_high, right_low) + dot(left_low, right_high))
 
 
 def eliminate(panel, first):
@@ -461,56 +512,62 @@
     )
 
 
-def update_kernel(dims, anomaly_ref, mean_ref, packed_ref, *refs):
+def transform_kernel(total, packed_ref, out_ref):
+    out_ref[...] = transform_of(packed_ref, total)
+
+
+def update_kernel(dims, sources, transform_ref, *refs):
     clusters, terms, members, cols = dims
-    slots, transform_ref = refs[:clusters], refs[clusters]
+    slots = return_slots(clusters)
+    out = dict(zip(slots, refs[len(sources) :]))
     total = clusters * members
     own = own_cluster(clusters)
-    transform_ref[...] = transform_of(packed_ref, total)
-    transform = jnp.concatenate(
-        [
-            transform_ref[pl.ds(pl.multiple_of((own ^ slot) * members, members), members), :]
-            for slot in slot_order(clusters)
-        ],
-        axis=0,
-    )
-    step = 2 * cols
-    width = terms * cols
-    for first in range(0, width, step):
-        at = slice(first, min(first + step, width))
-        updated = product(transform, anomaly_ref[:, at], ((1,), (0,))) + mean_ref[0:1, at]
-        for k in range((at.stop - first) // cols):
-            for at_slot, ref in enumerate(slots):
-                ref[first // cols + k] = updated[
-                    at_slot * members : (at_slot + 1) * members, k * cols : (k + 1) * cols
+    for (source, part), ref in zip(sources, refs):
+        targets = [slot for slot in slots if (source, part) in pieces(slot)]
+        transform = jnp.concatenate(
+            [
+                transform_ref[pl.ds(pl.multiple_of((own ^ slot) * members, members), members), :]
+                for slot in targets
+            ],
+            axis=0,
+        )
+        updated = short_product(transform, ref[0:total, :], ((1,), (0,))) + ref[total : total + 1, :]
+        for place, slot in enumerate(targets):
+            held = pieces(slot)
+            first = sum(len(term_parts(terms)[k]) for _, k in held[: held.index((source, part))])
+            for term in range(len(term_parts(terms)[part])):
+                out[slot][first + term] = updated[
+                    place * members : (place + 1) * members, term * cols : (term + 1) * cols
                 ]
 
 
 def place_kernel(dims, *refs):
     clusters, fields, block_rows, cols = dims
-    slots, out_ref = refs[:clusters], refs[clusters]
+    out_ref = refs[-1]
     rows = clusters * block_rows
     own = own_cluster(clusters)
-    for slot, ref in zip(slot_order(clusters), slots):
-        first = (own ^ slot) * block_rows
-        for field in range(fields):
-            for row in range(block_rows):
+    for slot, ref in zip(return_slots(clusters), refs):
+        held = 0
+        for source, part in pieces(slot):
+            first = (own ^ (slot ^ source)) * block_rows
+            for term in term_parts(fields * block_rows)[part]:
+                field, row = divmod(term, block_rows)
                 at = field * rows + row + first
-                out_ref[pl.ds(at, 8, stride=fields * rows), :] = ref[field * block_rows + row]
-
-
-def place(slots, fields):
-    clusters = len(slots)
-    terms, members, cols = slots[0].shape
+                out_ref[pl.ds(at, 8, stride=fields * rows), :] = ref[held]
+                held += 1
+
+
+def place(values, clusters, fields, terms):
+    _, members, cols = values[0].shape
     rows = clusters * terms
     return pl.pallas_call(
         functools.partial(place_kernel, (clusters, fields, terms // fields, cols)),
         grid=(members // 8,),
         out_shape=f32(members * rows, cols),
-        in_specs=[pl.BlockSpec((terms, 8, cols), lambda i: (0, i, 0))] * clusters,
+        in_specs=[pl.BlockSpec((value.shape[0], 8, cols), lambda i: (0, i, 0)) for value in values],
         out_specs=pl.BlockSpec((8 * rows, cols), lambda i: (i, 0)),
         compiler_params=pltpu.CompilerParams(vmem_limit_bytes=VMEM_LIMIT),
-    )(*slots)
+    )(*values)
 
 
 def on_device(state, obs_values, obs_precision, obs_index):
@@ -520,22 +577,26 @@
     total = clusters * members
     width = terms * cols
     dims = (clusters, terms, members, cols)
-    arrived = exchange(forecast(state, clusters))
+    sizes = [len(part) for part in term_parts(terms)]
+    arrived = exchange(forecast(state, clusters), slot_order(clusters))
     observed = call(observed_kernel, f32(8, width), 3)(obs_values, obs_precision, obs_index)
-    packed, anomaly, mean = call(
+    packed, *parts = call(
         functools.partial(gram_kernel, dims),
-        [f32(448, LANES), f32(total, width), f32(8, width)],
+        [f32(448, LANES)] + [f32(total + 8, size * cols) for size in sizes],
         1 + clusters,
         [pltpu.VMEM((total + 8, width), jnp.float32)],
     )(observed, *arrived)
-    packed = total_over_devices(packed)
+    packed, held = total_over_devices(packed, parts)
+    transform = call(functools.partial(transform_kernel, total), f32(total, total), 1)(packed)
+    slots = return_slots(clusters)
+    sources = sorted({piece for slot in slots for piece in pieces(slot)})
     updated = call(
-        functools.partial(update_kernel, dims),
-        [f32(terms, members, cols)] * clusters,
-        3,
-        [pltpu.VMEM((total, total), jnp.float32)],
-    )(anomaly, mean, packed)
-    return place(exchange(updated), fields).reshape(members, fields, rows, cols)
+        functools.partial(update_kernel, dims, sources),
+        [f32(sum(sizes[part] for _, part in pieces(slot)), members, cols) for slot in slots],
+        1 + len(sources),
+    )(transform, *[held[source] for source in sources])
+    returned = exchange(updated, slots)
+    return place(returned, clusters, fields, terms).reshape(members, fields, rows, cols)
 
 
 def solution(mesh):

time: 93.2 us -> 88.6 us (0.951)
  starting transfers between devices: 45.4 us -> 40.4 us
  waiting for transfers between devices: 25.6 us -> 27.6 us
  Pallas kernels: 20.2 us -> 18.7 us
    ppermute x14 -> x12, starting transfers between devices: 25.9 us -> 17.7 us  [exchange(): lax.ppermute(value, ('group', 'member'), [(i, i ^ slot) for i in range(cl...]
    ppermute x11 -> x15, starting transfers between devices: 14.2 us -> 17.3 us  [flip(): lax.ppermute(value, axis, [(i, i ^ bits) for i in range(lax.axis_size(axi...]
    ppermute x11 -> x15, waiting for transfers between devices: 10.4 us -> 12.3 us  [flip(): lax.ppermute(value, axis, [(i, i ^ bits) for i in range(lax.axis_size(axi...]
    pallas_call x2 -> x3, Pallas kernels: 10.9 us -> 9.41 us  [the longest x1 7.25 us: on_device(): call(functools.partial(transform_kernel, total), f32(total, total), 1)]
    ppermute x14 -> x12, waiting for transfers between devices: 14.5 us -> 14.6 us  [exchange(): lax.ppermute(value, ('group', 'member'), [(i, i ^ slot) for i in range(cl...]
  transfers between devices with their start and end apart: 27 -> 29, of which waited for: 17 -> 16; matrix products, arithmetic and copies ran while one was open for 0% -> 0% of each run, Pallas kernels for 5% -> 14%
where the time goes in v5:
time: 88.6 us; the launch traced here: 88.5 us
  starting transfers between devices  40.4 us (46%)
  waiting for transfers between devices  27.6 us (31%)
  Pallas kernels  18.7 us (21%)
  local copies, waits for them, and re-layouts  1.49 us (2%)
    ppermute x12, starting transfers between devices, exchange(): lax.ppermute(value, ('group', 'member'), [(i, i ^ slot) for i in range(cl...  17.7 us
    ppermute x15, starting transfers between devices, flip(): lax.ppermute(value, axis, [(i, i ^ bits) for i in range(lax.axis_size(axi...  17.3 us
    ppermute x12, waiting for transfers between devices, exchange(): lax.ppermute(value, ('group', 'member'), [(i, i ^ slot) for i in range(cl...  14.6 us
    ppermute x15, waiting for transfers between devices, flip(): lax.ppermute(value, axis, [(i, i ^ bits) for i in range(lax.axis_size(axi...  12.3 us
    pallas_call x1, Pallas kernels, on_device(): call(functools.partial(transform_kernel, total), f32(total, total), 1)  7.25 us
    pallas_call x1, Pallas kernels, forecast(): call(functools.partial(interior_kernel, dims), f32(clusters, terms, membe...  4.32 us
    ppermute x1, starting transfers between devices, forecast(): lax.ppermute(to_next, 'space', [(i, i + 1) for i in range(count - 1)])  4.04 us
    pallas_call x1, Pallas kernels, place(): pl.pallas_call(functools.partial(place_kernel, (clusters, fields, terms /...  2.43 us
  transfers between devices with their start and end apart: 29, of which 16 were waited for; matrix products, arithmetic and copies ran while one was open for 0% of the time, Pallas kernels for 14%

profile of v5, /device:TPU:1, one launch (start us, length us, event | category | flops | bytes accessed | tf_op | source)
XLA Modules:
  0.0 88.5 jit_solution(13764830504138292489)
XLA Ops:
  0.0 1.4 %copy-done = f32[32,3,32,128]{3,2,1,0:T(8,128)S(1)} copy-done((f32[32,3,32,128]{3,2,1,0:T(8,128)S(1)}, f32[32,3,32,128]{3,2,1,0:T(8,128)}, u32[]{:S(2)}) %copy-start) | copy-done | bytes 1572888
  1.4 0.2 shard_map.47
  1.6 4.0 %collective-permute-start = (f32[9,32,128]{2,1,0:T(8,128)S(1)}, f32[9,32,128]{2,1,0:T(8,128)S(1)}, u32[]{:S(2)}, u32[]{:S(2)}) collective-permute-start(f32[9,32,128]{2,1,0:T(8,128)S(1)} %get-tuple-element.35), channel_id=1, source_target_pairs={{0,1},{1,2},{2,3},{4,5},{5,6},{6,7},{8,9},{9,10},{10,11},{12,13},{... | collective-permute-start | bytes 442376 | tf_op jit(solution)/shard_map/ppermute | solution.py:185
  5.7 1.3 %collective-permute-start.1 = (f32[9,32,128]{2,1,0:T(8,128)S(1)}, f32[9,32,128]{2,1,0:T(8,128)S(1)}, u32[]{:S(2)}, u32[]{:S(2)}) collective-permute-start(f32[9,32,128]{2,1,0:T(8,128)S(1)} %get-tuple-element.36), channel_id=1, source_target_pairs={{1,0},{2,1},{3,2},{5,4},{6,5},{7,6},{9,8},{10,9},{11,10},{13,12},{... | collective-permute-start | bytes 442376 | tf_op jit(solution)/shard_map/ppermute | solution.py:186
  7.0 4.3 %shard_map.48.interior_ref = f32[8,12,32,128]{3,2,1,0:T(8,128)S(1)} custom-call(f32[3072,128]{1,0:T(8,128)S(1)} %bitcast.23), custom_call_target="tpu_custom_call" | custom-call | flops 78643200 | bytes 6291456 | tf_op jit(solution)/shard_map/pallas_call | solution.py:190
  11.4 0.6 collective-permute-done.1.after_ref
  12.0 1.6 %shard_map.49 = (f32[12,32,128]{2,1,0:T(8,128)S(1)}, f32[12,32,128]{2,1,0:T(8,128)S(1)}, f32[12,32,128]{2,1,0:T(8,128)S(1)}, f32[12,32,128]{2,1,0:T(8,128)S(1)},...) custom-call(f32[3072,128]{1,0:T(8,128)S(1)} %bitcast.24, ...), custom_call_target="tpu_custom_call" | custom-call | tf_op jit(solution)/shard_map/pallas_call | solution.py:198
  13.6 1.3 %collective-permute-start.2 = (f32[12,32,128]{2,1,0:T(8,128)S(1)}, f32[12,32,128]{2,1,0:T(8,128)S(1)}, u32[]{:S(2)}, u32[]{:S(2)}) collective-permute-start(f32[12,32,128]{2,1,0:T(8,128)S(1)} %get-tuple-element.38), channel_id=1, source_target_pairs={{0,8},{4,12},{8,0},{12,4},{16,24},{20,28},{24,16},{28,20},{1,9},{5... | collective-permute-start | bytes 589832 | tf_op jit(solution)/shard_map/ppermute | solution.py:220
  14.8 1.2 %collective-permute-start.3 = (f32[12,32,128]{2,1,0:T(8,128)S(1)}, f32[12,32,128]{2,1,0:T(8,128)S(1)}, u32[]{:S(2)}, u32[]{:S(2)}) collective-permute-start(f32[12,32,128]{2,1,0:T(8,128)S(1)} %get-tuple-element.39), channel_id=1, source_target_pairs={{0,16},{4,20},{8,24},{12,28},{16,0},{20,4},{24,8},{28,12},{1,17},{... | collective-permute-start | bytes 589832 | tf_op jit(solution)/shard_map/ppermute | solution.py:220
  16.1 0.2 collective-permute-start.4
  16.3 3.8 %collective-permute-start.5 = (f32[12,32,128]{2,1,0:T(8,128)S(1)}, f32[12,32,128]{2,1,0:T(8,128)S(1)}, u32[]{:S(2)}, u32[]{:S(2)}) collective-permute-start(f32[12,32,128]{2,1,0:T(8,128)S(1)} %get-tuple-element.41), channel_id=1, source_target_pairs={{0,12},{4,8},{8,4},{12,0},{16,28},{20,24},{24,20},{28,16},{1,13},{... | collective-permute-start | bytes 589832 | tf_op jit(solution)/shard_map/ppermute | solution.py:220
  20.1 5.3 %collective-permute-start.7 = (f32[12,32,128]{2,1,0:T(8,128)S(1)}, f32[12,32,128]{2,1,0:T(8,128)S(1)}, u32[]{:S(2)}, u32[]{:S(2)}) collective-permute-start(f32[12,32,128]{2,1,0:T(8,128)S(1)} %get-tuple-element.43), channel_id=1, source_target_pairs={{0,28},{4,24},{8,20},{12,16},{16,12},{20,8},{24,4},{28,0},{1,29},{... | collective-permute-start | bytes 589832 | tf_op jit(solution)/shard_map/ppermute | solution.py:220
  25.4 1.6 %collective-permute-start.8 = (f32[12,32,128]{2,1,0:T(8,128)S(1)}, f32[12,32,128]{2,1,0:T(8,128)S(1)}, u32[]{:S(2)}, u32[]{:S(2)}) collective-permute-start(f32[12,32,128]{2,1,0:T(8,128)S(1)} %get-tuple-element.44), channel_id=1, source_target_pairs={{0,4},{4,0},{8,12},{12,8},{16,20},{20,16},{24,28},{28,24},{1,5},{5... | collective-permute-start | bytes 589832 | tf_op jit(solution)/shard_map/ppermute | solution.py:220
  26.9 0.7 shard_map.46.observed_ref
  27.7 3.5 %collective-permute-done.5.refs_4_ = f32[12,32,128]{2,1,0:T(8,128)S(1)} collective-permute-done((f32[12,32,128]{2,1,0:T(8,128)S(1)}, f32[12,32,128]{2,1,0:T(8,128)S(1)}, u32[]{:S(2)}, u32[]{:S(2)}) %collective-permute-start.5) | collective-permute-done | bytes 196640 | tf_op jit(solution)/shard_map/ppermute | solution.py:220
  31.2 3.1 %collective-permute-done.6.refs_5_ = f32[12,32,128]{2,1,0:T(8,128)S(1)} collective-permute-done((f32[12,32,128]{2,1,0:T(8,128)S(1)}, f32[12,32,128]{2,1,0:T(8,128)S(1)}, u32[]{:S(2)}, u32[]{:S(2)}) %collective-permute-start.6) | collective-permute-done | bytes 196640 | tf_op jit(solution)/shard_map/ppermute | solution.py:220
  34.4 1.3 %shard_map.50 = (f32[448,128]{1,0:T(8,128)S(1)}, f32[264,512]{1,0:T(8,128)S(1)}, f32[264,256]{1,0:T(8,128)S(1)}, f32[264,512]{1,0:T(8,128)S(1)}, f32[264,256]{1,0:T(8,128)S(1)}) custom-call(f32[8,1536]{1,0:T(8,128)S(1)} %shard_map.46.observed_ref, f32[12,32,128]{2,1,0:T(8,128)S(1)} %get-tuple-element.37.refs_0_, ...), custom_call_target="tpu_custom_call" | custom-call | tf_op jit(solution)/shard_map/pallas_call | solution.py:583
  35.8 1.3 %collective-permute-done.9 = f32[224,128]{1,0:T(8,128)S(1)} collective-permute-done((f32[224,128]{1,0:T(8,128)S(1)}, f32[224,128]{1,0:T(8,128)S(1)}, u32[]{:S(2)}, u32[]{:S(2)}) %collective-permute-start.9) | collective-permute-done | bytes 114720 | tf_op jit(solution)/shard_map/ppermute | solution.py:328
  37.1 1.0 %collective-permute-start.11 = (f32[56,128]{1,0:T(8,128)S(1)}, f32[56,128]{1,0:T(8,128)S(1)}, u32[]{:S(2)}, u32[]{:S(2)}) collective-permute-start(f32[56,128]{1,0:T(8,128)S(1)} %get-tuple-element.71), channel_id=1, source_target_pairs={{0,16},{8,24},{16,0},{24,8},{1,17},{9,25},{17,1},{25,9},{2,18},{10... | collective-permute-start | bytes 86024 | tf_op jit(solution)/shard_map/ppermute | solution.py:328
  38.1 0.9 %collective-permute-start.12 = (f32[56,128]{1,0:T(8,128)S(1)}, f32[56,128]{1,0:T(8,128)S(1)}, u32[]{:S(2)}, u32[]{:S(2)}) collective-permute-start(f32[56,128]{1,0:T(8,128)S(1)} %get-tuple-element.72), channel_id=1, source_target_pairs={{0,24},{8,16},{16,8},{24,0},{1,25},{9,17},{17,9},{25,1},{2,26},{10... | collective-permute-start | bytes 86024 | tf_op jit(solution)/shard_map/ppermute | solution.py:328
  39.0 0.8 collective-permute-start.10
  39.9 1.9 %collective-permute-done.12 = f32[56,128]{1,0:T(8,128)S(1)} collective-permute-done((f32[56,128]{1,0:T(8,128)S(1)}, f32[56,128]{1,0:T(8,128)S(1)}, u32[]{:S(2)}, u32[]{:S(2)}) %collective-permute-start.12) | collective-permute-done | bytes 28704 | tf_op jit(solution)/shard_map/ppermute | solution.py:328
  41.8 1.2 %collective-permute-start.16 = (f32[264,512]{1,0:T(8,128)S(1)}, f32[264,512]{1,0:T(8,128)S(1)}, u32[]{:S(2)}, u32[]{:S(2)}) collective-permute-start(f32[264,512]{1,0:T(8,128)S(1)} %get-tuple-element.49.refs_0_), channel_id=1, source_target_pairs={{0,8},{8,0},{16,24},{24,16},{1,9},{9,1},{17,25},{25,17},{2,10},{10... | collective-permute-start | bytes 1622024 | tf_op jit(solution)/shard_map/ppermute | solution.py:328
  43.1 0.5 collective-permute-start.17
  43.6 1.8 %collective-permute-start.15 = (f32[56,128]{1,0:T(8,128)S(1)}, f32[56,128]{1,0:T(8,128)S(1)}, u32[]{:S(2)}, u32[]{:S(2)}) collective-permute-start(f32[56,128]{1,0:T(8,128)S(1)} %bitcast_add_fusion), channel_id=1, source_target_pairs={{0,1},{1,0},{2,3},{3,2},{4,5},{5,4},{6,7},{7,6},{8,9},{9,8},{10,11... | collective-permute-start | bytes 86024 | tf_op jit(solution)/shard_map/ppermute | solution.py:328
  45.4 2.3 %collective-permute-start.14 = (f32[56,128]{1,0:T(8,128)S(1)}, f32[56,128]{1,0:T(8,128)S(1)}, u32[]{:S(2)}, u32[]{:S(2)}) collective-permute-start(f32[56,128]{1,0:T(8,128)S(1)} %bitcast_add_fusion), channel_id=1, source_target_pairs={{0,2},{1,3},{2,0},{3,1},{4,6},{5,7},{6,4},{7,5},{8,10},{9,11},{10,... | collective-permute-start | bytes 86024 | tf_op jit(solution)/shard_map/ppermute | solution.py:328
  47.7 1.6 %collective-permute-done.14 = f32[56,128]{1,0:T(8,128)S(1)} collective-permute-done((f32[56,128]{1,0:T(8,128)S(1)}, f32[56,128]{1,0:T(8,128)S(1)}, u32[]{:S(2)}, u32[]{:S(2)}) %collective-permute-start.14) | collective-permute-done | bytes 28704 | tf_op jit(solution)/shard_map/ppermute | solution.py:328
  49.3 2.9 %collective-permute-done.13 = f32[56,128]{1,0:T(8,128)S(1)} collective-permute-done((f32[56,128]{1,0:T(8,128)S(1)}, f32[56,128]{1,0:T(8,128)S(1)}, u32[]{:S(2)}, u32[]{:S(2)}) %collective-permute-start.13) | collective-permute-done | bytes 28704 | tf_op jit(solution)/shard_map/ppermute | solution.py:328
  52.2 1.7 %collective-permute-done.16.refs_4_ = f32[264,512]{1,0:T(8,128)S(1)} collective-permute-done((f32[264,512]{1,0:T(8,128)S(1)}, f32[264,512]{1,0:T(8,128)S(1)}, u32[]{:S(2)}, u32[]{:S(2)}) %collective-permute-start.16) | collective-permute-done | bytes 540704 | tf_op jit(solution)/shard_map/ppermute | solution.py:328
  53.9 1.3 %collective-permute-done.17.refs_6_ = f32[264,512]{1,0:T(8,128)S(1)} collective-permute-done((f32[264,512]{1,0:T(8,128)S(1)}, f32[264,512]{1,0:T(8,128)S(1)}, u32[]{:S(2)}, u32[]{:S(2)}) %collective-permute-start.17) | collective-permute-done | bytes 540704 | tf_op jit(solution)/shard_map/ppermute | solution.py:328
  55.3 1.4 %collective-permute-start.19 = (f32[56,128]{1,0:T(8,128)S(1)}, f32[56,128]{1,0:T(8,128)S(1)}, u32[]{:S(2)}, u32[]{:S(2)}) collective-permute-start(f32[56,128]{1,0:T(8,128)S(1)} %add_add_fusion), channel_id=1, source_target_pairs={{0,16},{8,24},{16,0},{24,8},{1,17},{9,25},{17,1},{25,9},{2,18},{10... | collective-permute-start | bytes 86024 | tf_op jit(solution)/shard_map/ppermute | solution.py:328
  56.6 1.2 %collective-permute-start.18 = (f32[56,128]{1,0:T(8,128)S(1)}, f32[56,128]{1,0:T(8,128)S(1)}, u32[]{:S(2)}, u32[]{:S(2)}) collective-permute-start(f32[56,128]{1,0:T(8,128)S(1)} %add_add_fusion), channel_id=1, source_target_pairs={{0,8},{8,0},{16,24},{24,16},{1,9},{9,1},{17,25},{25,17},{2,10},{10... | collective-permute-start | bytes 86024 | tf_op jit(solution)/shard_map/ppermute | solution.py:328
  57.8 1.0 %collective-permute-done.20 = f32[56,128]{1,0:T(8,128)S(1)} collective-permute-done((f32[56,128]{1,0:T(8,128)S(1)}, f32[56,128]{1,0:T(8,128)S(1)}, u32[]{:S(2)}, u32[]{:S(2)}) %collective-permute-start.20) | collective-permute-done | bytes 28704 | tf_op jit(solution)/shard_map/ppermute | solution.py:328
  58.8 0.6 collective-permute-done.18
  59.4 4.4 %collective-permute-start.21 = (f32[224,128]{1,0:T(8,128)S(1)}, f32[224,128]{1,0:T(8,128)S(1)}, u32[]{:S(2)}, u32[]{:S(2)}) collective-permute-start(f32[224,128]{1,0:T(8,128)S(1)} %pad_maximum_fusion.2), channel_id=1, source_target_pairs={{0,4},{4,0},{1,5},{5,1},{2,6},{6,2},{3,7},{7,3},{8,12},{12,8},{9,1... | collective-permute-start | bytes 344072 | tf_op jit(solution)/shard_map/ppermute | solution.py:328
  63.8 1.2 %collective-permute-start.22 = (f32[264,256]{1,0:T(8,128)S(1)}, f32[264,256]{1,0:T(8,128)S(1)}, u32[]{:S(2)}, u32[]{:S(2)}) collective-permute-start(f32[264,256]{1,0:T(8,128)S(1)} %get-tuple-element.56.refs_1_), channel_id=1, source_target_pairs={{0,8},{8,0},{16,24},{24,16},{1,9},{9,1},{17,25},{25,17},{2,10},{10... | collective-permute-start | bytes 811016 | tf_op jit(solution)/shard_map/ppermute | solution.py:328
  65.0 0.5 collective-permute-start.23
  65.5 7.2 %shard_map.51.transform_ref = f32[256,256]{1,0:T(8,128)S(1)} custom-call(f32[448,128]{1,0:T(8,128)S(1)} %pad_maximum_fusion.packed_ref), custom_call_target="tpu_custom_call" | custom-call | tf_op jit(solution)/shard_map/pallas_call | solution.py:590
  72.8 0.9 %shard_map.52 = (f32[24,32,128]{2,1,0:T(8,128)S(1)}, f32[12,32,128]{2,1,0:T(8,128)S(1)}, f32[12,32,128]{2,1,0:T(8,128)S(1)}, f32[12,32,128]{2,1,0:T(8,128)S(1)},...) custom-call(f32[256,256]{1,0:T(8,128)S(1)} %shard_map.51.transform_ref, ...), custom_call_target="tpu_custom_call" | custom-call | tf_op jit(solution)/shard_map/pallas_call | solution.py:593
  73.7 1.1 %collective-permute-start.28 = (f32[24,32,128]{2,1,0:T(8,128)S(1)}, f32[24,32,128]{2,1,0:T(8,128)S(1)}, u32[]{:S(2)}, u32[]{:S(2)}) collective-permute-start(f32[24,32,128]{2,1,0:T(8,128)S(1)} %get-tuple-element.64), channel_id=1, source_target_pairs={{0,4},{4,0},{8,12},{12,8},{16,20},{20,16},{24,28},{28,24},{1,5},{5... | collective-permute-start | bytes 1179656 | tf_op jit(solution)/shard_map/ppermute | solution.py:220
  74.9 0.3 collective-permute-start.24
  75.2 0.5 collective-permute-start.25
  75.7 1.7 %collective-permute-start.26 = (f32[12,32,128]{2,1,0:T(8,128)S(1)}, f32[12,32,128]{2,1,0:T(8,128)S(1)}, u32[]{:S(2)}, u32[]{:S(2)}) collective-permute-start(f32[12,32,128]{2,1,0:T(8,128)S(1)} %get-tuple-element.62), channel_id=1, source_target_pairs={{0,12},{4,8},{8,4},{12,0},{16,28},{20,24},{24,20},{28,16},{1,13},{... | collective-permute-start | bytes 589832 | tf_op jit(solution)/shard_map/ppermute | solution.py:220
  77.4 0.7 collective-permute-start.27
  78.1 3.3 %collective-permute-done.24.refs_1_ = f32[12,32,128]{2,1,0:T(8,128)S(1)} collective-permute-done((f32[12,32,128]{2,1,0:T(8,128)S(1)}, f32[12,32,128]{2,1,0:T(8,128)S(1)}, u32[]{:S(2)}, u32[]{:S(2)}) %collective-permute-start.24) | collective-permute-done | bytes 196640 | tf_op jit(solution)/shard_map/ppermute | solution.py:220
  81.4 4.4 %collective-permute-done.26.refs_3_ = f32[12,32,128]{2,1,0:T(8,128)S(1)} collective-permute-done((f32[12,32,128]{2,1,0:T(8,128)S(1)}, f32[12,32,128]{2,1,0:T(8,128)S(1)}, u32[]{:S(2)}, u32[]{:S(2)}) %collective-permute-start.26) | collective-permute-done | bytes 196640 | tf_op jit(solution)/shard_map/ppermute | solution.py:220
  85.7 0.3 collective-permute-done.27.refs_4_
  86.0 2.4 %shard_map.53 = f32[3072,128]{1,0:T(8,128)} custom-call(f32[24,32,128]{2,1,0:T(8,128)S(1)} %get-tuple-element.59.refs_0_, f32[12,32,128]{2,1,0:T(8,128)S(1)} %collective-permute-done.24.refs_1_, f32[12,32,128]{2,1,0:T(8,128)S(1)} %collective-permute-done.25.refs_2_, f32[12,32,128]{2,1,0:T(8,128)S(1)} %collective-permute-done.26.refs_3_, ...), custom_call_target="tpu_custom_call" | custom-call | tf_op jit(solution)/shard_map/pallas_call | solution.py:563
  (36 shorter events, 0.6 us)
Async XLA Ops:
  0.0 1.4 %copy-start = (f32[32,3,32,128]{3,2,1,0:T(8,128)S(1)}, f32[32,3,32,128]{3,2,1,0:T(8,128)}, u32[]{:S(2)}) copy-start(f32[32,3,32,128]{3,2,1,0:T(8,128)} %bottom_ref.1) | copy-start | bytes 4718596
  1.6 9.7 %collective-permute-start = (f32[9,32,128]{2,1,0:T(8,128)S(1)}, f32[9,32,128]{2,1,0:T(8,128)S(1)}, u32[]{:S(2)}, u32[]{:S(2)}) collective-permute-start(f32[9,32,128]{2,1,0:T(8,128)S(1)} %get-tuple-element.35), channel_id=1, source_target_pairs={{0,1},{1,2},{2,3},{4,5},{5,6},{6,7},{8,9},{9,10},{10,11},{12,13},{... | collective-permute-start | bytes 442376 | tf_op jit(solution)/shard_map/ppermute | solution.py:185
  5.7 6.3 %collective-permute-start.1 = (f32[9,32,128]{2,1,0:T(8,128)S(1)}, f32[9,32,128]{2,1,0:T(8,128)S(1)}, u32[]{:S(2)}, u32[]{:S(2)}) collective-permute-start(f32[9,32,128]{2,1,0:T(8,128)S(1)} %get-tuple-element.36), channel_id=1, source_target_pairs={{1,0},{2,1},{3,2},{5,4},{6,5},{7,6},{9,8},{10,9},{11,10},{13,12},{... | collective-permute-start | bytes 442376 | tf_op jit(solution)/shard_map/ppermute | solution.py:186
  11.3 15.6 %copy-start.1 = (f32[1,768]{1,0:T(1,128)S(1)}, f32[1,768]{1,0:T(1,128)}, u32[]{:S(2)}) copy-start(f32[1,768]{1,0:T(1,128)} %values_ref.1) | copy-start | bytes 9220
  11.3 15.6 %copy-start.2 = (f32[1,768]{1,0:T(1,128)S(1)}, f32[1,768]{1,0:T(1,128)}, u32[]{:S(2)}) copy-start(f32[1,768]{1,0:T(1,128)} %precision_ref.1) | copy-start | bytes 9220
  11.3 15.6 %copy-start.3 = (s32[1,768]{1,0:T(1,128)S(1)}, s32[1,768]{1,0:T(1,128)}, u32[]{:S(2)}) copy-start(s32[1,768]{1,0:T(1,128)} %index_ref.1) | copy-start | bytes 9220
  13.6 6.6 %collective-permute-start.2 = (f32[12,32,128]{2,1,0:T(8,128)S(1)}, f32[12,32,128]{2,1,0:T(8,128)S(1)}, u32[]{:S(2)}, u32[]{:S(2)}) collective-permute-start(f32[12,32,128]{2,1,0:T(8,128)S(1)} %get-tuple-element.38), channel_id=1, source_target_pairs={{0,8},{4,12},{8,0},{12,4},{16,24},{20,28},{24,16},{28,20},{1,9},{5... | collective-permute-start | bytes 589832 | tf_op jit(solution)/shard_map/ppermute | solution.py:220
  14.8 10.5 %collective-permute-start.3 = (f32[12,32,128]{2,1,0:T(8,128)S(1)}, f32[12,32,128]{2,1,0:T(8,128)S(1)}, u32[]{:S(2)}, u32[]{:S(2)}) collective-permute-start(f32[12,32,128]{2,1,0:T(8,128)S(1)} %get-tuple-element.39), channel_id=1, source_target_pairs={{0,16},{4,20},{8,24},{12,28},{16,0},{20,4},{24,8},{28,12},{1,17},{... | collective-permute-start | bytes 589832 | tf_op jit(solution)/shard_map/ppermute | solution.py:220
  16.1 11.6 %collective-permute-start.4 = (f32[12,32,128]{2,1,0:T(8,128)S(1)}, f32[12,32,128]{2,1,0:T(8,128)S(1)}, u32[]{:S(2)}, u32[]{:S(2)}) collective-permute-start(f32[12,32,128]{2,1,0:T(8,128)S(1)} %get-tuple-element.40), channel_id=1, source_target_pairs={{0,24},{4,28},{8,16},{12,20},{16,8},{20,12},{24,0},{28,4},{1,25},{... | collective-permute-start | bytes 589832 | tf_op jit(solution)/shard_map/ppermute | solution.py:220
  16.3 15.0 %collective-permute-start.5 = (f32[12,32,128]{2,1,0:T(8,128)S(1)}, f32[12,32,128]{2,1,0:T(8,128)S(1)}, u32[]{:S(2)}, u32[]{:S(2)}) collective-permute-start(f32[12,32,128]{2,1,0:T(8,128)S(1)} %get-tuple-element.41), channel_id=1, source_target_pairs={{0,12},{4,8},{8,4},{12,0},{16,28},{20,24},{24,20},{28,16},{1,13},{... | collective-permute-start | bytes 589832 | tf_op jit(solution)/shard_map/ppermute | solution.py:220
  20.1 14.3 %collective-permute-start.6 = (f32[12,32,128]{2,1,0:T(8,128)S(1)}, f32[12,32,128]{2,1,0:T(8,128)S(1)}, u32[]{:S(2)}, u32[]{:S(2)}) collective-permute-start(f32[12,32,128]{2,1,0:T(8,128)S(1)} %get-tuple-element.42), channel_id=1, source_target_pairs={{0,20},{4,16},{8,28},{12,24},{16,4},{20,0},{24,12},{28,8},{1,21},{... | collective-permute-start | bytes 589832 | tf_op jit(solution)/shard_map/ppermute | solution.py:220
  20.1 14.3 %collective-permute-start.7 = (f32[12,32,128]{2,1,0:T(8,128)S(1)}, f32[12,32,128]{2,1,0:T(8,128)S(1)}, u32[]{:S(2)}, u32[]{:S(2)}) collective-permute-start(f32[12,32,128]{2,1,0:T(8,128)S(1)} %get-tuple-element.43), channel_id=1, source_target_pairs={{0,28},{4,24},{8,20},{12,16},{16,12},{20,8},{24,4},{28,0},{1,29},{... | collective-permute-start | bytes 589832 | tf_op jit(solution)/shard_map/ppermute | solution.py:220
  25.4 9.0 %collective-permute-start.8 = (f32[12,32,128]{2,1,0:T(8,128)S(1)}, f32[12,32,128]{2,1,0:T(8,128)S(1)}, u32[]{:S(2)}, u32[]{:S(2)}) collective-permute-start(f32[12,32,128]{2,1,0:T(8,128)S(1)} %get-tuple-element.44), channel_id=1, source_target_pairs={{0,4},{4,0},{8,12},{12,8},{16,20},{20,16},{24,28},{28,24},{1,5},{5... | collective-permute-start | bytes 589832 | tf_op jit(solution)/shard_map/ppermute | solution.py:220
  35.7 1.4 %collective-permute-start.9 = (f32[224,128]{1,0:T(8,128)S(1)}, f32[224,128]{1,0:T(8,128)S(1)}, u32[]{:S(2)}, u32[]{:S(2)}) collective-permute-start(f32[224,128]{1,0:T(8,128)S(1)} %constant_dynamic-slice_fusion), channel_id=1, source_target_pairs={{0,4},{4,0},{1,5},{5,1},{2,6},{6,2},{3,7},{7,3},{8,12},{12,8},{9,1... | collective-permute-start | bytes 344072 | tf_op jit(solution)/shard_map/ppermute | solution.py:328
  37.1 2.8 %collective-permute-start.11 = (f32[56,128]{1,0:T(8,128)S(1)}, f32[56,128]{1,0:T(8,128)S(1)}, u32[]{:S(2)}, u32[]{:S(2)}) collective-permute-start(f32[56,128]{1,0:T(8,128)S(1)} %get-tuple-element.71), channel_id=1, source_target_pairs={{0,16},{8,24},{16,0},{24,8},{1,17},{9,25},{17,1},{25,9},{2,18},{10... | collective-permute-start | bytes 86024 | tf_op jit(solution)/shard_map/ppermute | solution.py:328
  38.1 3.6 %collective-permute-start.12 = (f32[56,128]{1,0:T(8,128)S(1)}, f32[56,128]{1,0:T(8,128)S(1)}, u32[]{:S(2)}, u32[]{:S(2)}) collective-permute-start(f32[56,128]{1,0:T(8,128)S(1)} %get-tuple-element.72), channel_id=1, source_target_pairs={{0,24},{8,16},{16,8},{24,0},{1,25},{9,17},{17,9},{25,1},{2,26},{10... | collective-permute-start | bytes 86024 | tf_op jit(solution)/shard_map/ppermute | solution.py:328
  39.0 2.8 %collective-permute-start.10 = (f32[56,128]{1,0:T(8,128)S(1)}, f32[56,128]{1,0:T(8,128)S(1)}, u32[]{:S(2)}, u32[]{:S(2)}) collective-permute-start(f32[56,128]{1,0:T(8,128)S(1)} %get-tuple-element.73), channel_id=1, source_target_pairs={{0,8},{8,0},{16,24},{24,16},{1,9},{9,1},{17,25},{25,17},{2,10},{10... | collective-permute-start | bytes 86024 | tf_op jit(solution)/shard_map/ppermute | solution.py:328
  41.8 12.0 %collective-permute-start.16 = (f32[264,512]{1,0:T(8,128)S(1)}, f32[264,512]{1,0:T(8,128)S(1)}, u32[]{:S(2)}, u32[]{:S(2)}) collective-permute-start(f32[264,512]{1,0:T(8,128)S(1)} %get-tuple-element.49.refs_0_), channel_id=1, source_target_pairs={{0,8},{8,0},{16,24},{24,16},{1,9},{9,1},{17,25},{25,17},{2,10},{10... | collective-permute-start | bytes 1622024 | tf_op jit(solution)/shard_map/ppermute | solution.py:328
  43.1 12.1 %collective-permute-start.17 = (f32[264,512]{1,0:T(8,128)S(1)}, f32[264,512]{1,0:T(8,128)S(1)}, u32[]{:S(2)}, u32[]{:S(2)}) collective-permute-start(f32[264,512]{1,0:T(8,128)S(1)} %get-tuple-element.50.refs_2_), channel_id=1, source_target_pairs={{0,16},{8,24},{16,0},{24,8},{1,17},{9,25},{17,1},{25,9},{2,18},{10... | collective-permute-start | bytes 1622024 | tf_op jit(solution)/shard_map/ppermute | solution.py:328
  43.6 4.1 %collective-permute-start.15 = (f32[56,128]{1,0:T(8,128)S(1)}, f32[56,128]{1,0:T(8,128)S(1)}, u32[]{:S(2)}, u32[]{:S(2)}) collective-permute-start(f32[56,128]{1,0:T(8,128)S(1)} %bitcast_add_fusion), channel_id=1, source_target_pairs={{0,1},{1,0},{2,3},{3,2},{4,5},{5,4},{6,7},{7,6},{8,9},{9,8},{10,11... | collective-permute-start | bytes 86024 | tf_op jit(solution)/shard_map/ppermute | solution.py:328
  45.4 3.9 %collective-permute-start.14 = (f32[56,128]{1,0:T(8,128)S(1)}, f32[56,128]{1,0:T(8,128)S(1)}, u32[]{:S(2)}, u32[]{:S(2)}) collective-permute-start(f32[56,128]{1,0:T(8,128)S(1)} %bitcast_add_fusion), channel_id=1, source_target_pairs={{0,2},{1,3},{2,0},{3,1},{4,6},{5,7},{6,4},{7,5},{8,10},{9,11},{10,... | collective-permute-start | bytes 86024 | tf_op jit(solution)/shard_map/ppermute | solution.py:328
  47.7 4.5 %collective-permute-start.13 = (f32[56,128]{1,0:T(8,128)S(1)}, f32[56,128]{1,0:T(8,128)S(1)}, u32[]{:S(2)}, u32[]{:S(2)}) collective-permute-start(f32[56,128]{1,0:T(8,128)S(1)} %bitcast_add_fusion), channel_id=1, source_target_pairs={{0,3},{1,2},{2,1},{3,0},{4,7},{5,6},{6,5},{7,4},{8,11},{9,10},{10,... | collective-permute-start | bytes 86024 | tf_op jit(solution)/shard_map/ppermute | solution.py:328
  55.2 3.6 %collective-permute-start.20 = (f32[56,128]{1,0:T(8,128)S(1)}, f32[56,128]{1,0:T(8,128)S(1)}, u32[]{:S(2)}, u32[]{:S(2)}) collective-permute-start(f32[56,128]{1,0:T(8,128)S(1)} %add_add_fusion), channel_id=1, source_target_pairs={{0,24},{8,16},{16,8},{24,0},{1,25},{9,17},{17,9},{25,1},{2,26},{10... | collective-permute-start | bytes 86024 | tf_op jit(solution)/shard_map/ppermute | solution.py:328
  55.3 3.5 %collective-permute-start.19 = (f32[56,128]{1,0:T(8,128)S(1)}, f32[56,128]{1,0:T(8,128)S(1)}, u32[]{:S(2)}, u32[]{:S(2)}) collective-permute-start(f32[56,128]{1,0:T(8,128)S(1)} %add_add_fusion), channel_id=1, source_target_pairs={{0,16},{8,24},{16,0},{24,8},{1,17},{9,25},{17,1},{25,9},{2,18},{10... | collective-permute-start | bytes 86024 | tf_op jit(solution)/shard_map/ppermute | solution.py:328
  56.6 2.7 %collective-permute-start.18 = (f32[56,128]{1,0:T(8,128)S(1)}, f32[56,128]{1,0:T(8,128)S(1)}, u32[]{:S(2)}, u32[]{:S(2)}) collective-permute-start(f32[56,128]{1,0:T(8,128)S(1)} %add_add_fusion), channel_id=1, source_target_pairs={{0,8},{8,0},{16,24},{24,16},{1,9},{9,1},{17,25},{25,17},{2,10},{10... | collective-permute-start | bytes 86024 | tf_op jit(solution)/shard_map/ppermute | solution.py:328
  59.4 6.1 %collective-permute-start.21 = (f32[224,128]{1,0:T(8,128)S(1)}, f32[224,128]{1,0:T(8,128)S(1)}, u32[]{:S(2)}, u32[]{:S(2)}) collective-permute-start(f32[224,128]{1,0:T(8,128)S(1)} %pad_maximum_fusion.2), channel_id=1, source_target_pairs={{0,4},{4,0},{1,5},{5,1},{2,6},{6,2},{3,7},{7,3},{8,12},{12,8},{9,1... | collective-permute-start | bytes 344072 | tf_op jit(solution)/shard_map/ppermute | solution.py:328
  63.8 9.0 %collective-permute-start.22 = (f32[264,256]{1,0:T(8,128)S(1)}, f32[264,256]{1,0:T(8,128)S(1)}, u32[]{:S(2)}, u32[]{:S(2)}) collective-permute-start(f32[264,256]{1,0:T(8,128)S(1)} %get-tuple-element.56.refs_1_), channel_id=1, source_target_pairs={{0,8},{8,0},{16,24},{24,16},{1,9},{9,1},{17,25},{25,17},{2,10},{10... | collective-permute-start | bytes 811016 | tf_op jit(solution)/shard_map/ppermute | solution.py:328
  65.0 7.8 %collective-permute-start.23 = (f32[264,256]{1,0:T(8,128)S(1)}, f32[264,256]{1,0:T(8,128)S(1)}, u32[]{:S(2)}, u32[]{:S(2)}) collective-permute-start(f32[264,256]{1,0:T(8,128)S(1)} %get-tuple-element.58.refs_3_), channel_id=1, source_target_pairs={{0,16},{8,24},{16,0},{24,8},{1,17},{9,25},{17,1},{25,9},{2,18},{10... | collective-permute-start | bytes 811016 | tf_op jit(solution)/shard_map/ppermute | solution.py:328
  73.7 12.3 %collective-permute-start.28 = (f32[24,32,128]{2,1,0:T(8,128)S(1)}, f32[24,32,128]{2,1,0:T(8,128)S(1)}, u32[]{:S(2)}, u32[]{:S(2)}) collective-permute-start(f32[24,32,128]{2,1,0:T(8,128)S(1)} %get-tuple-element.64), channel_id=1, source_target_pairs={{0,4},{4,0},{8,12},{12,8},{16,20},{20,16},{24,28},{28,24},{1,5},{5... | collective-permute-start | bytes 1179656 | tf_op jit(solution)/shard_map/ppermute | solution.py:220
  74.9 6.5 %collective-permute-start.24 = (f32[12,32,128]{2,1,0:T(8,128)S(1)}, f32[12,32,128]{2,1,0:T(8,128)S(1)}, u32[]{:S(2)}, u32[]{:S(2)}) collective-permute-start(f32[12,32,128]{2,1,0:T(8,128)S(1)} %get-tuple-element.60), channel_id=1, source_target_pairs={{0,8},{4,12},{8,0},{12,4},{16,24},{20,28},{24,16},{28,20},{1,9},{5... | collective-permute-start | bytes 589832 | tf_op jit(solution)/shard_map/ppermute | solution.py:220
  75.2 6.2 %collective-permute-start.25 = (f32[12,32,128]{2,1,0:T(8,128)S(1)}, f32[12,32,128]{2,1,0:T(8,128)S(1)}, u32[]{:S(2)}, u32[]{:S(2)}) collective-permute-start(f32[12,32,128]{2,1,0:T(8,128)S(1)} %get-tuple-element.61), channel_id=1, source_target_pairs={{0,16},{4,20},{8,24},{12,28},{16,0},{20,4},{24,8},{28,12},{1,17},{... | collective-permute-start | bytes 589832 | tf_op jit(solution)/shard_map/ppermute | solution.py:220
  75.7 10.0 %collective-permute-start.26 = (f32[12,32,128]{2,1,0:T(8,128)S(1)}, f32[12,32,128]{2,1,0:T(8,128)S(1)}, u32[]{:S(2)}, u32[]{:S(2)}) collective-permute-start(f32[12,32,128]{2,1,0:T(8,128)S(1)} %get-tuple-element.62), channel_id=1, source_target_pairs={{0,12},{4,8},{8,4},{12,0},{16,28},{20,24},{24,20},{28,16},{1,13},{... | collective-permute-start | bytes 589832 | tf_op jit(solution)/shard_map/ppermute | solution.py:220
  77.4 8.6 %collective-permute-start.27 = (f32[12,32,128]{2,1,0:T(8,128)S(1)}, f32[12,32,128]{2,1,0:T(8,128)S(1)}, u32[]{:S(2)}, u32[]{:S(2)}) collective-permute-start(f32[12,32,128]{2,1,0:T(8,128)S(1)} %get-tuple-element.63), channel_id=1, source_target_pairs={{0,20},{4,16},{8,28},{12,24},{16,4},{20,0},{24,12},{28,8},{1,21},{... | collective-permute-start | bytes 589832 | tf_op jit(solution)/shard_map/ppermute | solution.py:220

commit v6 on v5

--- a/solution.py
+++ b/solution.py
@@ -41,13 +41,16 @@
     return jax.ShapeDtypeStruct(shape, jnp.float32)
 
 
-def pack_kernel(top_ref, bottom_ref, to_prev_ref, to_next_ref):
-    fields, edge = top_ref.shape[1], top_ref.shape[2]
+def pack_kernel(top_ref, bottom_ref, outer_ref, inner_ref):
+    edge = top_ref.shape[2]
+    even = lax.rem(lax.axis_index("space"), 2) == 0
     at = 0
     for field, rows in enumerate(HALO):
         for row in range(rows):
-            to_prev_ref[at] = top_ref[:, field, row, :]
-            to_next_ref[at] = bottom_ref[:, field, edge - rows + row, :]
+            to_prev = top_ref[:, field, row, :]
+            to_next = bottom_ref[:, field, edge - rows + row, :]
+            outer_ref[at] = jnp.where(even, to_prev, to_next)
+            inner_ref[at] = jnp.where(even, to_next, to_prev)
             at += 1
 
 
@@ -135,11 +138,12 @@
     return lax.axis_index("group") * lax.axis_size("member") + lax.axis_index("member")
 
 
-def edge_kernel(dims, state_ref, before_ref, after_ref, interior_ref, *refs):
+def edge_kernel(dims, state_ref, outer_ref, inner_ref, interior_ref, *refs):
     members, fields, rows, cols, block_rows, edge = dims
     clusters = rows // block_rows
     slots, edges_ref = refs[:clusters], refs[clusters]
     here = lax.axis_index("space")
+    even = lax.rem(here, 2) == 0
     has_before = (here > 0).astype(jnp.float32)
     has_after = (here < lax.axis_size("space") - 1).astype(jnp.float32)
     own = own_cluster(clusters)
@@ -156,9 +160,13 @@
         def load(field, row):
             offset = sum(HALO[:field])
             if row < 0:
-                return before_ref[offset + HALO[field] + row, at : at + 8, :]
+                held = offset + HALO[field] + row
+                outer, inner = outer_ref[held, at : at + 8, :], inner_ref[held, at : at + 8, :]
+                return jnp.where(even, outer, inner)
             if row >= rows:
-                return after_ref[offset + row - rows, at : at + 8, :]
+                held = offset + row - rows
+                outer, inner = outer_ref[held, at : at + 8, :], inner_ref[held, at : at + 8, :]
+                return jnp.where(even, inner, outer)
             start = (at * fields + field) * rows + row
             return state_ref[pl.ds(start, 8, stride=fields * rows), :]
 
@@ -180,10 +188,14 @@
     block_rows = rows // clusters
     terms = fields * block_rows
     edge = -(-4 // block_rows) * block_rows
-    to_prev, to_next = pack_edges(state)
+    outer, inner = pack_edges(state)
     count = lax.axis_size("space")
-    before = lax.ppermute(to_next, "space", [(i, i + 1) for i in range(count - 1)])
-    after = lax.ppermute(to_prev, "space", [(i + 1, i) for i in range(count - 1)])
+
+    def trade(value, first):
+        pairs = [(i, i + 1) for i in range(first, count - 1, 2)]
+        return lax.ppermute(value, "space", pairs + [(j, i) for i, j in pairs])
+
+    outer, inner = trade(outer, 1), trade(inner, 0)
     dims = (members, fields, rows, cols, block_rows, edge)
     flat = state.reshape(members * fields * rows, cols)
     size = members * fields * rows * cols
@@ -200,7 +212,7 @@
         [f32(terms, members, cols)] * clusters,
         4,
         [pltpu.VMEM((clusters, terms, members, cols), jnp.float32)],
-    )(flat, before, after, interior)
+    )(flat, outer, inner, interior)
 
 
 def slot_order(clusters):
@@ -542,30 +554,48 @@
 
 
 def place_kernel(dims, *refs):
-    clusters, fields, block_rows, cols = dims
-    out_ref = refs[-1]
+    clusters, fields, block_rows, members, cols, groups = dims
+    slots = return_slots(clusters)
+    values, (out_ref, placed_ref, sent) = refs[: len(slots)], refs[len(slots) :]
     rows = clusters * block_rows
     own = own_cluster(clusters)
-    for slot, ref in zip(return_slots(clusters), refs):
-        held = 0
-        for source, part in pieces(slot):
-            first = (own ^ (slot ^ source)) * block_rows
-            for term in term_parts(fields * block_rows)[part]:
-                field, row = divmod(term, block_rows)
-                at = field * rows + row + first
-                out_ref[pl.ds(at, 8, stride=fields * rows), :] = ref[held]
-                held += 1
+    size = members // groups
+    copies = []
+    for group in range(groups):
+        for slot, ref in zip(slots, values):
+            held = 0
+            for source, part in pieces(slot):
+                first = (own ^ (slot ^ source)) * block_rows
+                for term in term_parts(fields * block_rows)[part]:
+                    field, row = divmod(term, block_rows)
+                    at = group * size * fields * rows + field * rows + row + first
+                    placed_ref[pl.ds(at, size, stride=fields * rows), :] = ref[
+                        held, group * size : (group + 1) * size, :
+                    ]
+                    held += 1
+        span = pl.ds(group * size * fields * rows, size * fields * rows)
+        copies.append(pltpu.make_async_copy(placed_ref.at[span], out_ref.at[span], sent.at[group]))
+        copies[-1].start()
+    for copy in copies:
+        copy.wait()
 
 
 def place(values, clusters, fields, terms):
     _, members, cols = values[0].shape
     rows = clusters * terms
+    groups = members // 8
+    spec = pl.BlockSpec(memory_space=pltpu.VMEM)
     return pl.pallas_call(
-        functools.partial(place_kernel, (clusters, fields, terms // fields, cols)),
-        grid=(members // 8,),
+        functools.partial(
+            place_kernel, (clusters, fields, terms // fields, members, cols, groups)
+        ),
         out_shape=f32(members * rows, cols),
-        in_specs=[pl.BlockSpec((value.shape[0], 8, cols), lambda i: (0, i, 0)) for value in values],
-        out_specs=pl.BlockSpec((8 * rows, cols), lambda i: (i, 0)),
+        in_specs=[spec] * len(values),
+        out_specs=pl.BlockSpec(memory_space=pl.ANY),
+        scratch_shapes=[
+            pltpu.VMEM((members * rows, cols), jnp.float32),
+            pltpu.SemaphoreType.DMA((groups,)),
+        ],
         compiler_params=pltpu.CompilerParams(vmem_limit_bytes=VMEM_LIMIT),
     )(*values)
 

time: 88.6 us -> 87.6 us (0.989)
  no operation moved by 1% of the time
where the time goes in v6:
time: 87.6 us; the launch traced here: 87.4 us
  starting transfers between devices  40.1 us (46%)
  waiting for transfers between devices  27.5 us (31%)
  Pallas kernels  18.1 us (21%)
  local copies, waits for them, and re-layouts  1.49 us (2%)
    ppermute x12, starting transfers between devices, exchange(): lax.ppermute(value, ('group', 'member'), [(i, i ^ slot) for i in range(cl...  17.4 us
    ppermute x15, starting transfers between devices, flip(): lax.ppermute(value, axis, [(i, i ^ bits) for i in range(lax.axis_size(axi...  17.3 us
    ppermute x12, waiting for transfers between devices, exchange(): lax.ppermute(value, ('group', 'member'), [(i, i ^ slot) for i in range(cl...  14.6 us
    ppermute x15, waiting for transfers between devices, flip(): lax.ppermute(value, axis, [(i, i ^ bits) for i in range(lax.axis_size(axi...  12.9 us
    pallas_call x1, Pallas kernels, on_device(): call(functools.partial(transform_kernel, total), f32(total, total), 1)  7.25 us
    ppermute x2, starting transfers between devices, trade(): return lax.ppermute(value, 'space', pairs + [(j, i) for i, j in pairs])  5.4 us
    pallas_call x1, Pallas kernels, forecast(): call(functools.partial(interior_kernel, dims), f32(clusters, terms, membe...  4.31 us
  transfers between devices with their start and end apart: 29, of which 16 were waited for; matrix products, arithmetic and copies ran while one was open for 0% of the time, Pallas kernels for 14%

profile of v6, /device:TPU:1, one launch (start us, length us, event | category | flops | bytes accessed | tf_op | source)
XLA Modules:
  0.0 87.4 jit_solution(12358842593618971037)
XLA Ops:
  0.0 1.4 %copy-done = f32[32,3,32,128]{3,2,1,0:T(8,128)S(1)} copy-done((f32[32,3,32,128]{3,2,1,0:T(8,128)S(1)}, f32[32,3,32,128]{3,2,1,0:T(8,128)}, u32[]{:S(2)}) %copy-start) | copy-done | bytes 1572888
  1.4 0.3 shard_map.47
  1.8 0.7 collective-permute-start
  2.4 4.7 %collective-permute-start.1 = (f32[9,32,128]{2,1,0:T(8,128)S(1)}, f32[9,32,128]{2,1,0:T(8,128)S(1)}, u32[]{:S(2)}, u32[]{:S(2)}) collective-permute-start(f32[9,32,128]{2,1,0:T(8,128)S(1)} %get-tuple-element.36), channel_id=1, source_target_pairs={{0,1},{2,3},{1,0},{3,2},{4,5},{6,7},{5,4},{7,6},{8,9},{10,11},{9,8... | collective-permute-start | bytes 442376 | tf_op jit(solution)/shard_map/ppermute | solution.py:196
  7.2 4.3 %shard_map.48.interior_ref = f32[8,12,32,128]{3,2,1,0:T(8,128)S(1)} custom-call(f32[3072,128]{1,0:T(8,128)S(1)} %bitcast.23), custom_call_target="tpu_custom_call" | custom-call | flops 78643200 | bytes 6291456 | tf_op jit(solution)/shard_map/pallas_call | solution.py:202
  11.5 1.6 %shard_map.49 = (f32[12,32,128]{2,1,0:T(8,128)S(1)}, f32[12,32,128]{2,1,0:T(8,128)S(1)}, f32[12,32,128]{2,1,0:T(8,128)S(1)}, f32[12,32,128]{2,1,0:T(8,128)S(1)},...) custom-call(f32[3072,128]{1,0:T(8,128)S(1)} %bitcast.24, ...), custom_call_target="tpu_custom_call" | custom-call | tf_op jit(solution)/shard_map/pallas_call | solution.py:210
  13.1 1.3 %collective-permute-start.2 = (f32[12,32,128]{2,1,0:T(8,128)S(1)}, f32[12,32,128]{2,1,0:T(8,128)S(1)}, u32[]{:S(2)}, u32[]{:S(2)}) collective-permute-start(f32[12,32,128]{2,1,0:T(8,128)S(1)} %get-tuple-element.38), channel_id=1, source_target_pairs={{0,8},{4,12},{8,0},{12,4},{16,24},{20,28},{24,16},{28,20},{1,9},{5... | collective-permute-start | bytes 589832 | tf_op jit(solution)/shard_map/ppermute | solution.py:232
  14.4 1.2 %collective-permute-start.3 = (f32[12,32,128]{2,1,0:T(8,128)S(1)}, f32[12,32,128]{2,1,0:T(8,128)S(1)}, u32[]{:S(2)}, u32[]{:S(2)}) collective-permute-start(f32[12,32,128]{2,1,0:T(8,128)S(1)} %get-tuple-element.39), channel_id=1, source_target_pairs={{0,16},{4,20},{8,24},{12,28},{16,0},{20,4},{24,8},{28,12},{1,17},{... | collective-permute-start | bytes 589832 | tf_op jit(solution)/shard_map/ppermute | solution.py:232
  15.8 3.2 %collective-permute-start.5 = (f32[12,32,128]{2,1,0:T(8,128)S(1)}, f32[12,32,128]{2,1,0:T(8,128)S(1)}, u32[]{:S(2)}, u32[]{:S(2)}) collective-permute-start(f32[12,32,128]{2,1,0:T(8,128)S(1)} %get-tuple-element.41), channel_id=1, source_target_pairs={{0,12},{4,8},{8,4},{12,0},{16,28},{20,24},{24,20},{28,16},{1,13},{... | collective-permute-start | bytes 589832 | tf_op jit(solution)/shard_map/ppermute | solution.py:232
  19.0 5.3 %collective-permute-start.7 = (f32[12,32,128]{2,1,0:T(8,128)S(1)}, f32[12,32,128]{2,1,0:T(8,128)S(1)}, u32[]{:S(2)}, u32[]{:S(2)}) collective-permute-start(f32[12,32,128]{2,1,0:T(8,128)S(1)} %get-tuple-element.43), channel_id=1, source_target_pairs={{0,28},{4,24},{8,20},{12,16},{16,12},{20,8},{24,4},{28,0},{1,29},{... | collective-permute-start | bytes 589832 | tf_op jit(solution)/shard_map/ppermute | solution.py:232
  24.3 2.3 %collective-permute-start.8 = (f32[12,32,128]{2,1,0:T(8,128)S(1)}, f32[12,32,128]{2,1,0:T(8,128)S(1)}, u32[]{:S(2)}, u32[]{:S(2)}) collective-permute-start(f32[12,32,128]{2,1,0:T(8,128)S(1)} %get-tuple-element.44), channel_id=1, source_target_pairs={{0,4},{4,0},{8,12},{12,8},{16,20},{20,16},{24,28},{28,24},{1,5},{5... | collective-permute-start | bytes 589832 | tf_op jit(solution)/shard_map/ppermute | solution.py:232
  26.6 0.7 shard_map.46.observed_ref
  27.3 3.0 %collective-permute-done.5.refs_4_ = f32[12,32,128]{2,1,0:T(8,128)S(1)} collective-permute-done((f32[12,32,128]{2,1,0:T(8,128)S(1)}, f32[12,32,128]{2,1,0:T(8,128)S(1)}, u32[]{:S(2)}, u32[]{:S(2)}) %collective-permute-start.5) | collective-permute-done | bytes 196640 | tf_op jit(solution)/shard_map/ppermute | solution.py:232
  30.3 3.4 %collective-permute-done.6.refs_5_ = f32[12,32,128]{2,1,0:T(8,128)S(1)} collective-permute-done((f32[12,32,128]{2,1,0:T(8,128)S(1)}, f32[12,32,128]{2,1,0:T(8,128)S(1)}, u32[]{:S(2)}, u32[]{:S(2)}) %collective-permute-start.6) | collective-permute-done | bytes 196640 | tf_op jit(solution)/shard_map/ppermute | solution.py:232
  33.7 1.3 %shard_map.50 = (f32[448,128]{1,0:T(8,128)S(1)}, f32[264,512]{1,0:T(8,128)S(1)}, f32[264,256]{1,0:T(8,128)S(1)}, f32[264,512]{1,0:T(8,128)S(1)}, f32[264,256]{1,0:T(8,128)S(1)}) custom-call(f32[8,1536]{1,0:T(8,128)S(1)} %shard_map.46.observed_ref, f32[12,32,128]{2,1,0:T(8,128)S(1)} %get-tuple-element.37.refs_0_, ...), custom_call_target="tpu_custom_call" | custom-call | tf_op jit(solution)/shard_map/pallas_call | solution.py:613
  35.0 1.3 %collective-permute-done.9 = f32[224,128]{1,0:T(8,128)S(1)} collective-permute-done((f32[224,128]{1,0:T(8,128)S(1)}, f32[224,128]{1,0:T(8,128)S(1)}, u32[]{:S(2)}, u32[]{:S(2)}) %collective-permute-start.9) | collective-permute-done | bytes 114720 | tf_op jit(solution)/shard_map/ppermute | solution.py:340
  36.4 1.3 %collective-permute-start.11 = (f32[56,128]{1,0:T(8,128)S(1)}, f32[56,128]{1,0:T(8,128)S(1)}, u32[]{:S(2)}, u32[]{:S(2)}) collective-permute-start(f32[56,128]{1,0:T(8,128)S(1)} %get-tuple-element.71), channel_id=1, source_target_pairs={{0,16},{8,24},{16,0},{24,8},{1,17},{9,25},{17,1},{25,9},{2,18},{10... | collective-permute-start | bytes 86024 | tf_op jit(solution)/shard_map/ppermute | solution.py:340
  37.7 0.9 %collective-permute-start.12 = (f32[56,128]{1,0:T(8,128)S(1)}, f32[56,128]{1,0:T(8,128)S(1)}, u32[]{:S(2)}, u32[]{:S(2)}) collective-permute-start(f32[56,128]{1,0:T(8,128)S(1)} %get-tuple-element.72), channel_id=1, source_target_pairs={{0,24},{8,16},{16,8},{24,0},{1,25},{9,17},{17,9},{25,1},{2,26},{10... | collective-permute-start | bytes 86024 | tf_op jit(solution)/shard_map/ppermute | solution.py:340
  38.6 0.5 collective-permute-start.10
  39.2 2.1 %collective-permute-done.12 = f32[56,128]{1,0:T(8,128)S(1)} collective-permute-done((f32[56,128]{1,0:T(8,128)S(1)}, f32[56,128]{1,0:T(8,128)S(1)}, u32[]{:S(2)}, u32[]{:S(2)}) %collective-permute-start.12) | collective-permute-done | bytes 28704 | tf_op jit(solution)/shard_map/ppermute | solution.py:340
  41.3 0.3 collective-permute-done.10
  41.6 0.3 collective-permute-start.16
  41.9 1.5 %collective-permute-start.17 = (f32[264,512]{1,0:T(8,128)S(1)}, f32[264,512]{1,0:T(8,128)S(1)}, u32[]{:S(2)}, u32[]{:S(2)}) collective-permute-start(f32[264,512]{1,0:T(8,128)S(1)} %get-tuple-element.50.refs_2_), channel_id=1, source_target_pairs={{0,16},{8,24},{16,0},{24,8},{1,17},{9,25},{17,1},{25,9},{2,18},{10... | collective-permute-start | bytes 1622024 | tf_op jit(solution)/shard_map/ppermute | solution.py:340
  43.4 1.3 %collective-permute-start.14 = (f32[56,128]{1,0:T(8,128)S(1)}, f32[56,128]{1,0:T(8,128)S(1)}, u32[]{:S(2)}, u32[]{:S(2)}) collective-permute-start(f32[56,128]{1,0:T(8,128)S(1)} %bitcast_add_fusion), channel_id=1, source_target_pairs={{0,2},{1,3},{2,0},{3,1},{4,6},{5,7},{6,4},{7,5},{8,10},{9,11},{10,... | collective-permute-start | bytes 86024 | tf_op jit(solution)/shard_map/ppermute | solution.py:340
  44.8 2.2 %collective-permute-start.13 = (f32[56,128]{1,0:T(8,128)S(1)}, f32[56,128]{1,0:T(8,128)S(1)}, u32[]{:S(2)}, u32[]{:S(2)}) collective-permute-start(f32[56,128]{1,0:T(8,128)S(1)} %bitcast_add_fusion), channel_id=1, source_target_pairs={{0,3},{1,2},{2,1},{3,0},{4,7},{5,6},{6,5},{7,4},{8,11},{9,10},{10,... | collective-permute-start | bytes 86024 | tf_op jit(solution)/shard_map/ppermute | solution.py:340
  47.1 2.2 %collective-permute-done.13 = f32[56,128]{1,0:T(8,128)S(1)} collective-permute-done((f32[56,128]{1,0:T(8,128)S(1)}, f32[56,128]{1,0:T(8,128)S(1)}, u32[]{:S(2)}, u32[]{:S(2)}) %collective-permute-start.13) | collective-permute-done | bytes 28704 | tf_op jit(solution)/shard_map/ppermute | solution.py:340
  49.3 4.5 %collective-permute-done.16.refs_4_ = f32[264,512]{1,0:T(8,128)S(1)} collective-permute-done((f32[264,512]{1,0:T(8,128)S(1)}, f32[264,512]{1,0:T(8,128)S(1)}, u32[]{:S(2)}, u32[]{:S(2)}) %collective-permute-start.16) | collective-permute-done | bytes 540704 | tf_op jit(solution)/shard_map/ppermute | solution.py:340
  53.8 1.5 %collective-permute-start.20 = (f32[56,128]{1,0:T(8,128)S(1)}, f32[56,128]{1,0:T(8,128)S(1)}, u32[]{:S(2)}, u32[]{:S(2)}) collective-permute-start(f32[56,128]{1,0:T(8,128)S(1)} %add_add_fusion), channel_id=1, source_target_pairs={{0,24},{8,16},{16,8},{24,0},{1,25},{9,17},{17,9},{25,1},{2,26},{10... | collective-permute-start | bytes 86024 | tf_op jit(solution)/shard_map/ppermute | solution.py:340
  55.3 0.8 collective-permute-start.19
  56.2 0.4 collective-permute-start.18
  56.5 0.9 %collective-permute-done.20 = f32[56,128]{1,0:T(8,128)S(1)} collective-permute-done((f32[56,128]{1,0:T(8,128)S(1)}, f32[56,128]{1,0:T(8,128)S(1)}, u32[]{:S(2)}, u32[]{:S(2)}) %collective-permute-start.20) | collective-permute-done | bytes 28704 | tf_op jit(solution)/shard_map/ppermute | solution.py:340
  57.4 0.6 collective-permute-done.19
  58.1 0.8 collective-permute-done.18
  58.9 4.6 %collective-permute-start.21 = (f32[224,128]{1,0:T(8,128)S(1)}, f32[224,128]{1,0:T(8,128)S(1)}, u32[]{:S(2)}, u32[]{:S(2)}) collective-permute-start(f32[224,128]{1,0:T(8,128)S(1)} %pad_maximum_fusion.2), channel_id=1, source_target_pairs={{0,4},{4,0},{1,5},{5,1},{2,6},{6,2},{3,7},{7,3},{8,12},{12,8},{9,1... | collective-permute-start | bytes 344072 | tf_op jit(solution)/shard_map/ppermute | solution.py:340
  63.5 0.3 collective-permute-start.22
  63.9 1.5 %collective-permute-start.23 = (f32[264,256]{1,0:T(8,128)S(1)}, f32[264,256]{1,0:T(8,128)S(1)}, u32[]{:S(2)}, u32[]{:S(2)}) collective-permute-start(f32[264,256]{1,0:T(8,128)S(1)} %get-tuple-element.58.refs_3_), channel_id=1, source_target_pairs={{0,16},{8,24},{16,0},{24,8},{1,17},{9,25},{17,1},{25,9},{2,18},{10... | collective-permute-start | bytes 811016 | tf_op jit(solution)/shard_map/ppermute | solution.py:340
  65.4 7.2 %shard_map.51.transform_ref = f32[256,256]{1,0:T(8,128)S(1)} custom-call(f32[448,128]{1,0:T(8,128)S(1)} %pad_maximum_fusion.packed_ref), custom_call_target="tpu_custom_call" | custom-call | tf_op jit(solution)/shard_map/pallas_call | solution.py:620
  72.7 0.9 %shard_map.52 = (f32[24,32,128]{2,1,0:T(8,128)S(1)}, f32[12,32,128]{2,1,0:T(8,128)S(1)}, f32[12,32,128]{2,1,0:T(8,128)S(1)}, f32[12,32,128]{2,1,0:T(8,128)S(1)},...) custom-call(f32[256,256]{1,0:T(8,128)S(1)} %shard_map.51.transform_ref, ...), custom_call_target="tpu_custom_call" | custom-call | tf_op jit(solution)/shard_map/pallas_call | solution.py:623
  73.6 0.7 collective-permute-start.28
  74.3 0.6 collective-permute-start.24
  74.9 0.5 collective-permute-start.25
  75.4 1.8 %collective-permute-start.26 = (f32[12,32,128]{2,1,0:T(8,128)S(1)}, f32[12,32,128]{2,1,0:T(8,128)S(1)}, u32[]{:S(2)}, u32[]{:S(2)}) collective-permute-start(f32[12,32,128]{2,1,0:T(8,128)S(1)} %get-tuple-element.62), channel_id=1, source_target_pairs={{0,12},{4,8},{8,4},{12,0},{16,28},{20,24},{24,20},{28,16},{1,13},{... | collective-permute-start | bytes 589832 | tf_op jit(solution)/shard_map/ppermute | solution.py:232
  77.2 0.3 collective-permute-start.27
  77.5 3.3 %collective-permute-done.24.refs_1_ = f32[12,32,128]{2,1,0:T(8,128)S(1)} collective-permute-done((f32[12,32,128]{2,1,0:T(8,128)S(1)}, f32[12,32,128]{2,1,0:T(8,128)S(1)}, u32[]{:S(2)}, u32[]{:S(2)}) %collective-permute-start.24) | collective-permute-done | bytes 196640 | tf_op jit(solution)/shard_map/ppermute | solution.py:232
  80.8 0.3 collective-permute-done.25.refs_2_
  81.1 4.2 %collective-permute-done.26.refs_3_ = f32[12,32,128]{2,1,0:T(8,128)S(1)} collective-permute-done((f32[12,32,128]{2,1,0:T(8,128)S(1)}, f32[12,32,128]{2,1,0:T(8,128)S(1)}, u32[]{:S(2)}, u32[]{:S(2)}) %collective-permute-start.26) | collective-permute-done | bytes 196640 | tf_op jit(solution)/shard_map/ppermute | solution.py:232
  85.3 0.5 collective-permute-done.27.refs_4_
  85.8 1.7 %shard_map.53 = f32[3072,128]{1,0:T(8,128)} custom-call(f32[24,32,128]{2,1,0:T(8,128)S(1)} %get-tuple-element.59.refs_0_, f32[12,32,128]{2,1,0:T(8,128)S(1)} %collective-permute-done.24.refs_1_, f32[12,32,128]{2,1,0:T(8,128)S(1)} %collective-permute-done.25.refs_2_, f32[12,32,128]{2,1,0:T(8,128)S(1)} %collective-permute-done.26.refs_3_, ...), custom_call_target="tpu_custom_call" | custom-call | tf_op jit(solution)/shard_map/pallas_call | solution.py:588
  (36 shorter events, 0.7 us)
Async XLA Ops:
  0.0 1.4 %copy-start = (f32[32,3,32,128]{3,2,1,0:T(8,128)S(1)}, f32[32,3,32,128]{3,2,1,0:T(8,128)}, u32[]{:S(2)}) copy-start(f32[32,3,32,128]{3,2,1,0:T(8,128)} %bottom_ref.1) | copy-start | bytes 4718596
  1.8 9.8 %collective-permute-start = (f32[9,32,128]{2,1,0:T(8,128)S(1)}, f32[9,32,128]{2,1,0:T(8,128)S(1)}, u32[]{:S(2)}, u32[]{:S(2)}) collective-permute-start(f32[9,32,128]{2,1,0:T(8,128)S(1)} %get-tuple-element.35), channel_id=1, source_target_pairs={{1,2},{2,1},{5,6},{6,5},{9,10},{10,9},{13,14},{14,13},{17,18},{18,... | collective-permute-start | bytes 442376 | tf_op jit(solution)/shard_map/ppermute | solution.py:196
  2.4 9.1 %collective-permute-start.1 = (f32[9,32,128]{2,1,0:T(8,128)S(1)}, f32[9,32,128]{2,1,0:T(8,128)S(1)}, u32[]{:S(2)}, u32[]{:S(2)}) collective-permute-start(f32[9,32,128]{2,1,0:T(8,128)S(1)} %get-tuple-element.36), channel_id=1, source_target_pairs={{0,1},{2,3},{1,0},{3,2},{4,5},{6,7},{5,4},{7,6},{8,9},{10,11},{9,8... | collective-permute-start | bytes 442376 | tf_op jit(solution)/shard_map/ppermute | solution.py:196
  11.5 15.1 %copy-start.1 = (f32[1,768]{1,0:T(1,128)S(1)}, f32[1,768]{1,0:T(1,128)}, u32[]{:S(2)}) copy-start(f32[1,768]{1,0:T(1,128)} %values_ref.1) | copy-start | bytes 9220
  11.5 15.1 %copy-start.2 = (f32[1,768]{1,0:T(1,128)S(1)}, f32[1,768]{1,0:T(1,128)}, u32[]{:S(2)}) copy-start(f32[1,768]{1,0:T(1,128)} %precision_ref.1) | copy-start | bytes 9220
  11.5 15.1 %copy-start.3 = (s32[1,768]{1,0:T(1,128)S(1)}, s32[1,768]{1,0:T(1,128)}, u32[]{:S(2)}) copy-start(s32[1,768]{1,0:T(1,128)} %index_ref.1) | copy-start | bytes 9220
  13.1 5.9 %collective-permute-start.2 = (f32[12,32,128]{2,1,0:T(8,128)S(1)}, f32[12,32,128]{2,1,0:T(8,128)S(1)}, u32[]{:S(2)}, u32[]{:S(2)}) collective-permute-start(f32[12,32,128]{2,1,0:T(8,128)S(1)} %get-tuple-element.38), channel_id=1, source_target_pairs={{0,8},{4,12},{8,0},{12,4},{16,24},{20,28},{24,16},{28,20},{1,9},{5... | collective-permute-start | bytes 589832 | tf_op jit(solution)/shard_map/ppermute | solution.py:232
  14.4 9.9 %collective-permute-start.3 = (f32[12,32,128]{2,1,0:T(8,128)S(1)}, f32[12,32,128]{2,1,0:T(8,128)S(1)}, u32[]{:S(2)}, u32[]{:S(2)}) collective-permute-start(f32[12,32,128]{2,1,0:T(8,128)S(1)} %get-tuple-element.39), channel_id=1, source_target_pairs={{0,16},{4,20},{8,24},{12,28},{16,0},{20,4},{24,8},{28,12},{1,17},{... | collective-permute-start | bytes 589832 | tf_op jit(solution)/shard_map/ppermute | solution.py:232
  15.6 11.7 %collective-permute-start.4 = (f32[12,32,128]{2,1,0:T(8,128)S(1)}, f32[12,32,128]{2,1,0:T(8,128)S(1)}, u32[]{:S(2)}, u32[]{:S(2)}) collective-permute-start(f32[12,32,128]{2,1,0:T(8,128)S(1)} %get-tuple-element.40), channel_id=1, source_target_pairs={{0,24},{4,28},{8,16},{12,20},{16,8},{20,12},{24,0},{28,4},{1,25},{... | collective-permute-start | bytes 589832 | tf_op jit(solution)/shard_map/ppermute | solution.py:232
  15.8 14.5 %collective-permute-start.5 = (f32[12,32,128]{2,1,0:T(8,128)S(1)}, f32[12,32,128]{2,1,0:T(8,128)S(1)}, u32[]{:S(2)}, u32[]{:S(2)}) collective-permute-start(f32[12,32,128]{2,1,0:T(8,128)S(1)} %get-tuple-element.41), channel_id=1, source_target_pairs={{0,12},{4,8},{8,4},{12,0},{16,28},{20,24},{24,20},{28,16},{1,13},{... | collective-permute-start | bytes 589832 | tf_op jit(solution)/shard_map/ppermute | solution.py:232
  19.0 14.7 %collective-permute-start.6 = (f32[12,32,128]{2,1,0:T(8,128)S(1)}, f32[12,32,128]{2,1,0:T(8,128)S(1)}, u32[]{:S(2)}, u32[]{:S(2)}) collective-permute-start(f32[12,32,128]{2,1,0:T(8,128)S(1)} %get-tuple-element.42), channel_id=1, source_target_pairs={{0,20},{4,16},{8,28},{12,24},{16,4},{20,0},{24,12},{28,8},{1,21},{... | collective-permute-start | bytes 589832 | tf_op jit(solution)/shard_map/ppermute | solution.py:232
  19.0 14.6 %collective-permute-start.7 = (f32[12,32,128]{2,1,0:T(8,128)S(1)}, f32[12,32,128]{2,1,0:T(8,128)S(1)}, u32[]{:S(2)}, u32[]{:S(2)}) collective-permute-start(f32[12,32,128]{2,1,0:T(8,128)S(1)} %get-tuple-element.43), channel_id=1, source_target_pairs={{0,28},{4,24},{8,20},{12,16},{16,12},{20,8},{24,4},{28,0},{1,29},{... | collective-permute-start | bytes 589832 | tf_op jit(solution)/shard_map/ppermute | solution.py:232
  24.3 9.4 %collective-permute-start.8 = (f32[12,32,128]{2,1,0:T(8,128)S(1)}, f32[12,32,128]{2,1,0:T(8,128)S(1)}, u32[]{:S(2)}, u32[]{:S(2)}) collective-permute-start(f32[12,32,128]{2,1,0:T(8,128)S(1)} %get-tuple-element.44), channel_id=1, source_target_pairs={{0,4},{4,0},{8,12},{12,8},{16,20},{20,16},{24,28},{28,24},{1,5},{5... | collective-permute-start | bytes 589832 | tf_op jit(solution)/shard_map/ppermute | solution.py:232
  34.9 1.4 %collective-permute-start.9 = (f32[224,128]{1,0:T(8,128)S(1)}, f32[224,128]{1,0:T(8,128)S(1)}, u32[]{:S(2)}, u32[]{:S(2)}) collective-permute-start(f32[224,128]{1,0:T(8,128)S(1)} %constant_dynamic-slice_fusion), channel_id=1, source_target_pairs={{0,4},{4,0},{1,5},{5,1},{2,6},{6,2},{3,7},{7,3},{8,12},{12,8},{9,1... | collective-permute-start | bytes 344072 | tf_op jit(solution)/shard_map/ppermute | solution.py:340
  36.4 2.8 %collective-permute-start.11 = (f32[56,128]{1,0:T(8,128)S(1)}, f32[56,128]{1,0:T(8,128)S(1)}, u32[]{:S(2)}, u32[]{:S(2)}) collective-permute-start(f32[56,128]{1,0:T(8,128)S(1)} %get-tuple-element.71), channel_id=1, source_target_pairs={{0,16},{8,24},{16,0},{24,8},{1,17},{9,25},{17,1},{25,9},{2,18},{10... | collective-permute-start | bytes 86024 | tf_op jit(solution)/shard_map/ppermute | solution.py:340
  37.7 3.6 %collective-permute-start.12 = (f32[56,128]{1,0:T(8,128)S(1)}, f32[56,128]{1,0:T(8,128)S(1)}, u32[]{:S(2)}, u32[]{:S(2)}) collective-permute-start(f32[56,128]{1,0:T(8,128)S(1)} %get-tuple-element.72), channel_id=1, source_target_pairs={{0,24},{8,16},{16,8},{24,0},{1,25},{9,17},{17,9},{25,1},{2,26},{10... | collective-permute-start | bytes 86024 | tf_op jit(solution)/shard_map/ppermute | solution.py:340
  38.6 3.0 %collective-permute-start.10 = (f32[56,128]{1,0:T(8,128)S(1)}, f32[56,128]{1,0:T(8,128)S(1)}, u32[]{:S(2)}, u32[]{:S(2)}) collective-permute-start(f32[56,128]{1,0:T(8,128)S(1)} %get-tuple-element.73), channel_id=1, source_target_pairs={{0,8},{8,0},{16,24},{24,16},{1,9},{9,1},{17,25},{25,17},{2,10},{10... | collective-permute-start | bytes 86024 | tf_op jit(solution)/shard_map/ppermute | solution.py:340
  41.6 12.2 %collective-permute-start.16 = (f32[264,512]{1,0:T(8,128)S(1)}, f32[264,512]{1,0:T(8,128)S(1)}, u32[]{:S(2)}, u32[]{:S(2)}) collective-permute-start(f32[264,512]{1,0:T(8,128)S(1)} %get-tuple-element.49.refs_0_), channel_id=1, source_target_pairs={{0,8},{8,0},{16,24},{24,16},{1,9},{9,1},{17,25},{25,17},{2,10},{10... | collective-permute-start | bytes 1622024 | tf_op jit(solution)/shard_map/ppermute | solution.py:340
  41.9 11.9 %collective-permute-start.17 = (f32[264,512]{1,0:T(8,128)S(1)}, f32[264,512]{1,0:T(8,128)S(1)}, u32[]{:S(2)}, u32[]{:S(2)}) collective-permute-start(f32[264,512]{1,0:T(8,128)S(1)} %get-tuple-element.50.refs_2_), channel_id=1, source_target_pairs={{0,16},{8,24},{16,0},{24,8},{1,17},{9,25},{17,1},{25,9},{2,18},{10... | collective-permute-start | bytes 1622024 | tf_op jit(solution)/shard_map/ppermute | solution.py:340
  43.4 3.6 %collective-permute-start.15 = (f32[56,128]{1,0:T(8,128)S(1)}, f32[56,128]{1,0:T(8,128)S(1)}, u32[]{:S(2)}, u32[]{:S(2)}) collective-permute-start(f32[56,128]{1,0:T(8,128)S(1)} %bitcast_add_fusion), channel_id=1, source_target_pairs={{0,1},{1,0},{2,3},{3,2},{4,5},{5,4},{6,7},{7,6},{8,9},{9,8},{10,11... | collective-permute-start | bytes 86024 | tf_op jit(solution)/shard_map/ppermute | solution.py:340
  43.4 3.6 %collective-permute-start.14 = (f32[56,128]{1,0:T(8,128)S(1)}, f32[56,128]{1,0:T(8,128)S(1)}, u32[]{:S(2)}, u32[]{:S(2)}) collective-permute-start(f32[56,128]{1,0:T(8,128)S(1)} %bitcast_add_fusion), channel_id=1, source_target_pairs={{0,2},{1,3},{2,0},{3,1},{4,6},{5,7},{6,4},{7,5},{8,10},{9,11},{10,... | collective-permute-start | bytes 86024 | tf_op jit(solution)/shard_map/ppermute | solution.py:340
  44.8 4.5 %collective-permute-start.13 = (f32[56,128]{1,0:T(8,128)S(1)}, f32[56,128]{1,0:T(8,128)S(1)}, u32[]{:S(2)}, u32[]{:S(2)}) collective-permute-start(f32[56,128]{1,0:T(8,128)S(1)} %bitcast_add_fusion), channel_id=1, source_target_pairs={{0,3},{1,2},{2,1},{3,0},{4,7},{5,6},{6,5},{7,4},{8,11},{9,10},{10,... | collective-permute-start | bytes 86024 | tf_op jit(solution)/shard_map/ppermute | solution.py:340
  53.8 3.6 %collective-permute-start.20 = (f32[56,128]{1,0:T(8,128)S(1)}, f32[56,128]{1,0:T(8,128)S(1)}, u32[]{:S(2)}, u32[]{:S(2)}) collective-permute-start(f32[56,128]{1,0:T(8,128)S(1)} %add_add_fusion), channel_id=1, source_target_pairs={{0,24},{8,16},{16,8},{24,0},{1,25},{9,17},{17,9},{25,1},{2,26},{10... | collective-permute-start | bytes 86024 | tf_op jit(solution)/shard_map/ppermute | solution.py:340
  55.3 2.7 %collective-permute-start.19 = (f32[56,128]{1,0:T(8,128)S(1)}, f32[56,128]{1,0:T(8,128)S(1)}, u32[]{:S(2)}, u32[]{:S(2)}) collective-permute-start(f32[56,128]{1,0:T(8,128)S(1)} %add_add_fusion), channel_id=1, source_target_pairs={{0,16},{8,24},{16,0},{24,8},{1,17},{9,25},{17,1},{25,9},{2,18},{10... | collective-permute-start | bytes 86024 | tf_op jit(solution)/shard_map/ppermute | solution.py:340
  56.2 2.7 %collective-permute-start.18 = (f32[56,128]{1,0:T(8,128)S(1)}, f32[56,128]{1,0:T(8,128)S(1)}, u32[]{:S(2)}, u32[]{:S(2)}) collective-permute-start(f32[56,128]{1,0:T(8,128)S(1)} %add_add_fusion), channel_id=1, source_target_pairs={{0,8},{8,0},{16,24},{24,16},{1,9},{9,1},{17,25},{25,17},{2,10},{10... | collective-permute-start | bytes 86024 | tf_op jit(solution)/shard_map/ppermute | solution.py:340
  58.9 6.4 %collective-permute-start.21 = (f32[224,128]{1,0:T(8,128)S(1)}, f32[224,128]{1,0:T(8,128)S(1)}, u32[]{:S(2)}, u32[]{:S(2)}) collective-permute-start(f32[224,128]{1,0:T(8,128)S(1)} %pad_maximum_fusion.2), channel_id=1, source_target_pairs={{0,4},{4,0},{1,5},{5,1},{2,6},{6,2},{3,7},{7,3},{8,12},{12,8},{9,1... | collective-permute-start | bytes 344072 | tf_op jit(solution)/shard_map/ppermute | solution.py:340
  63.5 9.1 %collective-permute-start.22 = (f32[264,256]{1,0:T(8,128)S(1)}, f32[264,256]{1,0:T(8,128)S(1)}, u32[]{:S(2)}, u32[]{:S(2)}) collective-permute-start(f32[264,256]{1,0:T(8,128)S(1)} %get-tuple-element.56.refs_1_), channel_id=1, source_target_pairs={{0,8},{8,0},{16,24},{24,16},{1,9},{9,1},{17,25},{25,17},{2,10},{10... | collective-permute-start | bytes 811016 | tf_op jit(solution)/shard_map/ppermute | solution.py:340
  63.9 8.8 %collective-permute-start.23 = (f32[264,256]{1,0:T(8,128)S(1)}, f32[264,256]{1,0:T(8,128)S(1)}, u32[]{:S(2)}, u32[]{:S(2)}) collective-permute-start(f32[264,256]{1,0:T(8,128)S(1)} %get-tuple-element.58.refs_3_), channel_id=1, source_target_pairs={{0,16},{8,24},{16,0},{24,8},{1,17},{9,25},{17,1},{25,9},{2,18},{10... | collective-permute-start | bytes 811016 | tf_op jit(solution)/shard_map/ppermute | solution.py:340
  73.6 12.2 %collective-permute-start.28 = (f32[24,32,128]{2,1,0:T(8,128)S(1)}, f32[24,32,128]{2,1,0:T(8,128)S(1)}, u32[]{:S(2)}, u32[]{:S(2)}) collective-permute-start(f32[24,32,128]{2,1,0:T(8,128)S(1)} %get-tuple-element.64), channel_id=1, source_target_pairs={{0,4},{4,0},{8,12},{12,8},{16,20},{20,16},{24,28},{28,24},{1,5},{5... | collective-permute-start | bytes 1179656 | tf_op jit(solution)/shard_map/ppermute | solution.py:232
  74.3 6.5 %collective-permute-start.24 = (f32[12,32,128]{2,1,0:T(8,128)S(1)}, f32[12,32,128]{2,1,0:T(8,128)S(1)}, u32[]{:S(2)}, u32[]{:S(2)}) collective-permute-start(f32[12,32,128]{2,1,0:T(8,128)S(1)} %get-tuple-element.60), channel_id=1, source_target_pairs={{0,8},{4,12},{8,0},{12,4},{16,24},{20,28},{24,16},{28,20},{1,9},{5... | collective-permute-start | bytes 589832 | tf_op jit(solution)/shard_map/ppermute | solution.py:232
  74.9 6.1 %collective-permute-start.25 = (f32[12,32,128]{2,1,0:T(8,128)S(1)}, f32[12,32,128]{2,1,0:T(8,128)S(1)}, u32[]{:S(2)}, u32[]{:S(2)}) collective-permute-start(f32[12,32,128]{2,1,0:T(8,128)S(1)} %get-tuple-element.61), channel_id=1, source_target_pairs={{0,16},{4,20},{8,24},{12,28},{16,0},{20,4},{24,8},{28,12},{1,17},{... | collective-permute-start | bytes 589832 | tf_op jit(solution)/shard_map/ppermute | solution.py:232
  75.4 9.8 %collective-permute-start.26 = (f32[12,32,128]{2,1,0:T(8,128)S(1)}, f32[12,32,128]{2,1,0:T(8,128)S(1)}, u32[]{:S(2)}, u32[]{:S(2)}) collective-permute-start(f32[12,32,128]{2,1,0:T(8,128)S(1)} %get-tuple-element.62), channel_id=1, source_target_pairs={{0,12},{4,8},{8,4},{12,0},{16,28},{20,24},{24,20},{28,16},{1,13},{... | collective-permute-start | bytes 589832 | tf_op jit(solution)/shard_map/ppermute | solution.py:232
  77.2 8.5 %collective-permute-start.27 = (f32[12,32,128]{2,1,0:T(8,128)S(1)}, f32[12,32,128]{2,1,0:T(8,128)S(1)}, u32[]{:S(2)}, u32[]{:S(2)}) collective-permute-start(f32[12,32,128]{2,1,0:T(8,128)S(1)} %get-tuple-element.63), channel_id=1, source_target_pairs={{0,20},{4,16},{8,28},{12,24},{16,4},{20,0},{24,12},{28,8},{1,21},{... | collective-permute-start | bytes 589832 | tf_op jit(solution)/shard_map/ppermute | solution.py:232

commit v7 on v6

--- a/solution.py
+++ b/solution.py
@@ -15,6 +15,7 @@
 HALO_ROWS = sum(HALO)
 LANES = 128
 DIRECT = 8
+GROUP = 32
 VMEM_LIMIT = 40 * 1024 * 1024
 
 
@@ -119,15 +120,16 @@
 
 def interior_kernel(dims, state_ref, out_ref):
     members, fields, rows, cols, block_rows, edge = dims
-    for at in range(0, members, 8):
+    group = min(members, GROUP)
+    for at in range(0, members, group):
 
         def load(field, row):
             start = (at * fields + field) * rows + row
-            return state_ref[pl.ds(start, 8, stride=fields * rows), :]
+            return state_ref[pl.ds(start, group, stride=fields * rows), :]
 
         def store(field, row, value):
             block, within = divmod(row, block_rows)
-            out_ref[block, field * block_rows + within, at : at + 8, :] = value
+            out_ref[block, field * block_rows + within, at : at + group, :] = value
 
         sweep(edge, rows - edge, rows, cols, load, store, lambda value, row: value)
 
@@ -140,6 +142,7 @@
 
 def edge_kernel(dims, state_ref, outer_ref, inner_ref, interior_ref, *refs):
     members, fields, rows, cols, block_rows, edge = dims
+    group = min(members, GROUP)
     clusters = rows // block_rows
     slots, edges_ref = refs[:clusters], refs[clusters]
     here = lax.axis_index("space")
@@ -155,24 +158,24 @@
             return value * has_after
         return value
 
-    for at in range(0, members, 8):
+    for at in range(0, members, group):
 
         def load(field, row):
             offset = sum(HALO[:field])
             if row < 0:
                 held = offset + HALO[field] + row
-                outer, inner = outer_ref[held, at : at + 8, :], inner_ref[held, at : at + 8, :]
+                outer, inner = outer_ref[held, at : at + group, :], inner_ref[held, at : at + group, :]
                 return jnp.where(even, outer, inner)
             if row >= rows:
                 held = offset + row - rows
-                outer, inner = outer_ref[held, at : at + 8, :], inner_ref[held, at : at + 8, :]
+                outer, inner = outer_ref[held, at : at + group, :], inner_ref[held, at : at + group, :]
                 return jnp.where(even, inner, outer)
             start = (at * fields + field) * rows + row
-            return state_ref[pl.ds(start, 8, stride=fields * rows), :]
+            return state_ref[pl.ds(start, group, stride=fields * rows), :]
 
         def store(field, row, value):
             block, within = divmod(row, block_rows)
-            edges_ref[block, field * block_rows + within, at : at + 8, :] = value
+            edges_ref[block, field * block_rows + within, at : at + group, :] = value
 
         sweep(0, edge, rows, cols, load, store, inside)
         sweep(rows - edge, rows, rows, cols, load, store, inside)

time: 87.6 us -> 85.8 us (0.979)
  Pallas kernels: 18.1 us -> 14.7 us
  waiting for transfers between devices: 27.5 us -> 28.7 us
    pallas_call x1, Pallas kernels: 4.31 us -> 1.6 us  [forecast(): call(functools.partial(interior_kernel, dims), f32(clusters, terms, membe...]
    ppermute x2, waiting for transfers between devices: 0.01 us -> 1.61 us  [trade(): return lax.ppermute(value, 'space', pairs + [(j, i) for i, j in pairs])]
  transfers between devices with their start and end apart: 29 -> 29, of which waited for: 16 -> 17; matrix products, arithmetic and copies ran while one was open for 0% -> 0% of each run, Pallas kernels for 14% -> 11%
where the time goes in v7:
time: 85.8 us; the launch traced here: 85.7 us
  starting transfers between devices  40.4 us (47%)
  waiting for transfers between devices  28.7 us (33%)
  Pallas kernels  14.7 us (17%)
  local copies, waits for them, and re-layouts  1.49 us (2%)
    ppermute x12, starting transfers between devices, exchange(): lax.ppermute(value, ('group', 'member'), [(i, i ^ slot) for i in range(cl...  17.7 us
    ppermute x15, starting transfers between devices, flip(): lax.ppermute(value, axis, [(i, i ^ bits) for i in range(lax.axis_size(axi...  17.4 us
    ppermute x12, waiting for transfers between devices, exchange(): lax.ppermute(value, ('group', 'member'), [(i, i ^ slot) for i in range(cl...  14.4 us
    ppermute x15, waiting for transfers between devices, flip(): lax.ppermute(value, axis, [(i, i ^ bits) for i in range(lax.axis_size(axi...  12.7 us
    pallas_call x1, Pallas kernels, on_device(): call(functools.partial(transform_kernel, total), f32(total, total), 1)  7.25 us
    ppermute x2, starting transfers between devices, trade(): return lax.ppermute(value, 'space', pairs + [(j, i) for i, j in pairs])  5.4 us
  transfers between devices with their start and end apart: 29, of which 17 were waited for; matrix products, arithmetic and copies ran while one was open for 0% of the time, Pallas kernels for 11%

profile of v7, /device:TPU:1, one launch (start us, length us, event | category | flops | bytes accessed | tf_op | source)
XLA Modules:
  0.0 85.7 jit_solution(3883413434374802685)
XLA Ops:
  0.0 1.4 %copy-done = f32[32,3,32,128]{3,2,1,0:T(8,128)S(1)} copy-done((f32[32,3,32,128]{3,2,1,0:T(8,128)S(1)}, f32[32,3,32,128]{3,2,1,0:T(8,128)}, u32[]{:S(2)}) %copy-start) | copy-done | bytes 1572888
  1.4 0.3 shard_map.47
  1.8 0.7 collective-permute-start
  2.4 4.7 %collective-permute-start.1 = (f32[9,32,128]{2,1,0:T(8,128)S(1)}, f32[9,32,128]{2,1,0:T(8,128)S(1)}, u32[]{:S(2)}, u32[]{:S(2)}) collective-permute-start(f32[9,32,128]{2,1,0:T(8,128)S(1)} %get-tuple-element.36), channel_id=1, source_target_pairs={{0,1},{2,3},{1,0},{3,2},{4,5},{6,7},{5,4},{7,6},{8,9},{10,11},{9,8... | collective-permute-start | bytes 442376 | tf_op jit(solution)/shard_map/ppermute | solution.py:199
  7.2 1.6 %shard_map.48.interior_ref = f32[8,12,32,128]{3,2,1,0:T(8,128)S(1)} custom-call(f32[3072,128]{1,0:T(8,128)S(1)} %bitcast.23), custom_call_target="tpu_custom_call" | custom-call | flops 78643200 | bytes 6291456 | tf_op jit(solution)/shard_map/pallas_call | solution.py:205
  8.8 1.6 %collective-permute-done.1.inner_ref = f32[9,32,128]{2,1,0:T(8,128)S(1)} collective-permute-done((f32[9,32,128]{2,1,0:T(8,128)S(1)}, f32[9,32,128]{2,1,0:T(8,128)S(1)}, u32[]{:S(2)}, u32[]{:S(2)}) %collective-permute-start.1) | collective-permute-done | bytes 147488 | tf_op jit(solution)/shard_map/ppermute | solution.py:199
  10.4 0.9 %shard_map.49 = (f32[12,32,128]{2,1,0:T(8,128)S(1)}, f32[12,32,128]{2,1,0:T(8,128)S(1)}, f32[12,32,128]{2,1,0:T(8,128)S(1)}, f32[12,32,128]{2,1,0:T(8,128)S(1)},...) custom-call(f32[3072,128]{1,0:T(8,128)S(1)} %bitcast.24, ...), custom_call_target="tpu_custom_call" | custom-call | tf_op jit(solution)/shard_map/pallas_call | solution.py:213
  11.3 1.3 %collective-permute-start.2 = (f32[12,32,128]{2,1,0:T(8,128)S(1)}, f32[12,32,128]{2,1,0:T(8,128)S(1)}, u32[]{:S(2)}, u32[]{:S(2)}) collective-permute-start(f32[12,32,128]{2,1,0:T(8,128)S(1)} %get-tuple-element.38), channel_id=1, source_target_pairs={{0,8},{4,12},{8,0},{12,4},{16,24},{20,28},{24,16},{28,20},{1,9},{5... | collective-permute-start | bytes 589832 | tf_op jit(solution)/shard_map/ppermute | solution.py:235
  12.6 1.2 %collective-permute-start.3 = (f32[12,32,128]{2,1,0:T(8,128)S(1)}, f32[12,32,128]{2,1,0:T(8,128)S(1)}, u32[]{:S(2)}, u32[]{:S(2)}) collective-permute-start(f32[12,32,128]{2,1,0:T(8,128)S(1)} %get-tuple-element.39), channel_id=1, source_target_pairs={{0,16},{4,20},{8,24},{12,28},{16,0},{20,4},{24,8},{28,12},{1,17},{... | collective-permute-start | bytes 589832 | tf_op jit(solution)/shard_map/ppermute | solution.py:235
  14.0 3.5 %collective-permute-start.5 = (f32[12,32,128]{2,1,0:T(8,128)S(1)}, f32[12,32,128]{2,1,0:T(8,128)S(1)}, u32[]{:S(2)}, u32[]{:S(2)}) collective-permute-start(f32[12,32,128]{2,1,0:T(8,128)S(1)} %get-tuple-element.41), channel_id=1, source_target_pairs={{0,12},{4,8},{8,4},{12,0},{16,28},{20,24},{24,20},{28,16},{1,13},{... | collective-permute-start | bytes 589832 | tf_op jit(solution)/shard_map/ppermute | solution.py:235
  17.6 5.3 %collective-permute-start.7 = (f32[12,32,128]{2,1,0:T(8,128)S(1)}, f32[12,32,128]{2,1,0:T(8,128)S(1)}, u32[]{:S(2)}, u32[]{:S(2)}) collective-permute-start(f32[12,32,128]{2,1,0:T(8,128)S(1)} %get-tuple-element.43), channel_id=1, source_target_pairs={{0,28},{4,24},{8,20},{12,16},{16,12},{20,8},{24,4},{28,0},{1,29},{... | collective-permute-start | bytes 589832 | tf_op jit(solution)/shard_map/ppermute | solution.py:235
  22.8 2.2 %collective-permute-start.8 = (f32[12,32,128]{2,1,0:T(8,128)S(1)}, f32[12,32,128]{2,1,0:T(8,128)S(1)}, u32[]{:S(2)}, u32[]{:S(2)}) collective-permute-start(f32[12,32,128]{2,1,0:T(8,128)S(1)} %get-tuple-element.44), channel_id=1, source_target_pairs={{0,4},{4,0},{8,12},{12,8},{16,20},{20,16},{24,28},{28,24},{1,5},{5... | collective-permute-start | bytes 589832 | tf_op jit(solution)/shard_map/ppermute | solution.py:235
  25.1 0.7 shard_map.46.observed_ref
  25.8 2.7 %collective-permute-done.5.refs_4_ = f32[12,32,128]{2,1,0:T(8,128)S(1)} collective-permute-done((f32[12,32,128]{2,1,0:T(8,128)S(1)}, f32[12,32,128]{2,1,0:T(8,128)S(1)}, u32[]{:S(2)}, u32[]{:S(2)}) %collective-permute-start.5) | collective-permute-done | bytes 196640 | tf_op jit(solution)/shard_map/ppermute | solution.py:235
  28.6 3.4 %collective-permute-done.6.refs_5_ = f32[12,32,128]{2,1,0:T(8,128)S(1)} collective-permute-done((f32[12,32,128]{2,1,0:T(8,128)S(1)}, f32[12,32,128]{2,1,0:T(8,128)S(1)}, u32[]{:S(2)}, u32[]{:S(2)}) %collective-permute-start.6) | collective-permute-done | bytes 196640 | tf_op jit(solution)/shard_map/ppermute | solution.py:235
  32.0 1.3 %shard_map.50 = (f32[448,128]{1,0:T(8,128)S(1)}, f32[264,512]{1,0:T(8,128)S(1)}, f32[264,256]{1,0:T(8,128)S(1)}, f32[264,512]{1,0:T(8,128)S(1)}, f32[264,256]{1,0:T(8,128)S(1)}) custom-call(f32[8,1536]{1,0:T(8,128)S(1)} %shard_map.46.observed_ref, f32[12,32,128]{2,1,0:T(8,128)S(1)} %get-tuple-element.37.refs_0_, ...), custom_call_target="tpu_custom_call" | custom-call | tf_op jit(solution)/shard_map/pallas_call | solution.py:616
  33.4 1.3 %collective-permute-done.9 = f32[224,128]{1,0:T(8,128)S(1)} collective-permute-done((f32[224,128]{1,0:T(8,128)S(1)}, f32[224,128]{1,0:T(8,128)S(1)}, u32[]{:S(2)}, u32[]{:S(2)}) %collective-permute-start.9) | collective-permute-done | bytes 114720 | tf_op jit(solution)/shard_map/ppermute | solution.py:343
  34.7 1.2 %collective-permute-start.11 = (f32[56,128]{1,0:T(8,128)S(1)}, f32[56,128]{1,0:T(8,128)S(1)}, u32[]{:S(2)}, u32[]{:S(2)}) collective-permute-start(f32[56,128]{1,0:T(8,128)S(1)} %get-tuple-element.71), channel_id=1, source_target_pairs={{0,16},{8,24},{16,0},{24,8},{1,17},{9,25},{17,1},{25,9},{2,18},{10... | collective-permute-start | bytes 86024 | tf_op jit(solution)/shard_map/ppermute | solution.py:343
  35.9 0.9 %collective-permute-start.12 = (f32[56,128]{1,0:T(8,128)S(1)}, f32[56,128]{1,0:T(8,128)S(1)}, u32[]{:S(2)}, u32[]{:S(2)}) collective-permute-start(f32[56,128]{1,0:T(8,128)S(1)} %get-tuple-element.72), channel_id=1, source_target_pairs={{0,24},{8,16},{16,8},{24,0},{1,25},{9,17},{17,9},{25,1},{2,26},{10... | collective-permute-start | bytes 86024 | tf_op jit(solution)/shard_map/ppermute | solution.py:343
  36.8 0.6 collective-permute-start.10
  37.5 2.0 %collective-permute-done.12 = f32[56,128]{1,0:T(8,128)S(1)} collective-permute-done((f32[56,128]{1,0:T(8,128)S(1)}, f32[56,128]{1,0:T(8,128)S(1)}, u32[]{:S(2)}, u32[]{:S(2)}) %collective-permute-start.12) | collective-permute-done | bytes 28704 | tf_op jit(solution)/shard_map/ppermute | solution.py:343
  39.8 0.5 collective-permute-start.16
  40.2 1.4 %collective-permute-start.17 = (f32[264,512]{1,0:T(8,128)S(1)}, f32[264,512]{1,0:T(8,128)S(1)}, u32[]{:S(2)}, u32[]{:S(2)}) collective-permute-start(f32[264,512]{1,0:T(8,128)S(1)} %get-tuple-element.50.refs_2_), channel_id=1, source_target_pairs={{0,16},{8,24},{16,0},{24,8},{1,17},{9,25},{17,1},{25,9},{2,18},{10... | collective-permute-start | bytes 1622024 | tf_op jit(solution)/shard_map/ppermute | solution.py:343
  41.7 0.8 collective-permute-start.15
  42.5 0.5 collective-permute-start.14
  43.0 2.2 %collective-permute-start.13 = (f32[56,128]{1,0:T(8,128)S(1)}, f32[56,128]{1,0:T(8,128)S(1)}, u32[]{:S(2)}, u32[]{:S(2)}) collective-permute-start(f32[56,128]{1,0:T(8,128)S(1)} %bitcast_add_fusion), channel_id=1, source_target_pairs={{0,3},{1,2},{2,1},{3,0},{4,7},{5,6},{6,5},{7,4},{8,11},{9,10},{10,... | collective-permute-start | bytes 86024 | tf_op jit(solution)/shard_map/ppermute | solution.py:343
  45.2 0.9 %collective-permute-done.14 = f32[56,128]{1,0:T(8,128)S(1)} collective-permute-done((f32[56,128]{1,0:T(8,128)S(1)}, f32[56,128]{1,0:T(8,128)S(1)}, u32[]{:S(2)}, u32[]{:S(2)}) %collective-permute-start.14) | collective-permute-done | bytes 28704 | tf_op jit(solution)/shard_map/ppermute | solution.py:343
  46.1 1.4 %collective-permute-done.13 = f32[56,128]{1,0:T(8,128)S(1)} collective-permute-done((f32[56,128]{1,0:T(8,128)S(1)}, f32[56,128]{1,0:T(8,128)S(1)}, u32[]{:S(2)}, u32[]{:S(2)}) %collective-permute-start.13) | collective-permute-done | bytes 28704 | tf_op jit(solution)/shard_map/ppermute | solution.py:343
  47.6 4.4 %collective-permute-done.16.refs_4_ = f32[264,512]{1,0:T(8,128)S(1)} collective-permute-done((f32[264,512]{1,0:T(8,128)S(1)}, f32[264,512]{1,0:T(8,128)S(1)}, u32[]{:S(2)}, u32[]{:S(2)}) %collective-permute-start.16) | collective-permute-done | bytes 540704 | tf_op jit(solution)/shard_map/ppermute | solution.py:343
  52.0 1.6 %collective-permute-start.20 = (f32[56,128]{1,0:T(8,128)S(1)}, f32[56,128]{1,0:T(8,128)S(1)}, u32[]{:S(2)}, u32[]{:S(2)}) collective-permute-start(f32[56,128]{1,0:T(8,128)S(1)} %add_add_fusion), channel_id=1, source_target_pairs={{0,24},{8,16},{16,8},{24,0},{1,25},{9,17},{17,9},{25,1},{2,26},{10... | collective-permute-start | bytes 86024 | tf_op jit(solution)/shard_map/ppermute | solution.py:343
  53.6 0.8 collective-permute-start.19
  54.4 0.4 collective-permute-start.18
  54.7 0.9 %collective-permute-done.20 = f32[56,128]{1,0:T(8,128)S(1)} collective-permute-done((f32[56,128]{1,0:T(8,128)S(1)}, f32[56,128]{1,0:T(8,128)S(1)}, u32[]{:S(2)}, u32[]{:S(2)}) %collective-permute-start.20) | collective-permute-done | bytes 28704 | tf_op jit(solution)/shard_map/ppermute | solution.py:343
  55.6 0.7 collective-permute-done.19
  56.3 0.8 collective-permute-done.18
  57.1 4.6 %collective-permute-start.21 = (f32[224,128]{1,0:T(8,128)S(1)}, f32[224,128]{1,0:T(8,128)S(1)}, u32[]{:S(2)}, u32[]{:S(2)}) collective-permute-start(f32[224,128]{1,0:T(8,128)S(1)} %pad_maximum_fusion.2), channel_id=1, source_target_pairs={{0,4},{4,0},{1,5},{5,1},{2,6},{6,2},{3,7},{7,3},{8,12},{12,8},{9,1... | collective-permute-start | bytes 344072 | tf_op jit(solution)/shard_map/ppermute | solution.py:343
  61.7 0.4 collective-permute-start.22
  62.2 1.4 %collective-permute-start.23 = (f32[264,256]{1,0:T(8,128)S(1)}, f32[264,256]{1,0:T(8,128)S(1)}, u32[]{:S(2)}, u32[]{:S(2)}) collective-permute-start(f32[264,256]{1,0:T(8,128)S(1)} %get-tuple-element.58.refs_3_), channel_id=1, source_target_pairs={{0,16},{8,24},{16,0},{24,8},{1,17},{9,25},{17,1},{25,9},{2,18},{10... | collective-permute-start | bytes 811016 | tf_op jit(solution)/shard_map/ppermute | solution.py:343
  63.6 7.3 %shard_map.51.transform_ref = f32[256,256]{1,0:T(8,128)S(1)} custom-call(f32[448,128]{1,0:T(8,128)S(1)} %pad_maximum_fusion.packed_ref), custom_call_target="tpu_custom_call" | custom-call | tf_op jit(solution)/shard_map/pallas_call | solution.py:623
  70.9 0.9 %shard_map.52 = (f32[24,32,128]{2,1,0:T(8,128)S(1)}, f32[12,32,128]{2,1,0:T(8,128)S(1)}, f32[12,32,128]{2,1,0:T(8,128)S(1)}, f32[12,32,128]{2,1,0:T(8,128)S(1)},...) custom-call(f32[256,256]{1,0:T(8,128)S(1)} %shard_map.51.transform_ref, ...), custom_call_target="tpu_custom_call" | custom-call | tf_op jit(solution)/shard_map/pallas_call | solution.py:626
  71.8 0.7 collective-permute-start.28
  72.5 0.6 collective-permute-start.24
  73.1 0.5 collective-permute-start.25
  73.7 1.8 %collective-permute-start.26 = (f32[12,32,128]{2,1,0:T(8,128)S(1)}, f32[12,32,128]{2,1,0:T(8,128)S(1)}, u32[]{:S(2)}, u32[]{:S(2)}) collective-permute-start(f32[12,32,128]{2,1,0:T(8,128)S(1)} %get-tuple-element.62), channel_id=1, source_target_pairs={{0,12},{4,8},{8,4},{12,0},{16,28},{20,24},{24,20},{28,16},{1,13},{... | collective-permute-start | bytes 589832 | tf_op jit(solution)/shard_map/ppermute | solution.py:235
  75.7 3.3 %collective-permute-done.24.refs_1_ = f32[12,32,128]{2,1,0:T(8,128)S(1)} collective-permute-done((f32[12,32,128]{2,1,0:T(8,128)S(1)}, f32[12,32,128]{2,1,0:T(8,128)S(1)}, u32[]{:S(2)}, u32[]{:S(2)}) %collective-permute-start.24) | collective-permute-done | bytes 196640 | tf_op jit(solution)/shard_map/ppermute | solution.py:235
  79.3 4.2 %collective-permute-done.26.refs_3_ = f32[12,32,128]{2,1,0:T(8,128)S(1)} collective-permute-done((f32[12,32,128]{2,1,0:T(8,128)S(1)}, f32[12,32,128]{2,1,0:T(8,128)S(1)}, u32[]{:S(2)}, u32[]{:S(2)}) %collective-permute-start.26) | collective-permute-done | bytes 196640 | tf_op jit(solution)/shard_map/ppermute | solution.py:235
  83.5 0.5 collective-permute-done.27.refs_4_
  84.0 1.7 %shard_map.53 = f32[3072,128]{1,0:T(8,128)} custom-call(f32[24,32,128]{2,1,0:T(8,128)S(1)} %get-tuple-element.59.refs_0_, f32[12,32,128]{2,1,0:T(8,128)S(1)} %collective-permute-done.24.refs_1_, f32[12,32,128]{2,1,0:T(8,128)S(1)} %collective-permute-done.25.refs_2_, f32[12,32,128]{2,1,0:T(8,128)S(1)} %collective-permute-done.26.refs_3_, ...), custom_call_target="tpu_custom_call" | custom-call | tf_op jit(solution)/shard_map/pallas_call | solution.py:591
  (36 shorter events, 1.4 us)
Async XLA Ops:
  0.0 1.4 %copy-start = (f32[32,3,32,128]{3,2,1,0:T(8,128)S(1)}, f32[32,3,32,128]{3,2,1,0:T(8,128)}, u32[]{:S(2)}) copy-start(f32[32,3,32,128]{3,2,1,0:T(8,128)} %bottom_ref.1) | copy-start | bytes 4718596
  1.8 7.0 %collective-permute-start = (f32[9,32,128]{2,1,0:T(8,128)S(1)}, f32[9,32,128]{2,1,0:T(8,128)S(1)}, u32[]{:S(2)}, u32[]{:S(2)}) collective-permute-start(f32[9,32,128]{2,1,0:T(8,128)S(1)} %get-tuple-element.35), channel_id=1, source_target_pairs={{1,2},{2,1},{5,6},{6,5},{9,10},{10,9},{13,14},{14,13},{17,18},{18,... | collective-permute-start | bytes 442376 | tf_op jit(solution)/shard_map/ppermute | solution.py:199
  2.4 8.0 %collective-permute-start.1 = (f32[9,32,128]{2,1,0:T(8,128)S(1)}, f32[9,32,128]{2,1,0:T(8,128)S(1)}, u32[]{:S(2)}, u32[]{:S(2)}) collective-permute-start(f32[9,32,128]{2,1,0:T(8,128)S(1)} %get-tuple-element.36), channel_id=1, source_target_pairs={{0,1},{2,3},{1,0},{3,2},{4,5},{6,7},{5,4},{7,6},{8,9},{10,11},{9,8... | collective-permute-start | bytes 442376 | tf_op jit(solution)/shard_map/ppermute | solution.py:199
  8.8 16.3 %copy-start.1 = (f32[1,768]{1,0:T(1,128)S(1)}, f32[1,768]{1,0:T(1,128)}, u32[]{:S(2)}) copy-start(f32[1,768]{1,0:T(1,128)} %values_ref.1) | copy-start | bytes 9220
  8.8 16.3 %copy-start.2 = (f32[1,768]{1,0:T(1,128)S(1)}, f32[1,768]{1,0:T(1,128)}, u32[]{:S(2)}) copy-start(f32[1,768]{1,0:T(1,128)} %precision_ref.1) | copy-start | bytes 9220
  8.8 16.3 %copy-start.3 = (s32[1,768]{1,0:T(1,128)S(1)}, s32[1,768]{1,0:T(1,128)}, u32[]{:S(2)}) copy-start(s32[1,768]{1,0:T(1,128)} %index_ref.1) | copy-start | bytes 9220
  11.3 6.2 %collective-permute-start.2 = (f32[12,32,128]{2,1,0:T(8,128)S(1)}, f32[12,32,128]{2,1,0:T(8,128)S(1)}, u32[]{:S(2)}, u32[]{:S(2)}) collective-permute-start(f32[12,32,128]{2,1,0:T(8,128)S(1)} %get-tuple-element.38), channel_id=1, source_target_pairs={{0,8},{4,12},{8,0},{12,4},{16,24},{20,28},{24,16},{28,20},{1,9},{5... | collective-permute-start | bytes 589832 | tf_op jit(solution)/shard_map/ppermute | solution.py:235
  12.6 10.2 %collective-permute-start.3 = (f32[12,32,128]{2,1,0:T(8,128)S(1)}, f32[12,32,128]{2,1,0:T(8,128)S(1)}, u32[]{:S(2)}, u32[]{:S(2)}) collective-permute-start(f32[12,32,128]{2,1,0:T(8,128)S(1)} %get-tuple-element.39), channel_id=1, source_target_pairs={{0,16},{4,20},{8,24},{12,28},{16,0},{20,4},{24,8},{28,12},{1,17},{... | collective-permute-start | bytes 589832 | tf_op jit(solution)/shard_map/ppermute | solution.py:235
  13.9 12.0 %collective-permute-start.4 = (f32[12,32,128]{2,1,0:T(8,128)S(1)}, f32[12,32,128]{2,1,0:T(8,128)S(1)}, u32[]{:S(2)}, u32[]{:S(2)}) collective-permute-start(f32[12,32,128]{2,1,0:T(8,128)S(1)} %get-tuple-element.40), channel_id=1, source_target_pairs={{0,24},{4,28},{8,16},{12,20},{16,8},{20,12},{24,0},{28,4},{1,25},{... | collective-permute-start | bytes 589832 | tf_op jit(solution)/shard_map/ppermute | solution.py:235
  14.0 14.5 %collective-permute-start.5 = (f32[12,32,128]{2,1,0:T(8,128)S(1)}, f32[12,32,128]{2,1,0:T(8,128)S(1)}, u32[]{:S(2)}, u32[]{:S(2)}) collective-permute-start(f32[12,32,128]{2,1,0:T(8,128)S(1)} %get-tuple-element.41), channel_id=1, source_target_pairs={{0,12},{4,8},{8,4},{12,0},{16,28},{20,24},{24,20},{28,16},{1,13},{... | collective-permute-start | bytes 589832 | tf_op jit(solution)/shard_map/ppermute | solution.py:235
  17.5 14.5 %collective-permute-start.6 = (f32[12,32,128]{2,1,0:T(8,128)S(1)}, f32[12,32,128]{2,1,0:T(8,128)S(1)}, u32[]{:S(2)}, u32[]{:S(2)}) collective-permute-start(f32[12,32,128]{2,1,0:T(8,128)S(1)} %get-tuple-element.42), channel_id=1, source_target_pairs={{0,20},{4,16},{8,28},{12,24},{16,4},{20,0},{24,12},{28,8},{1,21},{... | collective-permute-start | bytes 589832 | tf_op jit(solution)/shard_map/ppermute | solution.py:235
  17.6 14.4 %collective-permute-start.7 = (f32[12,32,128]{2,1,0:T(8,128)S(1)}, f32[12,32,128]{2,1,0:T(8,128)S(1)}, u32[]{:S(2)}, u32[]{:S(2)}) collective-permute-start(f32[12,32,128]{2,1,0:T(8,128)S(1)} %get-tuple-element.43), channel_id=1, source_target_pairs={{0,28},{4,24},{8,20},{12,16},{16,12},{20,8},{24,4},{28,0},{1,29},{... | collective-permute-start | bytes 589832 | tf_op jit(solution)/shard_map/ppermute | solution.py:235
  22.8 9.1 %collective-permute-start.8 = (f32[12,32,128]{2,1,0:T(8,128)S(1)}, f32[12,32,128]{2,1,0:T(8,128)S(1)}, u32[]{:S(2)}, u32[]{:S(2)}) collective-permute-start(f32[12,32,128]{2,1,0:T(8,128)S(1)} %get-tuple-element.44), channel_id=1, source_target_pairs={{0,4},{4,0},{8,12},{12,8},{16,20},{20,16},{24,28},{28,24},{1,5},{5... | collective-permute-start | bytes 589832 | tf_op jit(solution)/shard_map/ppermute | solution.py:235
  33.3 1.4 %collective-permute-start.9 = (f32[224,128]{1,0:T(8,128)S(1)}, f32[224,128]{1,0:T(8,128)S(1)}, u32[]{:S(2)}, u32[]{:S(2)}) collective-permute-start(f32[224,128]{1,0:T(8,128)S(1)} %constant_dynamic-slice_fusion), channel_id=1, source_target_pairs={{0,4},{4,0},{1,5},{5,1},{2,6},{6,2},{3,7},{7,3},{8,12},{12,8},{9,1... | collective-permute-start | bytes 344072 | tf_op jit(solution)/shard_map/ppermute | solution.py:343
  34.7 2.8 %collective-permute-start.11 = (f32[56,128]{1,0:T(8,128)S(1)}, f32[56,128]{1,0:T(8,128)S(1)}, u32[]{:S(2)}, u32[]{:S(2)}) collective-permute-start(f32[56,128]{1,0:T(8,128)S(1)} %get-tuple-element.71), channel_id=1, source_target_pairs={{0,16},{8,24},{16,0},{24,8},{1,17},{9,25},{17,1},{25,9},{2,18},{10... | collective-permute-start | bytes 86024 | tf_op jit(solution)/shard_map/ppermute | solution.py:343
  35.9 3.6 %collective-permute-start.12 = (f32[56,128]{1,0:T(8,128)S(1)}, f32[56,128]{1,0:T(8,128)S(1)}, u32[]{:S(2)}, u32[]{:S(2)}) collective-permute-start(f32[56,128]{1,0:T(8,128)S(1)} %get-tuple-element.72), channel_id=1, source_target_pairs={{0,24},{8,16},{16,8},{24,0},{1,25},{9,17},{17,9},{25,1},{2,26},{10... | collective-permute-start | bytes 86024 | tf_op jit(solution)/shard_map/ppermute | solution.py:343
  36.8 3.0 %collective-permute-start.10 = (f32[56,128]{1,0:T(8,128)S(1)}, f32[56,128]{1,0:T(8,128)S(1)}, u32[]{:S(2)}, u32[]{:S(2)}) collective-permute-start(f32[56,128]{1,0:T(8,128)S(1)} %get-tuple-element.73), channel_id=1, source_target_pairs={{0,8},{8,0},{16,24},{24,16},{1,9},{9,1},{17,25},{25,17},{2,10},{10... | collective-permute-start | bytes 86024 | tf_op jit(solution)/shard_map/ppermute | solution.py:343
  39.8 12.2 %collective-permute-start.16 = (f32[264,512]{1,0:T(8,128)S(1)}, f32[264,512]{1,0:T(8,128)S(1)}, u32[]{:S(2)}, u32[]{:S(2)}) collective-permute-start(f32[264,512]{1,0:T(8,128)S(1)} %get-tuple-element.49.refs_0_), channel_id=1, source_target_pairs={{0,8},{8,0},{16,24},{24,16},{1,9},{9,1},{17,25},{25,17},{2,10},{10... | collective-permute-start | bytes 1622024 | tf_op jit(solution)/shard_map/ppermute | solution.py:343
  40.2 11.7 %collective-permute-start.17 = (f32[264,512]{1,0:T(8,128)S(1)}, f32[264,512]{1,0:T(8,128)S(1)}, u32[]{:S(2)}, u32[]{:S(2)}) collective-permute-start(f32[264,512]{1,0:T(8,128)S(1)} %get-tuple-element.50.refs_2_), channel_id=1, source_target_pairs={{0,16},{8,24},{16,0},{24,8},{1,17},{9,25},{17,1},{25,9},{2,18},{10... | collective-permute-start | bytes 1622024 | tf_op jit(solution)/shard_map/ppermute | solution.py:343
  41.7 3.6 %collective-permute-start.15 = (f32[56,128]{1,0:T(8,128)S(1)}, f32[56,128]{1,0:T(8,128)S(1)}, u32[]{:S(2)}, u32[]{:S(2)}) collective-permute-start(f32[56,128]{1,0:T(8,128)S(1)} %bitcast_add_fusion), channel_id=1, source_target_pairs={{0,1},{1,0},{2,3},{3,2},{4,5},{5,4},{6,7},{7,6},{8,9},{9,8},{10,11... | collective-permute-start | bytes 86024 | tf_op jit(solution)/shard_map/ppermute | solution.py:343
  42.5 3.6 %collective-permute-start.14 = (f32[56,128]{1,0:T(8,128)S(1)}, f32[56,128]{1,0:T(8,128)S(1)}, u32[]{:S(2)}, u32[]{:S(2)}) collective-permute-start(f32[56,128]{1,0:T(8,128)S(1)} %bitcast_add_fusion), channel_id=1, source_target_pairs={{0,2},{1,3},{2,0},{3,1},{4,6},{5,7},{6,4},{7,5},{8,10},{9,11},{10,... | collective-permute-start | bytes 86024 | tf_op jit(solution)/shard_map/ppermute | solution.py:343
  43.0 4.6 %collective-permute-start.13 = (f32[56,128]{1,0:T(8,128)S(1)}, f32[56,128]{1,0:T(8,128)S(1)}, u32[]{:S(2)}, u32[]{:S(2)}) collective-permute-start(f32[56,128]{1,0:T(8,128)S(1)} %bitcast_add_fusion), channel_id=1, source_target_pairs={{0,3},{1,2},{2,1},{3,0},{4,7},{5,6},{6,5},{7,4},{8,11},{9,10},{10,... | collective-permute-start | bytes 86024 | tf_op jit(solution)/shard_map/ppermute | solution.py:343
  52.0 3.6 %collective-permute-start.20 = (f32[56,128]{1,0:T(8,128)S(1)}, f32[56,128]{1,0:T(8,128)S(1)}, u32[]{:S(2)}, u32[]{:S(2)}) collective-permute-start(f32[56,128]{1,0:T(8,128)S(1)} %add_add_fusion), channel_id=1, source_target_pairs={{0,24},{8,16},{16,8},{24,0},{1,25},{9,17},{17,9},{25,1},{2,26},{10... | collective-permute-start | bytes 86024 | tf_op jit(solution)/shard_map/ppermute | solution.py:343
  53.6 2.7 %collective-permute-start.19 = (f32[56,128]{1,0:T(8,128)S(1)}, f32[56,128]{1,0:T(8,128)S(1)}, u32[]{:S(2)}, u32[]{:S(2)}) collective-permute-start(f32[56,128]{1,0:T(8,128)S(1)} %add_add_fusion), channel_id=1, source_target_pairs={{0,16},{8,24},{16,0},{24,8},{1,17},{9,25},{17,1},{25,9},{2,18},{10... | collective-permute-start | bytes 86024 | tf_op jit(solution)/shard_map/ppermute | solution.py:343
  54.4 2.7 %collective-permute-start.18 = (f32[56,128]{1,0:T(8,128)S(1)}, f32[56,128]{1,0:T(8,128)S(1)}, u32[]{:S(2)}, u32[]{:S(2)}) collective-permute-start(f32[56,128]{1,0:T(8,128)S(1)} %add_add_fusion), channel_id=1, source_target_pairs={{0,8},{8,0},{16,24},{24,16},{1,9},{9,1},{17,25},{25,17},{2,10},{10... | collective-permute-start | bytes 86024 | tf_op jit(solution)/shard_map/ppermute | solution.py:343
  57.1 6.4 %collective-permute-start.21 = (f32[224,128]{1,0:T(8,128)S(1)}, f32[224,128]{1,0:T(8,128)S(1)}, u32[]{:S(2)}, u32[]{:S(2)}) collective-permute-start(f32[224,128]{1,0:T(8,128)S(1)} %pad_maximum_fusion.2), channel_id=1, source_target_pairs={{0,4},{4,0},{1,5},{5,1},{2,6},{6,2},{3,7},{7,3},{8,12},{12,8},{9,1... | collective-permute-start | bytes 344072 | tf_op jit(solution)/shard_map/ppermute | solution.py:343
  61.7 9.1 %collective-permute-start.22 = (f32[264,256]{1,0:T(8,128)S(1)}, f32[264,256]{1,0:T(8,128)S(1)}, u32[]{:S(2)}, u32[]{:S(2)}) collective-permute-start(f32[264,256]{1,0:T(8,128)S(1)} %get-tuple-element.56.refs_1_), channel_id=1, source_target_pairs={{0,8},{8,0},{16,24},{24,16},{1,9},{9,1},{17,25},{25,17},{2,10},{10... | collective-permute-start | bytes 811016 | tf_op jit(solution)/shard_map/ppermute | solution.py:343
  62.2 8.7 %collective-permute-start.23 = (f32[264,256]{1,0:T(8,128)S(1)}, f32[264,256]{1,0:T(8,128)S(1)}, u32[]{:S(2)}, u32[]{:S(2)}) collective-permute-start(f32[264,256]{1,0:T(8,128)S(1)} %get-tuple-element.58.refs_3_), channel_id=1, source_target_pairs={{0,16},{8,24},{16,0},{24,8},{1,17},{9,25},{17,1},{25,9},{2,18},{10... | collective-permute-start | bytes 811016 | tf_op jit(solution)/shard_map/ppermute | solution.py:343
  71.8 12.1 %collective-permute-start.28 = (f32[24,32,128]{2,1,0:T(8,128)S(1)}, f32[24,32,128]{2,1,0:T(8,128)S(1)}, u32[]{:S(2)}, u32[]{:S(2)}) collective-permute-start(f32[24,32,128]{2,1,0:T(8,128)S(1)} %get-tuple-element.64), channel_id=1, source_target_pairs={{0,4},{4,0},{8,12},{12,8},{16,20},{20,16},{24,28},{28,24},{1,5},{5... | collective-permute-start | bytes 1179656 | tf_op jit(solution)/shard_map/ppermute | solution.py:235
  72.5 6.5 %collective-permute-start.24 = (f32[12,32,128]{2,1,0:T(8,128)S(1)}, f32[12,32,128]{2,1,0:T(8,128)S(1)}, u32[]{:S(2)}, u32[]{:S(2)}) collective-permute-start(f32[12,32,128]{2,1,0:T(8,128)S(1)} %get-tuple-element.60), channel_id=1, source_target_pairs={{0,8},{4,12},{8,0},{12,4},{16,24},{20,28},{24,16},{28,20},{1,9},{5... | collective-permute-start | bytes 589832 | tf_op jit(solution)/shard_map/ppermute | solution.py:235
  73.1 6.1 %collective-permute-start.25 = (f32[12,32,128]{2,1,0:T(8,128)S(1)}, f32[12,32,128]{2,1,0:T(8,128)S(1)}, u32[]{:S(2)}, u32[]{:S(2)}) collective-permute-start(f32[12,32,128]{2,1,0:T(8,128)S(1)} %get-tuple-element.61), channel_id=1, source_target_pairs={{0,16},{4,20},{8,24},{12,28},{16,0},{20,4},{24,8},{28,12},{1,17},{... | collective-permute-start | bytes 589832 | tf_op jit(solution)/shard_map/ppermute | solution.py:235
  73.7 9.8 %collective-permute-start.26 = (f32[12,32,128]{2,1,0:T(8,128)S(1)}, f32[12,32,128]{2,1,0:T(8,128)S(1)}, u32[]{:S(2)}, u32[]{:S(2)}) collective-permute-start(f32[12,32,128]{2,1,0:T(8,128)S(1)} %get-tuple-element.62), channel_id=1, source_target_pairs={{0,12},{4,8},{8,4},{12,0},{16,28},{20,24},{24,20},{28,16},{1,13},{... | collective-permute-start | bytes 589832 | tf_op jit(solution)/shard_map/ppermute | solution.py:235
  75.4 8.5 %collective-permute-start.27 = (f32[12,32,128]{2,1,0:T(8,128)S(1)}, f32[12,32,128]{2,1,0:T(8,128)S(1)}, u32[]{:S(2)}, u32[]{:S(2)}) collective-permute-start(f32[12,32,128]{2,1,0:T(8,128)S(1)} %get-tuple-element.63), channel_id=1, source_target_pairs={{0,20},{4,16},{8,28},{12,24},{16,4},{20,0},{24,12},{28,8},{1,21},{... | collective-permute-start | bytes 589832 | tf_op jit(solution)/shard_map/ppermute | solution.py:235

commit v8 on v7

--- a/solution.py
+++ b/solution.py
@@ -327,7 +327,7 @@
         scaled_ref[total : total + 8, at] = jnp.concatenate(
             [innovation, jnp.zeros((7, cols), jnp.float32)], axis=0
         )
-    result = short_product(scaled_ref[...], scaled_ref[0:total, :], ((1,), (1,)))
+    result = short_product(scaled_ref[...], scaled_ref[0:total, :], ((1,), (1,)), low_terms=True)
     at = 0
     for first in range(0, total, half):
         out_ref[at : at + total - first, :] = result[first:total, first : first + half]
@@ -380,7 +380,7 @@
     return whole_sum, held
 
 
-def short_product(left, right, contract):
+def short_product(left, right, contract, low_terms=False):
     left_high, right_high = left.astype(jnp.bfloat16), right.astype(jnp.bfloat16)
     left_low = (left - left_high.astype(jnp.float32)).astype(jnp.bfloat16)
     right_low = (right - right_high.astype(jnp.float32)).astype(jnp.bfloat16)
@@ -388,7 +388,10 @@
     def dot(x, y):
         return lax.dot_general(x, y, (contract, ((), ())), preferred_element_type=jnp.float32)
 
-    return dot(left_high, right_high) + (dot(left_high, right_low) + dot(left_low, right_high))
+    small = dot(left_high, right_low) + dot(left_low, right_high)
+    if low_terms:
+        small = small + dot(left_low, right_low)
+    return dot(left_high, right_high) + small
 
 
 def eliminate(panel, first):

time: 85.8 us -> 86 us (level)
  no operation moved by 1% of the time
where the time goes in v8:
time: 86 us; the launch traced here: 85.9 us
  starting transfers between devices  40.4 us (47%)
  waiting for transfers between devices  28.7 us (33%)
  Pallas kernels  14.9 us (17%)
  local copies, waits for them, and re-layouts  1.49 us (2%)
    ppermute x12, starting transfers between devices, exchange(): lax.ppermute(value, ('group', 'member'), [(i, i ^ slot) for i in range(cl...  17.7 us
    ppermute x15, starting transfers between devices, flip(): lax.ppermute(value, axis, [(i, i ^ bits) for i in range(lax.axis_size(axi...  17.4 us
    ppermute x12, waiting for transfers between devices, exchange(): lax.ppermute(value, ('group', 'member'), [(i, i ^ slot) for i in range(cl...  14.4 us
    ppermute x15, waiting for transfers between devices, flip(): lax.ppermute(value, axis, [(i, i ^ bits) for i in range(lax.axis_size(axi...  12.7 us
    pallas_call x1, Pallas kernels, on_device(): call(functools.partial(transform_kernel, total), f32(total, total), 1)  7.25 us
    ppermute x2, starting transfers between devices, trade(): return lax.ppermute(value, 'space', pairs + [(j, i) for i, j in pairs])  5.4 us
  transfers between devices with their start and end apart: 29, of which 17 were waited for; matrix products, arithmetic and copies ran while one was open for 0% of the time, Pallas kernels for 11%

profile of v8, /device:TPU:1, one launch (start us, length us, event | category | flops | bytes accessed | tf_op | source)
XLA Modules:
  0.0 85.9 jit_solution(4740341800832038670)
XLA Ops:
  0.0 1.4 %copy-done = f32[32,3,32,128]{3,2,1,0:T(8,128)S(1)} copy-done((f32[32,3,32,128]{3,2,1,0:T(8,128)S(1)}, f32[32,3,32,128]{3,2,1,0:T(8,128)}, u32[]{:S(2)}) %copy-start) | copy-done | bytes 1572888
  1.4 0.3 shard_map.47
  1.8 0.7 collective-permute-start
  2.4 4.7 %collective-permute-start.1 = (f32[9,32,128]{2,1,0:T(8,128)S(1)}, f32[9,32,128]{2,1,0:T(8,128)S(1)}, u32[]{:S(2)}, u32[]{:S(2)}) collective-permute-start(f32[9,32,128]{2,1,0:T(8,128)S(1)} %get-tuple-element.36), channel_id=1, source_target_pairs={{0,1},{2,3},{1,0},{3,2},{4,5},{6,7},{5,4},{7,6},{8,9},{10,11},{9,8... | collective-permute-start | bytes 442376 | tf_op jit(solution)/shard_map/ppermute | solution.py:199
  7.2 1.6 %shard_map.48.interior_ref = f32[8,12,32,128]{3,2,1,0:T(8,128)S(1)} custom-call(f32[3072,128]{1,0:T(8,128)S(1)} %bitcast.23), custom_call_target="tpu_custom_call" | custom-call | flops 78643200 | bytes 6291456 | tf_op jit(solution)/shard_map/pallas_call | solution.py:205
  8.8 1.6 %collective-permute-done.1.inner_ref = f32[9,32,128]{2,1,0:T(8,128)S(1)} collective-permute-done((f32[9,32,128]{2,1,0:T(8,128)S(1)}, f32[9,32,128]{2,1,0:T(8,128)S(1)}, u32[]{:S(2)}, u32[]{:S(2)}) %collective-permute-start.1) | collective-permute-done | bytes 147488 | tf_op jit(solution)/shard_map/ppermute | solution.py:199
  10.4 0.9 %shard_map.49 = (f32[12,32,128]{2,1,0:T(8,128)S(1)}, f32[12,32,128]{2,1,0:T(8,128)S(1)}, f32[12,32,128]{2,1,0:T(8,128)S(1)}, f32[12,32,128]{2,1,0:T(8,128)S(1)},...) custom-call(f32[3072,128]{1,0:T(8,128)S(1)} %bitcast.24, ...), custom_call_target="tpu_custom_call" | custom-call | tf_op jit(solution)/shard_map/pallas_call | solution.py:213
  11.3 1.3 %collective-permute-start.2 = (f32[12,32,128]{2,1,0:T(8,128)S(1)}, f32[12,32,128]{2,1,0:T(8,128)S(1)}, u32[]{:S(2)}, u32[]{:S(2)}) collective-permute-start(f32[12,32,128]{2,1,0:T(8,128)S(1)} %get-tuple-element.38), channel_id=1, source_target_pairs={{0,8},{4,12},{8,0},{12,4},{16,24},{20,28},{24,16},{28,20},{1,9},{5... | collective-permute-start | bytes 589832 | tf_op jit(solution)/shard_map/ppermute | solution.py:235
  12.6 1.2 %collective-permute-start.3 = (f32[12,32,128]{2,1,0:T(8,128)S(1)}, f32[12,32,128]{2,1,0:T(8,128)S(1)}, u32[]{:S(2)}, u32[]{:S(2)}) collective-permute-start(f32[12,32,128]{2,1,0:T(8,128)S(1)} %get-tuple-element.39), channel_id=1, source_target_pairs={{0,16},{4,20},{8,24},{12,28},{16,0},{20,4},{24,8},{28,12},{1,17},{... | collective-permute-start | bytes 589832 | tf_op jit(solution)/shard_map/ppermute | solution.py:235
  14.0 3.5 %collective-permute-start.5 = (f32[12,32,128]{2,1,0:T(8,128)S(1)}, f32[12,32,128]{2,1,0:T(8,128)S(1)}, u32[]{:S(2)}, u32[]{:S(2)}) collective-permute-start(f32[12,32,128]{2,1,0:T(8,128)S(1)} %get-tuple-element.41), channel_id=1, source_target_pairs={{0,12},{4,8},{8,4},{12,0},{16,28},{20,24},{24,20},{28,16},{1,13},{... | collective-permute-start | bytes 589832 | tf_op jit(solution)/shard_map/ppermute | solution.py:235
  17.6 5.3 %collective-permute-start.7 = (f32[12,32,128]{2,1,0:T(8,128)S(1)}, f32[12,32,128]{2,1,0:T(8,128)S(1)}, u32[]{:S(2)}, u32[]{:S(2)}) collective-permute-start(f32[12,32,128]{2,1,0:T(8,128)S(1)} %get-tuple-element.43), channel_id=1, source_target_pairs={{0,28},{4,24},{8,20},{12,16},{16,12},{20,8},{24,4},{28,0},{1,29},{... | collective-permute-start | bytes 589832 | tf_op jit(solution)/shard_map/ppermute | solution.py:235
  22.8 2.2 %collective-permute-start.8 = (f32[12,32,128]{2,1,0:T(8,128)S(1)}, f32[12,32,128]{2,1,0:T(8,128)S(1)}, u32[]{:S(2)}, u32[]{:S(2)}) collective-permute-start(f32[12,32,128]{2,1,0:T(8,128)S(1)} %get-tuple-element.44), channel_id=1, source_target_pairs={{0,4},{4,0},{8,12},{12,8},{16,20},{20,16},{24,28},{28,24},{1,5},{5... | collective-permute-start | bytes 589832 | tf_op jit(solution)/shard_map/ppermute | solution.py:235
  25.1 0.7 shard_map.46.observed_ref
  25.8 2.7 %collective-permute-done.5.refs_4_ = f32[12,32,128]{2,1,0:T(8,128)S(1)} collective-permute-done((f32[12,32,128]{2,1,0:T(8,128)S(1)}, f32[12,32,128]{2,1,0:T(8,128)S(1)}, u32[]{:S(2)}, u32[]{:S(2)}) %collective-permute-start.5) | collective-permute-done | bytes 196640 | tf_op jit(solution)/shard_map/ppermute | solution.py:235
  28.6 3.4 %collective-permute-done.6.refs_5_ = f32[12,32,128]{2,1,0:T(8,128)S(1)} collective-permute-done((f32[12,32,128]{2,1,0:T(8,128)S(1)}, f32[12,32,128]{2,1,0:T(8,128)S(1)}, u32[]{:S(2)}, u32[]{:S(2)}) %collective-permute-start.6) | collective-permute-done | bytes 196640 | tf_op jit(solution)/shard_map/ppermute | solution.py:235
  32.0 1.5 %shard_map.50 = (f32[448,128]{1,0:T(8,128)S(1)}, f32[264,512]{1,0:T(8,128)S(1)}, f32[264,256]{1,0:T(8,128)S(1)}, f32[264,512]{1,0:T(8,128)S(1)}, f32[264,256]{1,0:T(8,128)S(1)}) custom-call(f32[8,1536]{1,0:T(8,128)S(1)} %shard_map.46.observed_ref, f32[12,32,128]{2,1,0:T(8,128)S(1)} %get-tuple-element.37.refs_0_, ...), custom_call_target="tpu_custom_call" | custom-call | tf_op jit(solution)/shard_map/pallas_call | solution.py:619
  33.6 1.3 %collective-permute-done.9 = f32[224,128]{1,0:T(8,128)S(1)} collective-permute-done((f32[224,128]{1,0:T(8,128)S(1)}, f32[224,128]{1,0:T(8,128)S(1)}, u32[]{:S(2)}, u32[]{:S(2)}) %collective-permute-start.9) | collective-permute-done | bytes 114720 | tf_op jit(solution)/shard_map/ppermute | solution.py:343
  34.9 1.2 %collective-permute-start.11 = (f32[56,128]{1,0:T(8,128)S(1)}, f32[56,128]{1,0:T(8,128)S(1)}, u32[]{:S(2)}, u32[]{:S(2)}) collective-permute-start(f32[56,128]{1,0:T(8,128)S(1)} %get-tuple-element.71), channel_id=1, source_target_pairs={{0,16},{8,24},{16,0},{24,8},{1,17},{9,25},{17,1},{25,9},{2,18},{10... | collective-permute-start | bytes 86024 | tf_op jit(solution)/shard_map/ppermute | solution.py:343
  36.1 0.9 %collective-permute-start.12 = (f32[56,128]{1,0:T(8,128)S(1)}, f32[56,128]{1,0:T(8,128)S(1)}, u32[]{:S(2)}, u32[]{:S(2)}) collective-permute-start(f32[56,128]{1,0:T(8,128)S(1)} %get-tuple-element.72), channel_id=1, source_target_pairs={{0,24},{8,16},{16,8},{24,0},{1,25},{9,17},{17,9},{25,1},{2,26},{10... | collective-permute-start | bytes 86024 | tf_op jit(solution)/shard_map/ppermute | solution.py:343
  37.0 0.6 collective-permute-start.10
  37.7 2.0 %collective-permute-done.12 = f32[56,128]{1,0:T(8,128)S(1)} collective-permute-done((f32[56,128]{1,0:T(8,128)S(1)}, f32[56,128]{1,0:T(8,128)S(1)}, u32[]{:S(2)}, u32[]{:S(2)}) %collective-permute-start.12) | collective-permute-done | bytes 28704 | tf_op jit(solution)/shard_map/ppermute | solution.py:343
  40.0 0.5 collective-permute-start.16
  40.5 1.4 %collective-permute-start.17 = (f32[264,512]{1,0:T(8,128)S(1)}, f32[264,512]{1,0:T(8,128)S(1)}, u32[]{:S(2)}, u32[]{:S(2)}) collective-permute-start(f32[264,512]{1,0:T(8,128)S(1)} %get-tuple-element.50.refs_2_), channel_id=1, source_target_pairs={{0,16},{8,24},{16,0},{24,8},{1,17},{9,25},{17,1},{25,9},{2,18},{10... | collective-permute-start | bytes 1622024 | tf_op jit(solution)/shard_map/ppermute | solution.py:343
  41.9 0.8 collective-permute-start.15
  42.7 0.5 collective-permute-start.14
  43.2 2.2 %collective-permute-start.13 = (f32[56,128]{1,0:T(8,128)S(1)}, f32[56,128]{1,0:T(8,128)S(1)}, u32[]{:S(2)}, u32[]{:S(2)}) collective-permute-start(f32[56,128]{1,0:T(8,128)S(1)} %bitcast_add_fusion), channel_id=1, source_target_pairs={{0,3},{1,2},{2,1},{3,0},{4,7},{5,6},{6,5},{7,4},{8,11},{9,10},{10,... | collective-permute-start | bytes 86024 | tf_op jit(solution)/shard_map/ppermute | solution.py:343
  45.4 0.9 %collective-permute-done.14 = f32[56,128]{1,0:T(8,128)S(1)} collective-permute-done((f32[56,128]{1,0:T(8,128)S(1)}, f32[56,128]{1,0:T(8,128)S(1)}, u32[]{:S(2)}, u32[]{:S(2)}) %collective-permute-start.14) | collective-permute-done | bytes 28704 | tf_op jit(solution)/shard_map/ppermute | solution.py:343
  46.3 1.4 %collective-permute-done.13 = f32[56,128]{1,0:T(8,128)S(1)} collective-permute-done((f32[56,128]{1,0:T(8,128)S(1)}, f32[56,128]{1,0:T(8,128)S(1)}, u32[]{:S(2)}, u32[]{:S(2)}) %collective-permute-start.13) | collective-permute-done | bytes 28704 | tf_op jit(solution)/shard_map/ppermute | solution.py:343
  47.8 4.4 %collective-permute-done.16.refs_4_ = f32[264,512]{1,0:T(8,128)S(1)} collective-permute-done((f32[264,512]{1,0:T(8,128)S(1)}, f32[264,512]{1,0:T(8,128)S(1)}, u32[]{:S(2)}, u32[]{:S(2)}) %collective-permute-start.16) | collective-permute-done | bytes 540704 | tf_op jit(solution)/shard_map/ppermute | solution.py:343
  52.2 1.6 %collective-permute-start.20 = (f32[56,128]{1,0:T(8,128)S(1)}, f32[56,128]{1,0:T(8,128)S(1)}, u32[]{:S(2)}, u32[]{:S(2)}) collective-permute-start(f32[56,128]{1,0:T(8,128)S(1)} %add_add_fusion), channel_id=1, source_target_pairs={{0,24},{8,16},{16,8},{24,0},{1,25},{9,17},{17,9},{25,1},{2,26},{10... | collective-permute-start | bytes 86024 | tf_op jit(solution)/shard_map/ppermute | solution.py:343
  53.8 0.8 collective-permute-start.19
  54.6 0.4 collective-permute-start.18
  55.0 0.9 %collective-permute-done.20 = f32[56,128]{1,0:T(8,128)S(1)} collective-permute-done((f32[56,128]{1,0:T(8,128)S(1)}, f32[56,128]{1,0:T(8,128)S(1)}, u32[]{:S(2)}, u32[]{:S(2)}) %collective-permute-start.20) | collective-permute-done | bytes 28704 | tf_op jit(solution)/shard_map/ppermute | solution.py:343
  55.8 0.7 collective-permute-done.19
  56.5 0.8 collective-permute-done.18
  57.4 4.6 %collective-permute-start.21 = (f32[224,128]{1,0:T(8,128)S(1)}, f32[224,128]{1,0:T(8,128)S(1)}, u32[]{:S(2)}, u32[]{:S(2)}) collective-permute-start(f32[224,128]{1,0:T(8,128)S(1)} %pad_maximum_fusion.2), channel_id=1, source_target_pairs={{0,4},{4,0},{1,5},{5,1},{2,6},{6,2},{3,7},{7,3},{8,12},{12,8},{9,1... | collective-permute-start | bytes 344072 | tf_op jit(solution)/shard_map/ppermute | solution.py:343
  62.0 0.4 collective-permute-start.22
  62.4 1.4 %collective-permute-start.23 = (f32[264,256]{1,0:T(8,128)S(1)}, f32[264,256]{1,0:T(8,128)S(1)}, u32[]{:S(2)}, u32[]{:S(2)}) collective-permute-start(f32[264,256]{1,0:T(8,128)S(1)} %get-tuple-element.58.refs_3_), channel_id=1, source_target_pairs={{0,16},{8,24},{16,0},{24,8},{1,17},{9,25},{17,1},{25,9},{2,18},{10... | collective-permute-start | bytes 811016 | tf_op jit(solution)/shard_map/ppermute | solution.py:343
  63.8 7.3 %shard_map.51.transform_ref = f32[256,256]{1,0:T(8,128)S(1)} custom-call(f32[448,128]{1,0:T(8,128)S(1)} %pad_maximum_fusion.packed_ref), custom_call_target="tpu_custom_call" | custom-call | tf_op jit(solution)/shard_map/pallas_call | solution.py:626
  71.1 0.9 %shard_map.52 = (f32[24,32,128]{2,1,0:T(8,128)S(1)}, f32[12,32,128]{2,1,0:T(8,128)S(1)}, f32[12,32,128]{2,1,0:T(8,128)S(1)}, f32[12,32,128]{2,1,0:T(8,128)S(1)},...) custom-call(f32[256,256]{1,0:T(8,128)S(1)} %shard_map.51.transform_ref, ...), custom_call_target="tpu_custom_call" | custom-call | tf_op jit(solution)/shard_map/pallas_call | solution.py:629
  72.0 0.7 collective-permute-start.28
  72.7 0.6 collective-permute-start.24
  73.3 0.5 collective-permute-start.25
  73.9 1.8 %collective-permute-start.26 = (f32[12,32,128]{2,1,0:T(8,128)S(1)}, f32[12,32,128]{2,1,0:T(8,128)S(1)}, u32[]{:S(2)}, u32[]{:S(2)}) collective-permute-start(f32[12,32,128]{2,1,0:T(8,128)S(1)} %get-tuple-element.62), channel_id=1, source_target_pairs={{0,12},{4,8},{8,4},{12,0},{16,28},{20,24},{24,20},{28,16},{1,13},{... | collective-permute-start | bytes 589832 | tf_op jit(solution)/shard_map/ppermute | solution.py:235
  75.9 3.3 %collective-permute-done.24.refs_1_ = f32[12,32,128]{2,1,0:T(8,128)S(1)} collective-permute-done((f32[12,32,128]{2,1,0:T(8,128)S(1)}, f32[12,32,128]{2,1,0:T(8,128)S(1)}, u32[]{:S(2)}, u32[]{:S(2)}) %collective-permute-start.24) | collective-permute-done | bytes 196640 | tf_op jit(solution)/shard_map/ppermute | solution.py:235
  79.5 4.2 %collective-permute-done.26.refs_3_ = f32[12,32,128]{2,1,0:T(8,128)S(1)} collective-permute-done((f32[12,32,128]{2,1,0:T(8,128)S(1)}, f32[12,32,128]{2,1,0:T(8,128)S(1)}, u32[]{:S(2)}, u32[]{:S(2)}) %collective-permute-start.26) | collective-permute-done | bytes 196640 | tf_op jit(solution)/shard_map/ppermute | solution.py:235
  83.7 0.5 collective-permute-done.27.refs_4_
  84.2 1.7 %shard_map.53 = f32[3072,128]{1,0:T(8,128)} custom-call(f32[24,32,128]{2,1,0:T(8,128)S(1)} %get-tuple-element.59.refs_0_, f32[12,32,128]{2,1,0:T(8,128)S(1)} %collective-permute-done.24.refs_1_, f32[12,32,128]{2,1,0:T(8,128)S(1)} %collective-permute-done.25.refs_2_, f32[12,32,128]{2,1,0:T(8,128)S(1)} %collective-permute-done.26.refs_3_, ...), custom_call_target="tpu_custom_call" | custom-call | tf_op jit(solution)/shard_map/pallas_call | solution.py:594
  (36 shorter events, 1.4 us)
Async XLA Ops:
  0.0 1.4 %copy-start = (f32[32,3,32,128]{3,2,1,0:T(8,128)S(1)}, f32[32,3,32,128]{3,2,1,0:T(8,128)}, u32[]{:S(2)}) copy-start(f32[32,3,32,128]{3,2,1,0:T(8,128)} %bottom_ref.1) | copy-start | bytes 4718596
  1.8 7.0 %collective-permute-start = (f32[9,32,128]{2,1,0:T(8,128)S(1)}, f32[9,32,128]{2,1,0:T(8,128)S(1)}, u32[]{:S(2)}, u32[]{:S(2)}) collective-permute-start(f32[9,32,128]{2,1,0:T(8,128)S(1)} %get-tuple-element.35), channel_id=1, source_target_pairs={{1,2},{2,1},{5,6},{6,5},{9,10},{10,9},{13,14},{14,13},{17,18},{18,... | collective-permute-start | bytes 442376 | tf_op jit(solution)/shard_map/ppermute | solution.py:199
  2.4 8.0 %collective-permute-start.1 = (f32[9,32,128]{2,1,0:T(8,128)S(1)}, f32[9,32,128]{2,1,0:T(8,128)S(1)}, u32[]{:S(2)}, u32[]{:S(2)}) collective-permute-start(f32[9,32,128]{2,1,0:T(8,128)S(1)} %get-tuple-element.36), channel_id=1, source_target_pairs={{0,1},{2,3},{1,0},{3,2},{4,5},{6,7},{5,4},{7,6},{8,9},{10,11},{9,8... | collective-permute-start | bytes 442376 | tf_op jit(solution)/shard_map/ppermute | solution.py:199
  8.8 16.3 %copy-start.1 = (f32[1,768]{1,0:T(1,128)S(1)}, f32[1,768]{1,0:T(1,128)}, u32[]{:S(2)}) copy-start(f32[1,768]{1,0:T(1,128)} %values_ref.1) | copy-start | bytes 9220
  8.8 16.3 %copy-start.2 = (f32[1,768]{1,0:T(1,128)S(1)}, f32[1,768]{1,0:T(1,128)}, u32[]{:S(2)}) copy-start(f32[1,768]{1,0:T(1,128)} %precision_ref.1) | copy-start | bytes 9220
  8.8 16.3 %copy-start.3 = (s32[1,768]{1,0:T(1,128)S(1)}, s32[1,768]{1,0:T(1,128)}, u32[]{:S(2)}) copy-start(s32[1,768]{1,0:T(1,128)} %index_ref.1) | copy-start | bytes 9220
  11.3 6.2 %collective-permute-start.2 = (f32[12,32,128]{2,1,0:T(8,128)S(1)}, f32[12,32,128]{2,1,0:T(8,128)S(1)}, u32[]{:S(2)}, u32[]{:S(2)}) collective-permute-start(f32[12,32,128]{2,1,0:T(8,128)S(1)} %get-tuple-element.38), channel_id=1, source_target_pairs={{0,8},{4,12},{8,0},{12,4},{16,24},{20,28},{24,16},{28,20},{1,9},{5... | collective-permute-start | bytes 589832 | tf_op jit(solution)/shard_map/ppermute | solution.py:235
  12.6 10.2 %collective-permute-start.3 = (f32[12,32,128]{2,1,0:T(8,128)S(1)}, f32[12,32,128]{2,1,0:T(8,128)S(1)}, u32[]{:S(2)}, u32[]{:S(2)}) collective-permute-start(f32[12,32,128]{2,1,0:T(8,128)S(1)} %get-tuple-element.39), channel_id=1, source_target_pairs={{0,16},{4,20},{8,24},{12,28},{16,0},{20,4},{24,8},{28,12},{1,17},{... | collective-permute-start | bytes 589832 | tf_op jit(solution)/shard_map/ppermute | solution.py:235
  13.9 12.0 %collective-permute-start.4 = (f32[12,32,128]{2,1,0:T(8,128)S(1)}, f32[12,32,128]{2,1,0:T(8,128)S(1)}, u32[]{:S(2)}, u32[]{:S(2)}) collective-permute-start(f32[12,32,128]{2,1,0:T(8,128)S(1)} %get-tuple-element.40), channel_id=1, source_target_pairs={{0,24},{4,28},{8,16},{12,20},{16,8},{20,12},{24,0},{28,4},{1,25},{... | collective-permute-start | bytes 589832 | tf_op jit(solution)/shard_map/ppermute | solution.py:235
  14.0 14.5 %collective-permute-start.5 = (f32[12,32,128]{2,1,0:T(8,128)S(1)}, f32[12,32,128]{2,1,0:T(8,128)S(1)}, u32[]{:S(2)}, u32[]{:S(2)}) collective-permute-start(f32[12,32,128]{2,1,0:T(8,128)S(1)} %get-tuple-element.41), channel_id=1, source_target_pairs={{0,12},{4,8},{8,4},{12,0},{16,28},{20,24},{24,20},{28,16},{1,13},{... | collective-permute-start | bytes 589832 | tf_op jit(solution)/shard_map/ppermute | solution.py:235
  17.5 14.5 %collective-permute-start.6 = (f32[12,32,128]{2,1,0:T(8,128)S(1)}, f32[12,32,128]{2,1,0:T(8,128)S(1)}, u32[]{:S(2)}, u32[]{:S(2)}) collective-permute-start(f32[12,32,128]{2,1,0:T(8,128)S(1)} %get-tuple-element.42), channel_id=1, source_target_pairs={{0,20},{4,16},{8,28},{12,24},{16,4},{20,0},{24,12},{28,8},{1,21},{... | collective-permute-start | bytes 589832 | tf_op jit(solution)/shard_map/ppermute | solution.py:235
  17.6 14.4 %collective-permute-start.7 = (f32[12,32,128]{2,1,0:T(8,128)S(1)}, f32[12,32,128]{2,1,0:T(8,128)S(1)}, u32[]{:S(2)}, u32[]{:S(2)}) collective-permute-start(f32[12,32,128]{2,1,0:T(8,128)S(1)} %get-tuple-element.43), channel_id=1, source_target_pairs={{0,28},{4,24},{8,20},{12,16},{16,12},{20,8},{24,4},{28,0},{1,29},{... | collective-permute-start | bytes 589832 | tf_op jit(solution)/shard_map/ppermute | solution.py:235
  22.8 9.1 %collective-permute-start.8 = (f32[12,32,128]{2,1,0:T(8,128)S(1)}, f32[12,32,128]{2,1,0:T(8,128)S(1)}, u32[]{:S(2)}, u32[]{:S(2)}) collective-permute-start(f32[12,32,128]{2,1,0:T(8,128)S(1)} %get-tuple-element.44), channel_id=1, source_target_pairs={{0,4},{4,0},{8,12},{12,8},{16,20},{20,16},{24,28},{28,24},{1,5},{5... | collective-permute-start | bytes 589832 | tf_op jit(solution)/shard_map/ppermute | solution.py:235
  33.5 1.4 %collective-permute-start.9 = (f32[224,128]{1,0:T(8,128)S(1)}, f32[224,128]{1,0:T(8,128)S(1)}, u32[]{:S(2)}, u32[]{:S(2)}) collective-permute-start(f32[224,128]{1,0:T(8,128)S(1)} %constant_dynamic-slice_fusion), channel_id=1, source_target_pairs={{0,4},{4,0},{1,5},{5,1},{2,6},{6,2},{3,7},{7,3},{8,12},{12,8},{9,1... | collective-permute-start | bytes 344072 | tf_op jit(solution)/shard_map/ppermute | solution.py:343
  34.9 2.8 %collective-permute-start.11 = (f32[56,128]{1,0:T(8,128)S(1)}, f32[56,128]{1,0:T(8,128)S(1)}, u32[]{:S(2)}, u32[]{:S(2)}) collective-permute-start(f32[56,128]{1,0:T(8,128)S(1)} %get-tuple-element.71), channel_id=1, source_target_pairs={{0,16},{8,24},{16,0},{24,8},{1,17},{9,25},{17,1},{25,9},{2,18},{10... | collective-permute-start | bytes 86024 | tf_op jit(solution)/shard_map/ppermute | solution.py:343
  36.1 3.6 %collective-permute-start.12 = (f32[56,128]{1,0:T(8,128)S(1)}, f32[56,128]{1,0:T(8,128)S(1)}, u32[]{:S(2)}, u32[]{:S(2)}) collective-permute-start(f32[56,128]{1,0:T(8,128)S(1)} %get-tuple-element.72), channel_id=1, source_target_pairs={{0,24},{8,16},{16,8},{24,0},{1,25},{9,17},{17,9},{25,1},{2,26},{10... | collective-permute-start | bytes 86024 | tf_op jit(solution)/shard_map/ppermute | solution.py:343
  37.0 3.0 %collective-permute-start.10 = (f32[56,128]{1,0:T(8,128)S(1)}, f32[56,128]{1,0:T(8,128)S(1)}, u32[]{:S(2)}, u32[]{:S(2)}) collective-permute-start(f32[56,128]{1,0:T(8,128)S(1)} %get-tuple-element.73), channel_id=1, source_target_pairs={{0,8},{8,0},{16,24},{24,16},{1,9},{9,1},{17,25},{25,17},{2,10},{10... | collective-permute-start | bytes 86024 | tf_op jit(solution)/shard_map/ppermute | solution.py:343
  40.0 12.2 %collective-permute-start.16 = (f32[264,512]{1,0:T(8,128)S(1)}, f32[264,512]{1,0:T(8,128)S(1)}, u32[]{:S(2)}, u32[]{:S(2)}) collective-permute-start(f32[264,512]{1,0:T(8,128)S(1)} %get-tuple-element.49.refs_0_), channel_id=1, source_target_pairs={{0,8},{8,0},{16,24},{24,16},{1,9},{9,1},{17,25},{25,17},{2,10},{10... | collective-permute-start | bytes 1622024 | tf_op jit(solution)/shard_map/ppermute | solution.py:343
  40.5 11.7 %collective-permute-start.17 = (f32[264,512]{1,0:T(8,128)S(1)}, f32[264,512]{1,0:T(8,128)S(1)}, u32[]{:S(2)}, u32[]{:S(2)}) collective-permute-start(f32[264,512]{1,0:T(8,128)S(1)} %get-tuple-element.50.refs_2_), channel_id=1, source_target_pairs={{0,16},{8,24},{16,0},{24,8},{1,17},{9,25},{17,1},{25,9},{2,18},{10... | collective-permute-start | bytes 1622024 | tf_op jit(solution)/shard_map/ppermute | solution.py:343
  41.9 3.6 %collective-permute-start.15 = (f32[56,128]{1,0:T(8,128)S(1)}, f32[56,128]{1,0:T(8,128)S(1)}, u32[]{:S(2)}, u32[]{:S(2)}) collective-permute-start(f32[56,128]{1,0:T(8,128)S(1)} %bitcast_add_fusion), channel_id=1, source_target_pairs={{0,1},{1,0},{2,3},{3,2},{4,5},{5,4},{6,7},{7,6},{8,9},{9,8},{10,11... | collective-permute-start | bytes 86024 | tf_op jit(solution)/shard_map/ppermute | solution.py:343
  42.7 3.6 %collective-permute-start.14 = (f32[56,128]{1,0:T(8,128)S(1)}, f32[56,128]{1,0:T(8,128)S(1)}, u32[]{:S(2)}, u32[]{:S(2)}) collective-permute-start(f32[56,128]{1,0:T(8,128)S(1)} %bitcast_add_fusion), channel_id=1, source_target_pairs={{0,2},{1,3},{2,0},{3,1},{4,6},{5,7},{6,4},{7,5},{8,10},{9,11},{10,... | collective-permute-start | bytes 86024 | tf_op jit(solution)/shard_map/ppermute | solution.py:343
  43.2 4.6 %collective-permute-start.13 = (f32[56,128]{1,0:T(8,128)S(1)}, f32[56,128]{1,0:T(8,128)S(1)}, u32[]{:S(2)}, u32[]{:S(2)}) collective-permute-start(f32[56,128]{1,0:T(8,128)S(1)} %bitcast_add_fusion), channel_id=1, source_target_pairs={{0,3},{1,2},{2,1},{3,0},{4,7},{5,6},{6,5},{7,4},{8,11},{9,10},{10,... | collective-permute-start | bytes 86024 | tf_op jit(solution)/shard_map/ppermute | solution.py:343
  52.2 3.6 %collective-permute-start.20 = (f32[56,128]{1,0:T(8,128)S(1)}, f32[56,128]{1,0:T(8,128)S(1)}, u32[]{:S(2)}, u32[]{:S(2)}) collective-permute-start(f32[56,128]{1,0:T(8,128)S(1)} %add_add_fusion), channel_id=1, source_target_pairs={{0,24},{8,16},{16,8},{24,0},{1,25},{9,17},{17,9},{25,1},{2,26},{10... | collective-permute-start | bytes 86024 | tf_op jit(solution)/shard_map/ppermute | solution.py:343
  53.8 2.7 %collective-permute-start.19 = (f32[56,128]{1,0:T(8,128)S(1)}, f32[56,128]{1,0:T(8,128)S(1)}, u32[]{:S(2)}, u32[]{:S(2)}) collective-permute-start(f32[56,128]{1,0:T(8,128)S(1)} %add_add_fusion), channel_id=1, source_target_pairs={{0,16},{8,24},{16,0},{24,8},{1,17},{9,25},{17,1},{25,9},{2,18},{10... | collective-permute-start | bytes 86024 | tf_op jit(solution)/shard_map/ppermute | solution.py:343
  54.6 2.7 %collective-permute-start.18 = (f32[56,128]{1,0:T(8,128)S(1)}, f32[56,128]{1,0:T(8,128)S(1)}, u32[]{:S(2)}, u32[]{:S(2)}) collective-permute-start(f32[56,128]{1,0:T(8,128)S(1)} %add_add_fusion), channel_id=1, source_target_pairs={{0,8},{8,0},{16,24},{24,16},{1,9},{9,1},{17,25},{25,17},{2,10},{10... | collective-permute-start | bytes 86024 | tf_op jit(solution)/shard_map/ppermute | solution.py:343
  57.4 6.4 %collective-permute-start.21 = (f32[224,128]{1,0:T(8,128)S(1)}, f32[224,128]{1,0:T(8,128)S(1)}, u32[]{:S(2)}, u32[]{:S(2)}) collective-permute-start(f32[224,128]{1,0:T(8,128)S(1)} %pad_maximum_fusion.2), channel_id=1, source_target_pairs={{0,4},{4,0},{1,5},{5,1},{2,6},{6,2},{3,7},{7,3},{8,12},{12,8},{9,1... | collective-permute-start | bytes 344072 | tf_op jit(solution)/shard_map/ppermute | solution.py:343
  62.0 9.1 %collective-permute-start.22 = (f32[264,256]{1,0:T(8,128)S(1)}, f32[264,256]{1,0:T(8,128)S(1)}, u32[]{:S(2)}, u32[]{:S(2)}) collective-permute-start(f32[264,256]{1,0:T(8,128)S(1)} %get-tuple-element.56.refs_1_), channel_id=1, source_target_pairs={{0,8},{8,0},{16,24},{24,16},{1,9},{9,1},{17,25},{25,17},{2,10},{10... | collective-permute-start | bytes 811016 | tf_op jit(solution)/shard_map/ppermute | solution.py:343
  62.4 8.7 %collective-permute-start.23 = (f32[264,256]{1,0:T(8,128)S(1)}, f32[264,256]{1,0:T(8,128)S(1)}, u32[]{:S(2)}, u32[]{:S(2)}) collective-permute-start(f32[264,256]{1,0:T(8,128)S(1)} %get-tuple-element.58.refs_3_), channel_id=1, source_target_pairs={{0,16},{8,24},{16,0},{24,8},{1,17},{9,25},{17,1},{25,9},{2,18},{10... | collective-permute-start | bytes 811016 | tf_op jit(solution)/shard_map/ppermute | solution.py:343
  72.0 12.1 %collective-permute-start.28 = (f32[24,32,128]{2,1,0:T(8,128)S(1)}, f32[24,32,128]{2,1,0:T(8,128)S(1)}, u32[]{:S(2)}, u32[]{:S(2)}) collective-permute-start(f32[24,32,128]{2,1,0:T(8,128)S(1)} %get-tuple-element.64), channel_id=1, source_target_pairs={{0,4},{4,0},{8,12},{12,8},{16,20},{20,16},{24,28},{28,24},{1,5},{5... | collective-permute-start | bytes 1179656 | tf_op jit(solution)/shard_map/ppermute | solution.py:235
  72.7 6.5 %collective-permute-start.24 = (f32[12,32,128]{2,1,0:T(8,128)S(1)}, f32[12,32,128]{2,1,0:T(8,128)S(1)}, u32[]{:S(2)}, u32[]{:S(2)}) collective-permute-start(f32[12,32,128]{2,1,0:T(8,128)S(1)} %get-tuple-element.60), channel_id=1, source_target_pairs={{0,8},{4,12},{8,0},{12,4},{16,24},{20,28},{24,16},{28,20},{1,9},{5... | collective-permute-start | bytes 589832 | tf_op jit(solution)/shard_map/ppermute | solution.py:235
  73.3 6.1 %collective-permute-start.25 = (f32[12,32,128]{2,1,0:T(8,128)S(1)}, f32[12,32,128]{2,1,0:T(8,128)S(1)}, u32[]{:S(2)}, u32[]{:S(2)}) collective-permute-start(f32[12,32,128]{2,1,0:T(8,128)S(1)} %get-tuple-element.61), channel_id=1, source_target_pairs={{0,16},{4,20},{8,24},{12,28},{16,0},{20,4},{24,8},{28,12},{1,17},{... | collective-permute-start | bytes 589832 | tf_op jit(solution)/shard_map/ppermute | solution.py:235
  73.9 9.8 %collective-permute-start.26 = (f32[12,32,128]{2,1,0:T(8,128)S(1)}, f32[12,32,128]{2,1,0:T(8,128)S(1)}, u32[]{:S(2)}, u32[]{:S(2)}) collective-permute-start(f32[12,32,128]{2,1,0:T(8,128)S(1)} %get-tuple-element.62), channel_id=1, source_target_pairs={{0,12},{4,8},{8,4},{12,0},{16,28},{20,24},{24,20},{28,16},{1,13},{... | collective-permute-start | bytes 589832 | tf_op jit(solution)/shard_map/ppermute | solution.py:235
  75.6 8.5 %collective-permute-start.27 = (f32[12,32,128]{2,1,0:T(8,128)S(1)}, f32[12,32,128]{2,1,0:T(8,128)S(1)}, u32[]{:S(2)}, u32[]{:S(2)}) collective-permute-start(f32[12,32,128]{2,1,0:T(8,128)S(1)} %get-tuple-element.63), channel_id=1, source_target_pairs={{0,20},{4,16},{8,28},{12,24},{16,4},{20,0},{24,12},{28,8},{1,21},{... | collective-permute-start | bytes 589832 | tf_op jit(solution)/shard_map/ppermute | solution.py:235

commit v9 on v8

--- a/solution.py
+++ b/solution.py
@@ -499,10 +499,10 @@
                 factor[row, column] = product(left, inverse[column, column], LAST)
     for row in range(count):
         for column in range(row):
-            total_term = product(factor[row, column], inverse[column, column], ROWS)
+            total_term = short_product(factor[row, column], inverse[column, column], ROWS)
             for k in range(column + 1, row):
-                total_term = total_term + product(factor[row, k], inverse[k, column], ROWS)
-            inverse[row, column] = -product(inverse[row, row], total_term, ROWS)
+                total_term = total_term + short_product(factor[row, k], inverse[k, column], ROWS)
+            inverse[row, column] = -short_product(inverse[row, row], total_term, ROWS)
     inner = [
         sum(
             jnp.sum(inverse[row, column] * pull[column], axis=1, keepdims=True)

time: 86 us -> 86 us (level)
  no operation moved by 1% of the time
where the time goes in v9:
time: 86 us; the launch traced here: 85.9 us
  starting transfers between devices  40.4 us (47%)
  waiting for transfers between devices  28.8 us (33%)
  Pallas kernels  14.9 us (17%)
  local copies, waits for them, and re-layouts  1.49 us (2%)
    ppermute x12, starting transfers between devices, exchange(): lax.ppermute(value, ('group', 'member'), [(i, i ^ slot) for i in range(cl...  17.7 us
    ppermute x15, starting transfers between devices, flip(): lax.ppermute(value, axis, [(i, i ^ bits) for i in range(lax.axis_size(axi...  17.4 us
    ppermute x12, waiting for transfers between devices, exchange(): lax.ppermute(value, ('group', 'member'), [(i, i ^ slot) for i in range(cl...  14.4 us
    ppermute x15, waiting for transfers between devices, flip(): lax.ppermute(value, axis, [(i, i ^ bits) for i in range(lax.axis_size(axi...  12.7 us
    pallas_call x1, Pallas kernels, on_device(): call(functools.partial(transform_kernel, total), f32(total, total), 1)  7.23 us
    ppermute x2, starting transfers between devices, trade(): return lax.ppermute(value, 'space', pairs + [(j, i) for i, j in pairs])  5.4 us
  transfers between devices with their start and end apart: 29, of which 17 were waited for; matrix products, arithmetic and copies ran while one was open for 0% of the time, Pallas kernels for 11%

profile of v9, /device:TPU:1, one launch (start us, length us, event | category | flops | bytes accessed | tf_op | source)
XLA Modules:
  0.0 85.9 jit_solution(1847420977833610725)
XLA Ops:
  0.0 1.4 %copy-done = f32[32,3,32,128]{3,2,1,0:T(8,128)S(1)} copy-done((f32[32,3,32,128]{3,2,1,0:T(8,128)S(1)}, f32[32,3,32,128]{3,2,1,0:T(8,128)}, u32[]{:S(2)}) %copy-start) | copy-done | bytes 1572888
  1.4 0.3 shard_map.47
  1.8 0.7 collective-permute-start
  2.4 4.7 %collective-permute-start.1 = (f32[9,32,128]{2,1,0:T(8,128)S(1)}, f32[9,32,128]{2,1,0:T(8,128)S(1)}, u32[]{:S(2)}, u32[]{:S(2)}) collective-permute-start(f32[9,32,128]{2,1,0:T(8,128)S(1)} %get-tuple-element.36), channel_id=1, source_target_pairs={{0,1},{2,3},{1,0},{3,2},{4,5},{6,7},{5,4},{7,6},{8,9},{10,11},{9,8... | collective-permute-start | bytes 442376 | tf_op jit(solution)/shard_map/ppermute | solution.py:199
  7.2 1.6 %shard_map.48.interior_ref = f32[8,12,32,128]{3,2,1,0:T(8,128)S(1)} custom-call(f32[3072,128]{1,0:T(8,128)S(1)} %bitcast.23), custom_call_target="tpu_custom_call" | custom-call | flops 78643200 | bytes 6291456 | tf_op jit(solution)/shard_map/pallas_call | solution.py:205
  8.8 1.6 %collective-permute-done.1.inner_ref = f32[9,32,128]{2,1,0:T(8,128)S(1)} collective-permute-done((f32[9,32,128]{2,1,0:T(8,128)S(1)}, f32[9,32,128]{2,1,0:T(8,128)S(1)}, u32[]{:S(2)}, u32[]{:S(2)}) %collective-permute-start.1) | collective-permute-done | bytes 147488 | tf_op jit(solution)/shard_map/ppermute | solution.py:199
  10.4 0.9 %shard_map.49 = (f32[12,32,128]{2,1,0:T(8,128)S(1)}, f32[12,32,128]{2,1,0:T(8,128)S(1)}, f32[12,32,128]{2,1,0:T(8,128)S(1)}, f32[12,32,128]{2,1,0:T(8,128)S(1)},...) custom-call(f32[3072,128]{1,0:T(8,128)S(1)} %bitcast.24, ...), custom_call_target="tpu_custom_call" | custom-call | tf_op jit(solution)/shard_map/pallas_call | solution.py:213
  11.3 1.3 %collective-permute-start.2 = (f32[12,32,128]{2,1,0:T(8,128)S(1)}, f32[12,32,128]{2,1,0:T(8,128)S(1)}, u32[]{:S(2)}, u32[]{:S(2)}) collective-permute-start(f32[12,32,128]{2,1,0:T(8,128)S(1)} %get-tuple-element.38), channel_id=1, source_target_pairs={{0,8},{4,12},{8,0},{12,4},{16,24},{20,28},{24,16},{28,20},{1,9},{5... | collective-permute-start | bytes 589832 | tf_op jit(solution)/shard_map/ppermute | solution.py:235
  12.6 1.2 %collective-permute-start.3 = (f32[12,32,128]{2,1,0:T(8,128)S(1)}, f32[12,32,128]{2,1,0:T(8,128)S(1)}, u32[]{:S(2)}, u32[]{:S(2)}) collective-permute-start(f32[12,32,128]{2,1,0:T(8,128)S(1)} %get-tuple-element.39), channel_id=1, source_target_pairs={{0,16},{4,20},{8,24},{12,28},{16,0},{20,4},{24,8},{28,12},{1,17},{... | collective-permute-start | bytes 589832 | tf_op jit(solution)/shard_map/ppermute | solution.py:235
  14.0 3.5 %collective-permute-start.5 = (f32[12,32,128]{2,1,0:T(8,128)S(1)}, f32[12,32,128]{2,1,0:T(8,128)S(1)}, u32[]{:S(2)}, u32[]{:S(2)}) collective-permute-start(f32[12,32,128]{2,1,0:T(8,128)S(1)} %get-tuple-element.41), channel_id=1, source_target_pairs={{0,12},{4,8},{8,4},{12,0},{16,28},{20,24},{24,20},{28,16},{1,13},{... | collective-permute-start | bytes 589832 | tf_op jit(solution)/shard_map/ppermute | solution.py:235
  17.6 5.3 %collective-permute-start.7 = (f32[12,32,128]{2,1,0:T(8,128)S(1)}, f32[12,32,128]{2,1,0:T(8,128)S(1)}, u32[]{:S(2)}, u32[]{:S(2)}) collective-permute-start(f32[12,32,128]{2,1,0:T(8,128)S(1)} %get-tuple-element.43), channel_id=1, source_target_pairs={{0,28},{4,24},{8,20},{12,16},{16,12},{20,8},{24,4},{28,0},{1,29},{... | collective-permute-start | bytes 589832 | tf_op jit(solution)/shard_map/ppermute | solution.py:235
  22.8 2.2 %collective-permute-start.8 = (f32[12,32,128]{2,1,0:T(8,128)S(1)}, f32[12,32,128]{2,1,0:T(8,128)S(1)}, u32[]{:S(2)}, u32[]{:S(2)}) collective-permute-start(f32[12,32,128]{2,1,0:T(8,128)S(1)} %get-tuple-element.44), channel_id=1, source_target_pairs={{0,4},{4,0},{8,12},{12,8},{16,20},{20,16},{24,28},{28,24},{1,5},{5... | collective-permute-start | bytes 589832 | tf_op jit(solution)/shard_map/ppermute | solution.py:235
  25.1 0.7 shard_map.46.observed_ref
  25.8 2.7 %collective-permute-done.5.refs_4_ = f32[12,32,128]{2,1,0:T(8,128)S(1)} collective-permute-done((f32[12,32,128]{2,1,0:T(8,128)S(1)}, f32[12,32,128]{2,1,0:T(8,128)S(1)}, u32[]{:S(2)}, u32[]{:S(2)}) %collective-permute-start.5) | collective-permute-done | bytes 196640 | tf_op jit(solution)/shard_map/ppermute | solution.py:235
  28.6 3.4 %collective-permute-done.6.refs_5_ = f32[12,32,128]{2,1,0:T(8,128)S(1)} collective-permute-done((f32[12,32,128]{2,1,0:T(8,128)S(1)}, f32[12,32,128]{2,1,0:T(8,128)S(1)}, u32[]{:S(2)}, u32[]{:S(2)}) %collective-permute-start.6) | collective-permute-done | bytes 196640 | tf_op jit(solution)/shard_map/ppermute | solution.py:235
  32.0 1.5 %shard_map.50 = (f32[448,128]{1,0:T(8,128)S(1)}, f32[264,512]{1,0:T(8,128)S(1)}, f32[264,256]{1,0:T(8,128)S(1)}, f32[264,512]{1,0:T(8,128)S(1)}, f32[264,256]{1,0:T(8,128)S(1)}) custom-call(f32[8,1536]{1,0:T(8,128)S(1)} %shard_map.46.observed_ref, f32[12,32,128]{2,1,0:T(8,128)S(1)} %get-tuple-element.37.refs_0_, ...), custom_call_target="tpu_custom_call" | custom-call | tf_op jit(solution)/shard_map/pallas_call | solution.py:619
  33.6 1.3 %collective-permute-done.9 = f32[224,128]{1,0:T(8,128)S(1)} collective-permute-done((f32[224,128]{1,0:T(8,128)S(1)}, f32[224,128]{1,0:T(8,128)S(1)}, u32[]{:S(2)}, u32[]{:S(2)}) %collective-permute-start.9) | collective-permute-done | bytes 114720 | tf_op jit(solution)/shard_map/ppermute | solution.py:343
  34.9 1.2 %collective-permute-start.11 = (f32[56,128]{1,0:T(8,128)S(1)}, f32[56,128]{1,0:T(8,128)S(1)}, u32[]{:S(2)}, u32[]{:S(2)}) collective-permute-start(f32[56,128]{1,0:T(8,128)S(1)} %get-tuple-element.71), channel_id=1, source_target_pairs={{0,16},{8,24},{16,0},{24,8},{1,17},{9,25},{17,1},{25,9},{2,18},{10... | collective-permute-start | bytes 86024 | tf_op jit(solution)/shard_map/ppermute | solution.py:343
  36.1 0.9 %collective-permute-start.12 = (f32[56,128]{1,0:T(8,128)S(1)}, f32[56,128]{1,0:T(8,128)S(1)}, u32[]{:S(2)}, u32[]{:S(2)}) collective-permute-start(f32[56,128]{1,0:T(8,128)S(1)} %get-tuple-element.72), channel_id=1, source_target_pairs={{0,24},{8,16},{16,8},{24,0},{1,25},{9,17},{17,9},{25,1},{2,26},{10... | collective-permute-start | bytes 86024 | tf_op jit(solution)/shard_map/ppermute | solution.py:343
  37.0 0.6 collective-permute-start.10
  37.7 2.0 %collective-permute-done.12 = f32[56,128]{1,0:T(8,128)S(1)} collective-permute-done((f32[56,128]{1,0:T(8,128)S(1)}, f32[56,128]{1,0:T(8,128)S(1)}, u32[]{:S(2)}, u32[]{:S(2)}) %collective-permute-start.12) | collective-permute-done | bytes 28704 | tf_op jit(solution)/shard_map/ppermute | solution.py:343
  40.0 0.5 collective-permute-start.16
  40.5 1.4 %collective-permute-start.17 = (f32[264,512]{1,0:T(8,128)S(1)}, f32[264,512]{1,0:T(8,128)S(1)}, u32[]{:S(2)}, u32[]{:S(2)}) collective-permute-start(f32[264,512]{1,0:T(8,128)S(1)} %get-tuple-element.50.refs_2_), channel_id=1, source_target_pairs={{0,16},{8,24},{16,0},{24,8},{1,17},{9,25},{17,1},{25,9},{2,18},{10... | collective-permute-start | bytes 1622024 | tf_op jit(solution)/shard_map/ppermute | solution.py:343
  41.9 0.8 collective-permute-start.15
  42.7 0.5 collective-permute-start.14
  43.2 2.2 %collective-permute-start.13 = (f32[56,128]{1,0:T(8,128)S(1)}, f32[56,128]{1,0:T(8,128)S(1)}, u32[]{:S(2)}, u32[]{:S(2)}) collective-permute-start(f32[56,128]{1,0:T(8,128)S(1)} %bitcast_add_fusion), channel_id=1, source_target_pairs={{0,3},{1,2},{2,1},{3,0},{4,7},{5,6},{6,5},{7,4},{8,11},{9,10},{10,... | collective-permute-start | bytes 86024 | tf_op jit(solution)/shard_map/ppermute | solution.py:343
  45.4 0.9 %collective-permute-done.14 = f32[56,128]{1,0:T(8,128)S(1)} collective-permute-done((f32[56,128]{1,0:T(8,128)S(1)}, f32[56,128]{1,0:T(8,128)S(1)}, u32[]{:S(2)}, u32[]{:S(2)}) %collective-permute-start.14) | collective-permute-done | bytes 28704 | tf_op jit(solution)/shard_map/ppermute | solution.py:343
  46.3 1.4 %collective-permute-done.13 = f32[56,128]{1,0:T(8,128)S(1)} collective-permute-done((f32[56,128]{1,0:T(8,128)S(1)}, f32[56,128]{1,0:T(8,128)S(1)}, u32[]{:S(2)}, u32[]{:S(2)}) %collective-permute-start.13) | collective-permute-done | bytes 28704 | tf_op jit(solution)/shard_map/ppermute | solution.py:343
  47.8 4.4 %collective-permute-done.16.refs_4_ = f32[264,512]{1,0:T(8,128)S(1)} collective-permute-done((f32[264,512]{1,0:T(8,128)S(1)}, f32[264,512]{1,0:T(8,128)S(1)}, u32[]{:S(2)}, u32[]{:S(2)}) %collective-permute-start.16) | collective-permute-done | bytes 540704 | tf_op jit(solution)/shard_map/ppermute | solution.py:343
  52.2 1.6 %collective-permute-start.20 = (f32[56,128]{1,0:T(8,128)S(1)}, f32[56,128]{1,0:T(8,128)S(1)}, u32[]{:S(2)}, u32[]{:S(2)}) collective-permute-start(f32[56,128]{1,0:T(8,128)S(1)} %add_add_fusion), channel_id=1, source_target_pairs={{0,24},{8,16},{16,8},{24,0},{1,25},{9,17},{17,9},{25,1},{2,26},{10... | collective-permute-start | bytes 86024 | tf_op jit(solution)/shard_map/ppermute | solution.py:343
  53.8 0.8 collective-permute-start.19
  54.6 0.4 collective-permute-start.18
  55.0 0.9 %collective-permute-done.20 = f32[56,128]{1,0:T(8,128)S(1)} collective-permute-done((f32[56,128]{1,0:T(8,128)S(1)}, f32[56,128]{1,0:T(8,128)S(1)}, u32[]{:S(2)}, u32[]{:S(2)}) %collective-permute-start.20) | collective-permute-done | bytes 28704 | tf_op jit(solution)/shard_map/ppermute | solution.py:343
  55.8 0.7 collective-permute-done.19
  56.5 0.8 collective-permute-done.18
  57.4 4.6 %collective-permute-start.21 = (f32[224,128]{1,0:T(8,128)S(1)}, f32[224,128]{1,0:T(8,128)S(1)}, u32[]{:S(2)}, u32[]{:S(2)}) collective-permute-start(f32[224,128]{1,0:T(8,128)S(1)} %pad_maximum_fusion.2), channel_id=1, source_target_pairs={{0,4},{4,0},{1,5},{5,1},{2,6},{6,2},{3,7},{7,3},{8,12},{12,8},{9,1... | collective-permute-start | bytes 344072 | tf_op jit(solution)/shard_map/ppermute | solution.py:343
  62.0 0.4 collective-permute-start.22
  62.4 1.4 %collective-permute-start.23 = (f32[264,256]{1,0:T(8,128)S(1)}, f32[264,256]{1,0:T(8,128)S(1)}, u32[]{:S(2)}, u32[]{:S(2)}) collective-permute-start(f32[264,256]{1,0:T(8,128)S(1)} %get-tuple-element.58.refs_3_), channel_id=1, source_target_pairs={{0,16},{8,24},{16,0},{24,8},{1,17},{9,25},{17,1},{25,9},{2,18},{10... | collective-permute-start | bytes 811016 | tf_op jit(solution)/shard_map/ppermute | solution.py:343
  63.8 7.2 %shard_map.51.transform_ref = f32[256,256]{1,0:T(8,128)S(1)} custom-call(f32[448,128]{1,0:T(8,128)S(1)} %pad_maximum_fusion.packed_ref), custom_call_target="tpu_custom_call" | custom-call | tf_op jit(solution)/shard_map/pallas_call | solution.py:626
  71.1 0.9 %shard_map.52 = (f32[24,32,128]{2,1,0:T(8,128)S(1)}, f32[12,32,128]{2,1,0:T(8,128)S(1)}, f32[12,32,128]{2,1,0:T(8,128)S(1)}, f32[12,32,128]{2,1,0:T(8,128)S(1)},...) custom-call(f32[256,256]{1,0:T(8,128)S(1)} %shard_map.51.transform_ref, ...), custom_call_target="tpu_custom_call" | custom-call | tf_op jit(solution)/shard_map/pallas_call | solution.py:629
  72.0 0.7 collective-permute-start.28
  72.7 0.6 collective-permute-start.24
  73.3 0.5 collective-permute-start.25
  73.8 1.8 %collective-permute-start.26 = (f32[12,32,128]{2,1,0:T(8,128)S(1)}, f32[12,32,128]{2,1,0:T(8,128)S(1)}, u32[]{:S(2)}, u32[]{:S(2)}) collective-permute-start(f32[12,32,128]{2,1,0:T(8,128)S(1)} %get-tuple-element.62), channel_id=1, source_target_pairs={{0,12},{4,8},{8,4},{12,0},{16,28},{20,24},{24,20},{28,16},{1,13},{... | collective-permute-start | bytes 589832 | tf_op jit(solution)/shard_map/ppermute | solution.py:235
  75.9 3.3 %collective-permute-done.24.refs_1_ = f32[12,32,128]{2,1,0:T(8,128)S(1)} collective-permute-done((f32[12,32,128]{2,1,0:T(8,128)S(1)}, f32[12,32,128]{2,1,0:T(8,128)S(1)}, u32[]{:S(2)}, u32[]{:S(2)}) %collective-permute-start.24) | collective-permute-done | bytes 196640 | tf_op jit(solution)/shard_map/ppermute | solution.py:235
  79.5 4.2 %collective-permute-done.26.refs_3_ = f32[12,32,128]{2,1,0:T(8,128)S(1)} collective-permute-done((f32[12,32,128]{2,1,0:T(8,128)S(1)}, f32[12,32,128]{2,1,0:T(8,128)S(1)}, u32[]{:S(2)}, u32[]{:S(2)}) %collective-permute-start.26) | collective-permute-done | bytes 196640 | tf_op jit(solution)/shard_map/ppermute | solution.py:235
  83.7 0.5 collective-permute-done.27.refs_4_
  84.2 1.7 %shard_map.53 = f32[3072,128]{1,0:T(8,128)} custom-call(f32[24,32,128]{2,1,0:T(8,128)S(1)} %get-tuple-element.59.refs_0_, f32[12,32,128]{2,1,0:T(8,128)S(1)} %collective-permute-done.24.refs_1_, f32[12,32,128]{2,1,0:T(8,128)S(1)} %collective-permute-done.25.refs_2_, f32[12,32,128]{2,1,0:T(8,128)S(1)} %collective-permute-done.26.refs_3_, ...), custom_call_target="tpu_custom_call" | custom-call | tf_op jit(solution)/shard_map/pallas_call | solution.py:594
  (36 shorter events, 1.4 us)
Async XLA Ops:
  0.0 1.4 %copy-start = (f32[32,3,32,128]{3,2,1,0:T(8,128)S(1)}, f32[32,3,32,128]{3,2,1,0:T(8,128)}, u32[]{:S(2)}) copy-start(f32[32,3,32,128]{3,2,1,0:T(8,128)} %bottom_ref.1) | copy-start | bytes 4718596
  1.8 7.0 %collective-permute-start = (f32[9,32,128]{2,1,0:T(8,128)S(1)}, f32[9,32,128]{2,1,0:T(8,128)S(1)}, u32[]{:S(2)}, u32[]{:S(2)}) collective-permute-start(f32[9,32,128]{2,1,0:T(8,128)S(1)} %get-tuple-element.35), channel_id=1, source_target_pairs={{1,2},{2,1},{5,6},{6,5},{9,10},{10,9},{13,14},{14,13},{17,18},{18,... | collective-permute-start | bytes 442376 | tf_op jit(solution)/shard_map/ppermute | solution.py:199
  2.4 8.0 %collective-permute-start.1 = (f32[9,32,128]{2,1,0:T(8,128)S(1)}, f32[9,32,128]{2,1,0:T(8,128)S(1)}, u32[]{:S(2)}, u32[]{:S(2)}) collective-permute-start(f32[9,32,128]{2,1,0:T(8,128)S(1)} %get-tuple-element.36), channel_id=1, source_target_pairs={{0,1},{2,3},{1,0},{3,2},{4,5},{6,7},{5,4},{7,6},{8,9},{10,11},{9,8... | collective-permute-start | bytes 442376 | tf_op jit(solution)/shard_map/ppermute | solution.py:199
  8.8 16.3 %copy-start.1 = (f32[1,768]{1,0:T(1,128)S(1)}, f32[1,768]{1,0:T(1,128)}, u32[]{:S(2)}) copy-start(f32[1,768]{1,0:T(1,128)} %values_ref.1) | copy-start | bytes 9220
  8.8 16.3 %copy-start.2 = (f32[1,768]{1,0:T(1,128)S(1)}, f32[1,768]{1,0:T(1,128)}, u32[]{:S(2)}) copy-start(f32[1,768]{1,0:T(1,128)} %precision_ref.1) | copy-start | bytes 9220
  8.8 16.3 %copy-start.3 = (s32[1,768]{1,0:T(1,128)S(1)}, s32[1,768]{1,0:T(1,128)}, u32[]{:S(2)}) copy-start(s32[1,768]{1,0:T(1,128)} %index_ref.1) | copy-start | bytes 9220
  11.3 6.2 %collective-permute-start.2 = (f32[12,32,128]{2,1,0:T(8,128)S(1)}, f32[12,32,128]{2,1,0:T(8,128)S(1)}, u32[]{:S(2)}, u32[]{:S(2)}) collective-permute-start(f32[12,32,128]{2,1,0:T(8,128)S(1)} %get-tuple-element.38), channel_id=1, source_target_pairs={{0,8},{4,12},{8,0},{12,4},{16,24},{20,28},{24,16},{28,20},{1,9},{5... | collective-permute-start | bytes 589832 | tf_op jit(solution)/shard_map/ppermute | solution.py:235
  12.6 10.2 %collective-permute-start.3 = (f32[12,32,128]{2,1,0:T(8,128)S(1)}, f32[12,32,128]{2,1,0:T(8,128)S(1)}, u32[]{:S(2)}, u32[]{:S(2)}) collective-permute-start(f32[12,32,128]{2,1,0:T(8,128)S(1)} %get-tuple-element.39), channel_id=1, source_target_pairs={{0,16},{4,20},{8,24},{12,28},{16,0},{20,4},{24,8},{28,12},{1,17},{... | collective-permute-start | bytes 589832 | tf_op jit(solution)/shard_map/ppermute | solution.py:235
  13.9 12.0 %collective-permute-start.4 = (f32[12,32,128]{2,1,0:T(8,128)S(1)}, f32[12,32,128]{2,1,0:T(8,128)S(1)}, u32[]{:S(2)}, u32[]{:S(2)}) collective-permute-start(f32[12,32,128]{2,1,0:T(8,128)S(1)} %get-tuple-element.40), channel_id=1, source_target_pairs={{0,24},{4,28},{8,16},{12,20},{16,8},{20,12},{24,0},{28,4},{1,25},{... | collective-permute-start | bytes 589832 | tf_op jit(solution)/shard_map/ppermute | solution.py:235
  14.0 14.5 %collective-permute-start.5 = (f32[12,32,128]{2,1,0:T(8,128)S(1)}, f32[12,32,128]{2,1,0:T(8,128)S(1)}, u32[]{:S(2)}, u32[]{:S(2)}) collective-permute-start(f32[12,32,128]{2,1,0:T(8,128)S(1)} %get-tuple-element.41), channel_id=1, source_target_pairs={{0,12},{4,8},{8,4},{12,0},{16,28},{20,24},{24,20},{28,16},{1,13},{... | collective-permute-start | bytes 589832 | tf_op jit(solution)/shard_map/ppermute | solution.py:235
  17.5 14.5 %collective-permute-start.6 = (f32[12,32,128]{2,1,0:T(8,128)S(1)}, f32[12,32,128]{2,1,0:T(8,128)S(1)}, u32[]{:S(2)}, u32[]{:S(2)}) collective-permute-start(f32[12,32,128]{2,1,0:T(8,128)S(1)} %get-tuple-element.42), channel_id=1, source_target_pairs={{0,20},{4,16},{8,28},{12,24},{16,4},{20,0},{24,12},{28,8},{1,21},{... | collective-permute-start | bytes 589832 | tf_op jit(solution)/shard_map/ppermute | solution.py:235
  17.6 14.4 %collective-permute-start.7 = (f32[12,32,128]{2,1,0:T(8,128)S(1)}, f32[12,32,128]{2,1,0:T(8,128)S(1)}, u32[]{:S(2)}, u32[]{:S(2)}) collective-permute-start(f32[12,32,128]{2,1,0:T(8,128)S(1)} %get-tuple-element.43), channel_id=1, source_target_pairs={{0,28},{4,24},{8,20},{12,16},{16,12},{20,8},{24,4},{28,0},{1,29},{... | collective-permute-start | bytes 589832 | tf_op jit(solution)/shard_map/ppermute | solution.py:235
  22.8 9.1 %collective-permute-start.8 = (f32[12,32,128]{2,1,0:T(8,128)S(1)}, f32[12,32,128]{2,1,0:T(8,128)S(1)}, u32[]{:S(2)}, u32[]{:S(2)}) collective-permute-start(f32[12,32,128]{2,1,0:T(8,128)S(1)} %get-tuple-element.44), channel_id=1, source_target_pairs={{0,4},{4,0},{8,12},{12,8},{16,20},{20,16},{24,28},{28,24},{1,5},{5... | collective-permute-start | bytes 589832 | tf_op jit(solution)/shard_map/ppermute | solution.py:235
  33.5 1.4 %collective-permute-start.9 = (f32[224,128]{1,0:T(8,128)S(1)}, f32[224,128]{1,0:T(8,128)S(1)}, u32[]{:S(2)}, u32[]{:S(2)}) collective-permute-start(f32[224,128]{1,0:T(8,128)S(1)} %constant_dynamic-slice_fusion), channel_id=1, source_target_pairs={{0,4},{4,0},{1,5},{5,1},{2,6},{6,2},{3,7},{7,3},{8,12},{12,8},{9,1... | collective-permute-start | bytes 344072 | tf_op jit(solution)/shard_map/ppermute | solution.py:343
  34.9 2.8 %collective-permute-start.11 = (f32[56,128]{1,0:T(8,128)S(1)}, f32[56,128]{1,0:T(8,128)S(1)}, u32[]{:S(2)}, u32[]{:S(2)}) collective-permute-start(f32[56,128]{1,0:T(8,128)S(1)} %get-tuple-element.71), channel_id=1, source_target_pairs={{0,16},{8,24},{16,0},{24,8},{1,17},{9,25},{17,1},{25,9},{2,18},{10... | collective-permute-start | bytes 86024 | tf_op jit(solution)/shard_map/ppermute | solution.py:343
  36.1 3.6 %collective-permute-start.12 = (f32[56,128]{1,0:T(8,128)S(1)}, f32[56,128]{1,0:T(8,128)S(1)}, u32[]{:S(2)}, u32[]{:S(2)}) collective-permute-start(f32[56,128]{1,0:T(8,128)S(1)} %get-tuple-element.72), channel_id=1, source_target_pairs={{0,24},{8,16},{16,8},{24,0},{1,25},{9,17},{17,9},{25,1},{2,26},{10... | collective-permute-start | bytes 86024 | tf_op jit(solution)/shard_map/ppermute | solution.py:343
  37.0 3.0 %collective-permute-start.10 = (f32[56,128]{1,0:T(8,128)S(1)}, f32[56,128]{1,0:T(8,128)S(1)}, u32[]{:S(2)}, u32[]{:S(2)}) collective-permute-start(f32[56,128]{1,0:T(8,128)S(1)} %get-tuple-element.73), channel_id=1, source_target_pairs={{0,8},{8,0},{16,24},{24,16},{1,9},{9,1},{17,25},{25,17},{2,10},{10... | collective-permute-start | bytes 86024 | tf_op jit(solution)/shard_map/ppermute | solution.py:343
  40.0 12.2 %collective-permute-start.16 = (f32[264,512]{1,0:T(8,128)S(1)}, f32[264,512]{1,0:T(8,128)S(1)}, u32[]{:S(2)}, u32[]{:S(2)}) collective-permute-start(f32[264,512]{1,0:T(8,128)S(1)} %get-tuple-element.49.refs_0_), channel_id=1, source_target_pairs={{0,8},{8,0},{16,24},{24,16},{1,9},{9,1},{17,25},{25,17},{2,10},{10... | collective-permute-start | bytes 1622024 | tf_op jit(solution)/shard_map/ppermute | solution.py:343
  40.5 11.7 %collective-permute-start.17 = (f32[264,512]{1,0:T(8,128)S(1)}, f32[264,512]{1,0:T(8,128)S(1)}, u32[]{:S(2)}, u32[]{:S(2)}) collective-permute-start(f32[264,512]{1,0:T(8,128)S(1)} %get-tuple-element.50.refs_2_), channel_id=1, source_target_pairs={{0,16},{8,24},{16,0},{24,8},{1,17},{9,25},{17,1},{25,9},{2,18},{10... | collective-permute-start | bytes 1622024 | tf_op jit(solution)/shard_map/ppermute | solution.py:343
  41.9 3.6 %collective-permute-start.15 = (f32[56,128]{1,0:T(8,128)S(1)}, f32[56,128]{1,0:T(8,128)S(1)}, u32[]{:S(2)}, u32[]{:S(2)}) collective-permute-start(f32[56,128]{1,0:T(8,128)S(1)} %bitcast_add_fusion), channel_id=1, source_target_pairs={{0,1},{1,0},{2,3},{3,2},{4,5},{5,4},{6,7},{7,6},{8,9},{9,8},{10,11... | collective-permute-start | bytes 86024 | tf_op jit(solution)/shard_map/ppermute | solution.py:343
  42.7 3.6 %collective-permute-start.14 = (f32[56,128]{1,0:T(8,128)S(1)}, f32[56,128]{1,0:T(8,128)S(1)}, u32[]{:S(2)}, u32[]{:S(2)}) collective-permute-start(f32[56,128]{1,0:T(8,128)S(1)} %bitcast_add_fusion), channel_id=1, source_target_pairs={{0,2},{1,3},{2,0},{3,1},{4,6},{5,7},{6,4},{7,5},{8,10},{9,11},{10,... | collective-permute-start | bytes 86024 | tf_op jit(solution)/shard_map/ppermute | solution.py:343
  43.2 4.6 %collective-permute-start.13 = (f32[56,128]{1,0:T(8,128)S(1)}, f32[56,128]{1,0:T(8,128)S(1)}, u32[]{:S(2)}, u32[]{:S(2)}) collective-permute-start(f32[56,128]{1,0:T(8,128)S(1)} %bitcast_add_fusion), channel_id=1, source_target_pairs={{0,3},{1,2},{2,1},{3,0},{4,7},{5,6},{6,5},{7,4},{8,11},{9,10},{10,... | collective-permute-start | bytes 86024 | tf_op jit(solution)/shard_map/ppermute | solution.py:343
  52.2 3.6 %collective-permute-start.20 = (f32[56,128]{1,0:T(8,128)S(1)}, f32[56,128]{1,0:T(8,128)S(1)}, u32[]{:S(2)}, u32[]{:S(2)}) collective-permute-start(f32[56,128]{1,0:T(8,128)S(1)} %add_add_fusion), channel_id=1, source_target_pairs={{0,24},{8,16},{16,8},{24,0},{1,25},{9,17},{17,9},{25,1},{2,26},{10... | collective-permute-start | bytes 86024 | tf_op jit(solution)/shard_map/ppermute | solution.py:343
  53.8 2.7 %collective-permute-start.19 = (f32[56,128]{1,0:T(8,128)S(1)}, f32[56,128]{1,0:T(8,128)S(1)}, u32[]{:S(2)}, u32[]{:S(2)}) collective-permute-start(f32[56,128]{1,0:T(8,128)S(1)} %add_add_fusion), channel_id=1, source_target_pairs={{0,16},{8,24},{16,0},{24,8},{1,17},{9,25},{17,1},{25,9},{2,18},{10... | collective-permute-start | bytes 86024 | tf_op jit(solution)/shard_map/ppermute | solution.py:343
  54.6 2.7 %collective-permute-start.18 = (f32[56,128]{1,0:T(8,128)S(1)}, f32[56,128]{1,0:T(8,128)S(1)}, u32[]{:S(2)}, u32[]{:S(2)}) collective-permute-start(f32[56,128]{1,0:T(8,128)S(1)} %add_add_fusion), channel_id=1, source_target_pairs={{0,8},{8,0},{16,24},{24,16},{1,9},{9,1},{17,25},{25,17},{2,10},{10... | collective-permute-start | bytes 86024 | tf_op jit(solution)/shard_map/ppermute | solution.py:343
  57.4 6.4 %collective-permute-start.21 = (f32[224,128]{1,0:T(8,128)S(1)}, f32[224,128]{1,0:T(8,128)S(1)}, u32[]{:S(2)}, u32[]{:S(2)}) collective-permute-start(f32[224,128]{1,0:T(8,128)S(1)} %pad_maximum_fusion.2), channel_id=1, source_target_pairs={{0,4},{4,0},{1,5},{5,1},{2,6},{6,2},{3,7},{7,3},{8,12},{12,8},{9,1... | collective-permute-start | bytes 344072 | tf_op jit(solution)/shard_map/ppermute | solution.py:343
  62.0 9.1 %collective-permute-start.22 = (f32[264,256]{1,0:T(8,128)S(1)}, f32[264,256]{1,0:T(8,128)S(1)}, u32[]{:S(2)}, u32[]{:S(2)}) collective-permute-start(f32[264,256]{1,0:T(8,128)S(1)} %get-tuple-element.56.refs_1_), channel_id=1, source_target_pairs={{0,8},{8,0},{16,24},{24,16},{1,9},{9,1},{17,25},{25,17},{2,10},{10... | collective-permute-start | bytes 811016 | tf_op jit(solution)/shard_map/ppermute | solution.py:343
  62.4 8.7 %collective-permute-start.23 = (f32[264,256]{1,0:T(8,128)S(1)}, f32[264,256]{1,0:T(8,128)S(1)}, u32[]{:S(2)}, u32[]{:S(2)}) collective-permute-start(f32[264,256]{1,0:T(8,128)S(1)} %get-tuple-element.58.refs_3_), channel_id=1, source_target_pairs={{0,16},{8,24},{16,0},{24,8},{1,17},{9,25},{17,1},{25,9},{2,18},{10... | collective-permute-start | bytes 811016 | tf_op jit(solution)/shard_map/ppermute | solution.py:343
  72.0 12.2 %collective-permute-start.28 = (f32[24,32,128]{2,1,0:T(8,128)S(1)}, f32[24,32,128]{2,1,0:T(8,128)S(1)}, u32[]{:S(2)}, u32[]{:S(2)}) collective-permute-start(f32[24,32,128]{2,1,0:T(8,128)S(1)} %get-tuple-element.64), channel_id=1, source_target_pairs={{0,4},{4,0},{8,12},{12,8},{16,20},{20,16},{24,28},{28,24},{1,5},{5... | collective-permute-start | bytes 1179656 | tf_op jit(solution)/shard_map/ppermute | solution.py:235
  72.7 6.5 %collective-permute-start.24 = (f32[12,32,128]{2,1,0:T(8,128)S(1)}, f32[12,32,128]{2,1,0:T(8,128)S(1)}, u32[]{:S(2)}, u32[]{:S(2)}) collective-permute-start(f32[12,32,128]{2,1,0:T(8,128)S(1)} %get-tuple-element.60), channel_id=1, source_target_pairs={{0,8},{4,12},{8,0},{12,4},{16,24},{20,28},{24,16},{28,20},{1,9},{5... | collective-permute-start | bytes 589832 | tf_op jit(solution)/shard_map/ppermute | solution.py:235
  73.3 6.1 %collective-permute-start.25 = (f32[12,32,128]{2,1,0:T(8,128)S(1)}, f32[12,32,128]{2,1,0:T(8,128)S(1)}, u32[]{:S(2)}, u32[]{:S(2)}) collective-permute-start(f32[12,32,128]{2,1,0:T(8,128)S(1)} %get-tuple-element.61), channel_id=1, source_target_pairs={{0,16},{4,20},{8,24},{12,28},{16,0},{20,4},{24,8},{28,12},{1,17},{... | collective-permute-start | bytes 589832 | tf_op jit(solution)/shard_map/ppermute | solution.py:235
  73.8 9.8 %collective-permute-start.26 = (f32[12,32,128]{2,1,0:T(8,128)S(1)}, f32[12,32,128]{2,1,0:T(8,128)S(1)}, u32[]{:S(2)}, u32[]{:S(2)}) collective-permute-start(f32[12,32,128]{2,1,0:T(8,128)S(1)} %get-tuple-element.62), channel_id=1, source_target_pairs={{0,12},{4,8},{8,4},{12,0},{16,28},{20,24},{24,20},{28,16},{1,13},{... | collective-permute-start | bytes 589832 | tf_op jit(solution)/shard_map/ppermute | solution.py:235
  75.6 8.5 %collective-permute-start.27 = (f32[12,32,128]{2,1,0:T(8,128)S(1)}, f32[12,32,128]{2,1,0:T(8,128)S(1)}, u32[]{:S(2)}, u32[]{:S(2)}) collective-permute-start(f32[12,32,128]{2,1,0:T(8,128)S(1)} %get-tuple-element.63), channel_id=1, source_target_pairs={{0,20},{4,16},{8,28},{12,24},{16,4},{20,0},{24,12},{28,8},{1,21},{... | collective-permute-start | bytes 589832 | tf_op jit(solution)/shard_map/ppermute | solution.py:235
